TPU v7x, 256 devices: a whole 4x4x8 slice. The times are simulated.
256 devices in a mesh: clip: 4 (over y), frame: 8 (over x, core), tensor: 8 (over z).
Axes of the slice: x: 4, y: 4, z: 8, core: 2. Of those that a mesh axis runs over, the one named last changes fastest.
Arguments:
- spatial_qkv: bfloat16 [4, 16, 128, 3, 3072], P('clip', 'frame', None, None, 'tensor'), may hold values from -16 to 16
- w_qkv: bfloat16 [3072, 24, 3, 128], P(('clip', 'frame'), 'tensor'), may hold values from -0.109375 to 0.109375
- w_out: bfloat16 [24, 128, 3072], P('tensor', None, ('clip', 'frame')), may hold values from -0.109375 to 0.109375
- out_grad: bfloat16 [4, 16, 128, 3072], P('clip', 'frame', None, 'tensor'), may hold values from -6 to 6
- frame_clip: int32 [4, 16], P('clip'), may hold values from 0 to 7, never falling along the last dimension, each value on 1 to 4 neighbouring positions
- clip_patches: int32 [4, 8], P('clip'), may hold values from 32 to 128, as said below
Outputs:
- block_out: bfloat16 [4, 16, 128, 3072], P('clip', 'frame', None, 'tensor')
- qkv_grad: bfloat16 [4, 16, 128, 3, 3072], P('clip', 'frame', None, None, 'tensor')
- w_qkv_grad: float32 [3072, 24, 3, 128], P(('clip', 'frame'), 'tensor')
- w_out_grad: float32 [24, 128, 3072], P('tensor', None, ('clip', 'frame'))
Inputs may be any that keep to these rules, and one draw needn't show every extreme that they name: `frame_clip`: within a group, the frames of one clip stand together, clip numbers never fall, every one of the 8 clips has 1 to 4 frames and one has exactly 4. `clip_patches`: at least 32; 128 for one clip of every group.
All inputs are finite; a program needn't handle non-finite values.
Results may differ from a plain program's by a relative error of at most 0.022.
Values may be sent and summed in bfloat16 or wider, within the bound.
No kernel may reach another device: no remote copies, remote signals or barrier semaphores. Data moves between devices by JAX's collectives and lax.ppermute only.
A program may use at most 128 MiB of HBM per device.

v0:
```python
import math

import jax
import jax.numpy as jnp
from jax import lax
from jax.experimental import pallas as pl
from jax.experimental.pallas import tpu as pltpu
from jax.sharding import PartitionSpec as P

HD = 128
SCALE = 1.0 / math.sqrt(HD)
BF = jnp.bfloat16
F32 = jnp.float32
NT = (((1,), (1,)), ((), ()))
TN = (((0,), (0,)), ((), ()))


def dot(a, b, dims=(((1,), (0,)), ((), ()))):
    return lax.dot_general(a, b, dims, preferred_element_type=F32)


def softmax(query, keys, mask):
    scores = jnp.where(mask, dot(query, keys, NT) * SCALE, -1e30)
    expo = jnp.exp(scores - jnp.max(scores, axis=-1, keepdims=True))
    return expo / jnp.sum(expo, axis=-1, keepdims=True)


def attention_grads(query, keys, values, probs, cotangent):
    d_values = dot(probs.astype(BF), cotangent, TN).astype(BF)
    d_probs = dot(cotangent, values, NT).astype(BF).astype(F32)
    inner = jnp.sum(probs * d_probs, axis=-1, keepdims=True)
    d_scores = (probs * (d_probs - inner) * SCALE).astype(BF)
    return dot(d_scores, keys).astype(BF), dot(d_scores, query, TN).astype(BF), d_values


def spatial_forward(count_ref, qkv_ref, cot_ref, out_ref):
    frames, _, patches, width = qkv_ref.shape
    owners = out_ref.shape[0]
    block = patches // owners
    for f in range(frames):
        count = count_ref[f]
        keys_live = lax.broadcasted_iota(jnp.int32, (patches, patches), 1) < count
        rows_live = lax.broadcasted_iota(jnp.int32, (patches, 1), 0) < count
        pieces = []
        for h in range(width // HD):
            cols = slice(h * HD, (h + 1) * HD)
            probs = softmax(qkv_ref[f, 0, :, cols], qkv_ref[f, 1, :, cols], keys_live)
            mixed = dot(probs.astype(BF), qkv_ref[f, 2, :, cols])
            pieces.append(jnp.where(rows_live, mixed, 0.0).astype(BF))
        whole = jnp.concatenate(pieces, axis=1)
        gated = jnp.where(rows_live, cot_ref[f].astype(F32), 0.0).astype(BF)
        for s in range(owners):
            out_ref[s, 0, f] = whole[s * block : (s + 1) * block]
            out_ref[s, 1, f] = gated[s * block : (s + 1) * block]


def spatial_backward(count_ref, qkv_ref, cot_ref, sums_ref, out_ref, grad_ref):
    frames, _, patches, width = qkv_ref.shape
    owners = sums_ref.shape[0]
    for f in range(frames):
        count = count_ref[f]
        keys_live = lax.broadcasted_iota(jnp.int32, (patches, patches), 1) < count
        rows_live = lax.broadcasted_iota(jnp.int32, (patches, 1), 0) < count
        projected = jnp.concatenate([sums_ref[s, 0, f] for s in range(owners)], axis=0)
        back = jnp.concatenate([sums_ref[s, 1, f] for s in range(owners)], axis=0)
        d_spatial = cot_ref[f].astype(F32) + back.astype(F32)
        d_mixed = jnp.where(rows_live, d_spatial, 0.0).astype(BF)
        for h in range(width // HD):
            cols = slice(h * HD, (h + 1) * HD)
            query, keys, values = (qkv_ref[f, i, :, cols] for i in range(3))
            probs = softmax(query, keys, keys_live)
            mixed = dot(probs.astype(BF), values).astype(BF).astype(F32)
            total = mixed + projected[:, cols].astype(F32)
            out_ref[f, :, cols] = jnp.where(rows_live, total, 0.0).astype(BF)
            grads = attention_grads(query, keys, values, probs, d_mixed[:, cols])
            for i in range(3):
                grad_ref[f, i, :, cols] = grads[i]


def assemble_kernel(ranks, place_ref, *refs):
    blocks, refs = refs[: 2 * ranks], refs[2 * ranks :]
    feat_ref, gated_ref, own_ref, other_ref, flip_ref, sem = refs
    me, core = place_ref[3], place_ref[2]
    width = feat_ref.shape[1] // ranks
    copies = []
    for a, whole in enumerate((feat_ref, gated_ref)):
        for d in range(ranks):
            start = pl.multiple_of(lax.rem(me + d, ranks) * width, HD)
            i = a * ranks + d
            copies.append(
                pltpu.make_async_copy(blocks[i], whole.at[:, pl.ds(start, width)], sem.at[i])
            )
    for copy in copies:
        copy.start()
    for copy in copies:
        copy.wait()
    pieces = 32
    rows = feat_ref.shape[1] // pieces
    for a, whole in enumerate((feat_ref, gated_ref)):
        for z in range(ranks):
            part = slice(z * width, (z + 1) * width)
            flip_ref[part, :] = whole[:, part].T
        for i in range(pieces // 2):
            to = slice(i * rows, (i + 1) * rows)
            own_ref[a, to] = flip_ref[pl.ds(pl.multiple_of((2 * i + core) * rows, 16), rows), :]
            other_ref[a, to] = flip_ref[pl.ds(pl.multiple_of((2 * i + 1 - core) * rows, 16), rows), :]


def temporal_kernel(heads, row_key_ref, col_key_ref, feat_ref, gated_ref, _, *refs):
    w_hbm, sums_hbm, both_ref, w_ref, sums_ref, w_sem, out_sem = refs
    width = heads * HD
    slots = 4 * heads
    ranks, owners, _, rows, _ = sums_ref.shape
    loads = [
        pltpu.make_async_copy(w_hbm.at[i], w_ref.at[:, i * HD : (i + 1) * HD], w_sem.at[i])
        for i in range(slots)
    ]
    for copy in loads:
        copy.start()
    mask = row_key_ref[...] == col_key_ref[...]
    query, keys, values = [], [], []
    for h in range(heads):
        for i in range(3):
            loads[3 * h + i].wait()
        qkv = dot(feat_ref[...], w_ref[:, 3 * h * HD : 3 * (h + 1) * HD]).astype(BF)
        for i, parts in enumerate((query, keys, values)):
            parts.append(qkv[:, i * HD : (i + 1) * HD])
    for h in range(heads):
        loads[3 * heads + h].wait()
    cotangent = dot(gated_ref[...], w_ref[:, 3 * width :]).astype(BF)
    cotangent = [cotangent[:, h * HD : (h + 1) * HD] for h in range(heads)]
    each = range(heads)
    probs = [softmax(query[h], keys[h], mask) for h in each]
    for h in each:
        grads = attention_grads(query[h], keys[h], values[h], probs[h], cotangent[h])
        for i in range(3):
            start = (3 * h + i) * HD
            both_ref[:, start : start + HD] = grads[i]
        start = 3 * width + h * HD
        both_ref[:, start : start + HD] = dot(probs[h].astype(BF), values[h]).astype(BF)
    stores = []
    for z in range(ranks):
        part = slice(z * width, (z + 1) * width)
        projected = dot(both_ref[:, 3 * width :], w_ref[part, 3 * width :], NT).astype(BF)
        back = dot(both_ref[:, : 3 * width], w_ref[part, : 3 * width], NT).astype(BF)
        for s in range(owners):
            sums_ref[z, s, 0] = projected[s * rows : (s + 1) * rows]
            sums_ref[z, s, 1] = back[s * rows : (s + 1) * rows]
        stores.append(pltpu.make_async_copy(sums_ref.at[z], sums_hbm.at[z], out_sem.at[z]))
        stores[-1].start()
    for copy in stores:
        copy.wait()


def weight_grad_kernel(step, place_ref, own_ref, pair_ref, both_ref, pair_both_ref, out_ref):
    at_clip, at_x, core = place_ref[0], place_ref[1], place_ref[2]
    n, slots, rows, _ = out_ref.shape
    wide = both_ref.shape[1] * 3 // 4
    starts = []
    for r in range(n):
        clip = lax.rem(at_clip + jnp.where(core == 0, r, step), n)
        x = lax.rem(at_x + jnp.where(core == 0, step, r), n)
        starts.append(pl.multiple_of((clip * n + x) * rows, 16))
    for a, cols in ((0, slice(0, wide)), (1, slice(wide, 4 * wide // 3))):
        left = jnp.concatenate(
            [
                jnp.concatenate([ref[a, pl.ds(start, rows), :] for start in starts], axis=0)
                for ref in (own_ref, pair_ref)
            ],
            axis=1,
        )
        right = jnp.concatenate([both_ref[:, cols], pair_both_ref[:, cols]], axis=0)
        total = dot(left, right).astype(BF)
        for r in range(n):
            for s in range(total.shape[1] // HD):
                part = total[r * rows : (r + 1) * rows, s * HD : (s + 1) * HD]
                out_ref[r, a * (slots * 3 // 4) + s] = part


def shift(value, axis, step, size):
    return lax.ppermute(value, axis, [(i, (i + step) % size) for i in range(size)])


def pair_swap(value):
    return lax.ppermute(value, "frame", [(i, i ^ 1) for i in range(8)])


def spread(value, step, second):
    pairs = []
    for clip in range(4):
        for x in range(4):
            for core in range(2):
                to_clip, to_x = clip, x
                if (core == 0) != second:
                    to_x = (x + step) % 4
                else:
                    to_clip = (clip + step) % 4
                pairs.append((clip * 8 + x * 2 + core, to_clip * 8 + to_x * 2 + core))
    return lax.ppermute(value, ("clip", "frame"), pairs)


def ring_gather(value, axis, size, last_forward):
    found = {0: value}
    up = down = value
    for step in range(1, size // 2):
        up = shift(up, axis, 1, size)
        down = shift(down, axis, -1, size)
        found[size - step], found[step] = up, down
    found[size // 2] = shift(up, axis, 1, size) if last_forward else shift(down, axis, -1, size)
    return [found[d] for d in range(size)]


def add(*values):
    return sum(v.astype(F32) for v in values)


def body(spatial_qkv, w_qkv, w_out, out_grad, frame_clip, clip_patches):
    ranks = lax.axis_size("frame")
    width_ranks = lax.axis_size("tensor")
    at_frame = lax.axis_index("frame").astype(jnp.int32)
    at_clip = lax.axis_index("clip").astype(jnp.int32)
    at_width = lax.axis_index("tensor").astype(jnp.int32)
    clip_row = frame_clip[0]
    counts = clip_patches[0]
    total_frames = clip_row.shape[0]
    _, frames, patches, _, width = spatial_qkv.shape
    heads = width // HD
    block = patches // ranks
    rows_t = total_frames * block
    model = width * width_ranks
    slots = 4 * heads

    w_rows = w_qkv.shape[0]
    w_own = jnp.concatenate(
        [w_qkv.transpose(1, 2, 0, 3).reshape(3 * heads, w_rows, HD), w_out.transpose(0, 2, 1)],
        axis=0,
    )
    w_all = lax.all_gather(w_own, ("clip", "frame"), axis=1, tiled=True)

    own_clips = lax.dynamic_slice_in_dim(clip_row, at_frame * frames, frames, 0)
    member = own_clips[:, None] == jnp.arange(counts.shape[0], dtype=jnp.int32)[None, :]
    live = jnp.sum(jnp.where(member, counts[None, :], 0), axis=1).astype(jnp.int32)
    keys = (clip_row[:, None] * block + jnp.arange(block, dtype=jnp.int32)[None, :]).reshape(rows_t)

    qkv = spatial_qkv[0].transpose(0, 2, 1, 3)
    cot = out_grad[0]
    smem = pl.BlockSpec(memory_space=pltpu.SMEM)
    vmem = pl.BlockSpec(memory_space=pltpu.VMEM)
    hbm = pl.BlockSpec(memory_space=pltpu.HBM)
    sent = pl.pallas_call(
        spatial_forward,
        out_shape=jax.ShapeDtypeStruct((ranks, 2, frames, block, width), BF),
        in_specs=[smem, vmem, vmem],
        out_specs=vmem,
        compiler_params=pltpu.CompilerParams(vmem_limit_bytes=24 * 2**20),
    )(live, qkv, cot)
    cols = lax.all_to_all(sent, "frame", split_axis=0, concat_axis=0, tiled=True)
    blocks = []
    for a in range(2):
        rows = cols[:, a].reshape(rows_t, width)
        blocks += ring_gather(rows, "tensor", width_ranks, a == 0)

    place = jnp.stack([at_clip, at_frame // 2, at_frame % 2, at_width])
    halves = jax.ShapeDtypeStruct((2, model // 2, rows_t), BF)
    wide = jax.ShapeDtypeStruct((rows_t, model), BF)
    feats, gated, own_flip, other_flip = pl.pallas_call(
        lambda *refs: assemble_kernel(width_ranks, *refs),
        out_shape=[wide, wide, halves, halves],
        in_specs=[smem] + [hbm] * (2 * width_ranks),
        out_specs=[vmem] * 4,
        scratch_shapes=[
            pltpu.VMEM((model, rows_t), BF),
            pltpu.SemaphoreType.DMA((2 * width_ranks,)),
        ],
        compiler_params=pltpu.CompilerParams(vmem_limit_bytes=58 * 2**20),
    )(place, *blocks)
    pair_flip = pair_swap(other_flip)

    sums_shape = (width_ranks, ranks, 2, frames * block, width)
    sums, both = pl.pallas_call(
        lambda *refs: temporal_kernel(heads, *refs),
        out_shape=[
            jax.ShapeDtypeStruct(sums_shape, BF),
            jax.ShapeDtypeStruct((rows_t, 4 * width), BF),
        ],
        in_specs=[vmem] * 4 + [hbm] * 2,
        out_specs=[hbm, vmem],
        scratch_shapes=[
            pltpu.VMEM((model, 4 * width), BF),
            pltpu.VMEM(sums_shape, BF),
            pltpu.SemaphoreType.DMA((slots,)),
            pltpu.SemaphoreType.DMA((width_ranks,)),
        ],
        compiler_params=pltpu.CompilerParams(vmem_limit_bytes=56 * 2**20),
    )(keys[:, None], keys[None, :], feats, gated, pair_flip, w_all)

    own_sums = lax.psum_scatter(sums, "tensor", scatter_dimension=0, tiled=True)[0]
    pair_both = pair_swap(both)
    parts = {}
    for step in (2, 1, 3, 0):
        parts[step] = pl.pallas_call(
            lambda *refs, step=step: weight_grad_kernel(step, *refs),
            out_shape=jax.ShapeDtypeStruct((4, slots, w_rows, HD), BF),
            in_specs=[smem] + [vmem] * 4,
            out_specs=vmem,
            compiler_params=pltpu.CompilerParams(vmem_limit_bytes=24 * 2**20),
        )(place, own_flip, pair_flip, both, pair_both)
    arrived = [parts[0]] + [spread(parts[step], step, False) for step in (2, 1, 3)]
    partial = [add(*(part[i] for part in arrived)).astype(BF) for i in range(4)]
    grads = add(partial[0], *(spread(partial[step], step, True) for step in (2, 1, 3)))

    row_sums = lax.all_to_all(own_sums, "frame", split_axis=0, concat_axis=0, tiled=True)
    row_sums = row_sums.reshape(ranks, 2, frames, block, width)
    block_out, qkv_grad = pl.pallas_call(
        spatial_backward,
        out_shape=[
            jax.ShapeDtypeStruct((frames, patches, width), BF),
            jax.ShapeDtypeStruct((frames, 3, patches, width), BF),
        ],
        in_specs=[smem, vmem, vmem, vmem],
        out_specs=[vmem, vmem],
        compiler_params=pltpu.CompilerParams(vmem_limit_bytes=24 * 2**20),
    )(live, qkv, cot, row_sums)

    w_qkv_grad = grads[: 3 * heads].reshape(heads, 3, w_rows, HD).transpose(2, 0, 1, 3)
    w_out_grad = grads[3 * heads :].transpose(0, 2, 1)
    return (block_out[None], qkv_grad.transpose(0, 2, 1, 3)[None], w_qkv_grad, w_out_grad)


def solution(mesh):
    in_specs = (
        P("clip", "frame", None, None, "tensor"),
        P(("clip", "frame"), "tensor", None, None),
        P("tensor", None, ("clip", "frame")),
        P("clip", "frame", None, "tensor"),
        P("clip", None),
        P("clip", None),
    )
    out_specs = (
        P("clip", "frame", None, "tensor"),
        P("clip", "frame", None, None, "tensor"),
        P(("clip", "frame"), "tensor", None, None),
        P("tensor", None, ("clip", "frame")),
    )
    return jax.shard_map(body, mesh=mesh, in_specs=in_specs, out_specs=out_specs, check_vma=False)
```

profile of v0, /device:TPU:1, one launch (start us, length us, event | category | flops | bytes accessed | tf_op | source)
XLA Modules:
  0.0 160.1 jit_solution(13755710024787557071)
XLA Ops:
  7.2 1.8 %pad_maximum_fusion = bf16[12,96,128]{2,1,0:T(8,128)(2,1)} fusion(bf16[3,96,128]{2,1,0:T(8,128)(2,1)} %bitcast.55, bf16[9,96,128]{2,1,0:T(8,128)(2,1)} %bitcast.54), kind=kLoop, calls=%fused_computation.11 | loop fusion | flops 147456 | bytes 589824 | tf_op jit(solution)/shard_map/concatenate | solution.py:234
  9.1 0.7 dynamic-slice_bitcast_fusion
  9.8 0.8 fusion.6.count_ref
  10.7 0.9 copy-done.7
  11.6 2.6 %shard_map.93 = bf16[8,2,2,16,384]{4,3,2,1,0:T(8,128)(2,1)S(1)} custom-call(s32[2]{0:T(128)S(1)} %fusion.6.count_ref, bf16[2,3,128,384]{3,2,1,0:T(8,128)(2,1)S(1)} %bitcast.41, bf16[2,128,384]{2,1,0:T(8,128)(2,1)S(1)} %bitcast.44), custom_call_target="tpu_custom_call" | custom-call | tf_op jit(solution)/shard_map/pallas_call | solution.py:250
  14.2 13.7 %all_to_all.10 = bf16[8,2,2,16,384]{4,3,2,1,0:T(8,128)(2,1)S(1)} all-to-all(bf16[8,2,2,16,384]{4,3,2,1,0:T(8,128)(2,1)S(1)} %shard_map.93), channel_id=1, replica_groups=mesh['clip'=4,'frame'=8,'tensor'=8] {'frame'}, dimensions={0} | all-to-all | bytes 786432 | tf_op jit(solution)/shard_map/all_to_all | solution.py:257
  27.9 1.7 %collective-permute-start.3 = (bf16[256,384]{1,0:T(8,128)(2,1)S(1)}, bf16[256,384]{1,0:T(8,128)(2,1)S(1)}, u32[]{:S(2)}, u32[]{:S(2)}) collective-permute-start(bf16[256,384]{1,0:T(8,128)(2,1)S(1)} %bitcast.49), channel_id=1, source_target_pairs={{0,1},{1,2},{2,3},{3,4},{4,5},{5,6},{6,7},{7,0},{8,9},{9,10},{10,1... | collective-permute-start | bytes 589832 | tf_op jit(solution)/shard_map/ppermute | solution.py:181
  29.6 4.0 %collective-permute-start.7 = (bf16[256,384]{1,0:T(8,128)(2,1)S(1)}, bf16[256,384]{1,0:T(8,128)(2,1)S(1)}, u32[]{:S(2)}, u32[]{:S(2)}) collective-permute-start(bf16[256,384]{1,0:T(8,128)(2,1)S(1)} %bitcast.46), channel_id=1, source_target_pairs={{0,7},{1,0},{2,1},{3,2},{4,3},{5,4},{6,5},{7,6},{8,15},{9,8},{10,9... | collective-permute-start | bytes 589832 | tf_op jit(solution)/shard_map/ppermute | solution.py:181
  33.6 1.4 collective-permute-start
  35.1 3.0 %collective-permute-done.3.refs_8_ = bf16[256,384]{1,0:T(8,128)(2,1)S(1)} collective-permute-done((bf16[256,384]{1,0:T(8,128)(2,1)S(1)}, bf16[256,384]{1,0:T(8,128)(2,1)S(1)}, u32[]{:S(2)}, u32[]{:S(2)}) %collective-permute-start.3) | collective-permute-done | bytes 196640 | tf_op jit(solution)/shard_map/ppermute | solution.py:181
  38.1 2.7 %collective-permute-start.8 = (bf16[256,384]{1,0:T(8,128)(2,1)S(1)}, bf16[256,384]{1,0:T(8,128)(2,1)S(1)}, u32[]{:S(2)}, u32[]{:S(2)}) collective-permute-start(bf16[256,384]{1,0:T(8,128)(2,1)S(1)} %collective-permute-done.7.refs_10_), channel_id=1, source_target_pairs={{0,7},{1,0},{2,1},{3,2},{4,3},{5,4},{6,5},{7,6},{8,15},{9,8},{10,9... | collective-permute-start | bytes 589832 | tf_op jit(solution)/shard_map/ppermute | solution.py:181
  41.2 3.4 %collective-permute-start.1 = (bf16[256,384]{1,0:T(8,128)(2,1)S(1)}, bf16[256,384]{1,0:T(8,128)(2,1)S(1)}, u32[]{:S(2)}, u32[]{:S(2)}) collective-permute-start(bf16[256,384]{1,0:T(8,128)(2,1)S(1)} %collective-permute-done.refs_2_), channel_id=1, source_target_pairs={{0,7},{1,0},{2,1},{3,2},{4,3},{5,4},{6,5},{7,6},{8,15},{9,8},{10,9... | collective-permute-start | bytes 589832 | tf_op jit(solution)/shard_map/ppermute | solution.py:181
  44.6 1.6 collective-permute-done.4.refs_7_
  46.2 2.7 %collective-permute-start.9 = (bf16[256,384]{1,0:T(8,128)(2,1)S(1)}, bf16[256,384]{1,0:T(8,128)(2,1)S(1)}, u32[]{:S(2)}, u32[]{:S(2)}) collective-permute-start(bf16[256,384]{1,0:T(8,128)(2,1)S(1)} %collective-permute-done.8.refs_11_), channel_id=1, source_target_pairs={{0,7},{1,0},{2,1},{3,2},{4,3},{5,4},{6,5},{7,6},{8,15},{9,8},{10,9... | collective-permute-start | bytes 589832 | tf_op jit(solution)/shard_map/ppermute | solution.py:181
  49.1 3.4 %collective-permute-start.2 = (bf16[256,384]{1,0:T(8,128)(2,1)S(1)}, bf16[256,384]{1,0:T(8,128)(2,1)S(1)}, u32[]{:S(2)}, u32[]{:S(2)}) collective-permute-start(bf16[256,384]{1,0:T(8,128)(2,1)S(1)} %collective-permute-done.1.refs_3_), channel_id=1, source_target_pairs={{0,7},{1,0},{2,1},{3,2},{4,3},{5,4},{6,5},{7,6},{8,15},{9,8},{10,9... | collective-permute-start | bytes 589832 | tf_op jit(solution)/shard_map/ppermute | solution.py:181
  52.6 0.6 collective-permute-done.5.refs_6_
  53.2 3.1 %collective-permute-start.10 = (bf16[256,384]{1,0:T(8,128)(2,1)S(1)}, bf16[256,384]{1,0:T(8,128)(2,1)S(1)}, u32[]{:S(2)}, u32[]{:S(2)}) collective-permute-start(bf16[256,384]{1,0:T(8,128)(2,1)S(1)} %collective-permute-done.9.refs_12_), channel_id=1, source_target_pairs={{0,7},{1,0},{2,1},{3,2},{4,3},{5,4},{6,5},{7,6},{8,15},{9,8},{10,9... | collective-permute-start | bytes 589832 | tf_op jit(solution)/shard_map/ppermute | solution.py:181
  57.1 2.1 %collective-permute-done.13.refs_14_ = bf16[256,384]{1,0:T(8,128)(2,1)S(1)} collective-permute-done((bf16[256,384]{1,0:T(8,128)(2,1)S(1)}, bf16[256,384]{1,0:T(8,128)(2,1)S(1)}, u32[]{:S(2)}, u32[]{:S(2)}) %collective-permute-start.13) | collective-permute-done | bytes 196640 | tf_op jit(solution)/shard_map/ppermute | solution.py:181
  59.2 2.1 %collective-permute-done.6.refs_5_ = bf16[256,384]{1,0:T(8,128)(2,1)S(1)} collective-permute-done((bf16[256,384]{1,0:T(8,128)(2,1)S(1)}, bf16[256,384]{1,0:T(8,128)(2,1)S(1)}, u32[]{:S(2)}, u32[]{:S(2)}) %collective-permute-start.6) | collective-permute-done | bytes 196640 | tf_op jit(solution)/shard_map/ppermute | solution.py:181
  62.0 0.7 copy-done.28
  62.6 6.1 %shard_map.94 = (bf16[256,3072]{1,0:T(8,128)(2,1)}, bf16[256,3072]{1,0:T(8,128)(2,1)}, bf16[2,1536,256]{2,1,0:T(8,128)(2,1)}, bf16[2,1536,256]{2,1,0:T(8,128)(2,1)}) custom-call(s32[4]{0:T(128)} %pad_add_fusion.refs_0_, bf16[256,384]{1,0:T(8,128)(2,1)} %bitcast.51, bf16[256,384]{1,0:T(8,128)(2,1)} %copy-done.17, bf16[256,384]{1,0:T(8,128)(2,1)} %copy-done.21, ...), custom_call_target="tpu_custom_call" | custom-call | tf_op jit(solution)/shard_map/pallas_call | solution.py:266
  68.7 4.7 %collective-permute-start.14 = (bf16[2,1536,256]{2,1,0:T(8,128)(2,1)}, bf16[2,1536,256]{2,1,0:T(8,128)(2,1)S(1)}, u32[]{:S(2)}, u32[]{:S(2)}) collective-permute-start(bf16[2,1536,256]{2,1,0:T(8,128)(2,1)} %get-tuple-element.14), channel_id=1, source_target_pairs={{0,8},{8,0},{16,24},{24,16},{32,40},{40,32},{48,56},{56,48},{1,9},... | collective-permute-start | bytes 4718600 | tf_op jit(solution)/shard_map/ppermute | solution.py:185
  73.5 0.6 add.113.refs_1_
  74.1 0.8 add.134.refs_0_
  74.9 1.9 %collective-permute-done.14.refs_4_.refs_2_ = bf16[2,1536,256]{2,1,0:T(8,128)(2,1)S(1)} collective-permute-done((bf16[2,1536,256]{2,1,0:T(8,128)(2,1)}, bf16[2,1536,256]{2,1,0:T(8,128)(2,1)S(1)}, u32[]{:S(2)}, u32[]{:S(2)}) %collective-permute-start.14) | collective-permute-done | bytes 1572896 | tf_op jit(solution)/shard_map/ppermute | solution.py:185
  77.2 0.8 copy-done
  77.9 14.4 %shard_map.95 = (bf16[8,8,2,32,384]{4,3,2,1,0:T(8,128)(2,1)}, bf16[256,1536]{1,0:T(8,128)(2,1)}) custom-call(s32[256,1]{1,0:T(8,128)} %add.134.refs_0_, s32[1,256]{1,0:T(1,128)} %add.113.refs_1_, bf16[256,3072]{1,0:T(8,128)(2,1)} %get-tuple-element.12.refs_2_, bf16[256,3072]{1,0:T(8,128)(2,1)} %get-tuple-element.13.refs_3_, bf16[2,1536,256]{2,1,0:T(8,128)(2,1)} %copy-done, ...), custom_call_target="tpu_custom_call" | custom-call | tf_op jit(solution)/shard_map/pallas_call | solution.py:280
  92.7 2.3 %collective-permute-done.15.refs_4_ = bf16[256,1536]{1,0:T(8,128)(2,1)S(1)} collective-permute-done((bf16[256,1536]{1,0:T(8,128)(2,1)}, bf16[256,1536]{1,0:T(8,128)(2,1)S(1)}, u32[]{:S(2)}, u32[]{:S(2)}) %collective-permute-start.15) | collective-permute-done | bytes 786464 | tf_op jit(solution)/shard_map/ppermute | solution.py:185
  95.0 1.1 copy-done.3
  96.2 1.4 shard_map.98
  97.6 3.2 %collective-permute-start.16 = (bf16[4,12,96,128]{3,2,1,0:T(8,128)(2,1)S(1)}, bf16[4,12,96,128]{3,2,1,0:T(8,128)(2,1)S(1)}, u32[]{:S(2)}, u32[]{:S(2)}) collective-permute-start(bf16[4,12,96,128]{3,2,1,0:T(8,128)(2,1)S(1)} %shard_map.98), channel_id=1, source_target_pairs={{0,32},{8,136},{16,48},{24,152},{32,0},{40,168},{48,16},{56,184},{... | collective-permute-start | bytes 3538952 | tf_op jit(solution)/shard_map/ppermute | solution.py:199
  100.7 1.4 shard_map.99
  102.2 0.7 collective-permute-start.17
  102.9 1.4 shard_map.100
  104.3 2.1 %collective-permute-start.18 = (bf16[4,12,96,128]{3,2,1,0:T(8,128)(2,1)S(1)}, bf16[4,12,96,128]{3,2,1,0:T(8,128)(2,1)S(1)}, u32[]{:S(2)}, u32[]{:S(2)}) collective-permute-start(bf16[4,12,96,128]{3,2,1,0:T(8,128)(2,1)S(1)} %shard_map.100), channel_id=1, source_target_pairs={{0,48},{8,200},{16,0},{24,216},{32,16},{40,232},{48,32},{56,248},{... | collective-permute-start | bytes 3538952 | tf_op jit(solution)/shard_map/ppermute | solution.py:199
  106.4 1.4 shard_map.97
  107.9 6.9 %collective-permute-done.16 = bf16[4,12,96,128]{3,2,1,0:T(8,128)(2,1)S(1)} collective-permute-done((bf16[4,12,96,128]{3,2,1,0:T(8,128)(2,1)S(1)}, bf16[4,12,96,128]{3,2,1,0:T(8,128)(2,1)S(1)}, u32[]{:S(2)}, u32[]{:S(2)}) %collective-permute-start.16) | collective-permute-done | bytes 1179680 | tf_op jit(solution)/shard_map/ppermute | solution.py:199
  114.8 12.6 %collective-permute-done.17 = bf16[4,12,96,128]{3,2,1,0:T(8,128)(2,1)S(1)} collective-permute-done((bf16[4,12,96,128]{3,2,1,0:T(8,128)(2,1)S(1)}, bf16[4,12,96,128]{3,2,1,0:T(8,128)(2,1)S(1)}, u32[]{:S(2)}, u32[]{:S(2)}) %collective-permute-start.17) | collective-permute-done | bytes 1179680 | tf_op jit(solution)/shard_map/ppermute | solution.py:199
  127.4 0.6 collective-permute-done.18
  129.1 0.8 collective-permute-start.19
  129.9 1.9 %collective-permute-start.21 = (bf16[12,96,128]{2,1,0:T(8,128)(2,1)S(1)}, bf16[12,96,128]{2,1,0:T(8,128)(2,1)S(1)}, u32[]{:S(2)}, u32[]{:S(2)}) collective-permute-start(bf16[12,96,128]{2,1,0:T(8,128)(2,1)S(1)} %get-tuple-element.21), channel_id=1, source_target_pairs={{0,192},{8,56},{16,208},{24,8},{32,224},{40,24},{48,240},{56,40},{... | collective-permute-start | bytes 884744 | tf_op jit(solution)/shard_map/ppermute | solution.py:199
  131.8 3.3 %reduce-scatter.2.cloned.1.call-done = bf16[1,8,2,32,384]{4,3,2,1,0:T(8,128)(2,1)} async-done(((bf16[8,8,2,32,384]{4,3,2,1,0:T(8,128)(2,1)}), bf16[1,8,2,32,384]{4,3,2,1,0:T(8,128)(2,1)}) %reduce-scatter.2.cloned.1.call-update) | async-done | bytes 393232 | tf_op jit(solution)/shard_map/reduce_scatter | solution.py:297
  135.0 7.6 %all-to-all-start.1 = ((bf16[8,2,32,384]{3,2,1,0:T(8,128)(2,1)}), bf16[8,2,32,384]{3,2,1,0:T(8,128)(2,1)S(1)}, u32[]{:S(2)}, u32[]{:S(2)}) async-start(bf16[8,2,32,384]{3,2,1,0:T(8,128)(2,1)} %bitcast.53), calls=%async_computation.2 | async-start | bytes 786432 | tf_op jit(solution)/shard_map/all_to_all | solution.py:312
  142.6 1.5 fusion.1
  144.2 0.8 slice.98
  145.0 0.7 slice_bitcast_fusion
  145.6 5.0 %all-to-all-done.1 = bf16[8,2,32,384]{3,2,1,0:T(8,128)(2,1)S(1)} async-done(((bf16[8,2,32,384]{3,2,1,0:T(8,128)(2,1)}), bf16[8,2,32,384]{3,2,1,0:T(8,128)(2,1)S(1)}, u32[]{:S(2)}, u32[]{:S(2)}) %all-to-all-start.1) | async-done | bytes 393248 | tf_op jit(solution)/shard_map/all_to_all | solution.py:312
  150.7 2.5 %shard_map.96 = (bf16[2,128,384]{2,1,0:T(8,128)(2,1)}, bf16[2,3,128,384]{3,2,1,0:T(8,128)(2,1)}) custom-call(s32[2]{0:T(128)S(1)} %fusion.6.count_ref, bf16[2,3,128,384]{3,2,1,0:T(8,128)(2,1)S(1)} %bitcast.42, bf16[2,128,384]{2,1,0:T(8,128)(2,1)S(1)} %bitcast.45, bf16[8,2,2,16,384]{4,3,2,1,0:T(8,128)(2,1)S(1)} %bitcast.43), custom_call_target="tpu_custom_call" | custom-call | tf_op jit(solution)/shard_map/pallas_call | solution.py:314
  (86 shorter events, 4.3 us)
Async XLA Ops:
  7.2 3.5 %copy-start.5 = (bf16[1,2,128,3,384]{4,2,3,1,0:T(8,128)(2,1)S(1)}, bf16[1,2,128,3,384]{4,2,3,1,0:T(8,128)(2,1)}, u32[]{:S(2)}) copy-start(bf16[1,2,128,3,384]{4,2,3,1,0:T(8,128)(2,1)} %param.6) | copy-start | bytes 1769476
  7.2 70.0 %all-gather.2.cloned.1.call-start = ((), (), s32[]{:S(2)}) async-start(), calls=%async_computation.3 | async-start | bytes 9732096 | tf_op jit(solution)/shard_map/all_gather | solution.py:238
  9.0 126.0 %reduce-scatter.2.cloned.1.call-start = ((), (), s32[]{:S(2)}) async-start(), calls=%async_computation.4 | async-start | bytes 3538944 | tf_op jit(solution)/shard_map/reduce_scatter | solution.py:297
  27.9 33.4 %copy-start.13 = (bf16[8,1,2,16,384]{4,3,2,1,0:T(8,128)(2,1)}, bf16[8,1,2,16,384]{4,3,2,1,0:T(8,128)(2,1)S(1)}, u32[]{:S(2)}) copy-start(bf16[8,1,2,16,384]{4,3,2,1,0:T(8,128)(2,1)S(1)} %get-tuple-element.23) | copy-start | bytes 589828
  27.9 33.4 %copy-start.14 = (bf16[8,1,2,16,384]{4,3,2,1,0:T(8,128)(2,1)}, bf16[8,1,2,16,384]{4,3,2,1,0:T(8,128)(2,1)S(1)}, u32[]{:S(2)}) copy-start(bf16[8,1,2,16,384]{4,3,2,1,0:T(8,128)(2,1)S(1)} %get-tuple-element.24) | copy-start | bytes 589828
  27.9 10.1 %collective-permute-start.3 = (bf16[256,384]{1,0:T(8,128)(2,1)S(1)}, bf16[256,384]{1,0:T(8,128)(2,1)S(1)}, u32[]{:S(2)}, u32[]{:S(2)}) collective-permute-start(bf16[256,384]{1,0:T(8,128)(2,1)S(1)} %bitcast.49), channel_id=1, source_target_pairs={{0,1},{1,2},{2,3},{3,4},{4,5},{5,6},{6,7},{7,0},{8,9},{9,10},{10,1... | collective-permute-start | bytes 589832 | tf_op jit(solution)/shard_map/ppermute | solution.py:181
  29.6 8.5 %collective-permute-start.7 = (bf16[256,384]{1,0:T(8,128)(2,1)S(1)}, bf16[256,384]{1,0:T(8,128)(2,1)S(1)}, u32[]{:S(2)}, u32[]{:S(2)}) collective-permute-start(bf16[256,384]{1,0:T(8,128)(2,1)S(1)} %bitcast.46), channel_id=1, source_target_pairs={{0,7},{1,0},{2,1},{3,2},{4,3},{5,4},{6,5},{7,6},{8,15},{9,8},{10,9... | collective-permute-start | bytes 589832 | tf_op jit(solution)/shard_map/ppermute | solution.py:181
  33.6 7.6 %collective-permute-start = (bf16[256,384]{1,0:T(8,128)(2,1)S(1)}, bf16[256,384]{1,0:T(8,128)(2,1)S(1)}, u32[]{:S(2)}, u32[]{:S(2)}) collective-permute-start(bf16[256,384]{1,0:T(8,128)(2,1)S(1)} %bitcast.50), channel_id=1, source_target_pairs={{0,7},{1,0},{2,1},{3,2},{4,3},{5,4},{6,5},{7,6},{8,15},{9,8},{10,9... | collective-permute-start | bytes 589832 | tf_op jit(solution)/shard_map/ppermute | solution.py:181
  35.0 9.6 %collective-permute-start.11 = (bf16[256,384]{1,0:T(8,128)(2,1)S(1)}, bf16[256,384]{1,0:T(8,128)(2,1)S(1)}, u32[]{:S(2)}, u32[]{:S(2)}) collective-permute-start(bf16[256,384]{1,0:T(8,128)(2,1)S(1)} %bitcast.47), channel_id=1, source_target_pairs={{0,1},{1,2},{2,3},{3,4},{4,5},{5,6},{6,7},{7,0},{8,9},{9,10},{10,1... | collective-permute-start | bytes 589832 | tf_op jit(solution)/shard_map/ppermute | solution.py:181
  38.1 23.2 %copy-start.15 = (bf16[256,384]{1,0:T(8,128)(2,1)}, bf16[256,384]{1,0:T(8,128)(2,1)S(1)}, u32[]{:S(2)}) copy-start(bf16[256,384]{1,0:T(8,128)(2,1)S(1)} %collective-permute-done.3.refs_8_) | copy-start | bytes 589828
  38.1 8.1 %collective-permute-start.4 = (bf16[256,384]{1,0:T(8,128)(2,1)S(1)}, bf16[256,384]{1,0:T(8,128)(2,1)S(1)}, u32[]{:S(2)}, u32[]{:S(2)}) collective-permute-start(bf16[256,384]{1,0:T(8,128)(2,1)S(1)} %collective-permute-done.3.refs_8_), channel_id=1, source_target_pairs={{0,1},{1,2},{2,3},{3,4},{4,5},{5,6},{6,7},{7,0},{8,9},{9,10},{10,1... | collective-permute-start | bytes 589832 | tf_op jit(solution)/shard_map/ppermute | solution.py:181
  38.1 23.2 %copy-start.16 = (bf16[256,384]{1,0:T(8,128)(2,1)}, bf16[256,384]{1,0:T(8,128)(2,1)S(1)}, u32[]{:S(2)}) copy-start(bf16[256,384]{1,0:T(8,128)(2,1)S(1)} %collective-permute-done.7.refs_10_) | copy-start | bytes 589828
  38.1 8.1 %collective-permute-start.8 = (bf16[256,384]{1,0:T(8,128)(2,1)S(1)}, bf16[256,384]{1,0:T(8,128)(2,1)S(1)}, u32[]{:S(2)}, u32[]{:S(2)}) collective-permute-start(bf16[256,384]{1,0:T(8,128)(2,1)S(1)} %collective-permute-done.7.refs_10_), channel_id=1, source_target_pairs={{0,7},{1,0},{2,1},{3,2},{4,3},{5,4},{6,5},{7,6},{8,15},{9,8},{10,9... | collective-permute-start | bytes 589832 | tf_op jit(solution)/shard_map/ppermute | solution.py:181
  41.2 20.1 %copy-start.17 = (bf16[256,384]{1,0:T(8,128)(2,1)}, bf16[256,384]{1,0:T(8,128)(2,1)S(1)}, u32[]{:S(2)}) copy-start(bf16[256,384]{1,0:T(8,128)(2,1)S(1)} %collective-permute-done.refs_2_) | copy-start | bytes 589828
  41.2 7.9 %collective-permute-start.1 = (bf16[256,384]{1,0:T(8,128)(2,1)S(1)}, bf16[256,384]{1,0:T(8,128)(2,1)S(1)}, u32[]{:S(2)}, u32[]{:S(2)}) collective-permute-start(bf16[256,384]{1,0:T(8,128)(2,1)S(1)} %collective-permute-done.refs_2_), channel_id=1, source_target_pairs={{0,7},{1,0},{2,1},{3,2},{4,3},{5,4},{6,5},{7,6},{8,15},{9,8},{10,9... | collective-permute-start | bytes 589832 | tf_op jit(solution)/shard_map/ppermute | solution.py:181
  44.6 16.7 %copy-start.18 = (bf16[256,384]{1,0:T(8,128)(2,1)}, bf16[256,384]{1,0:T(8,128)(2,1)S(1)}, u32[]{:S(2)}) copy-start(bf16[256,384]{1,0:T(8,128)(2,1)S(1)} %collective-permute-done.11.refs_16_) | copy-start | bytes 589828
  44.6 7.9 %collective-permute-start.12 = (bf16[256,384]{1,0:T(8,128)(2,1)S(1)}, bf16[256,384]{1,0:T(8,128)(2,1)S(1)}, u32[]{:S(2)}, u32[]{:S(2)}) collective-permute-start(bf16[256,384]{1,0:T(8,128)(2,1)S(1)} %collective-permute-done.11.refs_16_), channel_id=1, source_target_pairs={{0,1},{1,2},{2,3},{3,4},{4,5},{5,6},{6,7},{7,0},{8,9},{9,10},{10,1... | collective-permute-start | bytes 589832 | tf_op jit(solution)/shard_map/ppermute | solution.py:181
  46.2 15.2 %copy-start.19 = (bf16[256,384]{1,0:T(8,128)(2,1)}, bf16[256,384]{1,0:T(8,128)(2,1)S(1)}, u32[]{:S(2)}) copy-start(bf16[256,384]{1,0:T(8,128)(2,1)S(1)} %collective-permute-done.4.refs_7_) | copy-start | bytes 589828
  46.2 7.0 %collective-permute-start.5 = (bf16[256,384]{1,0:T(8,128)(2,1)S(1)}, bf16[256,384]{1,0:T(8,128)(2,1)S(1)}, u32[]{:S(2)}, u32[]{:S(2)}) collective-permute-start(bf16[256,384]{1,0:T(8,128)(2,1)S(1)} %collective-permute-done.4.refs_7_), channel_id=1, source_target_pairs={{0,1},{1,2},{2,3},{3,4},{4,5},{5,6},{6,7},{7,0},{8,9},{9,10},{10,1... | collective-permute-start | bytes 589832 | tf_op jit(solution)/shard_map/ppermute | solution.py:181
  46.2 15.2 %copy-start.20 = (bf16[256,384]{1,0:T(8,128)(2,1)}, bf16[256,384]{1,0:T(8,128)(2,1)S(1)}, u32[]{:S(2)}) copy-start(bf16[256,384]{1,0:T(8,128)(2,1)S(1)} %collective-permute-done.8.refs_11_) | copy-start | bytes 589828
  46.2 7.0 %collective-permute-start.9 = (bf16[256,384]{1,0:T(8,128)(2,1)S(1)}, bf16[256,384]{1,0:T(8,128)(2,1)S(1)}, u32[]{:S(2)}, u32[]{:S(2)}) collective-permute-start(bf16[256,384]{1,0:T(8,128)(2,1)S(1)} %collective-permute-done.8.refs_11_), channel_id=1, source_target_pairs={{0,7},{1,0},{2,1},{3,2},{4,3},{5,4},{6,5},{7,6},{8,15},{9,8},{10,9... | collective-permute-start | bytes 589832 | tf_op jit(solution)/shard_map/ppermute | solution.py:181
  49.1 12.2 %copy-start.21 = (bf16[256,384]{1,0:T(8,128)(2,1)}, bf16[256,384]{1,0:T(8,128)(2,1)S(1)}, u32[]{:S(2)}) copy-start(bf16[256,384]{1,0:T(8,128)(2,1)S(1)} %collective-permute-done.1.refs_3_) | copy-start | bytes 589828
  49.1 8.0 %collective-permute-start.2 = (bf16[256,384]{1,0:T(8,128)(2,1)S(1)}, bf16[256,384]{1,0:T(8,128)(2,1)S(1)}, u32[]{:S(2)}, u32[]{:S(2)}) collective-permute-start(bf16[256,384]{1,0:T(8,128)(2,1)S(1)} %collective-permute-done.1.refs_3_), channel_id=1, source_target_pairs={{0,7},{1,0},{2,1},{3,2},{4,3},{5,4},{6,5},{7,6},{8,15},{9,8},{10,9... | collective-permute-start | bytes 589832 | tf_op jit(solution)/shard_map/ppermute | solution.py:181
  52.5 8.8 %copy-start.22 = (bf16[256,384]{1,0:T(8,128)(2,1)}, bf16[256,384]{1,0:T(8,128)(2,1)S(1)}, u32[]{:S(2)}) copy-start(bf16[256,384]{1,0:T(8,128)(2,1)S(1)} %collective-permute-done.12.refs_15_) | copy-start | bytes 589828
  52.5 6.6 %collective-permute-start.13 = (bf16[256,384]{1,0:T(8,128)(2,1)S(1)}, bf16[256,384]{1,0:T(8,128)(2,1)S(1)}, u32[]{:S(2)}, u32[]{:S(2)}) collective-permute-start(bf16[256,384]{1,0:T(8,128)(2,1)S(1)} %collective-permute-done.12.refs_15_), channel_id=1, source_target_pairs={{0,1},{1,2},{2,3},{3,4},{4,5},{5,6},{6,7},{7,0},{8,9},{9,10},{10,1... | collective-permute-start | bytes 589832 | tf_op jit(solution)/shard_map/ppermute | solution.py:181
  53.2 8.2 %copy-start.23 = (bf16[256,384]{1,0:T(8,128)(2,1)}, bf16[256,384]{1,0:T(8,128)(2,1)S(1)}, u32[]{:S(2)}) copy-start(bf16[256,384]{1,0:T(8,128)(2,1)S(1)} %collective-permute-done.5.refs_6_) | copy-start | bytes 589828
  53.2 8.1 %collective-permute-start.6 = (bf16[256,384]{1,0:T(8,128)(2,1)S(1)}, bf16[256,384]{1,0:T(8,128)(2,1)S(1)}, u32[]{:S(2)}, u32[]{:S(2)}) collective-permute-start(bf16[256,384]{1,0:T(8,128)(2,1)S(1)} %collective-permute-done.5.refs_6_), channel_id=1, source_target_pairs={{0,1},{1,2},{2,3},{3,4},{4,5},{5,6},{6,7},{7,0},{8,9},{9,10},{10,1... | collective-permute-start | bytes 589832 | tf_op jit(solution)/shard_map/ppermute | solution.py:181
  53.2 8.2 %copy-start.24 = (bf16[256,384]{1,0:T(8,128)(2,1)}, bf16[256,384]{1,0:T(8,128)(2,1)S(1)}, u32[]{:S(2)}) copy-start(bf16[256,384]{1,0:T(8,128)(2,1)S(1)} %collective-permute-done.9.refs_12_) | copy-start | bytes 589828
  53.2 8.1 %collective-permute-start.10 = (bf16[256,384]{1,0:T(8,128)(2,1)S(1)}, bf16[256,384]{1,0:T(8,128)(2,1)S(1)}, u32[]{:S(2)}, u32[]{:S(2)}) collective-permute-start(bf16[256,384]{1,0:T(8,128)(2,1)S(1)} %collective-permute-done.9.refs_12_), channel_id=1, source_target_pairs={{0,7},{1,0},{2,1},{3,2},{4,3},{5,4},{6,5},{7,6},{8,15},{9,8},{10,9... | collective-permute-start | bytes 589832 | tf_op jit(solution)/shard_map/ppermute | solution.py:181
  56.8 16.6 %copy-start.29 = (s32[1,16]{1,0:T(1,128)S(1)}, s32[1,16]{1,0:T(1,128)}, u32[]{:S(2)}) copy-start(s32[1,16]{1,0:T(1,128)} %param.10) | copy-start | bytes 196
  57.1 4.3 %copy-start.25 = (bf16[256,384]{1,0:T(8,128)(2,1)}, bf16[256,384]{1,0:T(8,128)(2,1)S(1)}, u32[]{:S(2)}) copy-start(bf16[256,384]{1,0:T(8,128)(2,1)S(1)} %collective-permute-done.2.refs_4_) | copy-start | bytes 589828
  59.2 2.2 %copy-start.26 = (bf16[256,384]{1,0:T(8,128)(2,1)}, bf16[256,384]{1,0:T(8,128)(2,1)S(1)}, u32[]{:S(2)}) copy-start(bf16[256,384]{1,0:T(8,128)(2,1)S(1)} %collective-permute-done.13.refs_14_) | copy-start | bytes 589828
  68.7 8.0 %collective-permute-start.14 = (bf16[2,1536,256]{2,1,0:T(8,128)(2,1)}, bf16[2,1536,256]{2,1,0:T(8,128)(2,1)S(1)}, u32[]{:S(2)}, u32[]{:S(2)}) collective-permute-start(bf16[2,1536,256]{2,1,0:T(8,128)(2,1)} %get-tuple-element.14), channel_id=1, source_target_pairs={{0,8},{8,0},{16,24},{24,16},{32,40},{40,32},{48,56},{56,48},{1,9},... | collective-permute-start | bytes 4718600 | tf_op jit(solution)/shard_map/ppermute | solution.py:185
  92.4 2.6 %copy-start.1 = (bf16[2,1536,256]{2,1,0:T(8,128)(2,1)S(1)}, bf16[2,1536,256]{2,1,0:T(8,128)(2,1)}, u32[]{:S(2)}) copy-start(bf16[2,1536,256]{2,1,0:T(8,128)(2,1)} %copy-done) | copy-start | bytes 4718596
  92.4 2.6 %copy-start.2 = (bf16[2,1536,256]{2,1,0:T(8,128)(2,1)S(1)}, bf16[2,1536,256]{2,1,0:T(8,128)(2,1)}, u32[]{:S(2)}) copy-start(bf16[2,1536,256]{2,1,0:T(8,128)(2,1)} %get-tuple-element.18.refs_1_) | copy-start | bytes 4718596
  92.4 2.6 %copy-start.9 = (s32[4]{0:T(128)S(1)}, s32[4]{0:T(128)}, u32[]{:S(2)}) copy-start(s32[4]{0:T(128)} %pad_add_fusion.refs_0_) | copy-start | bytes 52
  92.4 2.6 %collective-permute-start.15 = (bf16[256,1536]{1,0:T(8,128)(2,1)}, bf16[256,1536]{1,0:T(8,128)(2,1)S(1)}, u32[]{:S(2)}, u32[]{:S(2)}) collective-permute-start(bf16[256,1536]{1,0:T(8,128)(2,1)} %get-tuple-element.19.refs_3_), channel_id=1, source_target_pairs={{0,8},{8,0},{16,24},{24,16},{32,40},{40,32},{48,56},{56,48},{1,9},... | collective-permute-start | bytes 2359304 | tf_op jit(solution)/shard_map/ppermute | solution.py:185
  97.6 17.2 %collective-permute-start.16 = (bf16[4,12,96,128]{3,2,1,0:T(8,128)(2,1)S(1)}, bf16[4,12,96,128]{3,2,1,0:T(8,128)(2,1)S(1)}, u32[]{:S(2)}, u32[]{:S(2)}) collective-permute-start(bf16[4,12,96,128]{3,2,1,0:T(8,128)(2,1)S(1)} %shard_map.98), channel_id=1, source_target_pairs={{0,32},{8,136},{16,48},{24,152},{32,0},{40,168},{48,16},{56,184},{... | collective-permute-start | bytes 3538952 | tf_op jit(solution)/shard_map/ppermute | solution.py:199
  102.2 25.2 %collective-permute-start.17 = (bf16[4,12,96,128]{3,2,1,0:T(8,128)(2,1)S(1)}, bf16[4,12,96,128]{3,2,1,0:T(8,128)(2,1)S(1)}, u32[]{:S(2)}, u32[]{:S(2)}) collective-permute-start(bf16[4,12,96,128]{3,2,1,0:T(8,128)(2,1)S(1)} %shard_map.99), channel_id=1, source_target_pairs={{0,16},{8,72},{16,32},{24,88},{32,48},{40,104},{48,0},{56,120},{64... | collective-permute-start | bytes 3538952 | tf_op jit(solution)/shard_map/ppermute | solution.py:199
  104.3 23.7 %collective-permute-start.18 = (bf16[4,12,96,128]{3,2,1,0:T(8,128)(2,1)S(1)}, bf16[4,12,96,128]{3,2,1,0:T(8,128)(2,1)S(1)}, u32[]{:S(2)}, u32[]{:S(2)}) collective-permute-start(bf16[4,12,96,128]{3,2,1,0:T(8,128)(2,1)S(1)} %shard_map.100), channel_id=1, source_target_pairs={{0,48},{8,200},{16,0},{24,216},{32,16},{40,232},{48,32},{56,248},{... | collective-permute-start | bytes 3538952 | tf_op jit(solution)/shard_map/ppermute | solution.py:199
  107.8 20.6 %copy-start.4 = (bf16[4,12,96,128]{3,2,1,0:T(8,128)(2,1)}, bf16[4,12,96,128]{3,2,1,0:T(8,128)(2,1)S(1)}, u32[]{:S(2)}) copy-start(bf16[4,12,96,128]{3,2,1,0:T(8,128)(2,1)S(1)} %shard_map.97) | copy-start | bytes 3538948
  114.8 13.7 %copy-start.10 = (bf16[4,12,96,128]{3,2,1,0:T(8,128)(2,1)}, bf16[4,12,96,128]{3,2,1,0:T(8,128)(2,1)S(1)}, u32[]{:S(2)}) copy-start(bf16[4,12,96,128]{3,2,1,0:T(8,128)(2,1)S(1)} %collective-permute-done.16) | copy-start | bytes 3538948
  129.1 13.5 %collective-permute-start.19 = (bf16[12,96,128]{2,1,0:T(8,128)(2,1)S(1)}, bf16[12,96,128]{2,1,0:T(8,128)(2,1)S(1)}, u32[]{:S(2)}, u32[]{:S(2)}) collective-permute-start(bf16[12,96,128]{2,1,0:T(8,128)(2,1)S(1)} %get-tuple-element.20), channel_id=1, source_target_pairs={{0,128},{8,40},{16,144},{24,56},{32,160},{40,8},{48,176},{56,24},{... | collective-permute-start | bytes 884744 | tf_op jit(solution)/shard_map/ppermute | solution.py:199
  129.9 12.7 %collective-permute-start.21 = (bf16[12,96,128]{2,1,0:T(8,128)(2,1)S(1)}, bf16[12,96,128]{2,1,0:T(8,128)(2,1)S(1)}, u32[]{:S(2)}, u32[]{:S(2)}) collective-permute-start(bf16[12,96,128]{2,1,0:T(8,128)(2,1)S(1)} %get-tuple-element.21), channel_id=1, source_target_pairs={{0,192},{8,56},{16,208},{24,8},{32,224},{40,24},{48,240},{56,40},{... | collective-permute-start | bytes 884744 | tf_op jit(solution)/shard_map/ppermute | solution.py:199
  131.7 10.9 %collective-permute-start.20 = (bf16[12,96,128]{2,1,0:T(8,128)(2,1)S(1)}, bf16[12,96,128]{2,1,0:T(8,128)(2,1)S(1)}, u32[]{:S(2)}, u32[]{:S(2)}) collective-permute-start(bf16[12,96,128]{2,1,0:T(8,128)(2,1)S(1)} %get-tuple-element.22), channel_id=1, source_target_pairs={{0,64},{8,24},{16,80},{24,40},{32,96},{40,56},{48,112},{56,8},{64,... | collective-permute-start | bytes 884744 | tf_op jit(solution)/shard_map/ppermute | solution.py:199
  135.0 15.7 %all-to-all-start.1 = ((bf16[8,2,32,384]{3,2,1,0:T(8,128)(2,1)}), bf16[8,2,32,384]{3,2,1,0:T(8,128)(2,1)S(1)}, u32[]{:S(2)}, u32[]{:S(2)}) async-start(bf16[8,2,32,384]{3,2,1,0:T(8,128)(2,1)} %bitcast.53), calls=%async_computation.2 | async-start | bytes 786432 | tf_op jit(solution)/shard_map/all_to_all | solution.py:312
  144.2 6.5 %copy-start.6 = (bf16[1,2,128,3,384]{4,2,3,1,0:T(8,128)(2,1)S(1)}, bf16[1,2,128,3,384]{4,2,3,1,0:T(8,128)(2,1)}, u32[]{:S(2)}) copy-start(bf16[1,2,128,3,384]{4,2,3,1,0:T(8,128)(2,1)} %param.6) | copy-start | bytes 1769476
  144.2 6.5 %copy-start.8 = (bf16[1,2,128,384]{3,2,1,0:T(8,128)(2,1)S(1)}, bf16[1,2,128,384]{3,2,1,0:T(8,128)(2,1)}, u32[]{:S(2)}) copy-start(bf16[1,2,128,384]{3,2,1,0:T(8,128)(2,1)} %param.9) | copy-start | bytes 589828
  (7 other events, 6.8 us)
Sparse Core Ops, SparseCore 0:
  11.2 65.9 all-gather.1
  92.5 42.4 reduce-scatter.1
where the time goes:
time: 160 us
  starting transfers between devices  43.7 us (27%)
  waiting for transfers between devices  43.4 us (27%)
  Pallas kernels  31.3 us (20%)
  between operations  14.4 us (9%)
  blocking collectives  13.7 us (9%)
  local copies, waits for them, and re-layouts  8.32 us (5%)
  other arithmetic  5.25 us (3%)
    ppermute x14, starting transfers between devices, shift(): lax.ppermute(value, axis, [(i, (i + step) % size) for i in range(size)])  22.4 us
    ppermute x6, waiting for transfers between devices, spread(): return lax.ppermute(value, ('clip', 'frame'), pairs)  20.2 us
    pallas_call x1, Pallas kernels, body(): pl.pallas_call(lambda *refs: temporal_kernel(heads, *refs), out_shape=[ja...  14.4 us
    all_to_all x1, blocking collectives, body(): lax.all_to_all(sent, 'frame', split_axis=0, concat_axis=0, tiled=True)  13.7 us
    ppermute x14, waiting for transfers between devices, shift(): lax.ppermute(value, axis, [(i, (i + step) % size) for i in range(size)])  10.3 us
    ppermute x6, starting transfers between devices, spread(): return lax.ppermute(value, ('clip', 'frame'), pairs)  8.66 us
    all_to_all x1, starting transfers between devices, body(): lax.all_to_all(own_sums, 'frame', split_axis=0, concat_axis=0, tiled=True)  7.58 us
    pallas_call x1, Pallas kernels, body(): pl.pallas_call(lambda *refs: assemble_kernel(width_ranks, *refs), out_sha...  6.1 us
  transfers between devices with their start and end apart: 25, of which 16 were waited for; matrix products, arithmetic and copies ran while one was open for 4% of the time, Pallas kernels for 9%

commit v1 on v0

--- a/solution.py
+++ b/solution.py
@@ -77,77 +77,107 @@
                 grad_ref[f, i, :, cols] = grads[i]
 
 
-def assemble_kernel(ranks, place_ref, *refs):
-    blocks, refs = refs[: 2 * ranks], refs[2 * ranks :]
-    feat_ref, gated_ref, own_ref, other_ref, flip_ref, sem = refs
-    me, core = place_ref[3], place_ref[2]
-    width = feat_ref.shape[1] // ranks
-    copies = []
-    for a, whole in enumerate((feat_ref, gated_ref)):
-        for d in range(ranks):
-            start = pl.multiple_of(lax.rem(me + d, ranks) * width, HD)
-            i = a * ranks + d
-            copies.append(
-                pltpu.make_async_copy(blocks[i], whole.at[:, pl.ds(start, width)], sem.at[i])
-            )
-    for copy in copies:
-        copy.start()
-    for copy in copies:
-        copy.wait()
+def pack_kernel(qkv_ref, out_ref, packed_ref):
+    for ref, first in ((qkv_ref, 0), (out_ref, qkv_ref.shape[0])):
+        for s in range(ref.shape[0]):
+            packed_ref[:, (first + s) * HD : (first + s + 1) * HD] = ref[s]
+
+
+def flip_kernel(place_ref, whole_ref, own_ref, other_ref):
+    core = place_ref[2]
     pieces = 32
-    rows = feat_ref.shape[1] // pieces
-    for a, whole in enumerate((feat_ref, gated_ref)):
-        for z in range(ranks):
-            part = slice(z * width, (z + 1) * width)
-            flip_ref[part, :] = whole[:, part].T
-        for i in range(pieces // 2):
-            to = slice(i * rows, (i + 1) * rows)
-            own_ref[a, to] = flip_ref[pl.ds(pl.multiple_of((2 * i + core) * rows, 16), rows), :]
-            other_ref[a, to] = flip_ref[pl.ds(pl.multiple_of((2 * i + 1 - core) * rows, 16), rows), :]
-
-
-def temporal_kernel(heads, row_key_ref, col_key_ref, feat_ref, gated_ref, _, *refs):
-    w_hbm, sums_hbm, both_ref, w_ref, sums_ref, w_sem, out_sem = refs
+    owners, _, tokens, model = whole_ref.shape
+    rows = model // pieces
+    step = 4 * rows
+    for a in range(2):
+        for z in range(model // step):
+            part = whole_ref[:, a, :, z * step : (z + 1) * step]
+            flipped = part.reshape(owners * tokens, step).T
+            for i in range(2):
+                even = flipped[2 * i * rows : (2 * i + 1) * rows]
+                odd = flipped[(2 * i + 1) * rows : (2 * i + 2) * rows]
+                to = slice((2 * z + i) * rows, (2 * z + i + 1) * rows)
+                own_ref[a, to] = jnp.where(core == 0, even, odd)
+                other_ref[a, to] = jnp.where(core == 0, odd, even)
+
+
+def temporal_kernel(heads, place_ref, row_key_ref, col_key_ref, whole_hbm, *refs):
+    planes, refs = refs[:-8], refs[-8:]
+    sums_hbm, both_ref, w_ref, token_ref, sums_ref, w_sem, in_sem, out_sem = refs
+    at_clip, at_x, core = place_ref[0], place_ref[1], place_ref[2]
     width = heads * HD
-    slots = 4 * heads
     ranks, owners, _, rows, _ = sums_ref.shape
-    loads = [
-        pltpu.make_async_copy(w_hbm.at[i], w_ref.at[:, i * HD : (i + 1) * HD], w_sem.at[i])
-        for i in range(slots)
+    n, w_rows, _ = planes[0].shape
+    tokens = [
+        pltpu.make_async_copy(whole_hbm.at[:, a], token_ref.at[a], in_sem.at[a]) for a in range(2)
     ]
-    for copy in loads:
-        copy.start()
+    loads = [[] for _ in range(heads + 1)]
+    for half, owner in ((0, core), (1, 1 - core)):
+        for second in range(n):
+            for first in range(n):
+                clip = lax.rem(at_clip + n - jnp.where(owner == 0, second, first), n)
+                x = lax.rem(at_x + n - jnp.where(owner == 0, first, second), n)
+                start = pl.multiple_of((clip * 2 * n + x * 2 + owner) * w_rows, 16)
+                for g in range(heads + 1):
+                    cols = pl.ds(g * width, width)
+                    loads[g].append(
+                        pltpu.make_async_copy(
+                            planes[half * n + second].at[first, :, cols],
+                            w_ref.at[pl.ds(start, w_rows), cols],
+                            w_sem.at[g, len(loads[g])],
+                        )
+                    )
+
+    def start(g):
+        for copy in loads[g]:
+            copy.start()
+
+    def finish(g):
+        for copy in loads[g]:
+            copy.wait()
+
+    tokens[0].start()
+    start(0)
+    start(1)
     mask = row_key_ref[...] == col_key_ref[...]
+    tokens[0].wait()
+    feats = token_ref[0].reshape(owners * rows, -1)
     query, keys, values = [], [], []
     for h in range(heads):
-        for i in range(3):
-            loads[3 * h + i].wait()
-        qkv = dot(feat_ref[...], w_ref[:, 3 * h * HD : 3 * (h + 1) * HD]).astype(BF)
+        finish(h)
+        if h == 0:
+            tokens[1].start()
+        if h + 2 <= heads:
+            start(h + 2)
+        qkv = dot(feats, w_ref[:, h * width : (h + 1) * width]).astype(BF)
         for i, parts in enumerate((query, keys, values)):
             parts.append(qkv[:, i * HD : (i + 1) * HD])
-    for h in range(heads):
-        loads[3 * heads + h].wait()
-    cotangent = dot(gated_ref[...], w_ref[:, 3 * width :]).astype(BF)
-    cotangent = [cotangent[:, h * HD : (h + 1) * HD] for h in range(heads)]
     each = range(heads)
     probs = [softmax(query[h], keys[h], mask) for h in each]
+    mixed = [dot(probs[h].astype(BF), values[h]).astype(BF) for h in each]
+    tokens[1].wait()
+    finish(heads)
+    gated = token_ref[1].reshape(owners * rows, -1)
+    cotangent = dot(gated, w_ref[:, 3 * width :]).astype(BF)
     for h in each:
-        grads = attention_grads(query[h], keys[h], values[h], probs[h], cotangent[h])
+        cols = slice(h * HD, (h + 1) * HD)
+        grads = attention_grads(query[h], keys[h], values[h], probs[h], cotangent[:, cols])
         for i in range(3):
-            start = (3 * h + i) * HD
-            both_ref[:, start : start + HD] = grads[i]
-        start = 3 * width + h * HD
-        both_ref[:, start : start + HD] = dot(probs[h].astype(BF), values[h]).astype(BF)
+            both_ref[:, (3 * h + i) * HD : (3 * h + i + 1) * HD] = grads[i]
+        both_ref[:, 3 * width + h * HD : 3 * width + (h + 1) * HD] = mixed[h]
     stores = []
-    for z in range(ranks):
-        part = slice(z * width, (z + 1) * width)
+    pair = 2
+    for first in range(0, ranks, pair):
+        part = slice(first * width, (first + pair) * width)
         projected = dot(both_ref[:, 3 * width :], w_ref[part, 3 * width :], NT).astype(BF)
         back = dot(both_ref[:, : 3 * width], w_ref[part, : 3 * width], NT).astype(BF)
-        for s in range(owners):
-            sums_ref[z, s, 0] = projected[s * rows : (s + 1) * rows]
-            sums_ref[z, s, 1] = back[s * rows : (s + 1) * rows]
-        stores.append(pltpu.make_async_copy(sums_ref.at[z], sums_hbm.at[z], out_sem.at[z]))
-        stores[-1].start()
+        for i in range(pair):
+            z, cols = first + i, slice(i * width, (i + 1) * width)
+            for s in range(owners):
+                sums_ref[z, s, 0] = projected[s * rows : (s + 1) * rows, cols]
+                sums_ref[z, s, 1] = back[s * rows : (s + 1) * rows, cols]
+            stores.append(pltpu.make_async_copy(sums_ref.at[z], sums_hbm.at[z], out_sem.at[z]))
+            stores[-1].start()
     for copy in stores:
         copy.wait()
 
@@ -177,10 +207,6 @@
                 out_ref[r, a * (slots * 3 // 4) + s] = part
 
 
-def shift(value, axis, step, size):
-    return lax.ppermute(value, axis, [(i, (i + step) % size) for i in range(size)])
-
-
 def pair_swap(value):
     return lax.ppermute(value, "frame", [(i, i ^ 1) for i in range(8)])
 
@@ -197,17 +223,6 @@
                     to_clip = (clip + step) % 4
                 pairs.append((clip * 8 + x * 2 + core, to_clip * 8 + to_x * 2 + core))
     return lax.ppermute(value, ("clip", "frame"), pairs)
-
-
-def ring_gather(value, axis, size, last_forward):
-    found = {0: value}
-    up = down = value
-    for step in range(1, size // 2):
-        up = shift(up, axis, 1, size)
-        down = shift(down, axis, -1, size)
-        found[size - step], found[step] = up, down
-    found[size // 2] = shift(up, axis, 1, size) if last_forward else shift(down, axis, -1, size)
-    return [found[d] for d in range(size)]
 
 
 def add(*values):
@@ -231,11 +246,19 @@
     slots = 4 * heads
 
     w_rows = w_qkv.shape[0]
-    w_own = jnp.concatenate(
-        [w_qkv.transpose(1, 2, 0, 3).reshape(3 * heads, w_rows, HD), w_out.transpose(0, 2, 1)],
-        axis=0,
-    )
-    w_all = lax.all_gather(w_own, ("clip", "frame"), axis=1, tiled=True)
+    place = jnp.stack([at_clip, at_frame // 2, at_frame % 2, at_width])
+    smem = pl.BlockSpec(memory_space=pltpu.SMEM)
+    vmem = pl.BlockSpec(memory_space=pltpu.VMEM)
+    hbm = pl.BlockSpec(memory_space=pltpu.HBM)
+    packed = pl.pallas_call(
+        pack_kernel,
+        out_shape=jax.ShapeDtypeStruct((w_rows, slots * HD), BF),
+        in_specs=[vmem, vmem],
+        out_specs=vmem,
+    )(w_qkv.transpose(1, 2, 0, 3).reshape(3 * heads, w_rows, HD), w_out.transpose(0, 2, 1))
+    line = jnp.stack([packed] + [spread(packed, step, False) for step in (1, 2, 3)])
+    plane = [line] + [spread(line, step, True) for step in (1, 2, 3)]
+    plane += [pair_swap(rows) for rows in plane]
 
     own_clips = lax.dynamic_slice_in_dim(clip_row, at_frame * frames, frames, 0)
     member = own_clips[:, None] == jnp.arange(counts.shape[0], dtype=jnp.int32)[None, :]
@@ -244,9 +267,6 @@
 
     qkv = spatial_qkv[0].transpose(0, 2, 1, 3)
     cot = out_grad[0]
-    smem = pl.BlockSpec(memory_space=pltpu.SMEM)
-    vmem = pl.BlockSpec(memory_space=pltpu.VMEM)
-    hbm = pl.BlockSpec(memory_space=pltpu.HBM)
     sent = pl.pallas_call(
         spatial_forward,
         out_shape=jax.ShapeDtypeStruct((ranks, 2, frames, block, width), BF),
@@ -255,26 +275,8 @@
         compiler_params=pltpu.CompilerParams(vmem_limit_bytes=24 * 2**20),
     )(live, qkv, cot)
     cols = lax.all_to_all(sent, "frame", split_axis=0, concat_axis=0, tiled=True)
-    blocks = []
-    for a in range(2):
-        rows = cols[:, a].reshape(rows_t, width)
-        blocks += ring_gather(rows, "tensor", width_ranks, a == 0)
-
-    place = jnp.stack([at_clip, at_frame // 2, at_frame % 2, at_width])
-    halves = jax.ShapeDtypeStruct((2, model // 2, rows_t), BF)
-    wide = jax.ShapeDtypeStruct((rows_t, model), BF)
-    feats, gated, own_flip, other_flip = pl.pallas_call(
-        lambda *refs: assemble_kernel(width_ranks, *refs),
-        out_shape=[wide, wide, halves, halves],
-        in_specs=[smem] + [hbm] * (2 * width_ranks),
-        out_specs=[vmem] * 4,
-        scratch_shapes=[
-            pltpu.VMEM((model, rows_t), BF),
-            pltpu.SemaphoreType.DMA((2 * width_ranks,)),
-        ],
-        compiler_params=pltpu.CompilerParams(vmem_limit_bytes=58 * 2**20),
-    )(place, *blocks)
-    pair_flip = pair_swap(other_flip)
+    cols = cols.reshape(ranks, 2, frames * block, width)
+    whole = lax.all_gather(cols, "tensor", axis=3, tiled=True)
 
     sums_shape = (width_ranks, ranks, 2, frames * block, width)
     sums, both = pl.pallas_call(
@@ -283,17 +285,28 @@
             jax.ShapeDtypeStruct(sums_shape, BF),
             jax.ShapeDtypeStruct((rows_t, 4 * width), BF),
         ],
-        in_specs=[vmem] * 4 + [hbm] * 2,
+        in_specs=[smem, vmem, vmem] + [hbm] * (1 + len(plane)),
         out_specs=[hbm, vmem],
         scratch_shapes=[
             pltpu.VMEM((model, 4 * width), BF),
+            pltpu.VMEM((2, ranks, frames * block, model), BF),
             pltpu.VMEM(sums_shape, BF),
-            pltpu.SemaphoreType.DMA((slots,)),
+            pltpu.SemaphoreType.DMA((heads + 1, 4 * len(plane))),
+            pltpu.SemaphoreType.DMA((2,)),
             pltpu.SemaphoreType.DMA((width_ranks,)),
         ],
-        compiler_params=pltpu.CompilerParams(vmem_limit_bytes=56 * 2**20),
-    )(keys[:, None], keys[None, :], feats, gated, pair_flip, w_all)
-
+        compiler_params=pltpu.CompilerParams(vmem_limit_bytes=58 * 2**20),
+    )(place, keys[:, None], keys[None, :], whole, *plane)
+
+    halves = jax.ShapeDtypeStruct((2, model // 2, rows_t), BF)
+    own_flip, other_flip = pl.pallas_call(
+        flip_kernel,
+        out_shape=[halves, halves],
+        in_specs=[smem, vmem],
+        out_specs=[vmem] * 2,
+        compiler_params=pltpu.CompilerParams(vmem_limit_bytes=16 * 2**20),
+    )(place, whole)
+    pair_flip = pair_swap(other_flip)
     own_sums = lax.psum_scatter(sums, "tensor", scatter_dimension=0, tiled=True)[0]
     pair_both = pair_swap(both)
     parts = {}

time: 160 us -> 167 us (1.044)
  waiting for transfers between devices: 43.4 us -> 54.3 us
  starting transfers between devices: 43.7 us -> 40 us
    ppermute x6 -> x12, waiting for transfers between devices: 20.2 us -> 43.2 us  [spread(): return lax.ppermute(value, ('clip', 'frame'), pairs)]
    ppermute x14 -> x0, starting transfers between devices: 22.4 us -> none  [shift(): lax.ppermute(value, axis, [(i, (i + step) % size) for i in range(size)])]
    ppermute x2 -> x6, starting transfers between devices: 4.98 us -> 21.2 us  [pair_swap(): return lax.ppermute(value, 'frame', [(i, i ^ 1) for i in range(8)])]
    ppermute x14 -> x0, waiting for transfers between devices: 10.3 us -> none  [shift(): lax.ppermute(value, axis, [(i, (i + step) % size) for i in range(size)])]
    pallas_call x1 -> x2, Pallas kernels: 6.1 us -> 3.16 us  [the longest x1 1.76 us: body(): pl.pallas_call(pack_kernel, out_shape=jax.ShapeDtypeStruct((w_rows, slots...]
    ppermute x6 -> x12, starting transfers between devices: 8.66 us -> 11.3 us  [spread(): return lax.ppermute(value, ('clip', 'frame'), pairs)]
    concatenate x1 -> x0, other arithmetic: 1.77 us -> none  [body(): jnp.concatenate([w_qkv.transpose(1, 2, 0, 3).reshape(3 * heads, w_rows, H...]
    reduce_scatter x1, waiting for transfers between devices: 3.26 us -> 1.51 us  [body(): lax.psum_scatter(sums, 'tensor', scatter_dimension=0, tiled=True)[0]]
  transfers between devices with their start and end apart: 25 -> 21, of which waited for: 16 -> 12; matrix products, arithmetic and copies ran while one was open for 4% -> 4% of each run, Pallas kernels for 9% -> 5%
where the time goes in v1:
time: 167 us; the launch traced here: 166 us
  waiting for transfers between devices  54.3 us (33%)
  starting transfers between devices  40 us (24%)
  Pallas kernels  29.9 us (18%)
  blocking collectives  14.4 us (9%)
  between operations  14.2 us (9%)
  local copies, waits for them, and re-layouts  8.71 us (5%)
  other arithmetic  4.8 us (3%)
    ppermute x12, waiting for transfers between devices, spread(): return lax.ppermute(value, ('clip', 'frame'), pairs)  43.2 us
    ppermute x6, starting transfers between devices, pair_swap(): return lax.ppermute(value, 'frame', [(i, i ^ 1) for i in range(8)])  21.2 us
    pallas_call x1, Pallas kernels, body(): pl.pallas_call(lambda *refs: temporal_kernel(heads, *refs), out_shape=[ja...  15.9 us
    all_to_all x1, blocking collectives, body(): lax.all_to_all(sent, 'frame', split_axis=0, concat_axis=0, tiled=True)  14.4 us
    ppermute x12, starting transfers between devices, spread(): return lax.ppermute(value, ('clip', 'frame'), pairs)  11.3 us
    all_to_all x1, starting transfers between devices, body(): lax.all_to_all(own_sums, 'frame', split_axis=0, concat_axis=0, tiled=True)  7.37 us
    pallas_call x4, Pallas kernels, body(): pl.pallas_call(lambda *refs, step=step: weight_grad_kernel(step, *refs),...  5.66 us
    unnamed x26, local copies, waits for them, and re-layouts  5.12 us
  transfers between devices with their start and end apart: 21, of which 12 were waited for; matrix products, arithmetic and copies ran while one was open for 4% of the time, Pallas kernels for 5%

profile of v1, /device:TPU:1, one launch (start us, length us, event | category | flops | bytes accessed | tf_op | source)
XLA Modules:
  0.0 166.3 jit_solution(17847321670204096138)
XLA Ops:
  7.2 0.7 dynamic-slice_bitcast_fusion
  7.9 0.8 fusion.6.count_ref
  8.8 1.1 copy-done.2
  9.9 0.9 copy-done.4
  10.8 2.6 %shard_map.93 = bf16[8,2,2,16,384]{4,3,2,1,0:T(8,128)(2,1)S(1)} custom-call(s32[2]{0:T(128)S(1)} %fusion.6.count_ref, bf16[2,3,128,384]{3,2,1,0:T(8,128)(2,1)S(1)} %bitcast.44, bf16[2,128,384]{2,1,0:T(8,128)(2,1)S(1)} %bitcast.47), custom_call_target="tpu_custom_call" | custom-call | tf_op jit(solution)/shard_map/pallas_call | solution.py:270
  13.4 14.4 %all_to_all.10 = bf16[8,2,2,16,384]{4,3,2,1,0:T(8,128)(2,1)} all-to-all(bf16[8,2,2,16,384]{4,3,2,1,0:T(8,128)(2,1)S(1)} %shard_map.93), channel_id=1, replica_groups=mesh['clip'=4,'frame'=8,'tensor'=8] {'frame'}, dimensions={0} | all-to-all | bytes 786432 | tf_op jit(solution)/shard_map/all_to_all | solution.py:277
  27.8 1.8 %shard_map.94 = bf16[96,1536]{1,0:T(8,128)(2,1)} custom-call(bf16[9,96,128]{2,1,0:T(8,128)(2,1)} %bitcast.56, bf16[3,96,128]{2,1,0:T(8,128)(2,1)} %bitcast.57), custom_call_target="tpu_custom_call" | custom-call | tf_op jit(solution)/shard_map/pallas_call | solution.py:253
  29.6 2.1 %collective-permute-start.2 = (bf16[96,1536]{1,0:T(8,128)(2,1)}, bf16[96,1536]{1,0:T(8,128)(2,1)S(1)}, u32[]{:S(2)}, u32[]{:S(2)}) collective-permute-start(bf16[96,1536]{1,0:T(8,128)(2,1)} %shard_map.94), channel_id=1, source_target_pairs={{0,48},{8,200},{16,0},{24,216},{32,16},{40,232},{48,32},{56,248},{... | collective-permute-start | bytes 884744 | tf_op jit(solution)/shard_map/ppermute | solution.py:225
  32.1 0.7 collective-permute-start
  32.8 6.1 %collective-permute-done.2 = bf16[96,1536]{1,0:T(8,128)(2,1)S(1)} collective-permute-done((bf16[96,1536]{1,0:T(8,128)(2,1)}, bf16[96,1536]{1,0:T(8,128)(2,1)S(1)}, u32[]{:S(2)}, u32[]{:S(2)}) %collective-permute-start.2) | collective-permute-done | bytes 294944 | tf_op jit(solution)/shard_map/ppermute | solution.py:225
  39.4 3.1 %collective-permute-done = bf16[96,1536]{1,0:T(8,128)(2,1)S(1)} collective-permute-done((bf16[96,1536]{1,0:T(8,128)(2,1)}, bf16[96,1536]{1,0:T(8,128)(2,1)S(1)}, u32[]{:S(2)}, u32[]{:S(2)}) %collective-permute-start) | collective-permute-done | bytes 294944 | tf_op jit(solution)/shard_map/ppermute | solution.py:225
  42.5 1.1 pad_maximum_fusion.refs_4_
  43.6 0.7 collective-permute-start.5
  44.3 1.2 collective-permute-start.4
  45.5 3.0 %collective-permute-start.6 = (bf16[4,96,1536]{2,1,0:T(8,128)(2,1)S(1)}, bf16[4,96,1536]{2,1,0:T(8,128)(2,1)}, u32[]{:S(2)}, u32[]{:S(2)}) collective-permute-start(bf16[4,96,1536]{2,1,0:T(8,128)(2,1)S(1)} %pad_maximum_fusion.refs_4_), channel_id=1, source_target_pairs={{0,8},{8,0},{16,24},{24,16},{32,40},{40,32},{48,56},{56,48},{1,9},... | collective-permute-start | bytes 3538952 | tf_op jit(solution)/shard_map/ppermute | solution.py:211
  48.5 10.7 %collective-permute-done.5.refs_7_ = bf16[4,96,1536]{2,1,0:T(8,128)(2,1)S(1)} collective-permute-done((bf16[4,96,1536]{2,1,0:T(8,128)(2,1)S(1)}, bf16[4,96,1536]{2,1,0:T(8,128)(2,1)S(1)}, u32[]{:S(2)}, u32[]{:S(2)}) %collective-permute-start.5) | collective-permute-done | bytes 1179680 | tf_op jit(solution)/shard_map/ppermute | solution.py:225
  59.1 14.1 %collective-permute-start.9 = (bf16[4,96,1536]{2,1,0:T(8,128)(2,1)S(1)}, bf16[4,96,1536]{2,1,0:T(8,128)(2,1)}, u32[]{:S(2)}, u32[]{:S(2)}) collective-permute-start(bf16[4,96,1536]{2,1,0:T(8,128)(2,1)S(1)} %collective-permute-done.5.refs_7_), channel_id=1, source_target_pairs={{0,8},{8,0},{16,24},{24,16},{32,40},{40,32},{48,56},{56,48},{1,9},... | collective-permute-start | bytes 3538952 | tf_op jit(solution)/shard_map/ppermute | solution.py:211
  73.3 0.5 collective-permute-done.3.refs_5_
  73.9 3.4 %collective-permute-start.7 = (bf16[4,96,1536]{2,1,0:T(8,128)(2,1)}, bf16[4,96,1536]{2,1,0:T(8,128)(2,1)}, u32[]{:S(2)}, u32[]{:S(2)}) collective-permute-start(bf16[4,96,1536]{2,1,0:T(8,128)(2,1)} %collective-permute-done.3.refs_5_), channel_id=1, source_target_pairs={{0,8},{8,0},{16,24},{24,16},{32,40},{40,32},{48,56},{56,48},{1,9},... | collective-permute-start | bytes 3538952 | tf_op jit(solution)/shard_map/ppermute | solution.py:211
  77.4 0.6 add.114.refs_2_
  78.0 0.8 add.134.refs_1_
  78.8 0.6 pad_add_fusion.refs_0_.place_ref
  79.4 0.7 collective-permute-done.7.refs_9_
  80.1 15.9 %shard_map.95 = (bf16[8,8,2,32,384]{4,3,2,1,0:T(8,128)(2,1)}, bf16[256,1536]{1,0:T(8,128)(2,1)}) custom-call(s32[4]{0:T(128)} %pad_add_fusion.refs_0_.place_ref, s32[256,1]{1,0:T(8,128)} %add.134.refs_1_, s32[1,256]{1,0:T(1,128)} %add.114.refs_2_, bf16[8,2,32,3072]{3,2,1,0:T(8,128)(2,1)} %all-gather.2.cloned.1.call-done.refs_3_.whole_ref, ...), custom_call_target="tpu_custom_call" | custom-call | tf_op jit(solution)/shard_map/pallas_call | solution.py:282
  96.1 1.8 %copy-done.1 = bf16[8,2,32,3072]{3,2,1,0:T(8,128)(2,1)S(1)} copy-done((bf16[8,2,32,3072]{3,2,1,0:T(8,128)(2,1)S(1)}, bf16[8,2,32,3072]{3,2,1,0:T(8,128)(2,1)}, u32[]{:S(2)}) %copy-start.1) | copy-done | bytes 3145752
  98.0 1.4 shard_map.97
  99.4 0.5 collective-permute-start.10
  100.0 4.0 %collective-permute-done.11.refs_4_ = bf16[256,1536]{1,0:T(8,128)(2,1)S(1)} collective-permute-done((bf16[256,1536]{1,0:T(8,128)(2,1)S(1)}, bf16[256,1536]{1,0:T(8,128)(2,1)S(1)}, u32[]{:S(2)}, u32[]{:S(2)}) %collective-permute-start.11) | collective-permute-done | bytes 786464 | tf_op jit(solution)/shard_map/ppermute | solution.py:211
  104.0 1.4 shard_map.99
  105.4 0.7 collective-permute-start.12
  106.1 1.4 shard_map.100
  107.5 3.0 %collective-permute-start.13 = (bf16[4,12,96,128]{3,2,1,0:T(8,128)(2,1)S(1)}, bf16[4,12,96,128]{3,2,1,0:T(8,128)(2,1)S(1)}, u32[]{:S(2)}, u32[]{:S(2)}) collective-permute-start(bf16[4,12,96,128]{3,2,1,0:T(8,128)(2,1)S(1)} %shard_map.100), channel_id=1, source_target_pairs={{0,16},{8,72},{16,32},{24,88},{32,48},{40,104},{48,0},{56,120},{64... | collective-permute-start | bytes 3538952 | tf_op jit(solution)/shard_map/ppermute | solution.py:225
  110.5 1.4 shard_map.101
  112.0 1.4 shard_map.98
  113.4 9.2 %collective-permute-done.12 = bf16[4,12,96,128]{3,2,1,0:T(8,128)(2,1)S(1)} collective-permute-done((bf16[4,12,96,128]{3,2,1,0:T(8,128)(2,1)S(1)}, bf16[4,12,96,128]{3,2,1,0:T(8,128)(2,1)S(1)}, u32[]{:S(2)}, u32[]{:S(2)}) %collective-permute-start.12) | collective-permute-done | bytes 1179680 | tf_op jit(solution)/shard_map/ppermute | solution.py:225
  122.6 12.7 %collective-permute-done.13 = bf16[4,12,96,128]{3,2,1,0:T(8,128)(2,1)S(1)} collective-permute-done((bf16[4,12,96,128]{3,2,1,0:T(8,128)(2,1)S(1)}, bf16[4,12,96,128]{3,2,1,0:T(8,128)(2,1)S(1)}, u32[]{:S(2)}, u32[]{:S(2)}) %collective-permute-start.13) | collective-permute-done | bytes 1179680 | tf_op jit(solution)/shard_map/ppermute | solution.py:225
  135.7 0.7 copy-done.10
  136.3 0.5 fusion.3
  136.8 0.6 copy-done.11
  137.4 1.1 collective-permute-start.15
  138.5 1.0 collective-permute-start.17
  139.9 1.5 reduce-scatter.2.cloned.1.call-done
  141.4 7.4 %all-to-all-start.1 = ((bf16[8,2,32,384]{3,2,1,0:T(8,128)(2,1)}), bf16[8,2,32,384]{3,2,1,0:T(8,128)(2,1)S(1)}, u32[]{:S(2)}, u32[]{:S(2)}) async-start(bf16[8,2,32,384]{3,2,1,0:T(8,128)(2,1)} %bitcast.52), calls=%async_computation.2 | async-start | bytes 786432 | tf_op jit(solution)/shard_map/all_to_all | solution.py:325
  148.8 1.7 fusion.1
  150.5 0.8 slice.88
  151.3 0.7 slice_bitcast_fusion
  152.0 4.9 %all-to-all-done.1 = bf16[8,2,32,384]{3,2,1,0:T(8,128)(2,1)S(1)} async-done(((bf16[8,2,32,384]{3,2,1,0:T(8,128)(2,1)}), bf16[8,2,32,384]{3,2,1,0:T(8,128)(2,1)S(1)}, u32[]{:S(2)}, u32[]{:S(2)}) %all-to-all-start.1) | async-done | bytes 393248 | tf_op jit(solution)/shard_map/all_to_all | solution.py:325
  156.9 2.5 %shard_map.96 = (bf16[2,128,384]{2,1,0:T(8,128)(2,1)}, bf16[2,3,128,384]{3,2,1,0:T(8,128)(2,1)}) custom-call(s32[2]{0:T(128)S(1)} %fusion.6.count_ref, bf16[2,3,128,384]{3,2,1,0:T(8,128)(2,1)S(1)} %bitcast.45, bf16[2,128,384]{2,1,0:T(8,128)(2,1)S(1)} %bitcast.48, bf16[8,2,2,16,384]{4,3,2,1,0:T(8,128)(2,1)S(1)} %bitcast.46), custom_call_target="tpu_custom_call" | custom-call | tf_op jit(solution)/shard_map/pallas_call | solution.py:327
  (44 shorter events, 2.1 us)
Async XLA Ops:
  7.2 73.0 %all-gather.2.cloned.1.call-start = ((), (), s32[]{:S(2)}) async-start(), calls=%async_computation.3 | async-start | bytes 3538944 | tf_op jit(solution)/shard_map/all_gather | solution.py:279
  8.8 1.1 copy-start.2
  9.9 0.9 copy-start.4
  27.8 113.7 %reduce-scatter.2.cloned.1.call-start = ((), (), s32[]{:S(2)}) async-start(), calls=%async_computation.4 | async-start | bytes 3538944 | tf_op jit(solution)/shard_map/reduce_scatter | solution.py:310
  29.6 9.3 %collective-permute-start.2 = (bf16[96,1536]{1,0:T(8,128)(2,1)}, bf16[96,1536]{1,0:T(8,128)(2,1)S(1)}, u32[]{:S(2)}, u32[]{:S(2)}) collective-permute-start(bf16[96,1536]{1,0:T(8,128)(2,1)} %shard_map.94), channel_id=1, source_target_pairs={{0,48},{8,200},{16,0},{24,216},{32,16},{40,232},{48,32},{56,248},{... | collective-permute-start | bytes 884744 | tf_op jit(solution)/shard_map/ppermute | solution.py:225
  31.7 7.6 %collective-permute-start.1 = (bf16[96,1536]{1,0:T(8,128)(2,1)}, bf16[96,1536]{1,0:T(8,128)(2,1)S(1)}, u32[]{:S(2)}, u32[]{:S(2)}) collective-permute-start(bf16[96,1536]{1,0:T(8,128)(2,1)} %shard_map.94), channel_id=1, source_target_pairs={{0,32},{8,136},{16,48},{24,152},{32,0},{40,168},{48,16},{56,184},{... | collective-permute-start | bytes 884744 | tf_op jit(solution)/shard_map/ppermute | solution.py:225
  32.1 10.4 %collective-permute-start = (bf16[96,1536]{1,0:T(8,128)(2,1)}, bf16[96,1536]{1,0:T(8,128)(2,1)S(1)}, u32[]{:S(2)}, u32[]{:S(2)}) collective-permute-start(bf16[96,1536]{1,0:T(8,128)(2,1)} %shard_map.94), channel_id=1, source_target_pairs={{0,16},{8,72},{16,32},{24,88},{32,48},{40,104},{48,0},{56,120},{64... | collective-permute-start | bytes 884744 | tf_op jit(solution)/shard_map/ppermute | solution.py:225
  42.5 34.8 %copy-start.12 = (s32[1,16]{1,0:T(1,128)S(1)}, s32[1,16]{1,0:T(1,128)}, u32[]{:S(2)}) copy-start(s32[1,16]{1,0:T(1,128)} %param.10) | copy-start | bytes 196
  43.6 36.5 %copy-start.7 = (bf16[4,96,1536]{2,1,0:T(8,128)(2,1)}, bf16[4,96,1536]{2,1,0:T(8,128)(2,1)S(1)}, u32[]{:S(2)}) copy-start(bf16[4,96,1536]{2,1,0:T(8,128)(2,1)S(1)} %pad_maximum_fusion.refs_4_) | copy-start | bytes 3538948
  43.6 15.5 %collective-permute-start.5 = (bf16[4,96,1536]{2,1,0:T(8,128)(2,1)S(1)}, bf16[4,96,1536]{2,1,0:T(8,128)(2,1)S(1)}, u32[]{:S(2)}, u32[]{:S(2)}) collective-permute-start(bf16[4,96,1536]{2,1,0:T(8,128)(2,1)S(1)} %pad_maximum_fusion.refs_4_), channel_id=1, source_target_pairs={{0,192},{8,56},{16,208},{24,8},{32,224},{40,24},{48,240},{56,40},{... | collective-permute-start | bytes 3538952 | tf_op jit(solution)/shard_map/ppermute | solution.py:225
  44.3 29.0 %collective-permute-start.4 = (bf16[4,96,1536]{2,1,0:T(8,128)(2,1)S(1)}, bf16[4,96,1536]{2,1,0:T(8,128)(2,1)}, u32[]{:S(2)}, u32[]{:S(2)}) collective-permute-start(bf16[4,96,1536]{2,1,0:T(8,128)(2,1)S(1)} %pad_maximum_fusion.refs_4_), channel_id=1, source_target_pairs={{0,128},{8,40},{16,144},{24,56},{32,160},{40,8},{48,176},{56,24},{... | collective-permute-start | bytes 3538952 | tf_op jit(solution)/shard_map/ppermute | solution.py:225
  45.5 28.4 %collective-permute-start.3 = (bf16[4,96,1536]{2,1,0:T(8,128)(2,1)S(1)}, bf16[4,96,1536]{2,1,0:T(8,128)(2,1)}, u32[]{:S(2)}, u32[]{:S(2)}) collective-permute-start(bf16[4,96,1536]{2,1,0:T(8,128)(2,1)S(1)} %pad_maximum_fusion.refs_4_), channel_id=1, source_target_pairs={{0,64},{8,24},{16,80},{24,40},{32,96},{40,56},{48,112},{56,8},{64,... | collective-permute-start | bytes 3538952 | tf_op jit(solution)/shard_map/ppermute | solution.py:225
  45.5 34.0 %collective-permute-start.6 = (bf16[4,96,1536]{2,1,0:T(8,128)(2,1)S(1)}, bf16[4,96,1536]{2,1,0:T(8,128)(2,1)}, u32[]{:S(2)}, u32[]{:S(2)}) collective-permute-start(bf16[4,96,1536]{2,1,0:T(8,128)(2,1)S(1)} %pad_maximum_fusion.refs_4_), channel_id=1, source_target_pairs={{0,8},{8,0},{16,24},{24,16},{32,40},{40,32},{48,56},{56,48},{1,9},... | collective-permute-start | bytes 3538952 | tf_op jit(solution)/shard_map/ppermute | solution.py:211
  59.1 21.0 %copy-start.8 = (bf16[4,96,1536]{2,1,0:T(8,128)(2,1)}, bf16[4,96,1536]{2,1,0:T(8,128)(2,1)S(1)}, u32[]{:S(2)}) copy-start(bf16[4,96,1536]{2,1,0:T(8,128)(2,1)S(1)} %collective-permute-done.5.refs_7_) | copy-start | bytes 3538948
  59.1 20.3 %collective-permute-start.9 = (bf16[4,96,1536]{2,1,0:T(8,128)(2,1)S(1)}, bf16[4,96,1536]{2,1,0:T(8,128)(2,1)}, u32[]{:S(2)}, u32[]{:S(2)}) collective-permute-start(bf16[4,96,1536]{2,1,0:T(8,128)(2,1)S(1)} %collective-permute-done.5.refs_7_), channel_id=1, source_target_pairs={{0,8},{8,0},{16,24},{24,16},{32,40},{40,32},{48,56},{56,48},{1,9},... | collective-permute-start | bytes 3538952 | tf_op jit(solution)/shard_map/ppermute | solution.py:211
  73.3 6.2 %collective-permute-start.8 = (bf16[4,96,1536]{2,1,0:T(8,128)(2,1)}, bf16[4,96,1536]{2,1,0:T(8,128)(2,1)}, u32[]{:S(2)}, u32[]{:S(2)}) collective-permute-start(bf16[4,96,1536]{2,1,0:T(8,128)(2,1)} %collective-permute-done.4.refs_6_), channel_id=1, source_target_pairs={{0,8},{8,0},{16,24},{24,16},{32,40},{40,32},{48,56},{56,48},{1,9},... | collective-permute-start | bytes 3538952 | tf_op jit(solution)/shard_map/ppermute | solution.py:211
  73.9 6.2 %collective-permute-start.7 = (bf16[4,96,1536]{2,1,0:T(8,128)(2,1)}, bf16[4,96,1536]{2,1,0:T(8,128)(2,1)}, u32[]{:S(2)}, u32[]{:S(2)}) collective-permute-start(bf16[4,96,1536]{2,1,0:T(8,128)(2,1)} %collective-permute-done.3.refs_5_), channel_id=1, source_target_pairs={{0,8},{8,0},{16,24},{24,16},{32,40},{40,32},{48,56},{56,48},{1,9},... | collective-permute-start | bytes 3538952 | tf_op jit(solution)/shard_map/ppermute | solution.py:211
  80.1 16.0 %copy-start.6 = (s32[4]{0:T(128)S(1)}, s32[4]{0:T(128)}, u32[]{:S(2)}) copy-start(s32[4]{0:T(128)} %pad_add_fusion.refs_0_.place_ref) | copy-start | bytes 52
  96.1 1.9 %copy-start.1 = (bf16[8,2,32,3072]{3,2,1,0:T(8,128)(2,1)S(1)}, bf16[8,2,32,3072]{3,2,1,0:T(8,128)(2,1)}, u32[]{:S(2)}) copy-start(bf16[8,2,32,3072]{3,2,1,0:T(8,128)(2,1)} %all-gather.2.cloned.1.call-done.refs_3_.whole_ref) | copy-start | bytes 9437188
  98.0 1.9 %copy-start = (bf16[256,1536]{1,0:T(8,128)(2,1)S(1)}, bf16[256,1536]{1,0:T(8,128)(2,1)}, u32[]{:S(2)}) copy-start(bf16[256,1536]{1,0:T(8,128)(2,1)} %get-tuple-element.15.refs_3_) | copy-start | bytes 2359300
  99.4 4.6 %collective-permute-start.10 = (bf16[2,1536,256]{2,1,0:T(8,128)(2,1)S(1)}, bf16[2,1536,256]{2,1,0:T(8,128)(2,1)S(1)}, u32[]{:S(2)}, u32[]{:S(2)}) collective-permute-start(bf16[2,1536,256]{2,1,0:T(8,128)(2,1)S(1)} %get-tuple-element.14), channel_id=1, source_target_pairs={{0,8},{8,0},{16,24},{24,16},{32,40},{40,32},{48,56},{56,48},{1,9},... | collective-permute-start | bytes 4718600 | tf_op jit(solution)/shard_map/ppermute | solution.py:211
  99.8 4.2 %collective-permute-start.11 = (bf16[256,1536]{1,0:T(8,128)(2,1)S(1)}, bf16[256,1536]{1,0:T(8,128)(2,1)S(1)}, u32[]{:S(2)}, u32[]{:S(2)}) collective-permute-start(bf16[256,1536]{1,0:T(8,128)(2,1)S(1)} %copy-done), channel_id=1, source_target_pairs={{0,8},{8,0},{16,24},{24,16},{32,40},{40,32},{48,56},{56,48},{1,9},... | collective-permute-start | bytes 2359304 | tf_op jit(solution)/shard_map/ppermute | solution.py:211
  105.4 17.2 %collective-permute-start.12 = (bf16[4,12,96,128]{3,2,1,0:T(8,128)(2,1)S(1)}, bf16[4,12,96,128]{3,2,1,0:T(8,128)(2,1)S(1)}, u32[]{:S(2)}, u32[]{:S(2)}) collective-permute-start(bf16[4,12,96,128]{3,2,1,0:T(8,128)(2,1)S(1)} %shard_map.99), channel_id=1, source_target_pairs={{0,32},{8,136},{16,48},{24,152},{32,0},{40,168},{48,16},{56,184},{... | collective-permute-start | bytes 3538952 | tf_op jit(solution)/shard_map/ppermute | solution.py:225
  107.5 27.8 %collective-permute-start.13 = (bf16[4,12,96,128]{3,2,1,0:T(8,128)(2,1)S(1)}, bf16[4,12,96,128]{3,2,1,0:T(8,128)(2,1)S(1)}, u32[]{:S(2)}, u32[]{:S(2)}) collective-permute-start(bf16[4,12,96,128]{3,2,1,0:T(8,128)(2,1)S(1)} %shard_map.100), channel_id=1, source_target_pairs={{0,16},{8,72},{16,32},{24,88},{32,48},{40,104},{48,0},{56,120},{64... | collective-permute-start | bytes 3538952 | tf_op jit(solution)/shard_map/ppermute | solution.py:225
  111.9 23.7 %collective-permute-start.14 = (bf16[4,12,96,128]{3,2,1,0:T(8,128)(2,1)S(1)}, bf16[4,12,96,128]{3,2,1,0:T(8,128)(2,1)S(1)}, u32[]{:S(2)}, u32[]{:S(2)}) collective-permute-start(bf16[4,12,96,128]{3,2,1,0:T(8,128)(2,1)S(1)} %shard_map.101), channel_id=1, source_target_pairs={{0,48},{8,200},{16,0},{24,216},{32,16},{40,232},{48,32},{56,248},{... | collective-permute-start | bytes 3538952 | tf_op jit(solution)/shard_map/ppermute | solution.py:225
  122.6 18.8 %copy-start.9 = (bf16[4,12,96,128]{3,2,1,0:T(8,128)(2,1)}, bf16[4,12,96,128]{3,2,1,0:T(8,128)(2,1)S(1)}, u32[]{:S(2)}) copy-start(bf16[4,12,96,128]{3,2,1,0:T(8,128)(2,1)S(1)} %collective-permute-done.12) | copy-start | bytes 3538948
  135.3 1.0 copy-start.10
  136.3 1.0 copy-start.11
  137.4 11.4 %collective-permute-start.15 = (bf16[12,96,128]{2,1,0:T(8,128)(2,1)S(1)}, bf16[12,96,128]{2,1,0:T(8,128)(2,1)}, u32[]{:S(2)}, u32[]{:S(2)}) collective-permute-start(bf16[12,96,128]{2,1,0:T(8,128)(2,1)S(1)} %get-tuple-element.16), channel_id=1, source_target_pairs={{0,128},{8,40},{16,144},{24,56},{32,160},{40,8},{48,176},{56,24},{... | collective-permute-start | bytes 884744 | tf_op jit(solution)/shard_map/ppermute | solution.py:225
  138.5 10.4 %collective-permute-start.17 = (bf16[12,96,128]{2,1,0:T(8,128)(2,1)S(1)}, bf16[12,96,128]{2,1,0:T(8,128)(2,1)}, u32[]{:S(2)}, u32[]{:S(2)}) collective-permute-start(bf16[12,96,128]{2,1,0:T(8,128)(2,1)S(1)} %get-tuple-element.17), channel_id=1, source_target_pairs={{0,192},{8,56},{16,208},{24,8},{32,224},{40,24},{48,240},{56,40},{... | collective-permute-start | bytes 884744 | tf_op jit(solution)/shard_map/ppermute | solution.py:225
  139.5 9.3 %collective-permute-start.16 = (bf16[12,96,128]{2,1,0:T(8,128)(2,1)S(1)}, bf16[12,96,128]{2,1,0:T(8,128)(2,1)}, u32[]{:S(2)}, u32[]{:S(2)}) collective-permute-start(bf16[12,96,128]{2,1,0:T(8,128)(2,1)S(1)} %get-tuple-element.18), channel_id=1, source_target_pairs={{0,64},{8,24},{16,80},{24,40},{32,96},{40,56},{48,112},{56,8},{64,... | collective-permute-start | bytes 884744 | tf_op jit(solution)/shard_map/ppermute | solution.py:225
  141.4 15.5 %all-to-all-start.1 = ((bf16[8,2,32,384]{3,2,1,0:T(8,128)(2,1)}), bf16[8,2,32,384]{3,2,1,0:T(8,128)(2,1)S(1)}, u32[]{:S(2)}, u32[]{:S(2)}) async-start(bf16[8,2,32,384]{3,2,1,0:T(8,128)(2,1)} %bitcast.52), calls=%async_computation.2 | async-start | bytes 786432 | tf_op jit(solution)/shard_map/all_to_all | solution.py:325
  150.5 6.4 %copy-start.3 = (bf16[1,2,128,3,384]{4,2,3,1,0:T(8,128)(2,1)S(1)}, bf16[1,2,128,3,384]{4,2,3,1,0:T(8,128)(2,1)}, u32[]{:S(2)}) copy-start(bf16[1,2,128,3,384]{4,2,3,1,0:T(8,128)(2,1)} %param.6) | copy-start | bytes 1769476
  150.5 6.4 %copy-start.5 = (bf16[1,2,128,384]{3,2,1,0:T(8,128)(2,1)S(1)}, bf16[1,2,128,384]{3,2,1,0:T(8,128)(2,1)}, u32[]{:S(2)}) copy-start(bf16[1,2,128,384]{3,2,1,0:T(8,128)(2,1)} %param.9) | copy-start | bytes 589828
Sparse Core Ops, SparseCore 0:
  27.9 44.8 all-gather.1
  96.2 45.1 reduce-scatter.1

commit v2 on v1

v2 whole, which is shorter than its diff:
```python
import math

import jax
import jax.numpy as jnp
from jax import lax
from jax.experimental import pallas as pl
from jax.experimental.pallas import tpu as pltpu
from jax.sharding import PartitionSpec as P

HD = 128
SCALE = 1.0 / math.sqrt(HD)
BF = jnp.bfloat16
F32 = jnp.float32
NT = (((1,), (1,)), ((), ()))
TN = (((0,), (0,)), ((), ()))


def dot(a, b, dims=(((1,), (0,)), ((), ()))):
    return lax.dot_general(a, b, dims, preferred_element_type=F32)


def softmax(query, keys, mask):
    scores = jnp.where(mask, dot(query, keys, NT) * SCALE, -1e30)
    expo = jnp.exp(scores - jnp.max(scores, axis=-1, keepdims=True))
    return expo / jnp.sum(expo, axis=-1, keepdims=True)


def attention_grads(query, keys, values, probs, cotangent):
    d_values = dot(probs.astype(BF), cotangent, TN).astype(BF)
    d_probs = dot(cotangent, values, NT).astype(BF).astype(F32)
    inner = jnp.sum(probs * d_probs, axis=-1, keepdims=True)
    d_scores = (probs * (d_probs - inner) * SCALE).astype(BF)
    return dot(d_scores, keys).astype(BF), dot(d_scores, query, TN).astype(BF), d_values


def live_rows(row_ref, patch_ref, frame):
    return patch_ref[0, row_ref[0, frame]]


def spatial_forward(row_ref, patch_ref, qkv_ref, cot_ref, *refs):
    out_ref, whole_ref = refs
    frames, _, patches, width = qkv_ref.shape
    place = lax.axis_index("frame")
    owners = out_ref.shape[0]
    block = patches // owners
    for f in range(frames):
        count = live_rows(row_ref, patch_ref, place * frames + f)
        keys_live = lax.broadcasted_iota(jnp.int32, (patches, patches), 1) < count
        rows_live = lax.broadcasted_iota(jnp.int32, (patches, 1), 0) < count
        pieces = []
        for h in range(width // HD):
            cols = slice(h * HD, (h + 1) * HD)
            probs = softmax(qkv_ref[f, 0, :, cols], qkv_ref[f, 1, :, cols], keys_live)
            mixed = dot(probs.astype(BF), qkv_ref[f, 2, :, cols])
            pieces.append(jnp.where(rows_live, mixed, 0.0).astype(BF))
        whole_ref[0, f] = jnp.concatenate(pieces, axis=1)
        whole_ref[1, f] = jnp.where(rows_live, cot_ref[f].astype(F32), 0.0).astype(BF)
    for s in range(owners):
        out_ref[s] = whole_ref[:, :, s * block : (s + 1) * block, :]


def spatial_backward(row_ref, patch_ref, qkv_ref, cot_ref, *refs):
    blocks, (out_ref, grad_ref, whole_ref) = refs[:-3], refs[-3:]
    frames, _, patches, width = qkv_ref.shape
    place = lax.axis_index("frame")
    block = patches // len(blocks)
    for j, ref in enumerate(blocks):
        start = pl.multiple_of((place ^ j) * block, 16)
        for f in range(frames):
            whole_ref[:, f, pl.ds(start, block), :] = ref[:, f * block : (f + 1) * block, :]
    for f in range(frames):
        count = live_rows(row_ref, patch_ref, place * frames + f)
        keys_live = lax.broadcasted_iota(jnp.int32, (patches, patches), 1) < count
        rows_live = lax.broadcasted_iota(jnp.int32, (patches, 1), 0) < count
        d_spatial = cot_ref[f].astype(F32) + whole_ref[1, f].astype(F32)
        d_mixed = jnp.where(rows_live, d_spatial, 0.0).astype(BF)
        for h in range(width // HD):
            cols = slice(h * HD, (h + 1) * HD)
            query, keys, values = (qkv_ref[f, i, :, cols] for i in range(3))
            probs = softmax(query, keys, keys_live)
            mixed = dot(probs.astype(BF), values).astype(BF).astype(F32)
            total = mixed + whole_ref[0, f, :, cols].astype(F32)
            out_ref[f, :, cols] = jnp.where(rows_live, total, 0.0).astype(BF)
            grads = attention_grads(query, keys, values, probs, d_mixed[:, cols])
            for i in range(3):
                grad_ref[f, i, :, cols] = grads[i]


def pack_kernel(qkv_ref, out_ref, packed_ref):
    for ref, first in ((qkv_ref, 0), (out_ref, qkv_ref.shape[0])):
        for s in range(ref.shape[0]):
            packed_ref[:, (first + s) * HD : (first + s + 1) * HD] = ref[s]


def own_chip():
    place = lax.axis_index("frame")
    return lax.axis_index("clip"), place // 2, place % 2


def temporal_kernel(heads, row_key_ref, col_key_ref, whole_hbm, *refs):
    planes, refs = refs[:-11], refs[-11:]
    sums_hbm, both_ref, own_hbm, other_hbm, w_ref, token_ref, sums_ref, flip_ref = refs[:8]
    w_sem, in_sem, out_sem = refs[8:]
    at_clip, at_x, core = own_chip()
    place = lax.axis_index("frame")
    width = heads * HD
    ranks, owners, _, rows, _ = sums_ref.shape
    n, w_rows, _ = planes[0].shape
    tokens = [
        [
            pltpu.make_async_copy(
                whole_hbm.at[z, :, a],
                token_ref.at[a, :, :, z * width : (z + 1) * width],
                in_sem.at[a * ranks + z],
            )
            for z in range(ranks)
        ]
        for a in range(2)
    ]
    loads = [[], []]
    for half, owner in ((0, core), (1, 1 - core)):
        for second in range(n):
            for first in range(n):
                clip = lax.rem(at_clip + n - jnp.where(owner == 0, second, first), n)
                x = lax.rem(at_x + n - jnp.where(owner == 0, first, second), n)
                start = pl.multiple_of((clip * 2 * n + x * 2 + owner) * w_rows, 16)
                for g, cols in enumerate((pl.ds(0, 3 * width), pl.ds(3 * width, width))):
                    loads[g].append(
                        pltpu.make_async_copy(
                            planes[half * n + second].at[first, :, cols],
                            w_ref.at[pl.ds(start, w_rows), cols],
                            w_sem.at[g, len(loads[g])],
                        )
                    )
    for copy in tokens[0] + tokens[1] + loads[0]:
        copy.start()
    step = 4 * w_rows
    flips = []
    for a in range(2):
        for z in range(ranks):
            tokens[a][z].wait()
            part = token_ref[a, :, :, z * step : (z + 1) * step]
            flipped = part.reshape(owners * rows, step).T
            for i in range(2):
                even = flipped[2 * i * w_rows : (2 * i + 1) * w_rows]
                odd = flipped[(2 * i + 1) * w_rows : (2 * i + 2) * w_rows]
                to = slice((2 * z + i) * w_rows, (2 * z + i + 1) * w_rows)
                flip_ref[0, a, to] = jnp.where(core == 0, even, odd)
                flip_ref[1, a, to] = jnp.where(core == 0, odd, even)
    for i, ref in enumerate((own_hbm, other_hbm)):
        flips.append(pltpu.make_async_copy(flip_ref.at[i], ref, in_sem.at[2 * ranks + i]))
        flips[-1].start()
    mask = row_key_ref[...] == col_key_ref[...]
    for copy in loads[0]:
        copy.wait()
    for copy in loads[1]:
        copy.start()
    feats = token_ref[0].reshape(owners * rows, -1)
    query, keys, values = [], [], []
    for h in range(heads):
        qkv = dot(feats, w_ref[:, h * width : (h + 1) * width]).astype(BF)
        for i, parts in enumerate((query, keys, values)):
            parts.append(qkv[:, i * HD : (i + 1) * HD])
    each = range(heads)
    probs = [softmax(query[h], keys[h], mask) for h in each]
    mixed = [dot(probs[h].astype(BF), values[h]).astype(BF) for h in each]
    for copy in loads[1]:
        copy.wait()
    gated = token_ref[1].reshape(owners * rows, -1)
    cotangent = dot(gated, w_ref[:, 3 * width :]).astype(BF)
    for h in each:
        cols = slice(h * HD, (h + 1) * HD)
        grads = attention_grads(query[h], keys[h], values[h], probs[h], cotangent[:, cols])
        for i in range(3):
            both_ref[:, (3 * h + i) * HD : (3 * h + i + 1) * HD] = grads[i]
        both_ref[:, 3 * width + h * HD : 3 * width + (h + 1) * HD] = mixed[h]
    stores = []
    pair = 2
    for first in range(0, ranks, pair):
        part = slice(first * width, (first + pair) * width)
        projected = dot(both_ref[:, 3 * width :], w_ref[part, 3 * width :], NT).astype(BF)
        back = dot(both_ref[:, : 3 * width], w_ref[part, : 3 * width], NT).astype(BF)
        for i in range(pair):
            z, cols = first + i, slice(i * width, (i + 1) * width)
            for s in range(owners):
                sums_ref[z, s ^ place, 0] = projected[s * rows : (s + 1) * rows, cols]
                sums_ref[z, s ^ place, 1] = back[s * rows : (s + 1) * rows, cols]
            stores.append(pltpu.make_async_copy(sums_ref.at[z], sums_hbm.at[z], out_sem.at[z]))
            stores[-1].start()
    for copy in stores + flips:
        copy.wait()


def weight_grad_kernel(step, own_ref, pair_ref, both_ref, pair_both_ref, out_ref):
    at_clip, at_x, core = own_chip()
    n, slots, rows, _ = out_ref.shape
    wide = both_ref.shape[1] * 3 // 4
    starts = []
    for r in range(n):
        clip = lax.rem(at_clip + jnp.where(core == 0, r, step), n)
        x = lax.rem(at_x + jnp.where(core == 0, step, r), n)
        starts.append(pl.multiple_of((clip * n + x) * rows, 16))
    for a, cols in ((0, slice(0, wide)), (1, slice(wide, 4 * wide // 3))):
        left = jnp.concatenate(
            [
                jnp.concatenate([ref[a, pl.ds(start, rows), :] for start in starts], axis=0)
                for ref in (own_ref, pair_ref)
            ],
            axis=1,
        )
        right = jnp.concatenate([both_ref[:, cols], pair_both_ref[:, cols]], axis=0)
        total = dot(left, right).astype(BF)
        for r in range(n):
            for s in range(total.shape[1] // HD):
                part = total[r * rows : (r + 1) * rows, s * HD : (s + 1) * HD]
                out_ref[r, a * (slots * 3 // 4) + s] = part


def trade(value, j):
    return lax.ppermute(value, "frame", [(i, i ^ j) for i in range(8)])


def spread(value, step, second):
    pairs = []
    for clip in range(4):
        for x in range(4):
            for core in range(2):
                to_clip, to_x = clip, x
                if (core == 0) != second:
                    to_x = (x + step) % 4
                else:
                    to_clip = (clip + step) % 4
                pairs.append((clip * 8 + x * 2 + core, to_clip * 8 + to_x * 2 + core))
    return lax.ppermute(value, ("clip", "frame"), pairs)


def add(*values):
    return sum(v.astype(F32) for v in values)


def body(spatial_qkv, w_qkv, w_out, out_grad, frame_clip, clip_patches):
    ranks = lax.axis_size("frame")
    width_ranks = lax.axis_size("tensor")
    total_frames = frame_clip.shape[1]
    _, frames, patches, _, width = spatial_qkv.shape
    heads = width // HD
    block = patches // ranks
    rows_t = total_frames * block
    model = width * width_ranks
    slots = 4 * heads
    w_rows = w_qkv.shape[0]
    smem = pl.BlockSpec(memory_space=pltpu.SMEM)
    vmem = pl.BlockSpec(memory_space=pltpu.VMEM)
    hbm = pl.BlockSpec(memory_space=pltpu.HBM)

    qkv = spatial_qkv[0].transpose(0, 2, 1, 3)
    cot = out_grad[0]
    sent = pl.pallas_call(
        spatial_forward,
        out_shape=jax.ShapeDtypeStruct((ranks, 2, frames, block, width), BF),
        in_specs=[smem, smem, vmem, vmem],
        out_specs=vmem,
        scratch_shapes=[pltpu.VMEM((2, frames, patches, width), BF)],
        compiler_params=pltpu.CompilerParams(vmem_limit_bytes=58 * 2**20),
    )(frame_clip, clip_patches, qkv, cot)
    packed = pl.pallas_call(
        pack_kernel,
        out_shape=jax.ShapeDtypeStruct((w_rows, slots * HD), BF),
        in_specs=[vmem, vmem],
        out_specs=vmem,
    )(w_qkv.transpose(1, 2, 0, 3).reshape(3 * heads, w_rows, HD), w_out.transpose(0, 2, 1))
    near = [spread(packed, step, False) for step in (1, 2, 3)]
    cols = lax.all_to_all(sent, "frame", split_axis=0, concat_axis=0, tiled=True)
    cols = cols.reshape(ranks, 2, frames * block, width)
    cols, *near = lax.optimization_barrier([cols, *near])
    whole = lax.all_gather(cols, "tensor", axis=0, tiled=True)
    whole = whole.reshape((width_ranks,) + cols.shape)
    line = jnp.stack([packed] + near)
    plane = [line] + [spread(line, step, True) for step in (1, 2, 3)]
    plane += [trade(rows, 1) for rows in plane]

    clips = frame_clip[0][:, None] * block
    keys = (clips + jnp.arange(block, dtype=jnp.int32)[None, :]).reshape(rows_t)

    sums_shape = (width_ranks, ranks, 2, frames * block, width)
    halves = jax.ShapeDtypeStruct((2, model // 2, rows_t), BF)
    sums, both, own_flip, other_flip = pl.pallas_call(
        lambda *refs: temporal_kernel(heads, *refs),
        out_shape=[
            jax.ShapeDtypeStruct(sums_shape, BF),
            jax.ShapeDtypeStruct((rows_t, 4 * width), BF),
            halves,
            halves,
        ],
        in_specs=[vmem, vmem] + [hbm] * (1 + len(plane)),
        out_specs=[hbm, vmem, hbm, hbm],
        scratch_shapes=[
            pltpu.VMEM((model, 4 * width), BF),
            pltpu.VMEM((2, ranks, frames * block, model), BF),
            pltpu.VMEM(sums_shape, BF),
            pltpu.VMEM((2, 2, model // 2, rows_t), BF),
            pltpu.SemaphoreType.DMA((2, 4 * len(plane))),
            pltpu.SemaphoreType.DMA((2 * width_ranks + 2,)),
            pltpu.SemaphoreType.DMA((width_ranks,)),
        ],
        compiler_params=pltpu.CompilerParams(vmem_limit_bytes=58 * 2**20),
    )(keys[:, None], keys[None, :], whole, *plane)
    pair_flip = trade(other_flip, 1)
    own_sums = lax.psum_scatter(sums, "tensor", scatter_dimension=0, tiled=True)[0]
    pair_both = trade(both, 1)
    parts = {}
    for step in (2, 1, 3, 0):
        parts[step] = pl.pallas_call(
            lambda *refs, step=step: weight_grad_kernel(step, *refs),
            out_shape=jax.ShapeDtypeStruct((4, slots, w_rows, HD), BF),
            in_specs=[vmem] * 4,
            out_specs=vmem,
            compiler_params=pltpu.CompilerParams(vmem_limit_bytes=24 * 2**20),
        )(own_flip, pair_flip, both, pair_both)
    arrived = [parts[0]] + [spread(parts[step], step, False) for step in (2, 1, 3)]
    partial = [add(*(part[i] for part in arrived)).astype(BF) for i in range(4)]
    grads = add(partial[0], *(spread(partial[step], step, True) for step in (2, 1, 3)))

    traded = [own_sums[0]] + [trade(own_sums[j], j) for j in range(1, ranks)]
    block_out, qkv_grad = pl.pallas_call(
        spatial_backward,
        out_shape=[
            jax.ShapeDtypeStruct((frames, patches, width), BF),
            jax.ShapeDtypeStruct((frames, 3, patches, width), BF),
        ],
        in_specs=[smem, smem] + [vmem] * (2 + ranks),
        out_specs=[vmem, vmem],
        scratch_shapes=[pltpu.VMEM((2, frames, patches, width), BF)],
        compiler_params=pltpu.CompilerParams(vmem_limit_bytes=24 * 2**20),
    )(frame_clip, clip_patches, qkv, cot, *traded)

    w_qkv_grad = grads[: 3 * heads].reshape(heads, 3, w_rows, HD).transpose(2, 0, 1, 3)
    w_out_grad = grads[3 * heads :].transpose(0, 2, 1)
    return (block_out[None], qkv_grad.transpose(0, 2, 1, 3)[None], w_qkv_grad, w_out_grad)


def solution(mesh):
    in_specs = (
        P("clip", "frame", None, None, "tensor"),
        P(("clip", "frame"), "tensor", None, None),
        P("tensor", None, ("clip", "frame")),
        P("clip", "frame", None, "tensor"),
        P("clip", None),
        P("clip", None),
    )
    out_specs = (
        P("clip", "frame", None, "tensor"),
        P("clip", "frame", None, None, "tensor"),
        P(("clip", "frame"), "tensor", None, None),
        P("tensor", None, ("clip", "frame")),
    )
    return jax.shard_map(body, mesh=mesh, in_specs=in_specs, out_specs=out_specs, check_vma=False)
```

time: 167 us -> 165 us (0.988)
  waiting for transfers between devices: 54.3 us -> 68.9 us
  blocking collectives: 14.4 us -> 0 us
  starting transfers between devices: 40 us -> 44.7 us
  local copies, waits for them, and re-layouts: 8.71 us -> 5.59 us
  other arithmetic: 4.8 us -> 3.1 us
    all_to_all x1 -> x0, blocking collectives: 14.4 us -> none  [body(): lax.all_to_all(sent, 'frame', split_axis=0, concat_axis=0, tiled=True)]
    ppermute x12, waiting for transfers between devices: 43.2 us -> 54.4 us  [spread(): return lax.ppermute(value, ('clip', 'frame'), pairs)]
    all_gather x1, waiting for transfers between devices: 0.01 us -> 7.48 us  [body(): whole = lax.all_gather(cols, 'tensor', axis=0, tiled=True)]
    ppermute x12, starting transfers between devices: 11.3 us -> 16.5 us  [spread(): return lax.ppermute(value, ('clip', 'frame'), pairs)]
    all_to_all x1, waiting for transfers between devices: 4.9 us -> 0.01 us  [body(): lax.all_to_all(sent, 'frame', split_axis=0, concat_axis=0, tiled=True)]
    unnamed x26, local copies, waits for them, and re-layouts: 5.12 us -> 1.72 us
    pallas_call x4, Pallas kernels: 5.66 us -> 3.5 us  [body(): pl.pallas_call(lambda *refs, step=step: weight_grad_kernel(step, *refs),...]
    ppermute x6 -> x13, waiting for transfers between devices: 4.71 us -> 5.33 us  [trade(): return lax.ppermute(value, 'frame', [(i, i ^ j) for i in range(8)])]
  transfers between devices with their start and end apart: 21 -> 28, of which waited for: 12 -> 14; matrix products, arithmetic and copies ran while one was open for 4% -> 4% of each run, Pallas kernels for 5% -> 3%
where the time goes in v2:
time: 165 us
  waiting for transfers between devices  68.9 us (42%)
  starting transfers between devices  44.7 us (27%)
  Pallas kernels  28.4 us (17%)
  between operations  14.2 us (9%)
  local copies, waits for them, and re-layouts  5.59 us (3%)
  other arithmetic  3.1 us (2%)
    ppermute x12, waiting for transfers between devices, spread(): return lax.ppermute(value, ('clip', 'frame'), pairs)  54.4 us
    ppermute x13, starting transfers between devices, trade(): return lax.ppermute(value, 'frame', [(i, i ^ j) for i in range(8)])  21.5 us
    pallas_call x1, Pallas kernels, body(): pl.pallas_call(lambda *refs: temporal_kernel(heads, *refs), out_shape=[ja...  16.7 us
    ppermute x12, starting transfers between devices, spread(): return lax.ppermute(value, ('clip', 'frame'), pairs)  16.5 us
    all_gather x1, waiting for transfers between devices, body(): whole = lax.all_gather(cols, 'tensor', axis=0, tiled=True)  7.48 us
    all_to_all x1, starting transfers between devices, body(): lax.all_to_all(sent, 'frame', split_axis=0, concat_axis=0, tiled=True)  6.59 us
    ppermute x13, waiting for transfers between devices, trade(): return lax.ppermute(value, 'frame', [(i, i ^ j) for i in range(8)])  5.33 us
    pallas_call x1, Pallas kernels, body(): pl.pallas_call(spatial_forward, out_shape=jax.ShapeDtypeStruct((ranks, 2,...  3.93 us
  transfers between devices with their start and end apart: 28, of which 14 were waited for; matrix products, arithmetic and copies ran while one was open for 4% of the time, Pallas kernels for 3%

profile of v2, /device:TPU:1, one launch (start us, length us, event | category | flops | bytes accessed | tf_op | source)
XLA Modules:
  0.0 164.9 jit_solution(10969006625067198468)
XLA Ops:
  7.2 3.9 %shard_map.93 = bf16[8,2,2,16,384]{4,3,2,1,0:T(8,128)(2,1)} custom-call(s32[1,16]{1,0:T(1,128)} %row_ref.3, s32[1,8]{1,0:T(1,128)} %patch_ref.3, bf16[2,3,128,384]{3,2,1,0:T(8,128)(2,1)} %bitcast.52, bf16[2,128,384]{2,1,0:T(8,128)(2,1)} %bitcast.54), custom_call_target="tpu_custom_call" | custom-call | tf_op jit(solution)/shard_map/pallas_call | solution.py:258
  11.1 6.6 %all-to-all-start = ((bf16[8,2,2,16,384]{4,3,2,1,0:T(8,128)(2,1)}), bf16[8,2,2,16,384]{4,3,2,1,0:T(8,128)(2,1)S(1)}, u32[]{:S(2)}, u32[]{:S(2)}) async-start(bf16[8,2,2,16,384]{4,3,2,1,0:T(8,128)(2,1)} %shard_map.93), calls=%async_computation | async-start | bytes 786432 | tf_op jit(solution)/shard_map/all_to_all | solution.py:273
  17.7 1.8 %shard_map.94 = bf16[96,1536]{1,0:T(8,128)(2,1)} custom-call(bf16[9,96,128]{2,1,0:T(8,128)(2,1)} %bitcast.63, bf16[3,96,128]{2,1,0:T(8,128)(2,1)} %bitcast.64), custom_call_target="tpu_custom_call" | custom-call | tf_op jit(solution)/shard_map/pallas_call | solution.py:266
  19.4 1.9 %collective-permute-start.2 = (bf16[96,1536]{1,0:T(8,128)(2,1)}, bf16[96,1536]{1,0:T(8,128)(2,1)S(1)}, u32[]{:S(2)}, u32[]{:S(2)}) collective-permute-start(bf16[96,1536]{1,0:T(8,128)(2,1)} %shard_map.94), channel_id=1, source_target_pairs={{0,48},{8,200},{16,0},{24,216},{32,16},{40,232},{48,32},{56,248},{... | collective-permute-start | bytes 884744 | tf_op jit(solution)/shard_map/ppermute | solution.py:234
  21.7 0.7 collective-permute-start
  22.4 6.1 %collective-permute-done.2 = bf16[96,1536]{1,0:T(8,128)(2,1)S(1)} collective-permute-done((bf16[96,1536]{1,0:T(8,128)(2,1)}, bf16[96,1536]{1,0:T(8,128)(2,1)S(1)}, u32[]{:S(2)}, u32[]{:S(2)}) %collective-permute-start.2) | collective-permute-done | bytes 294944 | tf_op jit(solution)/shard_map/ppermute | solution.py:234
  29.0 3.1 %collective-permute-done = bf16[96,1536]{1,0:T(8,128)(2,1)S(1)} collective-permute-done((bf16[96,1536]{1,0:T(8,128)(2,1)}, bf16[96,1536]{1,0:T(8,128)(2,1)S(1)}, u32[]{:S(2)}, u32[]{:S(2)}) %collective-permute-start) | collective-permute-done | bytes 294944 | tf_op jit(solution)/shard_map/ppermute | solution.py:234
  32.1 0.7 copy-done.7
  33.0 1.1 pad_maximum_fusion.refs_3_
  34.1 2.4 %collective-permute-start.5 = (bf16[4,96,1536]{2,1,0:T(8,128)(2,1)S(1)}, bf16[4,96,1536]{2,1,0:T(8,128)(2,1)S(1)}, u32[]{:S(2)}, u32[]{:S(2)}) collective-permute-start(bf16[4,96,1536]{2,1,0:T(8,128)(2,1)S(1)} %pad_maximum_fusion.refs_3_), channel_id=1, source_target_pairs={{0,192},{8,56},{16,208},{24,8},{32,224},{40,24},{48,240},{56,40},{... | collective-permute-start | bytes 3538952 | tf_op jit(solution)/shard_map/ppermute | solution.py:234
  36.5 0.6 collective-permute-start.4
  37.1 0.6 collective-permute-start.3
  37.6 2.5 %collective-permute-start.6 = (bf16[4,96,1536]{2,1,0:T(8,128)(2,1)S(1)}, bf16[4,96,1536]{2,1,0:T(8,128)(2,1)}, u32[]{:S(2)}, u32[]{:S(2)}) collective-permute-start(bf16[4,96,1536]{2,1,0:T(8,128)(2,1)S(1)} %pad_maximum_fusion.refs_3_), channel_id=1, source_target_pairs={{0,8},{8,0},{16,24},{24,16},{32,40},{40,32},{48,56},{56,48},{1,9},... | collective-permute-start | bytes 3538952 | tf_op jit(solution)/shard_map/ppermute | solution.py:220
  40.1 22.1 %collective-permute-done.5.refs_6_ = bf16[4,96,1536]{2,1,0:T(8,128)(2,1)S(1)} collective-permute-done((bf16[4,96,1536]{2,1,0:T(8,128)(2,1)S(1)}, bf16[4,96,1536]{2,1,0:T(8,128)(2,1)S(1)}, u32[]{:S(2)}, u32[]{:S(2)}) %collective-permute-start.5) | collective-permute-done | bytes 1179680 | tf_op jit(solution)/shard_map/ppermute | solution.py:234
  62.3 2.7 %collective-permute-start.9 = (bf16[4,96,1536]{2,1,0:T(8,128)(2,1)S(1)}, bf16[4,96,1536]{2,1,0:T(8,128)(2,1)}, u32[]{:S(2)}, u32[]{:S(2)}) collective-permute-start(bf16[4,96,1536]{2,1,0:T(8,128)(2,1)S(1)} %collective-permute-done.5.refs_6_), channel_id=1, source_target_pairs={{0,8},{8,0},{16,24},{24,16},{32,40},{40,32},{48,56},{56,48},{1,9},... | collective-permute-start | bytes 3538952 | tf_op jit(solution)/shard_map/ppermute | solution.py:220
  65.0 1.0 collective-permute-done.3.refs_4_
  66.1 2.9 %collective-permute-start.7 = (bf16[4,96,1536]{2,1,0:T(8,128)(2,1)}, bf16[4,96,1536]{2,1,0:T(8,128)(2,1)}, u32[]{:S(2)}, u32[]{:S(2)}) collective-permute-start(bf16[4,96,1536]{2,1,0:T(8,128)(2,1)} %collective-permute-done.3.refs_4_), channel_id=1, source_target_pairs={{0,8},{8,0},{16,24},{24,16},{32,40},{40,32},{48,56},{56,48},{1,9},... | collective-permute-start | bytes 3538952 | tf_op jit(solution)/shard_map/ppermute | solution.py:220
  69.1 0.6 add.104.refs_1_
  69.7 0.8 add.124.refs_0_
  70.5 1.3 collective-permute-done.7.refs_8_
  71.8 7.5 %all-gather.2.cloned.1.call-done = bf16[64,2,32,384]{3,2,1,0:T(8,128)(2,1)} async-done(((bf16[8,2,32,384]{3,2,1,0:T(8,128)(2,1)}), bf16[64,2,32,384]{3,2,1,0:T(8,128)(2,1)}) %all-gather.2.cloned.1.call-update) | async-done | bytes 3145744 | tf_op jit(solution)/shard_map/all_gather | solution.py:276
  79.3 16.7 %shard_map.95 = (bf16[8,8,2,32,384]{4,3,2,1,0:T(8,128)(2,1)}, bf16[256,1536]{1,0:T(8,128)(2,1)}, bf16[2,1536,256]{2,1,0:T(8,128)(2,1)}, bf16[2,1536,256]{2,1,0:T(8,128)(2,1)}) custom-call(s32[256,1]{1,0:T(8,128)} %add.124.refs_0_, s32[1,256]{1,0:T(1,128)} %add.104.refs_1_, bf16[8,8,2,32,384]{4,3,2,1,0:T(8,128)(2,1)} %bitcast.56, ...), custom_call_target="tpu_custom_call" | custom-call | tf_op jit(solution)/shard_map/pallas_call | solution.py:287
  96.0 1.0 collective-permute-start.17
  97.1 0.9 collective-permute-start.18
  98.0 3.2 %collective-permute-done.18.refs_3_ = bf16[256,1536]{1,0:T(8,128)(2,1)S(1)} collective-permute-done((bf16[256,1536]{1,0:T(8,128)(2,1)S(1)}, bf16[256,1536]{1,0:T(8,128)(2,1)S(1)}, u32[]{:S(2)}, u32[]{:S(2)}) %collective-permute-start.18) | collective-permute-done | bytes 786464 | tf_op jit(solution)/shard_map/ppermute | solution.py:220
  101.2 0.9 shard_map.98
  102.1 3.0 %collective-permute-start.19 = (bf16[4,12,96,128]{3,2,1,0:T(8,128)(2,1)S(1)}, bf16[4,12,96,128]{3,2,1,0:T(8,128)(2,1)S(1)}, u32[]{:S(2)}, u32[]{:S(2)}) collective-permute-start(bf16[4,12,96,128]{3,2,1,0:T(8,128)(2,1)S(1)} %shard_map.98), channel_id=1, source_target_pairs={{0,32},{8,136},{16,48},{24,152},{32,0},{40,168},{48,16},{56,184},{... | collective-permute-start | bytes 3538952 | tf_op jit(solution)/shard_map/ppermute | solution.py:234
  105.1 0.9 shard_map.99
  106.4 0.9 shard_map.100
  107.3 2.4 %collective-permute-start.21 = (bf16[4,12,96,128]{3,2,1,0:T(8,128)(2,1)S(1)}, bf16[4,12,96,128]{3,2,1,0:T(8,128)(2,1)S(1)}, u32[]{:S(2)}, u32[]{:S(2)}) collective-permute-start(bf16[4,12,96,128]{3,2,1,0:T(8,128)(2,1)S(1)} %shard_map.100), channel_id=1, source_target_pairs={{0,48},{8,200},{16,0},{24,216},{32,16},{40,232},{48,32},{56,248},{... | collective-permute-start | bytes 3538952 | tf_op jit(solution)/shard_map/ppermute | solution.py:234
  109.7 0.9 shard_map.97
  110.6 8.7 %collective-permute-done.19 = bf16[4,12,96,128]{3,2,1,0:T(8,128)(2,1)S(1)} collective-permute-done((bf16[4,12,96,128]{3,2,1,0:T(8,128)(2,1)S(1)}, bf16[4,12,96,128]{3,2,1,0:T(8,128)(2,1)S(1)}, u32[]{:S(2)}, u32[]{:S(2)}) %collective-permute-start.19) | collective-permute-done | bytes 1179680 | tf_op jit(solution)/shard_map/ppermute | solution.py:234
  119.3 12.7 %collective-permute-done.20 = bf16[4,12,96,128]{3,2,1,0:T(8,128)(2,1)S(1)} collective-permute-done((bf16[4,12,96,128]{3,2,1,0:T(8,128)(2,1)S(1)}, bf16[4,12,96,128]{3,2,1,0:T(8,128)(2,1)S(1)}, u32[]{:S(2)}, u32[]{:S(2)}) %collective-permute-start.20) | collective-permute-done | bytes 1179680 | tf_op jit(solution)/shard_map/ppermute | solution.py:234
  132.1 0.5 fusion.3
  132.6 0.5 copy-done.11
  133.4 2.7 %collective-permute-start.22 = (bf16[12,96,128]{2,1,0:T(8,128)(2,1)S(1)}, bf16[12,96,128]{2,1,0:T(8,128)(2,1)S(1)}, u32[]{:S(2)}, u32[]{:S(2)}) collective-permute-start(bf16[12,96,128]{2,1,0:T(8,128)(2,1)S(1)} %get-tuple-element.24), channel_id=1, source_target_pairs={{0,128},{8,40},{16,144},{24,56},{32,160},{40,8},{48,176},{56,24},{... | collective-permute-start | bytes 884744 | tf_op jit(solution)/shard_map/ppermute | solution.py:234
  136.1 0.9 collective-permute-start.24
  137.0 0.6 collective-permute-start.23
  137.6 1.7 %reduce-scatter.2.cloned.1.call-done = bf16[1,8,2,32,384]{4,3,2,1,0:T(8,128)(2,1)} async-done(((bf16[8,8,2,32,384]{4,3,2,1,0:T(8,128)(2,1)}), bf16[1,8,2,32,384]{4,3,2,1,0:T(8,128)(2,1)}) %reduce-scatter.2.cloned.1.call-update) | async-done | bytes 393232 | tf_op jit(solution)/shard_map/reduce_scatter | solution.py:309
  139.3 1.0 slice_bitcast_fusion.1
  140.3 5.7 %collective-permute-start.16 = (bf16[2,32,384]{2,1,0:T(8,128)(2,1)S(1)}, bf16[2,32,384]{2,1,0:T(8,128)(2,1)S(1)}, u32[]{:S(2)}, u32[]{:S(2)}) collective-permute-start(bf16[2,32,384]{2,1,0:T(8,128)(2,1)S(1)} %get-tuple-element.27), channel_id=1, source_target_pairs={{0,56},{8,48},{16,40},{24,32},{32,24},{40,16},{48,8},{56,0},{1,57}... | collective-permute-start | bytes 147464 | tf_op jit(solution)/shard_map/ppermute | solution.py:220
  146.3 1.4 fusion.1
  147.8 3.0 %collective-permute-start.14 = (bf16[2,32,384]{2,1,0:T(8,128)(2,1)S(1)}, bf16[2,32,384]{2,1,0:T(8,128)(2,1)S(1)}, u32[]{:S(2)}, u32[]{:S(2)}) collective-permute-start(bf16[2,32,384]{2,1,0:T(8,128)(2,1)S(1)} %get-tuple-element.29), channel_id=1, source_target_pairs={{0,40},{8,32},{16,56},{24,48},{32,8},{40,0},{48,24},{56,16},{1,41}... | collective-permute-start | bytes 147464 | tf_op jit(solution)/shard_map/ppermute | solution.py:220
  151.4 1.5 collective-permute-start.11
  153.2 0.7 slice_bitcast_fusion
  153.9 0.8 slice.136
  154.7 0.6 collective-permute-done.13.refs_4_
  155.5 2.5 %shard_map.96 = (bf16[2,128,384]{2,1,0:T(8,128)(2,1)}, bf16[2,3,128,384]{3,2,1,0:T(8,128)(2,1)}) custom-call(s32[1,16]{1,0:T(1,128)S(1)} %copy-done.4, s32[1,8]{1,0:T(1,128)S(1)} %copy-done.5, bf16[2,3,128,384]{3,2,1,0:T(8,128)(2,1)S(1)} %bitcast.53, bf16[2,128,384]{2,1,0:T(8,128)(2,1)S(1)} %bitcast.55, bf16[2,32,384]{2,1,0:T(8,128)(2,1)S(1)} %get-tuple-element.34.refs_0_, ...), custom_call_target="tpu_custom_call" | custom-call | tf_op jit(solution)/shard_map/pallas_call | solution.py:325
  (54 shorter events, 3.6 us)
Async XLA Ops:
  11.1 21.0 %all-to-all-start = ((bf16[8,2,2,16,384]{4,3,2,1,0:T(8,128)(2,1)}), bf16[8,2,2,16,384]{4,3,2,1,0:T(8,128)(2,1)S(1)}, u32[]{:S(2)}, u32[]{:S(2)}) async-start(bf16[8,2,2,16,384]{4,3,2,1,0:T(8,128)(2,1)} %shard_map.93), calls=%async_computation | async-start | bytes 786432 | tf_op jit(solution)/shard_map/all_to_all | solution.py:273
  17.7 61.6 %all-gather.2.cloned.1.call-start = ((), (), s32[]{:S(2)}) async-start(), calls=%async_computation.2 | async-start | bytes 3538944 | tf_op jit(solution)/shard_map/all_gather | solution.py:276
  19.4 9.1 %collective-permute-start.2 = (bf16[96,1536]{1,0:T(8,128)(2,1)}, bf16[96,1536]{1,0:T(8,128)(2,1)S(1)}, u32[]{:S(2)}, u32[]{:S(2)}) collective-permute-start(bf16[96,1536]{1,0:T(8,128)(2,1)} %shard_map.94), channel_id=1, source_target_pairs={{0,48},{8,200},{16,0},{24,216},{32,16},{40,232},{48,32},{56,248},{... | collective-permute-start | bytes 884744 | tf_op jit(solution)/shard_map/ppermute | solution.py:234
  21.4 7.6 %collective-permute-start.1 = (bf16[96,1536]{1,0:T(8,128)(2,1)}, bf16[96,1536]{1,0:T(8,128)(2,1)S(1)}, u32[]{:S(2)}, u32[]{:S(2)}) collective-permute-start(bf16[96,1536]{1,0:T(8,128)(2,1)} %shard_map.94), channel_id=1, source_target_pairs={{0,32},{8,136},{16,48},{24,152},{32,0},{40,168},{48,16},{56,184},{... | collective-permute-start | bytes 884744 | tf_op jit(solution)/shard_map/ppermute | solution.py:234
  21.7 10.4 %collective-permute-start = (bf16[96,1536]{1,0:T(8,128)(2,1)}, bf16[96,1536]{1,0:T(8,128)(2,1)S(1)}, u32[]{:S(2)}, u32[]{:S(2)}) collective-permute-start(bf16[96,1536]{1,0:T(8,128)(2,1)} %shard_map.94), channel_id=1, source_target_pairs={{0,16},{8,72},{16,32},{24,88},{32,48},{40,104},{48,0},{56,120},{64... | collective-permute-start | bytes 884744 | tf_op jit(solution)/shard_map/ppermute | solution.py:234
  32.1 0.7 copy-start.7
  32.9 106.4 %reduce-scatter.2.cloned.1.call-start = ((), (), s32[]{:S(2)}) async-start(), calls=%async_computation.3 | async-start | bytes 3538944 | tf_op jit(solution)/shard_map/reduce_scatter | solution.py:309
  33.0 36.0 %copy-start.4 = (s32[1,16]{1,0:T(1,128)S(1)}, s32[1,16]{1,0:T(1,128)}, u32[]{:S(2)}) copy-start(s32[1,16]{1,0:T(1,128)} %row_ref.3) | copy-start | bytes 196
  34.1 45.2 %copy-start.6 = (bf16[4,96,1536]{2,1,0:T(8,128)(2,1)}, bf16[4,96,1536]{2,1,0:T(8,128)(2,1)S(1)}, u32[]{:S(2)}) copy-start(bf16[4,96,1536]{2,1,0:T(8,128)(2,1)S(1)} %pad_maximum_fusion.refs_3_) | copy-start | bytes 3538948
  34.1 28.2 %collective-permute-start.5 = (bf16[4,96,1536]{2,1,0:T(8,128)(2,1)S(1)}, bf16[4,96,1536]{2,1,0:T(8,128)(2,1)S(1)}, u32[]{:S(2)}, u32[]{:S(2)}) collective-permute-start(bf16[4,96,1536]{2,1,0:T(8,128)(2,1)S(1)} %pad_maximum_fusion.refs_3_), channel_id=1, source_target_pairs={{0,192},{8,56},{16,208},{24,8},{32,224},{40,24},{48,240},{56,40},{... | collective-permute-start | bytes 3538952 | tf_op jit(solution)/shard_map/ppermute | solution.py:234
  36.5 28.5 %collective-permute-start.4 = (bf16[4,96,1536]{2,1,0:T(8,128)(2,1)S(1)}, bf16[4,96,1536]{2,1,0:T(8,128)(2,1)S(1)}, u32[]{:S(2)}, u32[]{:S(2)}) collective-permute-start(bf16[4,96,1536]{2,1,0:T(8,128)(2,1)S(1)} %pad_maximum_fusion.refs_3_), channel_id=1, source_target_pairs={{0,128},{8,40},{16,144},{24,56},{32,160},{40,8},{48,176},{56,24},{... | collective-permute-start | bytes 3538952 | tf_op jit(solution)/shard_map/ppermute | solution.py:234
  37.1 29.0 %collective-permute-start.3 = (bf16[4,96,1536]{2,1,0:T(8,128)(2,1)S(1)}, bf16[4,96,1536]{2,1,0:T(8,128)(2,1)}, u32[]{:S(2)}, u32[]{:S(2)}) collective-permute-start(bf16[4,96,1536]{2,1,0:T(8,128)(2,1)S(1)} %pad_maximum_fusion.refs_3_), channel_id=1, source_target_pairs={{0,64},{8,24},{16,80},{24,40},{32,96},{40,56},{48,112},{56,8},{64,... | collective-permute-start | bytes 3538952 | tf_op jit(solution)/shard_map/ppermute | solution.py:234
  37.6 32.9 %collective-permute-start.6 = (bf16[4,96,1536]{2,1,0:T(8,128)(2,1)S(1)}, bf16[4,96,1536]{2,1,0:T(8,128)(2,1)}, u32[]{:S(2)}, u32[]{:S(2)}) collective-permute-start(bf16[4,96,1536]{2,1,0:T(8,128)(2,1)S(1)} %pad_maximum_fusion.refs_3_), channel_id=1, source_target_pairs={{0,8},{8,0},{16,24},{24,16},{32,40},{40,32},{48,56},{56,48},{1,9},... | collective-permute-start | bytes 3538952 | tf_op jit(solution)/shard_map/ppermute | solution.py:220
  62.3 17.0 %copy-start.8 = (bf16[4,96,1536]{2,1,0:T(8,128)(2,1)}, bf16[4,96,1536]{2,1,0:T(8,128)(2,1)S(1)}, u32[]{:S(2)}) copy-start(bf16[4,96,1536]{2,1,0:T(8,128)(2,1)S(1)} %collective-permute-done.5.refs_6_) | copy-start | bytes 3538948
  62.3 8.2 %collective-permute-start.9 = (bf16[4,96,1536]{2,1,0:T(8,128)(2,1)S(1)}, bf16[4,96,1536]{2,1,0:T(8,128)(2,1)}, u32[]{:S(2)}, u32[]{:S(2)}) collective-permute-start(bf16[4,96,1536]{2,1,0:T(8,128)(2,1)S(1)} %collective-permute-done.5.refs_6_), channel_id=1, source_target_pairs={{0,8},{8,0},{16,24},{24,16},{32,40},{40,32},{48,56},{56,48},{1,9},... | collective-permute-start | bytes 3538952 | tf_op jit(solution)/shard_map/ppermute | solution.py:220
  64.9 14.4 %copy-start.9 = (bf16[4,96,1536]{2,1,0:T(8,128)(2,1)}, bf16[4,96,1536]{2,1,0:T(8,128)(2,1)S(1)}, u32[]{:S(2)}) copy-start(bf16[4,96,1536]{2,1,0:T(8,128)(2,1)S(1)} %collective-permute-done.4.refs_5_) | copy-start | bytes 3538948
  64.9 5.5 %collective-permute-start.8 = (bf16[4,96,1536]{2,1,0:T(8,128)(2,1)S(1)}, bf16[4,96,1536]{2,1,0:T(8,128)(2,1)}, u32[]{:S(2)}, u32[]{:S(2)}) collective-permute-start(bf16[4,96,1536]{2,1,0:T(8,128)(2,1)S(1)} %collective-permute-done.4.refs_5_), channel_id=1, source_target_pairs={{0,8},{8,0},{16,24},{24,16},{32,40},{40,32},{48,56},{56,48},{1,9},... | collective-permute-start | bytes 3538952 | tf_op jit(solution)/shard_map/ppermute | solution.py:220
  66.1 5.7 %collective-permute-start.7 = (bf16[4,96,1536]{2,1,0:T(8,128)(2,1)}, bf16[4,96,1536]{2,1,0:T(8,128)(2,1)}, u32[]{:S(2)}, u32[]{:S(2)}) collective-permute-start(bf16[4,96,1536]{2,1,0:T(8,128)(2,1)} %collective-permute-done.3.refs_4_), channel_id=1, source_target_pairs={{0,8},{8,0},{16,24},{24,16},{32,40},{40,32},{48,56},{56,48},{1,9},... | collective-permute-start | bytes 3538952 | tf_op jit(solution)/shard_map/ppermute | solution.py:220
  96.0 1.1 copy-start.1
  96.0 5.2 %copy-start = (bf16[2,1536,256]{2,1,0:T(8,128)(2,1)S(1)}, bf16[2,1536,256]{2,1,0:T(8,128)(2,1)}, u32[]{:S(2)}) copy-start(bf16[2,1536,256]{2,1,0:T(8,128)(2,1)} %get-tuple-element.21.refs_0_) | copy-start | bytes 4718596
  96.0 5.2 %collective-permute-start.17 = (bf16[2,1536,256]{2,1,0:T(8,128)(2,1)}, bf16[2,1536,256]{2,1,0:T(8,128)(2,1)S(1)}, u32[]{:S(2)}, u32[]{:S(2)}) collective-permute-start(bf16[2,1536,256]{2,1,0:T(8,128)(2,1)} %get-tuple-element.22), channel_id=1, source_target_pairs={{0,8},{8,0},{16,24},{24,16},{32,40},{40,32},{48,56},{56,48},{1,9},... | collective-permute-start | bytes 4718600 | tf_op jit(solution)/shard_map/ppermute | solution.py:220
  97.1 4.1 %collective-permute-start.18 = (bf16[256,1536]{1,0:T(8,128)(2,1)S(1)}, bf16[256,1536]{1,0:T(8,128)(2,1)S(1)}, u32[]{:S(2)}, u32[]{:S(2)}) collective-permute-start(bf16[256,1536]{1,0:T(8,128)(2,1)S(1)} %copy-done.1), channel_id=1, source_target_pairs={{0,8},{8,0},{16,24},{24,16},{32,40},{40,32},{48,56},{56,48},{1,9},... | collective-permute-start | bytes 2359304 | tf_op jit(solution)/shard_map/ppermute | solution.py:220
  102.1 17.2 %collective-permute-start.19 = (bf16[4,12,96,128]{3,2,1,0:T(8,128)(2,1)S(1)}, bf16[4,12,96,128]{3,2,1,0:T(8,128)(2,1)S(1)}, u32[]{:S(2)}, u32[]{:S(2)}) collective-permute-start(bf16[4,12,96,128]{3,2,1,0:T(8,128)(2,1)S(1)} %shard_map.98), channel_id=1, source_target_pairs={{0,32},{8,136},{16,48},{24,152},{32,0},{40,168},{48,16},{56,184},{... | collective-permute-start | bytes 3538952 | tf_op jit(solution)/shard_map/ppermute | solution.py:234
  106.0 26.0 %collective-permute-start.20 = (bf16[4,12,96,128]{3,2,1,0:T(8,128)(2,1)S(1)}, bf16[4,12,96,128]{3,2,1,0:T(8,128)(2,1)S(1)}, u32[]{:S(2)}, u32[]{:S(2)}) collective-permute-start(bf16[4,12,96,128]{3,2,1,0:T(8,128)(2,1)S(1)} %shard_map.99), channel_id=1, source_target_pairs={{0,16},{8,72},{16,32},{24,88},{32,48},{40,104},{48,0},{56,120},{64... | collective-permute-start | bytes 3538952 | tf_op jit(solution)/shard_map/ppermute | solution.py:234
  107.3 24.8 %collective-permute-start.21 = (bf16[4,12,96,128]{3,2,1,0:T(8,128)(2,1)S(1)}, bf16[4,12,96,128]{3,2,1,0:T(8,128)(2,1)S(1)}, u32[]{:S(2)}, u32[]{:S(2)}) collective-permute-start(bf16[4,12,96,128]{3,2,1,0:T(8,128)(2,1)S(1)} %shard_map.100), channel_id=1, source_target_pairs={{0,48},{8,200},{16,0},{24,216},{32,16},{40,232},{48,32},{56,248},{... | collective-permute-start | bytes 3538952 | tf_op jit(solution)/shard_map/ppermute | solution.py:234
  119.3 13.3 %copy-start.10 = (bf16[4,12,96,128]{3,2,1,0:T(8,128)(2,1)}, bf16[4,12,96,128]{3,2,1,0:T(8,128)(2,1)S(1)}, u32[]{:S(2)}) copy-start(bf16[4,12,96,128]{3,2,1,0:T(8,128)(2,1)S(1)} %collective-permute-done.19) | copy-start | bytes 3538948
  132.0 1.1 copy-start.11
  132.1 1.3 copy-start.12
  133.4 12.9 %collective-permute-start.22 = (bf16[12,96,128]{2,1,0:T(8,128)(2,1)S(1)}, bf16[12,96,128]{2,1,0:T(8,128)(2,1)S(1)}, u32[]{:S(2)}, u32[]{:S(2)}) collective-permute-start(bf16[12,96,128]{2,1,0:T(8,128)(2,1)S(1)} %get-tuple-element.24), channel_id=1, source_target_pairs={{0,128},{8,40},{16,144},{24,56},{32,160},{40,8},{48,176},{56,24},{... | collective-permute-start | bytes 884744 | tf_op jit(solution)/shard_map/ppermute | solution.py:234
  136.1 10.2 %collective-permute-start.24 = (bf16[12,96,128]{2,1,0:T(8,128)(2,1)S(1)}, bf16[12,96,128]{2,1,0:T(8,128)(2,1)S(1)}, u32[]{:S(2)}, u32[]{:S(2)}) collective-permute-start(bf16[12,96,128]{2,1,0:T(8,128)(2,1)S(1)} %get-tuple-element.25), channel_id=1, source_target_pairs={{0,192},{8,56},{16,208},{24,8},{32,224},{40,24},{48,240},{56,40},{... | collective-permute-start | bytes 884744 | tf_op jit(solution)/shard_map/ppermute | solution.py:234
  137.0 9.3 %collective-permute-start.23 = (bf16[12,96,128]{2,1,0:T(8,128)(2,1)S(1)}, bf16[12,96,128]{2,1,0:T(8,128)(2,1)S(1)}, u32[]{:S(2)}, u32[]{:S(2)}) collective-permute-start(bf16[12,96,128]{2,1,0:T(8,128)(2,1)S(1)} %get-tuple-element.26), channel_id=1, source_target_pairs={{0,64},{8,24},{16,80},{24,40},{32,96},{40,56},{48,112},{56,8},{64,... | collective-permute-start | bytes 884744 | tf_op jit(solution)/shard_map/ppermute | solution.py:234
  140.3 11.1 %collective-permute-start.16 = (bf16[2,32,384]{2,1,0:T(8,128)(2,1)S(1)}, bf16[2,32,384]{2,1,0:T(8,128)(2,1)S(1)}, u32[]{:S(2)}, u32[]{:S(2)}) collective-permute-start(bf16[2,32,384]{2,1,0:T(8,128)(2,1)S(1)} %get-tuple-element.27), channel_id=1, source_target_pairs={{0,56},{8,48},{16,40},{24,32},{32,24},{40,16},{48,8},{56,0},{1,57}... | collective-permute-start | bytes 147464 | tf_op jit(solution)/shard_map/ppermute | solution.py:220
  146.0 6.9 %collective-permute-start.15 = (bf16[2,32,384]{2,1,0:T(8,128)(2,1)S(1)}, bf16[2,32,384]{2,1,0:T(8,128)(2,1)S(1)}, u32[]{:S(2)}, u32[]{:S(2)}) collective-permute-start(bf16[2,32,384]{2,1,0:T(8,128)(2,1)S(1)} %get-tuple-element.28), channel_id=1, source_target_pairs={{0,48},{8,56},{16,32},{24,40},{32,16},{40,24},{48,0},{56,8},{1,49}... | collective-permute-start | bytes 147464 | tf_op jit(solution)/shard_map/ppermute | solution.py:220
  147.8 7.7 %copy-start.2 = (bf16[1,2,128,3,384]{4,2,3,1,0:T(8,128)(2,1)S(1)}, bf16[1,2,128,3,384]{4,2,3,1,0:T(8,128)(2,1)}, u32[]{:S(2)}) copy-start(bf16[1,2,128,3,384]{4,2,3,1,0:T(8,128)(2,1)} %param.6) | copy-start | bytes 1769476
  147.8 7.7 %copy-start.3 = (bf16[1,2,128,384]{3,2,1,0:T(8,128)(2,1)S(1)}, bf16[1,2,128,384]{3,2,1,0:T(8,128)(2,1)}, u32[]{:S(2)}) copy-start(bf16[1,2,128,384]{3,2,1,0:T(8,128)(2,1)} %param.9) | copy-start | bytes 589828
  147.8 7.7 %copy-start.5 = (s32[1,8]{1,0:T(1,128)S(1)}, s32[1,8]{1,0:T(1,128)}, u32[]{:S(2)}) copy-start(s32[1,8]{1,0:T(1,128)} %patch_ref.3) | copy-start | bytes 100
  147.8 6.9 %collective-permute-start.14 = (bf16[2,32,384]{2,1,0:T(8,128)(2,1)S(1)}, bf16[2,32,384]{2,1,0:T(8,128)(2,1)S(1)}, u32[]{:S(2)}, u32[]{:S(2)}) collective-permute-start(bf16[2,32,384]{2,1,0:T(8,128)(2,1)S(1)} %get-tuple-element.29), channel_id=1, source_target_pairs={{0,40},{8,32},{16,56},{24,48},{32,8},{40,0},{48,24},{56,16},{1,41}... | collective-permute-start | bytes 147464 | tf_op jit(solution)/shard_map/ppermute | solution.py:220
  150.8 4.4 %collective-permute-start.13 = (bf16[2,32,384]{2,1,0:T(8,128)(2,1)S(1)}, bf16[2,32,384]{2,1,0:T(8,128)(2,1)S(1)}, u32[]{:S(2)}, u32[]{:S(2)}) collective-permute-start(bf16[2,32,384]{2,1,0:T(8,128)(2,1)S(1)} %get-tuple-element.30), channel_id=1, source_target_pairs={{0,32},{8,40},{16,48},{24,56},{32,0},{40,8},{48,16},{56,24},{1,33}... | collective-permute-start | bytes 147464 | tf_op jit(solution)/shard_map/ppermute | solution.py:220
  151.0 4.2 %collective-permute-start.12 = (bf16[2,32,384]{2,1,0:T(8,128)(2,1)S(1)}, bf16[2,32,384]{2,1,0:T(8,128)(2,1)S(1)}, u32[]{:S(2)}, u32[]{:S(2)}) collective-permute-start(bf16[2,32,384]{2,1,0:T(8,128)(2,1)S(1)} %get-tuple-element.31), channel_id=1, source_target_pairs={{0,24},{8,16},{16,8},{24,0},{32,56},{40,48},{48,40},{56,32},{1,25}... | collective-permute-start | bytes 147464 | tf_op jit(solution)/shard_map/ppermute | solution.py:220
  151.4 4.1 %collective-permute-start.11 = (bf16[2,32,384]{2,1,0:T(8,128)(2,1)S(1)}, bf16[2,32,384]{2,1,0:T(8,128)(2,1)S(1)}, u32[]{:S(2)}, u32[]{:S(2)}) collective-permute-start(bf16[2,32,384]{2,1,0:T(8,128)(2,1)S(1)} %get-tuple-element.32), channel_id=1, source_target_pairs={{0,16},{8,24},{16,0},{24,8},{32,48},{40,56},{48,32},{56,40},{1,17}... | collective-permute-start | bytes 147464 | tf_op jit(solution)/shard_map/ppermute | solution.py:220
  152.9 2.6 %collective-permute-start.10 = (bf16[2,32,384]{2,1,0:T(8,128)(2,1)S(1)}, bf16[2,32,384]{2,1,0:T(8,128)(2,1)S(1)}, u32[]{:S(2)}, u32[]{:S(2)}) collective-permute-start(bf16[2,32,384]{2,1,0:T(8,128)(2,1)S(1)} %get-tuple-element.33), channel_id=1, source_target_pairs={{0,8},{8,0},{16,24},{24,16},{32,40},{40,32},{48,56},{56,48},{1,9},... | collective-permute-start | bytes 147464 | tf_op jit(solution)/shard_map/ppermute | solution.py:220
Sparse Core Ops, SparseCore 0:
  33.0 46.2 all-gather.1
  96.1 43.0 reduce-scatter.1

commit v3 on v2

--- a/solution.py
+++ b/solution.py
@@ -60,14 +60,15 @@
 
 
 def spatial_backward(row_ref, patch_ref, qkv_ref, cot_ref, *refs):
-    blocks, (out_ref, grad_ref, whole_ref) = refs[:-3], refs[-3:]
+    sums_ref, out_ref, grad_ref, whole_ref = refs
     frames, _, patches, width = qkv_ref.shape
     place = lax.axis_index("frame")
-    block = patches // len(blocks)
-    for j, ref in enumerate(blocks):
-        start = pl.multiple_of((place ^ j) * block, 16)
+    owners = sums_ref.shape[0]
+    block = patches // owners
+    for s in range(owners):
         for f in range(frames):
-            whole_ref[:, f, pl.ds(start, block), :] = ref[:, f * block : (f + 1) * block, :]
+            part = sums_ref[s, :, f * block : (f + 1) * block, :]
+            whole_ref[:, f, s * block : (s + 1) * block, :] = part
     for f in range(frames):
         count = live_rows(row_ref, patch_ref, place * frames + f)
         keys_live = lax.broadcasted_iota(jnp.int32, (patches, patches), 1) < count
@@ -97,77 +98,88 @@
     return lax.axis_index("clip"), place // 2, place % 2
 
 
+def line_kernel(own_ref, near_1, near_2, near_3, line_ref):
+    at_clip, at_x, core = own_chip()
+    at = jnp.where(core == 0, at_x, at_clip)
+    for step, ref in enumerate((own_ref, near_1, near_2, near_3)):
+        line_ref[lax.rem(at + 4 - step, 4)] = ref[...]
+
+
+def flip_kernel(whole_ref, own_ref, other_ref):
+    _, _, core = own_chip()
+    pieces = 32
+    owners, _, tokens, model = whole_ref.shape
+    rows = model // pieces
+    step = 4 * rows
+    for a in range(2):
+        for z in range(model // step):
+            part = whole_ref[:, a, :, z * step : (z + 1) * step]
+            flipped = part.reshape(owners * tokens, step).T
+            for i in range(2):
+                even = flipped[2 * i * rows : (2 * i + 1) * rows]
+                odd = flipped[(2 * i + 1) * rows : (2 * i + 2) * rows]
+                to = slice((2 * z + i) * rows, (2 * z + i + 1) * rows)
+                own_ref[a, to] = jnp.where(core == 0, even, odd)
+                other_ref[a, to] = jnp.where(core == 0, odd, even)
+
+
 def temporal_kernel(heads, row_key_ref, col_key_ref, whole_hbm, *refs):
-    planes, refs = refs[:-11], refs[-11:]
-    sums_hbm, both_ref, own_hbm, other_hbm, w_ref, token_ref, sums_ref, flip_ref = refs[:8]
-    w_sem, in_sem, out_sem = refs[8:]
+    planes, refs = refs[:-8], refs[-8:]
+    sums_hbm, both_ref, w_ref, token_ref, sums_ref, w_sem, in_sem, out_sem = refs
     at_clip, at_x, core = own_chip()
-    place = lax.axis_index("frame")
     width = heads * HD
+    groups = heads + 1
     ranks, owners, _, rows, _ = sums_ref.shape
-    n, w_rows, _ = planes[0].shape
+    n = w_ref.shape[0]
     tokens = [
-        [
-            pltpu.make_async_copy(
-                whole_hbm.at[z, :, a],
-                token_ref.at[a, :, :, z * width : (z + 1) * width],
-                in_sem.at[a * ranks + z],
-            )
-            for z in range(ranks)
-        ]
-        for a in range(2)
+        pltpu.make_async_copy(whole_hbm.at[:, a], token_ref.at[a], in_sem.at[a]) for a in range(2)
     ]
-    loads = [[], []]
-    for half, owner in ((0, core), (1, 1 - core)):
-        for second in range(n):
-            for first in range(n):
-                clip = lax.rem(at_clip + n - jnp.where(owner == 0, second, first), n)
-                x = lax.rem(at_x + n - jnp.where(owner == 0, first, second), n)
-                start = pl.multiple_of((clip * 2 * n + x * 2 + owner) * w_rows, 16)
-                for g, cols in enumerate((pl.ds(0, 3 * width), pl.ds(3 * width, width))):
-                    loads[g].append(
-                        pltpu.make_async_copy(
-                            planes[half * n + second].at[first, :, cols],
-                            w_ref.at[pl.ds(start, w_rows), cols],
-                            w_sem.at[g, len(loads[g])],
-                        )
-                    )
-    for copy in tokens[0] + tokens[1] + loads[0]:
+
+    def load(g, act):
+        cols = pl.ds(g * width, width)
+
+        def for_core(known):
+            for i, plane in enumerate(planes):
+                step = i % n
+                if (i < n) == (known == 0):
+                    to = w_ref.at[lax.rem(at_clip + n - step, n), :, 0, :, cols]
+                else:
+                    to = w_ref.at[:, lax.rem(at_x + n - step, n), 1, :, cols]
+                act(pltpu.make_async_copy(plane.at[:, :, cols], to, w_sem.at[g, i]))
+
+        pl.when(core == 0)(lambda: for_core(0))
+        pl.when(core == 1)(lambda: for_core(1))
+
+    def start(copy):
         copy.start()
-    step = 4 * w_rows
-    flips = []
-    for a in range(2):
-        for z in range(ranks):
-            tokens[a][z].wait()
-            part = token_ref[a, :, :, z * step : (z + 1) * step]
-            flipped = part.reshape(owners * rows, step).T
-            for i in range(2):
-                even = flipped[2 * i * w_rows : (2 * i + 1) * w_rows]
-                odd = flipped[(2 * i + 1) * w_rows : (2 * i + 2) * w_rows]
-                to = slice((2 * z + i) * w_rows, (2 * z + i + 1) * w_rows)
-                flip_ref[0, a, to] = jnp.where(core == 0, even, odd)
-                flip_ref[1, a, to] = jnp.where(core == 0, odd, even)
-    for i, ref in enumerate((own_hbm, other_hbm)):
-        flips.append(pltpu.make_async_copy(flip_ref.at[i], ref, in_sem.at[2 * ranks + i]))
-        flips[-1].start()
+
+    def finish(copy):
+        copy.wait()
+
+    tokens[0].start()
+    load(0, start)
+    load(1, start)
+    tokens[1].start()
     mask = row_key_ref[...] == col_key_ref[...]
-    for copy in loads[0]:
-        copy.wait()
-    for copy in loads[1]:
-        copy.start()
+    tokens[0].wait()
     feats = token_ref[0].reshape(owners * rows, -1)
     query, keys, values = [], [], []
     for h in range(heads):
-        qkv = dot(feats, w_ref[:, h * width : (h + 1) * width]).astype(BF)
+        load(h, finish)
+        if h + 2 < groups:
+            load(h + 2, start)
+        w_head = w_ref[:, :, :, :, h * width : (h + 1) * width].reshape(-1, width)
+        qkv = dot(feats, w_head).astype(BF)
         for i, parts in enumerate((query, keys, values)):
             parts.append(qkv[:, i * HD : (i + 1) * HD])
     each = range(heads)
     probs = [softmax(query[h], keys[h], mask) for h in each]
     mixed = [dot(probs[h].astype(BF), values[h]).astype(BF) for h in each]
-    for copy in loads[1]:
-        copy.wait()
+    tokens[1].wait()
+    load(heads, finish)
     gated = token_ref[1].reshape(owners * rows, -1)
-    cotangent = dot(gated, w_ref[:, 3 * width :]).astype(BF)
+    w_last = w_ref[:, :, :, :, 3 * width :].reshape(-1, width)
+    cotangent = dot(gated, w_last).astype(BF)
     for h in each:
         cols = slice(h * HD, (h + 1) * HD)
         grads = attention_grads(query[h], keys[h], values[h], probs[h], cotangent[:, cols])
@@ -177,17 +189,17 @@
     stores = []
     pair = 2
     for first in range(0, ranks, pair):
-        part = slice(first * width, (first + pair) * width)
-        projected = dot(both_ref[:, 3 * width :], w_ref[part, 3 * width :], NT).astype(BF)
-        back = dot(both_ref[:, : 3 * width], w_ref[part, : 3 * width], NT).astype(BF)
+        w_part = w_ref[first // pair].reshape(pair * width, -1)
+        projected = dot(both_ref[:, 3 * width :], w_part[:, 3 * width :], NT).astype(BF)
+        back = dot(both_ref[:, : 3 * width], w_part[:, : 3 * width], NT).astype(BF)
         for i in range(pair):
             z, cols = first + i, slice(i * width, (i + 1) * width)
             for s in range(owners):
-                sums_ref[z, s ^ place, 0] = projected[s * rows : (s + 1) * rows, cols]
-                sums_ref[z, s ^ place, 1] = back[s * rows : (s + 1) * rows, cols]
+                sums_ref[z, s, 0] = projected[s * rows : (s + 1) * rows, cols]
+                sums_ref[z, s, 1] = back[s * rows : (s + 1) * rows, cols]
             stores.append(pltpu.make_async_copy(sums_ref.at[z], sums_hbm.at[z], out_sem.at[z]))
             stores[-1].start()
-    for copy in stores + flips:
+    for copy in stores:
         copy.wait()
 
 
@@ -272,10 +284,14 @@
     near = [spread(packed, step, False) for step in (1, 2, 3)]
     cols = lax.all_to_all(sent, "frame", split_axis=0, concat_axis=0, tiled=True)
     cols = cols.reshape(ranks, 2, frames * block, width)
-    cols, *near = lax.optimization_barrier([cols, *near])
-    whole = lax.all_gather(cols, "tensor", axis=0, tiled=True)
-    whole = whole.reshape((width_ranks,) + cols.shape)
-    line = jnp.stack([packed] + near)
+    cols, near[0], near[2] = lax.optimization_barrier([cols, near[0], near[2]])
+    whole = lax.all_gather(cols, "tensor", axis=3, tiled=True)
+    line = pl.pallas_call(
+        line_kernel,
+        out_shape=jax.ShapeDtypeStruct((4,) + packed.shape, BF),
+        in_specs=[vmem] * 4,
+        out_specs=vmem,
+    )(packed, *near)
     plane = [line] + [spread(line, step, True) for step in (1, 2, 3)]
     plane += [trade(rows, 1) for rows in plane]
 
@@ -283,28 +299,33 @@
     keys = (clips + jnp.arange(block, dtype=jnp.int32)[None, :]).reshape(rows_t)
 
     sums_shape = (width_ranks, ranks, 2, frames * block, width)
-    halves = jax.ShapeDtypeStruct((2, model // 2, rows_t), BF)
-    sums, both, own_flip, other_flip = pl.pallas_call(
+    sums, both = pl.pallas_call(
         lambda *refs: temporal_kernel(heads, *refs),
         out_shape=[
             jax.ShapeDtypeStruct(sums_shape, BF),
             jax.ShapeDtypeStruct((rows_t, 4 * width), BF),
-            halves,
-            halves,
         ],
         in_specs=[vmem, vmem] + [hbm] * (1 + len(plane)),
-        out_specs=[hbm, vmem, hbm, hbm],
+        out_specs=[hbm, vmem],
         scratch_shapes=[
-            pltpu.VMEM((model, 4 * width), BF),
+            pltpu.VMEM((4, 4, 2, w_rows, slots * HD), BF),
             pltpu.VMEM((2, ranks, frames * block, model), BF),
             pltpu.VMEM(sums_shape, BF),
-            pltpu.VMEM((2, 2, model // 2, rows_t), BF),
-            pltpu.SemaphoreType.DMA((2, 4 * len(plane))),
-            pltpu.SemaphoreType.DMA((2 * width_ranks + 2,)),
+            pltpu.SemaphoreType.DMA((heads + 1, len(plane))),
+            pltpu.SemaphoreType.DMA((2,)),
             pltpu.SemaphoreType.DMA((width_ranks,)),
         ],
         compiler_params=pltpu.CompilerParams(vmem_limit_bytes=58 * 2**20),
     )(keys[:, None], keys[None, :], whole, *plane)
+
+    halves = jax.ShapeDtypeStruct((2, model // 2, rows_t), BF)
+    own_flip, other_flip = pl.pallas_call(
+        flip_kernel,
+        out_shape=[halves, halves],
+        in_specs=[vmem],
+        out_specs=[vmem] * 2,
+        compiler_params=pltpu.CompilerParams(vmem_limit_bytes=16 * 2**20),
+    )(whole)
     pair_flip = trade(other_flip, 1)
     own_sums = lax.psum_scatter(sums, "tensor", scatter_dimension=0, tiled=True)[0]
     pair_both = trade(both, 1)
@@ -321,18 +342,18 @@
     partial = [add(*(part[i] for part in arrived)).astype(BF) for i in range(4)]
     grads = add(partial[0], *(spread(partial[step], step, True) for step in (2, 1, 3)))
 
-    traded = [own_sums[0]] + [trade(own_sums[j], j) for j in range(1, ranks)]
+    row_sums = lax.all_to_all(own_sums, "frame", split_axis=0, concat_axis=0, tiled=True)
     block_out, qkv_grad = pl.pallas_call(
         spatial_backward,
         out_shape=[
             jax.ShapeDtypeStruct((frames, patches, width), BF),
             jax.ShapeDtypeStruct((frames, 3, patches, width), BF),
         ],
-        in_specs=[smem, smem] + [vmem] * (2 + ranks),
+        in_specs=[smem, smem] + [vmem] * 3,
         out_specs=[vmem, vmem],
         scratch_shapes=[pltpu.VMEM((2, frames, patches, width), BF)],
         compiler_params=pltpu.CompilerParams(vmem_limit_bytes=24 * 2**20),
-    )(frame_clip, clip_patches, qkv, cot, *traded)
+    )(frame_clip, clip_patches, qkv, cot, row_sums)
 
     w_qkv_grad = grads[: 3 * heads].reshape(heads, 3, w_rows, HD).transpose(2, 0, 1, 3)
     w_out_grad = grads[3 * heads :].transpose(0, 2, 1)

time: 165 us -> 163 us (0.988)
  starting transfers between devices: 44.7 us -> 36.8 us
  waiting for transfers between devices: 68.9 us -> 73.1 us
    ppermute x13 -> x6, starting transfers between devices: 21.5 us -> 11.6 us  [trade(): return lax.ppermute(value, 'frame', [(i, i ^ j) for i in range(8)])]
    all_to_all x0 -> x1, starting transfers between devices: none -> 7.59 us  [body(): lax.all_to_all(own_sums, 'frame', split_axis=0, concat_axis=0, tiled=True)]
    all_gather x1, waiting for transfers between devices: 7.48 us -> 0.01 us  [body(): whole = lax.all_gather(cols, 'tensor', axis=3, tiled=True)]
    ppermute x12, waiting for transfers between devices: 54.4 us -> 60.1 us  [spread(): return lax.ppermute(value, ('clip', 'frame'), pairs)]
    ppermute x12, starting transfers between devices: 16.5 us -> 11 us  [spread(): return lax.ppermute(value, ('clip', 'frame'), pairs)]
    all_to_all x0 -> x1, waiting for transfers between devices: none -> 4.94 us  [body(): lax.all_to_all(own_sums, 'frame', split_axis=0, concat_axis=0, tiled=True)]
    pallas_call x0 -> x2, Pallas kernels: none -> 3.21 us  [the longest x1 2.35 us: body(): pl.pallas_call(line_kernel, out_shape=jax.ShapeDtypeStruct((4,) + packed....]
    pallas_call x1, Pallas kernels: 16.7 us -> 13.9 us  [body(): pl.pallas_call(lambda *refs: temporal_kernel(heads, *refs), out_shape=[ja...]
  transfers between devices with their start and end apart: 28 -> 22, of which waited for: 14 -> 11; matrix products, arithmetic and copies ran while one was open for 4% -> 4% of each run, Pallas kernels for 3% -> 5%
where the time goes in v3:
time: 163 us; the launch traced here: 162 us
  waiting for transfers between devices  73.1 us (45%)
  starting transfers between devices  36.8 us (23%)
  Pallas kernels  28.9 us (18%)
  between operations  14.2 us (9%)
  local copies, waits for them, and re-layouts  6.28 us (4%)
  other arithmetic  2.87 us (2%)
    ppermute x12, waiting for transfers between devices, spread(): return lax.ppermute(value, ('clip', 'frame'), pairs)  60.1 us
    pallas_call x1, Pallas kernels, body(): pl.pallas_call(lambda *refs: temporal_kernel(heads, *refs), out_shape=[ja...  13.9 us
    ppermute x6, starting transfers between devices, trade(): return lax.ppermute(value, 'frame', [(i, i ^ j) for i in range(8)])  11.6 us
    ppermute x12, starting transfers between devices, spread(): return lax.ppermute(value, ('clip', 'frame'), pairs)  11 us
    all_to_all x1, starting transfers between devices, body(): lax.all_to_all(own_sums, 'frame', split_axis=0, concat_axis=0, tiled=True)  7.59 us
    all_to_all x1, starting transfers between devices, body(): lax.all_to_all(sent, 'frame', split_axis=0, concat_axis=0, tiled=True)  6.59 us
    ppermute x6, waiting for transfers between devices, trade(): return lax.ppermute(value, 'frame', [(i, i ^ j) for i in range(8)])  5.11 us
    all_to_all x1, waiting for transfers between devices, body(): lax.all_to_all(own_sums, 'frame', split_axis=0, concat_axis=0, tiled=True)  4.94 us
  transfers between devices with their start and end apart: 22, of which 11 were waited for; matrix products, arithmetic and copies ran while one was open for 4% of the time, Pallas kernels for 5%

profile of v3, /device:TPU:1, one launch (start us, length us, event | category | flops | bytes accessed | tf_op | source)
XLA Modules:
  0.0 162.2 jit_solution(1699210598388581934)
XLA Ops:
  7.2 3.9 %shard_map.93 = bf16[8,2,2,16,384]{4,3,2,1,0:T(8,128)(2,1)} custom-call(s32[1,16]{1,0:T(1,128)} %row_ref.3, s32[1,8]{1,0:T(1,128)} %patch_ref.3, bf16[2,3,128,384]{3,2,1,0:T(8,128)(2,1)} %bitcast.32, bf16[2,128,384]{2,1,0:T(8,128)(2,1)} %bitcast.34), custom_call_target="tpu_custom_call" | custom-call | tf_op jit(solution)/shard_map/pallas_call | solution.py:270
  11.1 6.6 %all-to-all-start = ((bf16[8,2,2,16,384]{4,3,2,1,0:T(8,128)(2,1)}), bf16[8,2,2,16,384]{4,3,2,1,0:T(8,128)(2,1)S(1)}, u32[]{:S(2)}, u32[]{:S(2)}) async-start(bf16[8,2,2,16,384]{4,3,2,1,0:T(8,128)(2,1)} %shard_map.93), calls=%async_computation | async-start | bytes 786432 | tf_op jit(solution)/shard_map/all_to_all | solution.py:285
  17.7 1.8 %shard_map.94.own_ref = bf16[96,1536]{1,0:T(8,128)(2,1)} custom-call(bf16[9,96,128]{2,1,0:T(8,128)(2,1)} %bitcast.39, bf16[3,96,128]{2,1,0:T(8,128)(2,1)} %bitcast.40), custom_call_target="tpu_custom_call" | custom-call | tf_op jit(solution)/shard_map/pallas_call | solution.py:278
  19.4 1.9 %collective-permute-start.1 = (bf16[96,1536]{1,0:T(8,128)(2,1)}, bf16[96,1536]{1,0:T(8,128)(2,1)S(1)}, u32[]{:S(2)}, u32[]{:S(2)}) collective-permute-start(bf16[96,1536]{1,0:T(8,128)(2,1)} %shard_map.94.own_ref), channel_id=1, source_target_pairs={{0,48},{8,200},{16,0},{24,216},{32,16},{40,232},{48,32},{56,248},{... | collective-permute-start | bytes 884744 | tf_op jit(solution)/shard_map/ppermute | solution.py:246
  21.4 4.1 %collective-permute-done.1.near_3 = bf16[96,1536]{1,0:T(8,128)(2,1)S(1)} collective-permute-done((bf16[96,1536]{1,0:T(8,128)(2,1)}, bf16[96,1536]{1,0:T(8,128)(2,1)S(1)}, u32[]{:S(2)}, u32[]{:S(2)}) %collective-permute-start.1) | collective-permute-done | bytes 294944 | tf_op jit(solution)/shard_map/ppermute | solution.py:246
  25.5 3.1 %collective-permute-done.near_1 = bf16[96,1536]{1,0:T(8,128)(2,1)S(1)} collective-permute-done((bf16[96,1536]{1,0:T(8,128)(2,1)}, bf16[96,1536]{1,0:T(8,128)(2,1)S(1)}, u32[]{:S(2)}, u32[]{:S(2)}) %collective-permute-start) | collective-permute-done | bytes 294944 | tf_op jit(solution)/shard_map/ppermute | solution.py:246
  28.7 0.8 copy-done.6
  29.6 0.1 collective-permute-start.2
  29.7 7.6 %collective-permute-done.2.near_2 = bf16[96,1536]{1,0:T(8,128)(2,1)S(1)} collective-permute-done((bf16[96,1536]{1,0:T(8,128)(2,1)}, bf16[96,1536]{1,0:T(8,128)(2,1)S(1)}, u32[]{:S(2)}, u32[]{:S(2)}) %collective-permute-start.2) | collective-permute-done | bytes 294944 | tf_op jit(solution)/shard_map/ppermute | solution.py:246
  37.2 0.7 copy-done.14
  37.9 2.3 %shard_map.95.refs_3_ = bf16[4,96,1536]{2,1,0:T(8,128)(2,1)} custom-call(bf16[96,1536]{1,0:T(8,128)(2,1)} %shard_map.94.own_ref, bf16[96,1536]{1,0:T(8,128)(2,1)} %copy-done.13, bf16[96,1536]{1,0:T(8,128)(2,1)} %copy-done.14, bf16[96,1536]{1,0:T(8,128)(2,1)} %copy-done.12), custom_call_target="tpu_custom_call" | custom-call | tf_op jit(solution)/shard_map/pallas_call | solution.py:289
  40.3 2.3 %collective-permute-start.5 = (bf16[4,96,1536]{2,1,0:T(8,128)(2,1)}, bf16[4,96,1536]{2,1,0:T(8,128)(2,1)S(1)}, u32[]{:S(2)}, u32[]{:S(2)}) collective-permute-start(bf16[4,96,1536]{2,1,0:T(8,128)(2,1)} %shard_map.95.refs_3_), channel_id=1, source_target_pairs={{0,192},{8,56},{16,208},{24,8},{32,224},{40,24},{48,240},{56,40},{... | collective-permute-start | bytes 3538952 | tf_op jit(solution)/shard_map/ppermute | solution.py:246
  42.6 0.3 collective-permute-start.4
  42.9 0.6 collective-permute-start.3
  43.5 3.7 %collective-permute-start.6 = (bf16[4,96,1536]{2,1,0:T(8,128)(2,1)}, bf16[4,96,1536]{2,1,0:T(8,128)(2,1)}, u32[]{:S(2)}, u32[]{:S(2)}) collective-permute-start(bf16[4,96,1536]{2,1,0:T(8,128)(2,1)} %shard_map.95.refs_3_), channel_id=1, source_target_pairs={{0,8},{8,0},{16,24},{24,16},{32,40},{40,32},{48,56},{56,48},{1,9},... | collective-permute-start | bytes 3538952 | tf_op jit(solution)/shard_map/ppermute | solution.py:232
  47.1 21.6 %collective-permute-done.5.refs_6_ = bf16[4,96,1536]{2,1,0:T(8,128)(2,1)S(1)} collective-permute-done((bf16[4,96,1536]{2,1,0:T(8,128)(2,1)}, bf16[4,96,1536]{2,1,0:T(8,128)(2,1)S(1)}, u32[]{:S(2)}, u32[]{:S(2)}) %collective-permute-start.5) | collective-permute-done | bytes 1179680 | tf_op jit(solution)/shard_map/ppermute | solution.py:246
  68.7 3.5 %collective-permute-start.9 = (bf16[4,96,1536]{2,1,0:T(8,128)(2,1)S(1)}, bf16[4,96,1536]{2,1,0:T(8,128)(2,1)}, u32[]{:S(2)}, u32[]{:S(2)}) collective-permute-start(bf16[4,96,1536]{2,1,0:T(8,128)(2,1)S(1)} %collective-permute-done.5.refs_6_), channel_id=1, source_target_pairs={{0,8},{8,0},{16,24},{24,16},{32,40},{40,32},{48,56},{56,48},{1,9},... | collective-permute-start | bytes 3538952 | tf_op jit(solution)/shard_map/ppermute | solution.py:232
  72.2 0.1 collective-permute-start.8
  72.3 3.7 %collective-permute-start.7 = (bf16[4,96,1536]{2,1,0:T(8,128)(2,1)S(1)}, bf16[4,96,1536]{2,1,0:T(8,128)(2,1)}, u32[]{:S(2)}, u32[]{:S(2)}) collective-permute-start(bf16[4,96,1536]{2,1,0:T(8,128)(2,1)S(1)} %collective-permute-done.3.refs_4_), channel_id=1, source_target_pairs={{0,8},{8,0},{16,24},{24,16},{32,40},{40,32},{48,56},{56,48},{1,9},... | collective-permute-start | bytes 3538952 | tf_op jit(solution)/shard_map/ppermute | solution.py:232
  76.2 0.6 add.104.refs_1_
  76.8 0.8 add.124.refs_0_
  77.6 1.1 collective-permute-done.7.refs_8_
  78.7 13.9 %shard_map.96 = (bf16[8,8,2,32,384]{4,3,2,1,0:T(8,128)(2,1)}, bf16[256,1536]{1,0:T(8,128)(2,1)}) custom-call(s32[256,1]{1,0:T(8,128)} %add.124.refs_0_, s32[1,256]{1,0:T(1,128)} %add.104.refs_1_, bf16[8,2,32,3072]{3,2,1,0:T(8,128)(2,1)} %all-gather.2.cloned.1.call-done.refs_2_.whole_ref, bf16[4,96,1536]{2,1,0:T(8,128)(2,1)} %shard_map.95.refs_3_, ...), custom_call_target="tpu_custom_call" | custom-call | tf_op jit(solution)/shard_map/pallas_call | solution.py:302
  92.7 1.9 %copy-done = bf16[8,2,32,3072]{3,2,1,0:T(8,128)(2,1)S(1)} copy-done((bf16[8,2,32,3072]{3,2,1,0:T(8,128)(2,1)S(1)}, bf16[8,2,32,3072]{3,2,1,0:T(8,128)(2,1)}, u32[]{:S(2)}) %copy-start) | copy-done | bytes 3145752
  94.6 0.9 shard_map.98
  95.4 0.5 collective-permute-start.10
  95.9 0.2 collective-permute-start.11
  96.1 4.0 %collective-permute-done.11.refs_3_ = bf16[256,1536]{1,0:T(8,128)(2,1)S(1)} collective-permute-done((bf16[256,1536]{1,0:T(8,128)(2,1)S(1)}, bf16[256,1536]{1,0:T(8,128)(2,1)S(1)}, u32[]{:S(2)}, u32[]{:S(2)}) %collective-permute-start.11) | collective-permute-done | bytes 786464 | tf_op jit(solution)/shard_map/ppermute | solution.py:232
  100.1 0.9 shard_map.100
  100.9 0.7 collective-permute-start.12
  101.7 0.9 shard_map.101
  102.5 3.0 %collective-permute-start.13 = (bf16[4,12,96,128]{3,2,1,0:T(8,128)(2,1)S(1)}, bf16[4,12,96,128]{3,2,1,0:T(8,128)(2,1)S(1)}, u32[]{:S(2)}, u32[]{:S(2)}) collective-permute-start(bf16[4,12,96,128]{3,2,1,0:T(8,128)(2,1)S(1)} %shard_map.101), channel_id=1, source_target_pairs={{0,16},{8,72},{16,32},{24,88},{32,48},{40,104},{48,0},{56,120},{64... | collective-permute-start | bytes 3538952 | tf_op jit(solution)/shard_map/ppermute | solution.py:246
  105.6 0.9 shard_map.102
  106.6 0.9 shard_map.99
  107.4 10.5 %collective-permute-done.12 = bf16[4,12,96,128]{3,2,1,0:T(8,128)(2,1)S(1)} collective-permute-done((bf16[4,12,96,128]{3,2,1,0:T(8,128)(2,1)S(1)}, bf16[4,12,96,128]{3,2,1,0:T(8,128)(2,1)S(1)}, u32[]{:S(2)}, u32[]{:S(2)}) %collective-permute-start.12) | collective-permute-done | bytes 1179680 | tf_op jit(solution)/shard_map/ppermute | solution.py:246
  117.9 12.7 %collective-permute-done.13 = bf16[4,12,96,128]{3,2,1,0:T(8,128)(2,1)S(1)} collective-permute-done((bf16[4,12,96,128]{3,2,1,0:T(8,128)(2,1)S(1)}, bf16[4,12,96,128]{3,2,1,0:T(8,128)(2,1)S(1)}, u32[]{:S(2)}, u32[]{:S(2)}) %collective-permute-start.13) | collective-permute-done | bytes 1179680 | tf_op jit(solution)/shard_map/ppermute | solution.py:246
  130.6 0.4 collective-permute-done.14
  131.1 1.2 fusion.3
  132.3 0.5 collective-permute-start.15
  132.7 0.9 collective-permute-start.17
  133.6 0.6 collective-permute-start.16
  134.2 3.0 %reduce-scatter.2.cloned.1.call-done = bf16[1,8,2,32,384]{4,3,2,1,0:T(8,128)(2,1)} async-done(((bf16[8,8,2,32,384]{4,3,2,1,0:T(8,128)(2,1)}), bf16[1,8,2,32,384]{4,3,2,1,0:T(8,128)(2,1)}) %reduce-scatter.2.cloned.1.call-update) | async-done | bytes 393232 | tf_op jit(solution)/shard_map/reduce_scatter | solution.py:330
  137.1 7.6 %all-to-all-start.1 = ((bf16[8,2,32,384]{3,2,1,0:T(8,128)(2,1)}), bf16[8,2,32,384]{3,2,1,0:T(8,128)(2,1)S(1)}, u32[]{:S(2)}, u32[]{:S(2)}) async-start(bf16[8,2,32,384]{3,2,1,0:T(8,128)(2,1)} %bitcast.38), calls=%async_computation.2 | async-start | bytes 786432 | tf_op jit(solution)/shard_map/all_to_all | solution.py:345
  144.7 1.6 fusion.1
  146.4 0.8 slice.88
  147.2 0.7 slice_bitcast_fusion
  147.9 4.9 %all-to-all-done.1.refs_0_ = bf16[8,2,32,384]{3,2,1,0:T(8,128)(2,1)S(1)} async-done(((bf16[8,2,32,384]{3,2,1,0:T(8,128)(2,1)}), bf16[8,2,32,384]{3,2,1,0:T(8,128)(2,1)S(1)}, u32[]{:S(2)}, u32[]{:S(2)}) %all-to-all-start.1) | async-done | bytes 393248 | tf_op jit(solution)/shard_map/all_to_all | solution.py:345
  152.8 2.5 %shard_map.97 = (bf16[2,128,384]{2,1,0:T(8,128)(2,1)}, bf16[2,3,128,384]{3,2,1,0:T(8,128)(2,1)}) custom-call(s32[1,16]{1,0:T(1,128)S(1)} %copy-done.4, s32[1,8]{1,0:T(1,128)S(1)} %copy-done.5, bf16[2,3,128,384]{3,2,1,0:T(8,128)(2,1)S(1)} %bitcast.33, bf16[2,128,384]{2,1,0:T(8,128)(2,1)S(1)} %bitcast.35, bf16[8,2,32,384]{3,2,1,0:T(8,128)(2,1)S(1)} %all-to-all-done.1.refs_0_), custom_call_target="tpu_custom_call" | custom-call | tf_op jit(solution)/shard_map/pallas_call | solution.py:346
  (46 shorter events, 0.3 us)
Async XLA Ops:
  11.1 17.6 %all-to-all-start = ((bf16[8,2,2,16,384]{4,3,2,1,0:T(8,128)(2,1)}), bf16[8,2,2,16,384]{4,3,2,1,0:T(8,128)(2,1)S(1)}, u32[]{:S(2)}, u32[]{:S(2)}) async-start(bf16[8,2,2,16,384]{4,3,2,1,0:T(8,128)(2,1)} %shard_map.93), calls=%async_computation | async-start | bytes 786432 | tf_op jit(solution)/shard_map/all_to_all | solution.py:285
  17.7 61.0 %all-gather.2.cloned.1.call-start = ((), (), s32[]{:S(2)}) async-start(), calls=%async_computation.3 | async-start | bytes 3538944 | tf_op jit(solution)/shard_map/all_gather | solution.py:288
  19.4 6.1 %collective-permute-start.1 = (bf16[96,1536]{1,0:T(8,128)(2,1)}, bf16[96,1536]{1,0:T(8,128)(2,1)S(1)}, u32[]{:S(2)}, u32[]{:S(2)}) collective-permute-start(bf16[96,1536]{1,0:T(8,128)(2,1)} %shard_map.94.own_ref), channel_id=1, source_target_pairs={{0,48},{8,200},{16,0},{24,216},{32,16},{40,232},{48,32},{56,248},{... | collective-permute-start | bytes 884744 | tf_op jit(solution)/shard_map/ppermute | solution.py:246
  21.4 7.3 %collective-permute-start = (bf16[96,1536]{1,0:T(8,128)(2,1)}, bf16[96,1536]{1,0:T(8,128)(2,1)S(1)}, u32[]{:S(2)}, u32[]{:S(2)}) collective-permute-start(bf16[96,1536]{1,0:T(8,128)(2,1)} %shard_map.94.own_ref), channel_id=1, source_target_pairs={{0,16},{8,72},{16,32},{24,88},{32,48},{40,104},{48,0},{56,120},{64... | collective-permute-start | bytes 884744 | tf_op jit(solution)/shard_map/ppermute | solution.py:246
  25.5 11.7 %copy-start.12 = (bf16[96,1536]{1,0:T(8,128)(2,1)}, bf16[96,1536]{1,0:T(8,128)(2,1)S(1)}, u32[]{:S(2)}) copy-start(bf16[96,1536]{1,0:T(8,128)(2,1)S(1)} %collective-permute-done.1.near_3) | copy-start | bytes 884740
  28.7 8.6 %copy-start.13 = (bf16[96,1536]{1,0:T(8,128)(2,1)}, bf16[96,1536]{1,0:T(8,128)(2,1)S(1)}, u32[]{:S(2)}) copy-start(bf16[96,1536]{1,0:T(8,128)(2,1)S(1)} %collective-permute-done.near_1) | copy-start | bytes 884740
  28.7 0.8 copy-start.6
  29.5 46.6 %copy-start.4 = (s32[1,16]{1,0:T(1,128)S(1)}, s32[1,16]{1,0:T(1,128)}, u32[]{:S(2)}) copy-start(s32[1,16]{1,0:T(1,128)} %row_ref.3) | copy-start | bytes 196
  29.5 107.6 %reduce-scatter.2.cloned.1.call-start = ((), (), s32[]{:S(2)}) async-start(), calls=%async_computation.4 | async-start | bytes 3538944 | tf_op jit(solution)/shard_map/reduce_scatter | solution.py:330
  29.6 7.7 %collective-permute-start.2 = (bf16[96,1536]{1,0:T(8,128)(2,1)}, bf16[96,1536]{1,0:T(8,128)(2,1)S(1)}, u32[]{:S(2)}, u32[]{:S(2)}) collective-permute-start(bf16[96,1536]{1,0:T(8,128)(2,1)} %shard_map.94.own_ref), channel_id=1, source_target_pairs={{0,32},{8,136},{16,48},{24,152},{32,0},{40,168},{48,16},{56,184},{... | collective-permute-start | bytes 884744 | tf_op jit(solution)/shard_map/ppermute | solution.py:246
  37.2 0.7 copy-start.14
  40.3 28.4 %collective-permute-start.5 = (bf16[4,96,1536]{2,1,0:T(8,128)(2,1)}, bf16[4,96,1536]{2,1,0:T(8,128)(2,1)S(1)}, u32[]{:S(2)}, u32[]{:S(2)}) collective-permute-start(bf16[4,96,1536]{2,1,0:T(8,128)(2,1)} %shard_map.95.refs_3_), channel_id=1, source_target_pairs={{0,192},{8,56},{16,208},{24,8},{32,224},{40,24},{48,240},{56,40},{... | collective-permute-start | bytes 3538952 | tf_op jit(solution)/shard_map/ppermute | solution.py:246
  42.6 29.6 %collective-permute-start.4 = (bf16[4,96,1536]{2,1,0:T(8,128)(2,1)}, bf16[4,96,1536]{2,1,0:T(8,128)(2,1)S(1)}, u32[]{:S(2)}, u32[]{:S(2)}) collective-permute-start(bf16[4,96,1536]{2,1,0:T(8,128)(2,1)} %shard_map.95.refs_3_), channel_id=1, source_target_pairs={{0,128},{8,40},{16,144},{24,56},{32,160},{40,8},{48,176},{56,24},{... | collective-permute-start | bytes 3538952 | tf_op jit(solution)/shard_map/ppermute | solution.py:246
  42.9 29.5 %collective-permute-start.3 = (bf16[4,96,1536]{2,1,0:T(8,128)(2,1)}, bf16[4,96,1536]{2,1,0:T(8,128)(2,1)S(1)}, u32[]{:S(2)}, u32[]{:S(2)}) collective-permute-start(bf16[4,96,1536]{2,1,0:T(8,128)(2,1)} %shard_map.95.refs_3_), channel_id=1, source_target_pairs={{0,64},{8,24},{16,80},{24,40},{32,96},{40,56},{48,112},{56,8},{64,... | collective-permute-start | bytes 3538952 | tf_op jit(solution)/shard_map/ppermute | solution.py:246
  43.5 34.1 %collective-permute-start.6 = (bf16[4,96,1536]{2,1,0:T(8,128)(2,1)}, bf16[4,96,1536]{2,1,0:T(8,128)(2,1)}, u32[]{:S(2)}, u32[]{:S(2)}) collective-permute-start(bf16[4,96,1536]{2,1,0:T(8,128)(2,1)} %shard_map.95.refs_3_), channel_id=1, source_target_pairs={{0,8},{8,0},{16,24},{24,16},{32,40},{40,32},{48,56},{56,48},{1,9},... | collective-permute-start | bytes 3538952 | tf_op jit(solution)/shard_map/ppermute | solution.py:232
  68.7 10.0 %copy-start.7 = (bf16[4,96,1536]{2,1,0:T(8,128)(2,1)}, bf16[4,96,1536]{2,1,0:T(8,128)(2,1)S(1)}, u32[]{:S(2)}) copy-start(bf16[4,96,1536]{2,1,0:T(8,128)(2,1)S(1)} %collective-permute-done.5.refs_6_) | copy-start | bytes 3538948
  68.7 8.8 %collective-permute-start.9 = (bf16[4,96,1536]{2,1,0:T(8,128)(2,1)S(1)}, bf16[4,96,1536]{2,1,0:T(8,128)(2,1)}, u32[]{:S(2)}, u32[]{:S(2)}) collective-permute-start(bf16[4,96,1536]{2,1,0:T(8,128)(2,1)S(1)} %collective-permute-done.5.refs_6_), channel_id=1, source_target_pairs={{0,8},{8,0},{16,24},{24,16},{32,40},{40,32},{48,56},{56,48},{1,9},... | collective-permute-start | bytes 3538952 | tf_op jit(solution)/shard_map/ppermute | solution.py:232
  72.2 6.5 %copy-start.8 = (bf16[4,96,1536]{2,1,0:T(8,128)(2,1)}, bf16[4,96,1536]{2,1,0:T(8,128)(2,1)S(1)}, u32[]{:S(2)}) copy-start(bf16[4,96,1536]{2,1,0:T(8,128)(2,1)S(1)} %collective-permute-done.4.refs_5_) | copy-start | bytes 3538948
  72.2 5.3 %collective-permute-start.8 = (bf16[4,96,1536]{2,1,0:T(8,128)(2,1)S(1)}, bf16[4,96,1536]{2,1,0:T(8,128)(2,1)}, u32[]{:S(2)}, u32[]{:S(2)}) collective-permute-start(bf16[4,96,1536]{2,1,0:T(8,128)(2,1)S(1)} %collective-permute-done.4.refs_5_), channel_id=1, source_target_pairs={{0,8},{8,0},{16,24},{24,16},{32,40},{40,32},{48,56},{56,48},{1,9},... | collective-permute-start | bytes 3538952 | tf_op jit(solution)/shard_map/ppermute | solution.py:232
  72.3 6.4 %copy-start.9 = (bf16[4,96,1536]{2,1,0:T(8,128)(2,1)}, bf16[4,96,1536]{2,1,0:T(8,128)(2,1)S(1)}, u32[]{:S(2)}) copy-start(bf16[4,96,1536]{2,1,0:T(8,128)(2,1)S(1)} %collective-permute-done.3.refs_4_) | copy-start | bytes 3538948
  72.3 6.3 %collective-permute-start.7 = (bf16[4,96,1536]{2,1,0:T(8,128)(2,1)S(1)}, bf16[4,96,1536]{2,1,0:T(8,128)(2,1)}, u32[]{:S(2)}, u32[]{:S(2)}) collective-permute-start(bf16[4,96,1536]{2,1,0:T(8,128)(2,1)S(1)} %collective-permute-done.3.refs_4_), channel_id=1, source_target_pairs={{0,8},{8,0},{16,24},{24,16},{32,40},{40,32},{48,56},{56,48},{1,9},... | collective-permute-start | bytes 3538952 | tf_op jit(solution)/shard_map/ppermute | solution.py:232
  92.7 1.9 %copy-start = (bf16[8,2,32,3072]{3,2,1,0:T(8,128)(2,1)S(1)}, bf16[8,2,32,3072]{3,2,1,0:T(8,128)(2,1)}, u32[]{:S(2)}) copy-start(bf16[8,2,32,3072]{3,2,1,0:T(8,128)(2,1)} %all-gather.2.cloned.1.call-done.refs_2_.whole_ref) | copy-start | bytes 9437188
  94.5 1.3 copy-start.1
  95.4 4.6 %collective-permute-start.10 = (bf16[2,1536,256]{2,1,0:T(8,128)(2,1)S(1)}, bf16[2,1536,256]{2,1,0:T(8,128)(2,1)S(1)}, u32[]{:S(2)}, u32[]{:S(2)}) collective-permute-start(bf16[2,1536,256]{2,1,0:T(8,128)(2,1)S(1)} %get-tuple-element.20), channel_id=1, source_target_pairs={{0,8},{8,0},{16,24},{24,16},{32,40},{40,32},{48,56},{56,48},{1,9},... | collective-permute-start | bytes 4718600 | tf_op jit(solution)/shard_map/ppermute | solution.py:232
  95.9 4.2 %collective-permute-start.11 = (bf16[256,1536]{1,0:T(8,128)(2,1)S(1)}, bf16[256,1536]{1,0:T(8,128)(2,1)S(1)}, u32[]{:S(2)}, u32[]{:S(2)}) collective-permute-start(bf16[256,1536]{1,0:T(8,128)(2,1)S(1)} %copy-done.1), channel_id=1, source_target_pairs={{0,8},{8,0},{16,24},{24,16},{32,40},{40,32},{48,56},{56,48},{1,9},... | collective-permute-start | bytes 2359304 | tf_op jit(solution)/shard_map/ppermute | solution.py:232
  100.9 17.0 %collective-permute-start.12 = (bf16[4,12,96,128]{3,2,1,0:T(8,128)(2,1)S(1)}, bf16[4,12,96,128]{3,2,1,0:T(8,128)(2,1)S(1)}, u32[]{:S(2)}, u32[]{:S(2)}) collective-permute-start(bf16[4,12,96,128]{3,2,1,0:T(8,128)(2,1)S(1)} %shard_map.100), channel_id=1, source_target_pairs={{0,32},{8,136},{16,48},{24,152},{32,0},{40,168},{48,16},{56,184},{... | collective-permute-start | bytes 3538952 | tf_op jit(solution)/shard_map/ppermute | solution.py:246
  102.5 28.1 %collective-permute-start.13 = (bf16[4,12,96,128]{3,2,1,0:T(8,128)(2,1)S(1)}, bf16[4,12,96,128]{3,2,1,0:T(8,128)(2,1)S(1)}, u32[]{:S(2)}, u32[]{:S(2)}) collective-permute-start(bf16[4,12,96,128]{3,2,1,0:T(8,128)(2,1)S(1)} %shard_map.101), channel_id=1, source_target_pairs={{0,16},{8,72},{16,32},{24,88},{32,48},{40,104},{48,0},{56,120},{64... | collective-permute-start | bytes 3538952 | tf_op jit(solution)/shard_map/ppermute | solution.py:246
  106.5 24.6 %collective-permute-start.14 = (bf16[4,12,96,128]{3,2,1,0:T(8,128)(2,1)S(1)}, bf16[4,12,96,128]{3,2,1,0:T(8,128)(2,1)S(1)}, u32[]{:S(2)}, u32[]{:S(2)}) collective-permute-start(bf16[4,12,96,128]{3,2,1,0:T(8,128)(2,1)S(1)} %shard_map.102), channel_id=1, source_target_pairs={{0,48},{8,200},{16,0},{24,216},{32,16},{40,232},{48,32},{56,248},{... | collective-permute-start | bytes 3538952 | tf_op jit(solution)/shard_map/ppermute | solution.py:246
  130.6 1.6 %copy-start.10 = (bf16[4,12,96,128]{3,2,1,0:T(8,128)(2,1)}, bf16[4,12,96,128]{3,2,1,0:T(8,128)(2,1)S(1)}, u32[]{:S(2)}) copy-start(bf16[4,12,96,128]{3,2,1,0:T(8,128)(2,1)S(1)} %collective-permute-done.13) | copy-start | bytes 3538948
  131.1 1.2 copy-start.11
  132.3 12.5 %collective-permute-start.15 = (bf16[12,96,128]{2,1,0:T(8,128)(2,1)}, bf16[12,96,128]{2,1,0:T(8,128)(2,1)}, u32[]{:S(2)}, u32[]{:S(2)}) collective-permute-start(bf16[12,96,128]{2,1,0:T(8,128)(2,1)} %get-tuple-element.22), channel_id=1, source_target_pairs={{0,128},{8,40},{16,144},{24,56},{32,160},{40,8},{48,176},{56,24},{... | collective-permute-start | bytes 884744 | tf_op jit(solution)/shard_map/ppermute | solution.py:246
  132.7 12.0 %collective-permute-start.17 = (bf16[12,96,128]{2,1,0:T(8,128)(2,1)S(1)}, bf16[12,96,128]{2,1,0:T(8,128)(2,1)}, u32[]{:S(2)}, u32[]{:S(2)}) collective-permute-start(bf16[12,96,128]{2,1,0:T(8,128)(2,1)S(1)} %get-tuple-element.23), channel_id=1, source_target_pairs={{0,192},{8,56},{16,208},{24,8},{32,224},{40,24},{48,240},{56,40},{... | collective-permute-start | bytes 884744 | tf_op jit(solution)/shard_map/ppermute | solution.py:246
  133.6 11.1 %collective-permute-start.16 = (bf16[12,96,128]{2,1,0:T(8,128)(2,1)S(1)}, bf16[12,96,128]{2,1,0:T(8,128)(2,1)}, u32[]{:S(2)}, u32[]{:S(2)}) collective-permute-start(bf16[12,96,128]{2,1,0:T(8,128)(2,1)S(1)} %get-tuple-element.24), channel_id=1, source_target_pairs={{0,64},{8,24},{16,80},{24,40},{32,96},{40,56},{48,112},{56,8},{64,... | collective-permute-start | bytes 884744 | tf_op jit(solution)/shard_map/ppermute | solution.py:246
  137.1 15.7 %all-to-all-start.1 = ((bf16[8,2,32,384]{3,2,1,0:T(8,128)(2,1)}), bf16[8,2,32,384]{3,2,1,0:T(8,128)(2,1)S(1)}, u32[]{:S(2)}, u32[]{:S(2)}) async-start(bf16[8,2,32,384]{3,2,1,0:T(8,128)(2,1)} %bitcast.38), calls=%async_computation.2 | async-start | bytes 786432 | tf_op jit(solution)/shard_map/all_to_all | solution.py:345
  146.4 6.4 %copy-start.2 = (bf16[1,2,128,3,384]{4,2,3,1,0:T(8,128)(2,1)S(1)}, bf16[1,2,128,3,384]{4,2,3,1,0:T(8,128)(2,1)}, u32[]{:S(2)}) copy-start(bf16[1,2,128,3,384]{4,2,3,1,0:T(8,128)(2,1)} %param.6) | copy-start | bytes 1769476
  146.4 6.4 %copy-start.3 = (bf16[1,2,128,384]{3,2,1,0:T(8,128)(2,1)S(1)}, bf16[1,2,128,384]{3,2,1,0:T(8,128)(2,1)}, u32[]{:S(2)}) copy-start(bf16[1,2,128,384]{3,2,1,0:T(8,128)(2,1)} %param.9) | copy-start | bytes 589828
  146.4 6.4 %copy-start.5 = (s32[1,8]{1,0:T(1,128)S(1)}, s32[1,8]{1,0:T(1,128)}, u32[]{:S(2)}) copy-start(s32[1,8]{1,0:T(1,128)} %patch_ref.3) | copy-start | bytes 100
Sparse Core Ops, SparseCore 0:
  29.6 45.3 all-gather.1
  92.8 44.2 reduce-scatter.1

commit v4 on v0

--- a/solution.py
+++ b/solution.py
@@ -33,12 +33,18 @@
     return dot(d_scores, keys).astype(BF), dot(d_scores, query, TN).astype(BF), d_values
 
 
-def spatial_forward(count_ref, qkv_ref, cot_ref, out_ref):
+def live_rows(row_ref, patch_ref, frame):
+    return patch_ref[0, row_ref[0, frame]]
+
+
+def spatial_forward(row_ref, patch_ref, qkv_ref, cot_ref, *refs):
+    out_ref, whole_ref = refs
     frames, _, patches, width = qkv_ref.shape
+    place = lax.axis_index("frame")
     owners = out_ref.shape[0]
     block = patches // owners
     for f in range(frames):
-        count = count_ref[f]
+        count = live_rows(row_ref, patch_ref, place * frames + f)
         keys_live = lax.broadcasted_iota(jnp.int32, (patches, patches), 1) < count
         rows_live = lax.broadcasted_iota(jnp.int32, (patches, 1), 0) < count
         pieces = []
@@ -47,40 +53,49 @@
             probs = softmax(qkv_ref[f, 0, :, cols], qkv_ref[f, 1, :, cols], keys_live)
             mixed = dot(probs.astype(BF), qkv_ref[f, 2, :, cols])
             pieces.append(jnp.where(rows_live, mixed, 0.0).astype(BF))
-        whole = jnp.concatenate(pieces, axis=1)
-        gated = jnp.where(rows_live, cot_ref[f].astype(F32), 0.0).astype(BF)
-        for s in range(owners):
-            out_ref[s, 0, f] = whole[s * block : (s + 1) * block]
-            out_ref[s, 1, f] = gated[s * block : (s + 1) * block]
-
-
-def spatial_backward(count_ref, qkv_ref, cot_ref, sums_ref, out_ref, grad_ref):
+        whole_ref[0, f] = jnp.concatenate(pieces, axis=1)
+        whole_ref[1, f] = jnp.where(rows_live, cot_ref[f].astype(F32), 0.0).astype(BF)
+    for s in range(owners):
+        out_ref[s] = whole_ref[:, :, s * block : (s + 1) * block, :]
+
+
+def spatial_backward(row_ref, patch_ref, qkv_ref, cot_ref, *refs):
+    sums_ref, out_ref, grad_ref, whole_ref = refs
     frames, _, patches, width = qkv_ref.shape
+    place = lax.axis_index("frame")
     owners = sums_ref.shape[0]
+    block = patches // owners
+    for s in range(owners):
+        for f in range(frames):
+            part = sums_ref[s, :, f * block : (f + 1) * block, :]
+            whole_ref[:, f, s * block : (s + 1) * block, :] = part
     for f in range(frames):
-        count = count_ref[f]
+        count = live_rows(row_ref, patch_ref, place * frames + f)
         keys_live = lax.broadcasted_iota(jnp.int32, (patches, patches), 1) < count
         rows_live = lax.broadcasted_iota(jnp.int32, (patches, 1), 0) < count
-        projected = jnp.concatenate([sums_ref[s, 0, f] for s in range(owners)], axis=0)
-        back = jnp.concatenate([sums_ref[s, 1, f] for s in range(owners)], axis=0)
-        d_spatial = cot_ref[f].astype(F32) + back.astype(F32)
+        d_spatial = cot_ref[f].astype(F32) + whole_ref[1, f].astype(F32)
         d_mixed = jnp.where(rows_live, d_spatial, 0.0).astype(BF)
         for h in range(width // HD):
             cols = slice(h * HD, (h + 1) * HD)
             query, keys, values = (qkv_ref[f, i, :, cols] for i in range(3))
             probs = softmax(query, keys, keys_live)
             mixed = dot(probs.astype(BF), values).astype(BF).astype(F32)
-            total = mixed + projected[:, cols].astype(F32)
+            total = mixed + whole_ref[0, f, :, cols].astype(F32)
             out_ref[f, :, cols] = jnp.where(rows_live, total, 0.0).astype(BF)
             grads = attention_grads(query, keys, values, probs, d_mixed[:, cols])
             for i in range(3):
                 grad_ref[f, i, :, cols] = grads[i]
 
 
-def assemble_kernel(ranks, place_ref, *refs):
+def own_chip():
+    place = lax.axis_index("frame")
+    return lax.axis_index("clip"), place // 2, place % 2
+
+
+def assemble_kernel(ranks, *refs):
     blocks, refs = refs[: 2 * ranks], refs[2 * ranks :]
     feat_ref, gated_ref, own_ref, other_ref, flip_ref, sem = refs
-    me, core = place_ref[3], place_ref[2]
+    me, core = lax.axis_index("tensor"), own_chip()[2]
     width = feat_ref.shape[1] // ranks
     copies = []
     for a, whole in enumerate((feat_ref, gated_ref)):
@@ -106,8 +121,8 @@
             other_ref[a, to] = flip_ref[pl.ds(pl.multiple_of((2 * i + 1 - core) * rows, 16), rows), :]
 
 
-def temporal_kernel(heads, row_key_ref, col_key_ref, feat_ref, gated_ref, _, *refs):
-    w_hbm, sums_hbm, both_ref, w_ref, sums_ref, w_sem, out_sem = refs
+def temporal_kernel(heads, row_key_ref, col_key_ref, feat_hbm, gated_hbm, _, w_hbm, *refs):
+    sums_hbm, both_ref, feat_ref, gated_ref, w_ref, sums_ref, in_sem, w_sem, out_sem = refs
     width = heads * HD
     slots = 4 * heads
     ranks, owners, _, rows, _ = sums_ref.shape
@@ -115,45 +130,56 @@
         pltpu.make_async_copy(w_hbm.at[i], w_ref.at[:, i * HD : (i + 1) * HD], w_sem.at[i])
         for i in range(slots)
     ]
-    for copy in loads:
+    feat_load = pltpu.make_async_copy(feat_hbm, feat_ref, in_sem.at[0])
+    gated_load = pltpu.make_async_copy(gated_hbm, gated_ref, in_sem.at[1])
+    feat_load.start()
+    for copy in loads[:6]:
         copy.start()
     mask = row_key_ref[...] == col_key_ref[...]
+    feat_load.wait()
     query, keys, values = [], [], []
     for h in range(heads):
-        for i in range(3):
-            loads[3 * h + i].wait()
-        qkv = dot(feat_ref[...], w_ref[:, 3 * h * HD : 3 * (h + 1) * HD]).astype(BF)
+        for copy in loads[3 * h : 3 * h + 3]:
+            copy.wait()
+        if h == 0:
+            gated_load.start()
+        for copy in loads[3 * h + 6 : 3 * h + 9]:
+            copy.start()
+        qkv = dot(feat_ref[...], w_ref[:, h * width : (h + 1) * width]).astype(BF)
         for i, parts in enumerate((query, keys, values)):
             parts.append(qkv[:, i * HD : (i + 1) * HD])
-    for h in range(heads):
-        loads[3 * heads + h].wait()
-    cotangent = dot(gated_ref[...], w_ref[:, 3 * width :]).astype(BF)
-    cotangent = [cotangent[:, h * HD : (h + 1) * HD] for h in range(heads)]
     each = range(heads)
     probs = [softmax(query[h], keys[h], mask) for h in each]
+    mixed = [dot(probs[h].astype(BF), values[h]).astype(BF) for h in each]
+    gated_load.wait()
+    for copy in loads[9:]:
+        copy.wait()
+    cotangent = dot(gated_ref[...], w_ref[:, 3 * width :]).astype(BF)
     for h in each:
-        grads = attention_grads(query[h], keys[h], values[h], probs[h], cotangent[h])
+        cols = slice(h * HD, (h + 1) * HD)
+        grads = attention_grads(query[h], keys[h], values[h], probs[h], cotangent[:, cols])
         for i in range(3):
-            start = (3 * h + i) * HD
-            both_ref[:, start : start + HD] = grads[i]
-        start = 3 * width + h * HD
-        both_ref[:, start : start + HD] = dot(probs[h].astype(BF), values[h]).astype(BF)
+            both_ref[:, (3 * h + i) * HD : (3 * h + i + 1) * HD] = grads[i]
+        both_ref[:, 3 * width + h * HD : 3 * width + (h + 1) * HD] = mixed[h]
     stores = []
-    for z in range(ranks):
-        part = slice(z * width, (z + 1) * width)
-        projected = dot(both_ref[:, 3 * width :], w_ref[part, 3 * width :], NT).astype(BF)
-        back = dot(both_ref[:, : 3 * width], w_ref[part, : 3 * width], NT).astype(BF)
-        for s in range(owners):
-            sums_ref[z, s, 0] = projected[s * rows : (s + 1) * rows]
-            sums_ref[z, s, 1] = back[s * rows : (s + 1) * rows]
-        stores.append(pltpu.make_async_copy(sums_ref.at[z], sums_hbm.at[z], out_sem.at[z]))
-        stores[-1].start()
+    pair = 4
+    for first in range(0, ranks, pair):
+        w_part = w_ref.at[first * width : (first + pair) * width]
+        projected = dot(both_ref[:, 3 * width :], w_part[:, 3 * width :], NT).astype(BF)
+        back = dot(both_ref[:, : 3 * width], w_part[:, : 3 * width], NT).astype(BF)
+        for i in range(pair):
+            z, cols = first + i, slice(i * width, (i + 1) * width)
+            for s in range(owners):
+                sums_ref[z, s, 0] = projected[s * rows : (s + 1) * rows, cols]
+                sums_ref[z, s, 1] = back[s * rows : (s + 1) * rows, cols]
+            stores.append(pltpu.make_async_copy(sums_ref.at[z], sums_hbm.at[z], out_sem.at[z]))
+            stores[-1].start()
     for copy in stores:
         copy.wait()
 
 
-def weight_grad_kernel(step, place_ref, own_ref, pair_ref, both_ref, pair_both_ref, out_ref):
-    at_clip, at_x, core = place_ref[0], place_ref[1], place_ref[2]
+def weight_grad_kernel(step, own_ref, pair_ref, both_ref, pair_both_ref, out_ref):
+    at_clip, at_x, core = own_chip()
     n, slots, rows, _ = out_ref.shape
     wide = both_ref.shape[1] * 3 // 4
     starts = []
@@ -217,12 +243,7 @@
 def body(spatial_qkv, w_qkv, w_out, out_grad, frame_clip, clip_patches):
     ranks = lax.axis_size("frame")
     width_ranks = lax.axis_size("tensor")
-    at_frame = lax.axis_index("frame").astype(jnp.int32)
-    at_clip = lax.axis_index("clip").astype(jnp.int32)
-    at_width = lax.axis_index("tensor").astype(jnp.int32)
-    clip_row = frame_clip[0]
-    counts = clip_patches[0]
-    total_frames = clip_row.shape[0]
+    total_frames = frame_clip.shape[1]
     _, frames, patches, _, width = spatial_qkv.shape
     heads = width // HD
     block = patches // ranks
@@ -237,10 +258,8 @@
     )
     w_all = lax.all_gather(w_own, ("clip", "frame"), axis=1, tiled=True)
 
-    own_clips = lax.dynamic_slice_in_dim(clip_row, at_frame * frames, frames, 0)
-    member = own_clips[:, None] == jnp.arange(counts.shape[0], dtype=jnp.int32)[None, :]
-    live = jnp.sum(jnp.where(member, counts[None, :], 0), axis=1).astype(jnp.int32)
-    keys = (clip_row[:, None] * block + jnp.arange(block, dtype=jnp.int32)[None, :]).reshape(rows_t)
+    clips = frame_clip[0][:, None] * block
+    keys = (clips + jnp.arange(block, dtype=jnp.int32)[None, :]).reshape(rows_t)
 
     qkv = spatial_qkv[0].transpose(0, 2, 1, 3)
     cot = out_grad[0]
@@ -250,32 +269,33 @@
     sent = pl.pallas_call(
         spatial_forward,
         out_shape=jax.ShapeDtypeStruct((ranks, 2, frames, block, width), BF),
-        in_specs=[smem, vmem, vmem],
+        in_specs=[smem, smem, vmem, vmem],
         out_specs=vmem,
-        compiler_params=pltpu.CompilerParams(vmem_limit_bytes=24 * 2**20),
-    )(live, qkv, cot)
+        scratch_shapes=[pltpu.VMEM((2, frames, patches, width), BF)],
+        compiler_params=pltpu.CompilerParams(vmem_limit_bytes=58 * 2**20),
+    )(frame_clip, clip_patches, qkv, cot)
     cols = lax.all_to_all(sent, "frame", split_axis=0, concat_axis=0, tiled=True)
     blocks = []
     for a in range(2):
         rows = cols[:, a].reshape(rows_t, width)
         blocks += ring_gather(rows, "tensor", width_ranks, a == 0)
 
-    place = jnp.stack([at_clip, at_frame // 2, at_frame % 2, at_width])
     halves = jax.ShapeDtypeStruct((2, model // 2, rows_t), BF)
     wide = jax.ShapeDtypeStruct((rows_t, model), BF)
     feats, gated, own_flip, other_flip = pl.pallas_call(
         lambda *refs: assemble_kernel(width_ranks, *refs),
         out_shape=[wide, wide, halves, halves],
-        in_specs=[smem] + [hbm] * (2 * width_ranks),
+        in_specs=[hbm] * (2 * width_ranks),
         out_specs=[vmem] * 4,
         scratch_shapes=[
             pltpu.VMEM((model, rows_t), BF),
             pltpu.SemaphoreType.DMA((2 * width_ranks,)),
         ],
         compiler_params=pltpu.CompilerParams(vmem_limit_bytes=58 * 2**20),
-    )(place, *blocks)
+    )(*blocks)
     pair_flip = pair_swap(other_flip)
 
+    wide_scratch = pltpu.VMEM((rows_t, model), BF)
     sums_shape = (width_ranks, ranks, 2, frames * block, width)
     sums, both = pl.pallas_call(
         lambda *refs: temporal_kernel(heads, *refs),
@@ -283,11 +303,14 @@
             jax.ShapeDtypeStruct(sums_shape, BF),
             jax.ShapeDtypeStruct((rows_t, 4 * width), BF),
         ],
-        in_specs=[vmem] * 4 + [hbm] * 2,
+        in_specs=[vmem] * 2 + [hbm] * 4,
         out_specs=[hbm, vmem],
         scratch_shapes=[
+            wide_scratch,
+            wide_scratch,
             pltpu.VMEM((model, 4 * width), BF),
             pltpu.VMEM(sums_shape, BF),
+            pltpu.SemaphoreType.DMA((2,)),
             pltpu.SemaphoreType.DMA((slots,)),
             pltpu.SemaphoreType.DMA((width_ranks,)),
         ],
@@ -301,26 +324,26 @@
         parts[step] = pl.pallas_call(
             lambda *refs, step=step: weight_grad_kernel(step, *refs),
             out_shape=jax.ShapeDtypeStruct((4, slots, w_rows, HD), BF),
-            in_specs=[smem] + [vmem] * 4,
+            in_specs=[vmem] * 4,
             out_specs=vmem,
             compiler_params=pltpu.CompilerParams(vmem_limit_bytes=24 * 2**20),
-        )(place, own_flip, pair_flip, both, pair_both)
+        )(own_flip, pair_flip, both, pair_both)
     arrived = [parts[0]] + [spread(parts[step], step, False) for step in (2, 1, 3)]
     partial = [add(*(part[i] for part in arrived)).astype(BF) for i in range(4)]
     grads = add(partial[0], *(spread(partial[step], step, True) for step in (2, 1, 3)))
 
     row_sums = lax.all_to_all(own_sums, "frame", split_axis=0, concat_axis=0, tiled=True)
-    row_sums = row_sums.reshape(ranks, 2, frames, block, width)
     block_out, qkv_grad = pl.pallas_call(
         spatial_backward,
         out_shape=[
             jax.ShapeDtypeStruct((frames, patches, width), BF),
             jax.ShapeDtypeStruct((frames, 3, patches, width), BF),
         ],
-        in_specs=[smem, vmem, vmem, vmem],
+        in_specs=[smem, smem] + [vmem] * 3,
         out_specs=[vmem, vmem],
+        scratch_shapes=[pltpu.VMEM((2, frames, patches, width), BF)],
         compiler_params=pltpu.CompilerParams(vmem_limit_bytes=24 * 2**20),
-    )(live, qkv, cot, row_sums)
+    )(frame_clip, clip_patches, qkv, cot, row_sums)
 
     w_qkv_grad = grads[: 3 * heads].reshape(heads, 3, w_rows, HD).transpose(2, 0, 1, 3)
     w_out_grad = grads[3 * heads :].transpose(0, 2, 1)

time: 160 us -> 159 us (level)
  waiting for transfers between devices: 43.4 us -> 45.9 us
    pallas_call x4, Pallas kernels: 5.66 us -> 3.5 us  [body(): pl.pallas_call(lambda *refs, step=step: weight_grad_kernel(step, *refs),...]
    unnamed x60 -> x56, local copies, waits for them, and re-layouts: 4.68 us -> 4.35 us
  transfers between devices with their start and end apart: 25 -> 25, of which waited for: 16 -> 15; matrix products, arithmetic and copies ran while one was open for 4% -> 3% of each run, Pallas kernels for 9% -> 8%
where the time goes in v4:
time: 159 us
  waiting for transfers between devices  45.9 us (29%)
  starting transfers between devices  42.8 us (27%)
  Pallas kernels  29.8 us (19%)
  blocking collectives  14.7 us (9%)
  between operations  14.4 us (9%)
  local copies, waits for them, and re-layouts  7.25 us (5%)
  other arithmetic  3.78 us (2%)
    ppermute x14, starting transfers between devices, shift(): lax.ppermute(value, axis, [(i, (i + step) % size) for i in range(size)])  21.8 us
    ppermute x6, waiting for transfers between devices, spread(): return lax.ppermute(value, ('clip', 'frame'), pairs)  21.6 us
    all_to_all x1, blocking collectives, body(): lax.all_to_all(sent, 'frame', split_axis=0, concat_axis=0, tiled=True)  14.7 us
    pallas_call x1, Pallas kernels, body(): pl.pallas_call(lambda *refs: temporal_kernel(heads, *refs), out_shape=[ja...  14.1 us
    ppermute x14, waiting for transfers between devices, shift(): lax.ppermute(value, axis, [(i, (i + step) % size) for i in range(size)])  10.9 us
    ppermute x6, starting transfers between devices, spread(): return lax.ppermute(value, ('clip', 'frame'), pairs)  8.35 us
    all_to_all x1, starting transfers between devices, body(): lax.all_to_all(own_sums, 'frame', split_axis=0, concat_axis=0, tiled=True)  7.42 us
    pallas_call x1, Pallas kernels, body(): pl.pallas_call(lambda *refs: assemble_kernel(width_ranks, *refs), out_sha...  5.72 us
  transfers between devices with their start and end apart: 25, of which 15 were waited for; matrix products, arithmetic and copies ran while one was open for 3% of the time, Pallas kernels for 8%

profile of v4, /device:TPU:1, one launch (start us, length us, event | category | flops | bytes accessed | tf_op | source)
XLA Modules:
  0.0 158.5 jit_solution(8269354512888574134)
XLA Ops:
  7.2 1.7 %pad_maximum_fusion = bf16[12,96,128]{2,1,0:T(8,128)(2,1)} fusion(bf16[3,96,128]{2,1,0:T(8,128)(2,1)} %bitcast.46, bf16[9,96,128]{2,1,0:T(8,128)(2,1)} %bitcast.45), kind=kLoop, calls=%fused_computation.11 | loop fusion | flops 147456 | bytes 589824 | tf_op jit(solution)/shard_map/concatenate | solution.py:255
  9.0 3.9 %shard_map.93 = bf16[8,2,2,16,384]{4,3,2,1,0:T(8,128)(2,1)} custom-call(s32[1,16]{1,0:T(1,128)} %row_ref.3, s32[1,8]{1,0:T(1,128)} %patch_ref.3, bf16[2,3,128,384]{3,2,1,0:T(8,128)(2,1)} %bitcast.33, bf16[2,128,384]{2,1,0:T(8,128)(2,1)} %bitcast.35), custom_call_target="tpu_custom_call" | custom-call | tf_op jit(solution)/shard_map/pallas_call | solution.py:269
  12.9 14.7 %all_to_all.10 = bf16[8,2,2,16,384]{4,3,2,1,0:T(8,128)(2,1)S(1)} all-to-all(bf16[8,2,2,16,384]{4,3,2,1,0:T(8,128)(2,1)} %shard_map.93), channel_id=1, replica_groups=mesh['clip'=4,'frame'=8,'tensor'=8] {'frame'}, dimensions={0} | all-to-all | bytes 786432 | tf_op jit(solution)/shard_map/all_to_all | solution.py:277
  27.7 0.9 collective-permute-start.3
  28.6 4.0 %collective-permute-start.7 = (bf16[256,384]{1,0:T(8,128)(2,1)S(1)}, bf16[256,384]{1,0:T(8,128)(2,1)S(1)}, u32[]{:S(2)}, u32[]{:S(2)}) collective-permute-start(bf16[256,384]{1,0:T(8,128)(2,1)S(1)} %bitcast.37), channel_id=1, source_target_pairs={{0,7},{1,0},{2,1},{3,2},{4,3},{5,4},{6,5},{7,6},{8,15},{9,8},{10,9... | collective-permute-start | bytes 589832 | tf_op jit(solution)/shard_map/ppermute | solution.py:207
  32.6 1.4 collective-permute-start
  34.1 2.8 %collective-permute-done.3.refs_7_ = bf16[256,384]{1,0:T(8,128)(2,1)S(1)} collective-permute-done((bf16[256,384]{1,0:T(8,128)(2,1)S(1)}, bf16[256,384]{1,0:T(8,128)(2,1)S(1)}, u32[]{:S(2)}, u32[]{:S(2)}) %collective-permute-start.3) | collective-permute-done | bytes 196640 | tf_op jit(solution)/shard_map/ppermute | solution.py:207
  37.0 2.7 %collective-permute-start.8 = (bf16[256,384]{1,0:T(8,128)(2,1)S(1)}, bf16[256,384]{1,0:T(8,128)(2,1)S(1)}, u32[]{:S(2)}, u32[]{:S(2)}) collective-permute-start(bf16[256,384]{1,0:T(8,128)(2,1)S(1)} %collective-permute-done.7.refs_9_), channel_id=1, source_target_pairs={{0,7},{1,0},{2,1},{3,2},{4,3},{5,4},{6,5},{7,6},{8,15},{9,8},{10,9... | collective-permute-start | bytes 589832 | tf_op jit(solution)/shard_map/ppermute | solution.py:207
  39.6 0.6 collective-permute-done.refs_1_
  40.2 3.5 %collective-permute-start.1 = (bf16[256,384]{1,0:T(8,128)(2,1)S(1)}, bf16[256,384]{1,0:T(8,128)(2,1)S(1)}, u32[]{:S(2)}, u32[]{:S(2)}) collective-permute-start(bf16[256,384]{1,0:T(8,128)(2,1)S(1)} %collective-permute-done.refs_1_), channel_id=1, source_target_pairs={{0,7},{1,0},{2,1},{3,2},{4,3},{5,4},{6,5},{7,6},{8,15},{9,8},{10,9... | collective-permute-start | bytes 589832 | tf_op jit(solution)/shard_map/ppermute | solution.py:207
  43.7 1.3 collective-permute-done.4.refs_6_
  45.0 2.7 %collective-permute-start.9 = (bf16[256,384]{1,0:T(8,128)(2,1)S(1)}, bf16[256,384]{1,0:T(8,128)(2,1)S(1)}, u32[]{:S(2)}, u32[]{:S(2)}) collective-permute-start(bf16[256,384]{1,0:T(8,128)(2,1)S(1)} %collective-permute-done.8.refs_10_), channel_id=1, source_target_pairs={{0,7},{1,0},{2,1},{3,2},{4,3},{5,4},{6,5},{7,6},{8,15},{9,8},{10,9... | collective-permute-start | bytes 589832 | tf_op jit(solution)/shard_map/ppermute | solution.py:207
  47.9 3.5 %collective-permute-start.2 = (bf16[256,384]{1,0:T(8,128)(2,1)S(1)}, bf16[256,384]{1,0:T(8,128)(2,1)S(1)}, u32[]{:S(2)}, u32[]{:S(2)}) collective-permute-start(bf16[256,384]{1,0:T(8,128)(2,1)S(1)} %collective-permute-done.1.refs_2_), channel_id=1, source_target_pairs={{0,7},{1,0},{2,1},{3,2},{4,3},{5,4},{6,5},{7,6},{8,15},{9,8},{10,9... | collective-permute-start | bytes 589832 | tf_op jit(solution)/shard_map/ppermute | solution.py:207
  51.4 0.8 collective-permute-done.5.refs_5_
  52.2 3.0 %collective-permute-start.10 = (bf16[256,384]{1,0:T(8,128)(2,1)S(1)}, bf16[256,384]{1,0:T(8,128)(2,1)S(1)}, u32[]{:S(2)}, u32[]{:S(2)}) collective-permute-start(bf16[256,384]{1,0:T(8,128)(2,1)S(1)} %collective-permute-done.9.refs_11_), channel_id=1, source_target_pairs={{0,7},{1,0},{2,1},{3,2},{4,3},{5,4},{6,5},{7,6},{8,15},{9,8},{10,9... | collective-permute-start | bytes 589832 | tf_op jit(solution)/shard_map/ppermute | solution.py:207
  55.2 1.0 collective-permute-done.2.refs_3_
  56.2 2.1 %collective-permute-done.13.refs_13_ = bf16[256,384]{1,0:T(8,128)(2,1)S(1)} collective-permute-done((bf16[256,384]{1,0:T(8,128)(2,1)S(1)}, bf16[256,384]{1,0:T(8,128)(2,1)S(1)}, u32[]{:S(2)}, u32[]{:S(2)}) %collective-permute-start.13) | collective-permute-done | bytes 196640 | tf_op jit(solution)/shard_map/ppermute | solution.py:207
  58.3 2.1 %collective-permute-done.6.refs_4_ = bf16[256,384]{1,0:T(8,128)(2,1)S(1)} collective-permute-done((bf16[256,384]{1,0:T(8,128)(2,1)S(1)}, bf16[256,384]{1,0:T(8,128)(2,1)S(1)}, u32[]{:S(2)}, u32[]{:S(2)}) %collective-permute-start.6) | collective-permute-done | bytes 196640 | tf_op jit(solution)/shard_map/ppermute | solution.py:207
  60.5 0.5 copy-done.26
  61.1 0.7 copy-done.27
  61.7 5.7 %shard_map.94 = (bf16[256,3072]{1,0:T(8,128)(2,1)}, bf16[256,3072]{1,0:T(8,128)(2,1)}, bf16[2,1536,256]{2,1,0:T(8,128)(2,1)}, bf16[2,1536,256]{2,1,0:T(8,128)(2,1)}) custom-call(bf16[256,384]{1,0:T(8,128)(2,1)} %bitcast.42, bf16[256,384]{1,0:T(8,128)(2,1)} %copy-done.16, bf16[256,384]{1,0:T(8,128)(2,1)} %copy-done.20, bf16[256,384]{1,0:T(8,128)(2,1)} %copy-done.24, ...), custom_call_target="tpu_custom_call" | custom-call | tf_op jit(solution)/shard_map/pallas_call | solution.py:285
  67.5 4.7 %collective-permute-start.14 = (bf16[2,1536,256]{2,1,0:T(8,128)(2,1)}, bf16[2,1536,256]{2,1,0:T(8,128)(2,1)S(1)}, u32[]{:S(2)}, u32[]{:S(2)}) collective-permute-start(bf16[2,1536,256]{2,1,0:T(8,128)(2,1)} %get-tuple-element.14), channel_id=1, source_target_pairs={{0,8},{8,0},{16,24},{24,16},{32,40},{40,32},{48,56},{56,48},{1,9},... | collective-permute-start | bytes 4718600 | tf_op jit(solution)/shard_map/ppermute | solution.py:211
  72.2 0.6 add.104.refs_1_
  72.9 0.8 add.124.refs_0_
  73.6 2.5 %collective-permute-done.14.refs_4_.refs_1_ = bf16[2,1536,256]{2,1,0:T(8,128)(2,1)S(1)} collective-permute-done((bf16[2,1536,256]{2,1,0:T(8,128)(2,1)}, bf16[2,1536,256]{2,1,0:T(8,128)(2,1)S(1)}, u32[]{:S(2)}, u32[]{:S(2)}) %collective-permute-start.14) | collective-permute-done | bytes 1572896 | tf_op jit(solution)/shard_map/ppermute | solution.py:211
  76.3 0.9 copy-done
  77.3 14.1 %shard_map.95 = (bf16[8,8,2,32,384]{4,3,2,1,0:T(8,128)(2,1)}, bf16[256,1536]{1,0:T(8,128)(2,1)}) custom-call(s32[256,1]{1,0:T(8,128)} %add.124.refs_0_, s32[1,256]{1,0:T(1,128)} %add.104.refs_1_, bf16[256,3072]{1,0:T(8,128)(2,1)} %get-tuple-element.12.refs_2_, bf16[256,3072]{1,0:T(8,128)(2,1)} %get-tuple-element.13.refs_3_, bf16[2,1536,256]{2,1,0:T(8,128)(2,1)} %copy-done, ...), custom_call_target="tpu_custom_call" | custom-call | tf_op jit(solution)/shard_map/pallas_call | solution.py:300
  91.8 2.1 %collective-permute-done.15.refs_3_ = bf16[256,1536]{1,0:T(8,128)(2,1)S(1)} collective-permute-done((bf16[256,1536]{1,0:T(8,128)(2,1)}, bf16[256,1536]{1,0:T(8,128)(2,1)S(1)}, u32[]{:S(2)}, u32[]{:S(2)}) %collective-permute-start.15) | collective-permute-done | bytes 786464 | tf_op jit(solution)/shard_map/ppermute | solution.py:211
  94.0 1.1 copy-done.3
  95.1 0.9 shard_map.98
  96.0 2.8 %collective-permute-start.16 = (bf16[4,12,96,128]{3,2,1,0:T(8,128)(2,1)S(1)}, bf16[4,12,96,128]{3,2,1,0:T(8,128)(2,1)S(1)}, u32[]{:S(2)}, u32[]{:S(2)}) collective-permute-start(bf16[4,12,96,128]{3,2,1,0:T(8,128)(2,1)S(1)} %shard_map.98), channel_id=1, source_target_pairs={{0,32},{8,136},{16,48},{24,152},{32,0},{40,168},{48,16},{56,184},{... | collective-permute-start | bytes 3538952 | tf_op jit(solution)/shard_map/ppermute | solution.py:225
  98.8 0.9 shard_map.99
  100.1 0.9 shard_map.100
  101.0 2.4 %collective-permute-start.18 = (bf16[4,12,96,128]{3,2,1,0:T(8,128)(2,1)S(1)}, bf16[4,12,96,128]{3,2,1,0:T(8,128)(2,1)S(1)}, u32[]{:S(2)}, u32[]{:S(2)}) collective-permute-start(bf16[4,12,96,128]{3,2,1,0:T(8,128)(2,1)S(1)} %shard_map.100), channel_id=1, source_target_pairs={{0,48},{8,200},{16,0},{24,216},{32,16},{40,232},{48,32},{56,248},{... | collective-permute-start | bytes 3538952 | tf_op jit(solution)/shard_map/ppermute | solution.py:225
  103.4 0.9 shard_map.97
  104.3 8.9 %collective-permute-done.16 = bf16[4,12,96,128]{3,2,1,0:T(8,128)(2,1)S(1)} collective-permute-done((bf16[4,12,96,128]{3,2,1,0:T(8,128)(2,1)S(1)}, bf16[4,12,96,128]{3,2,1,0:T(8,128)(2,1)S(1)}, u32[]{:S(2)}, u32[]{:S(2)}) %collective-permute-start.16) | collective-permute-done | bytes 1179680 | tf_op jit(solution)/shard_map/ppermute | solution.py:225
  113.2 12.7 %collective-permute-done.17 = bf16[4,12,96,128]{3,2,1,0:T(8,128)(2,1)S(1)} collective-permute-done((bf16[4,12,96,128]{3,2,1,0:T(8,128)(2,1)S(1)}, bf16[4,12,96,128]{3,2,1,0:T(8,128)(2,1)S(1)}, u32[]{:S(2)}, u32[]{:S(2)}) %collective-permute-start.17) | collective-permute-done | bytes 1179680 | tf_op jit(solution)/shard_map/ppermute | solution.py:225
  126.4 0.5 copy-done.10
  127.3 1.2 collective-permute-start.19
  128.6 0.9 collective-permute-start.21
  129.4 0.6 collective-permute-start.20
  130.0 3.6 %reduce-scatter.2.cloned.1.call-done = bf16[1,8,2,32,384]{4,3,2,1,0:T(8,128)(2,1)} async-done(((bf16[8,8,2,32,384]{4,3,2,1,0:T(8,128)(2,1)}), bf16[1,8,2,32,384]{4,3,2,1,0:T(8,128)(2,1)}) %reduce-scatter.2.cloned.1.call-update) | async-done | bytes 393232 | tf_op jit(solution)/shard_map/reduce_scatter | solution.py:320
  133.6 7.4 %all-to-all-start.1 = ((bf16[8,2,32,384]{3,2,1,0:T(8,128)(2,1)}), bf16[8,2,32,384]{3,2,1,0:T(8,128)(2,1)S(1)}, u32[]{:S(2)}, u32[]{:S(2)}) async-start(bf16[8,2,32,384]{3,2,1,0:T(8,128)(2,1)} %bitcast.44), calls=%async_computation.2 | async-start | bytes 786432 | tf_op jit(solution)/shard_map/all_to_all | solution.py:335
  141.1 1.5 fusion.1
  142.6 0.8 slice.98
  143.4 0.7 slice_bitcast_fusion
  144.1 5.0 %all-to-all-done.1.refs_0_ = bf16[8,2,32,384]{3,2,1,0:T(8,128)(2,1)S(1)} async-done(((bf16[8,2,32,384]{3,2,1,0:T(8,128)(2,1)}), bf16[8,2,32,384]{3,2,1,0:T(8,128)(2,1)S(1)}, u32[]{:S(2)}, u32[]{:S(2)}) %all-to-all-start.1) | async-done | bytes 393248 | tf_op jit(solution)/shard_map/all_to_all | solution.py:335
  149.1 2.5 %shard_map.96 = (bf16[2,128,384]{2,1,0:T(8,128)(2,1)}, bf16[2,3,128,384]{3,2,1,0:T(8,128)(2,1)}) custom-call(s32[1,16]{1,0:T(1,128)S(1)} %copy-done.7, s32[1,8]{1,0:T(1,128)S(1)} %copy-done.8, bf16[2,3,128,384]{3,2,1,0:T(8,128)(2,1)S(1)} %bitcast.34, bf16[2,128,384]{2,1,0:T(8,128)(2,1)S(1)} %bitcast.36, bf16[8,2,32,384]{3,2,1,0:T(8,128)(2,1)S(1)} %all-to-all-done.1.refs_0_), custom_call_target="tpu_custom_call" | custom-call | tf_op jit(solution)/shard_map/pallas_call | solution.py:336
  (79 shorter events, 2.5 us)
Async XLA Ops:
  7.2 69.1 %all-gather.2.cloned.1.call-start = ((), (), s32[]{:S(2)}) async-start(), calls=%async_computation.3 | async-start | bytes 9732096 | tf_op jit(solution)/shard_map/all_gather | solution.py:259
  8.9 124.7 %reduce-scatter.2.cloned.1.call-start = ((), (), s32[]{:S(2)}) async-start(), calls=%async_computation.4 | async-start | bytes 3538944 | tf_op jit(solution)/shard_map/reduce_scatter | solution.py:320
  27.6 32.7 %copy-start.12 = (bf16[8,1,2,16,384]{4,3,2,1,0:T(8,128)(2,1)}, bf16[8,1,2,16,384]{4,3,2,1,0:T(8,128)(2,1)S(1)}, u32[]{:S(2)}) copy-start(bf16[8,1,2,16,384]{4,3,2,1,0:T(8,128)(2,1)S(1)} %get-tuple-element.23) | copy-start | bytes 589828
  27.6 32.7 %copy-start.13 = (bf16[8,1,2,16,384]{4,3,2,1,0:T(8,128)(2,1)}, bf16[8,1,2,16,384]{4,3,2,1,0:T(8,128)(2,1)S(1)}, u32[]{:S(2)}) copy-start(bf16[8,1,2,16,384]{4,3,2,1,0:T(8,128)(2,1)S(1)} %get-tuple-element.24) | copy-start | bytes 589828
  27.7 9.3 %collective-permute-start.3 = (bf16[256,384]{1,0:T(8,128)(2,1)S(1)}, bf16[256,384]{1,0:T(8,128)(2,1)S(1)}, u32[]{:S(2)}, u32[]{:S(2)}) collective-permute-start(bf16[256,384]{1,0:T(8,128)(2,1)S(1)} %bitcast.40), channel_id=1, source_target_pairs={{0,1},{1,2},{2,3},{3,4},{4,5},{5,6},{6,7},{7,0},{8,9},{9,10},{10,1... | collective-permute-start | bytes 589832 | tf_op jit(solution)/shard_map/ppermute | solution.py:207
  28.6 43.6 %copy-start.7 = (s32[1,16]{1,0:T(1,128)S(1)}, s32[1,16]{1,0:T(1,128)}, u32[]{:S(2)}) copy-start(s32[1,16]{1,0:T(1,128)} %row_ref.3) | copy-start | bytes 196
  28.6 8.4 %collective-permute-start.7 = (bf16[256,384]{1,0:T(8,128)(2,1)S(1)}, bf16[256,384]{1,0:T(8,128)(2,1)S(1)}, u32[]{:S(2)}, u32[]{:S(2)}) collective-permute-start(bf16[256,384]{1,0:T(8,128)(2,1)S(1)} %bitcast.37), channel_id=1, source_target_pairs={{0,7},{1,0},{2,1},{3,2},{4,3},{5,4},{6,5},{7,6},{8,15},{9,8},{10,9... | collective-permute-start | bytes 589832 | tf_op jit(solution)/shard_map/ppermute | solution.py:207
  32.6 7.6 %collective-permute-start = (bf16[256,384]{1,0:T(8,128)(2,1)S(1)}, bf16[256,384]{1,0:T(8,128)(2,1)S(1)}, u32[]{:S(2)}, u32[]{:S(2)}) collective-permute-start(bf16[256,384]{1,0:T(8,128)(2,1)S(1)} %bitcast.41), channel_id=1, source_target_pairs={{0,7},{1,0},{2,1},{3,2},{4,3},{5,4},{6,5},{7,6},{8,15},{9,8},{10,9... | collective-permute-start | bytes 589832 | tf_op jit(solution)/shard_map/ppermute | solution.py:207
  34.0 9.7 %collective-permute-start.11 = (bf16[256,384]{1,0:T(8,128)(2,1)S(1)}, bf16[256,384]{1,0:T(8,128)(2,1)S(1)}, u32[]{:S(2)}, u32[]{:S(2)}) collective-permute-start(bf16[256,384]{1,0:T(8,128)(2,1)S(1)} %bitcast.38), channel_id=1, source_target_pairs={{0,1},{1,2},{2,3},{3,4},{4,5},{5,6},{6,7},{7,0},{8,9},{9,10},{10,1... | collective-permute-start | bytes 589832 | tf_op jit(solution)/shard_map/ppermute | solution.py:207
  36.9 23.5 %copy-start.14 = (bf16[256,384]{1,0:T(8,128)(2,1)}, bf16[256,384]{1,0:T(8,128)(2,1)S(1)}, u32[]{:S(2)}) copy-start(bf16[256,384]{1,0:T(8,128)(2,1)S(1)} %collective-permute-done.3.refs_7_) | copy-start | bytes 589828
  36.9 8.1 %collective-permute-start.4 = (bf16[256,384]{1,0:T(8,128)(2,1)S(1)}, bf16[256,384]{1,0:T(8,128)(2,1)S(1)}, u32[]{:S(2)}, u32[]{:S(2)}) collective-permute-start(bf16[256,384]{1,0:T(8,128)(2,1)S(1)} %collective-permute-done.3.refs_7_), channel_id=1, source_target_pairs={{0,1},{1,2},{2,3},{3,4},{4,5},{5,6},{6,7},{7,0},{8,9},{9,10},{10,1... | collective-permute-start | bytes 589832 | tf_op jit(solution)/shard_map/ppermute | solution.py:207
  36.9 23.5 %copy-start.15 = (bf16[256,384]{1,0:T(8,128)(2,1)}, bf16[256,384]{1,0:T(8,128)(2,1)S(1)}, u32[]{:S(2)}) copy-start(bf16[256,384]{1,0:T(8,128)(2,1)S(1)} %collective-permute-done.7.refs_9_) | copy-start | bytes 589828
  37.0 8.1 %collective-permute-start.8 = (bf16[256,384]{1,0:T(8,128)(2,1)S(1)}, bf16[256,384]{1,0:T(8,128)(2,1)S(1)}, u32[]{:S(2)}, u32[]{:S(2)}) collective-permute-start(bf16[256,384]{1,0:T(8,128)(2,1)S(1)} %collective-permute-done.7.refs_9_), channel_id=1, source_target_pairs={{0,7},{1,0},{2,1},{3,2},{4,3},{5,4},{6,5},{7,6},{8,15},{9,8},{10,9... | collective-permute-start | bytes 589832 | tf_op jit(solution)/shard_map/ppermute | solution.py:207
  40.2 20.2 %copy-start.16 = (bf16[256,384]{1,0:T(8,128)(2,1)}, bf16[256,384]{1,0:T(8,128)(2,1)S(1)}, u32[]{:S(2)}) copy-start(bf16[256,384]{1,0:T(8,128)(2,1)S(1)} %collective-permute-done.refs_1_) | copy-start | bytes 589828
  40.2 7.7 %collective-permute-start.1 = (bf16[256,384]{1,0:T(8,128)(2,1)S(1)}, bf16[256,384]{1,0:T(8,128)(2,1)S(1)}, u32[]{:S(2)}, u32[]{:S(2)}) collective-permute-start(bf16[256,384]{1,0:T(8,128)(2,1)S(1)} %collective-permute-done.refs_1_), channel_id=1, source_target_pairs={{0,7},{1,0},{2,1},{3,2},{4,3},{5,4},{6,5},{7,6},{8,15},{9,8},{10,9... | collective-permute-start | bytes 589832 | tf_op jit(solution)/shard_map/ppermute | solution.py:207
  43.7 16.7 %copy-start.17 = (bf16[256,384]{1,0:T(8,128)(2,1)}, bf16[256,384]{1,0:T(8,128)(2,1)S(1)}, u32[]{:S(2)}) copy-start(bf16[256,384]{1,0:T(8,128)(2,1)S(1)} %collective-permute-done.11.refs_15_) | copy-start | bytes 589828
  43.7 7.7 %collective-permute-start.12 = (bf16[256,384]{1,0:T(8,128)(2,1)S(1)}, bf16[256,384]{1,0:T(8,128)(2,1)S(1)}, u32[]{:S(2)}, u32[]{:S(2)}) collective-permute-start(bf16[256,384]{1,0:T(8,128)(2,1)S(1)} %collective-permute-done.11.refs_15_), channel_id=1, source_target_pairs={{0,1},{1,2},{2,3},{3,4},{4,5},{5,6},{6,7},{7,0},{8,9},{9,10},{10,1... | collective-permute-start | bytes 589832 | tf_op jit(solution)/shard_map/ppermute | solution.py:207
  45.0 15.4 %copy-start.18 = (bf16[256,384]{1,0:T(8,128)(2,1)}, bf16[256,384]{1,0:T(8,128)(2,1)S(1)}, u32[]{:S(2)}) copy-start(bf16[256,384]{1,0:T(8,128)(2,1)S(1)} %collective-permute-done.4.refs_6_) | copy-start | bytes 589828
  45.0 7.2 %collective-permute-start.5 = (bf16[256,384]{1,0:T(8,128)(2,1)S(1)}, bf16[256,384]{1,0:T(8,128)(2,1)S(1)}, u32[]{:S(2)}, u32[]{:S(2)}) collective-permute-start(bf16[256,384]{1,0:T(8,128)(2,1)S(1)} %collective-permute-done.4.refs_6_), channel_id=1, source_target_pairs={{0,1},{1,2},{2,3},{3,4},{4,5},{5,6},{6,7},{7,0},{8,9},{9,10},{10,1... | collective-permute-start | bytes 589832 | tf_op jit(solution)/shard_map/ppermute | solution.py:207
  45.0 15.4 %copy-start.19 = (bf16[256,384]{1,0:T(8,128)(2,1)}, bf16[256,384]{1,0:T(8,128)(2,1)S(1)}, u32[]{:S(2)}) copy-start(bf16[256,384]{1,0:T(8,128)(2,1)S(1)} %collective-permute-done.8.refs_10_) | copy-start | bytes 589828
  45.0 7.2 %collective-permute-start.9 = (bf16[256,384]{1,0:T(8,128)(2,1)S(1)}, bf16[256,384]{1,0:T(8,128)(2,1)S(1)}, u32[]{:S(2)}, u32[]{:S(2)}) collective-permute-start(bf16[256,384]{1,0:T(8,128)(2,1)S(1)} %collective-permute-done.8.refs_10_), channel_id=1, source_target_pairs={{0,7},{1,0},{2,1},{3,2},{4,3},{5,4},{6,5},{7,6},{8,15},{9,8},{10,9... | collective-permute-start | bytes 589832 | tf_op jit(solution)/shard_map/ppermute | solution.py:207
  47.9 12.6 %copy-start.20 = (bf16[256,384]{1,0:T(8,128)(2,1)}, bf16[256,384]{1,0:T(8,128)(2,1)S(1)}, u32[]{:S(2)}) copy-start(bf16[256,384]{1,0:T(8,128)(2,1)S(1)} %collective-permute-done.1.refs_2_) | copy-start | bytes 589828
  47.9 8.3 %collective-permute-start.2 = (bf16[256,384]{1,0:T(8,128)(2,1)S(1)}, bf16[256,384]{1,0:T(8,128)(2,1)S(1)}, u32[]{:S(2)}, u32[]{:S(2)}) collective-permute-start(bf16[256,384]{1,0:T(8,128)(2,1)S(1)} %collective-permute-done.1.refs_2_), channel_id=1, source_target_pairs={{0,7},{1,0},{2,1},{3,2},{4,3},{5,4},{6,5},{7,6},{8,15},{9,8},{10,9... | collective-permute-start | bytes 589832 | tf_op jit(solution)/shard_map/ppermute | solution.py:207
  51.4 9.1 %copy-start.21 = (bf16[256,384]{1,0:T(8,128)(2,1)}, bf16[256,384]{1,0:T(8,128)(2,1)S(1)}, u32[]{:S(2)}) copy-start(bf16[256,384]{1,0:T(8,128)(2,1)S(1)} %collective-permute-done.12.refs_14_) | copy-start | bytes 589828
  51.4 6.9 %collective-permute-start.13 = (bf16[256,384]{1,0:T(8,128)(2,1)S(1)}, bf16[256,384]{1,0:T(8,128)(2,1)S(1)}, u32[]{:S(2)}, u32[]{:S(2)}) collective-permute-start(bf16[256,384]{1,0:T(8,128)(2,1)S(1)} %collective-permute-done.12.refs_14_), channel_id=1, source_target_pairs={{0,1},{1,2},{2,3},{3,4},{4,5},{5,6},{6,7},{7,0},{8,9},{9,10},{10,1... | collective-permute-start | bytes 589832 | tf_op jit(solution)/shard_map/ppermute | solution.py:207
  52.2 8.3 %copy-start.22 = (bf16[256,384]{1,0:T(8,128)(2,1)}, bf16[256,384]{1,0:T(8,128)(2,1)S(1)}, u32[]{:S(2)}) copy-start(bf16[256,384]{1,0:T(8,128)(2,1)S(1)} %collective-permute-done.5.refs_5_) | copy-start | bytes 589828
  52.2 8.2 %collective-permute-start.6 = (bf16[256,384]{1,0:T(8,128)(2,1)S(1)}, bf16[256,384]{1,0:T(8,128)(2,1)S(1)}, u32[]{:S(2)}, u32[]{:S(2)}) collective-permute-start(bf16[256,384]{1,0:T(8,128)(2,1)S(1)} %collective-permute-done.5.refs_5_), channel_id=1, source_target_pairs={{0,1},{1,2},{2,3},{3,4},{4,5},{5,6},{6,7},{7,0},{8,9},{9,10},{10,1... | collective-permute-start | bytes 589832 | tf_op jit(solution)/shard_map/ppermute | solution.py:207
  52.2 8.3 %copy-start.23 = (bf16[256,384]{1,0:T(8,128)(2,1)}, bf16[256,384]{1,0:T(8,128)(2,1)S(1)}, u32[]{:S(2)}) copy-start(bf16[256,384]{1,0:T(8,128)(2,1)S(1)} %collective-permute-done.9.refs_11_) | copy-start | bytes 589828
  52.2 8.1 %collective-permute-start.10 = (bf16[256,384]{1,0:T(8,128)(2,1)S(1)}, bf16[256,384]{1,0:T(8,128)(2,1)S(1)}, u32[]{:S(2)}, u32[]{:S(2)}) collective-permute-start(bf16[256,384]{1,0:T(8,128)(2,1)S(1)} %collective-permute-done.9.refs_11_), channel_id=1, source_target_pairs={{0,7},{1,0},{2,1},{3,2},{4,3},{5,4},{6,5},{7,6},{8,15},{9,8},{10,9... | collective-permute-start | bytes 589832 | tf_op jit(solution)/shard_map/ppermute | solution.py:207
  56.2 4.3 %copy-start.24 = (bf16[256,384]{1,0:T(8,128)(2,1)}, bf16[256,384]{1,0:T(8,128)(2,1)S(1)}, u32[]{:S(2)}) copy-start(bf16[256,384]{1,0:T(8,128)(2,1)S(1)} %collective-permute-done.2.refs_3_) | copy-start | bytes 589828
  58.3 2.2 %copy-start.25 = (bf16[256,384]{1,0:T(8,128)(2,1)}, bf16[256,384]{1,0:T(8,128)(2,1)S(1)}, u32[]{:S(2)}) copy-start(bf16[256,384]{1,0:T(8,128)(2,1)S(1)} %collective-permute-done.13.refs_13_) | copy-start | bytes 589828
  67.5 8.6 %collective-permute-start.14 = (bf16[2,1536,256]{2,1,0:T(8,128)(2,1)}, bf16[2,1536,256]{2,1,0:T(8,128)(2,1)S(1)}, u32[]{:S(2)}, u32[]{:S(2)}) collective-permute-start(bf16[2,1536,256]{2,1,0:T(8,128)(2,1)} %get-tuple-element.14), channel_id=1, source_target_pairs={{0,8},{8,0},{16,24},{24,16},{32,40},{40,32},{48,56},{56,48},{1,9},... | collective-permute-start | bytes 4718600 | tf_op jit(solution)/shard_map/ppermute | solution.py:211
  91.3 2.6 %copy-start.1 = (bf16[2,1536,256]{2,1,0:T(8,128)(2,1)S(1)}, bf16[2,1536,256]{2,1,0:T(8,128)(2,1)}, u32[]{:S(2)}) copy-start(bf16[2,1536,256]{2,1,0:T(8,128)(2,1)} %copy-done) | copy-start | bytes 4718596
  91.3 2.6 %copy-start.2 = (bf16[2,1536,256]{2,1,0:T(8,128)(2,1)S(1)}, bf16[2,1536,256]{2,1,0:T(8,128)(2,1)}, u32[]{:S(2)}) copy-start(bf16[2,1536,256]{2,1,0:T(8,128)(2,1)} %get-tuple-element.18.refs_0_) | copy-start | bytes 4718596
  91.4 2.6 %collective-permute-start.15 = (bf16[256,1536]{1,0:T(8,128)(2,1)}, bf16[256,1536]{1,0:T(8,128)(2,1)S(1)}, u32[]{:S(2)}, u32[]{:S(2)}) collective-permute-start(bf16[256,1536]{1,0:T(8,128)(2,1)} %get-tuple-element.19.refs_2_), channel_id=1, source_target_pairs={{0,8},{8,0},{16,24},{24,16},{32,40},{40,32},{48,56},{56,48},{1,9},... | collective-permute-start | bytes 2359304 | tf_op jit(solution)/shard_map/ppermute | solution.py:211
  96.0 17.2 %collective-permute-start.16 = (bf16[4,12,96,128]{3,2,1,0:T(8,128)(2,1)S(1)}, bf16[4,12,96,128]{3,2,1,0:T(8,128)(2,1)S(1)}, u32[]{:S(2)}, u32[]{:S(2)}) collective-permute-start(bf16[4,12,96,128]{3,2,1,0:T(8,128)(2,1)S(1)} %shard_map.98), channel_id=1, source_target_pairs={{0,32},{8,136},{16,48},{24,152},{32,0},{40,168},{48,16},{56,184},{... | collective-permute-start | bytes 3538952 | tf_op jit(solution)/shard_map/ppermute | solution.py:225
  99.7 26.2 %collective-permute-start.17 = (bf16[4,12,96,128]{3,2,1,0:T(8,128)(2,1)S(1)}, bf16[4,12,96,128]{3,2,1,0:T(8,128)(2,1)S(1)}, u32[]{:S(2)}, u32[]{:S(2)}) collective-permute-start(bf16[4,12,96,128]{3,2,1,0:T(8,128)(2,1)S(1)} %shard_map.99), channel_id=1, source_target_pairs={{0,16},{8,72},{16,32},{24,88},{32,48},{40,104},{48,0},{56,120},{64... | collective-permute-start | bytes 3538952 | tf_op jit(solution)/shard_map/ppermute | solution.py:225
  101.0 24.9 %collective-permute-start.18 = (bf16[4,12,96,128]{3,2,1,0:T(8,128)(2,1)S(1)}, bf16[4,12,96,128]{3,2,1,0:T(8,128)(2,1)S(1)}, u32[]{:S(2)}, u32[]{:S(2)}) collective-permute-start(bf16[4,12,96,128]{3,2,1,0:T(8,128)(2,1)S(1)} %shard_map.100), channel_id=1, source_target_pairs={{0,48},{8,200},{16,0},{24,216},{32,16},{40,232},{48,32},{56,248},{... | collective-permute-start | bytes 3538952 | tf_op jit(solution)/shard_map/ppermute | solution.py:225
  104.3 22.1 %copy-start.4 = (bf16[4,12,96,128]{3,2,1,0:T(8,128)(2,1)}, bf16[4,12,96,128]{3,2,1,0:T(8,128)(2,1)S(1)}, u32[]{:S(2)}) copy-start(bf16[4,12,96,128]{3,2,1,0:T(8,128)(2,1)S(1)} %shard_map.97) | copy-start | bytes 3538948
  113.2 13.2 %copy-start.9 = (bf16[4,12,96,128]{3,2,1,0:T(8,128)(2,1)}, bf16[4,12,96,128]{3,2,1,0:T(8,128)(2,1)S(1)}, u32[]{:S(2)}) copy-start(bf16[4,12,96,128]{3,2,1,0:T(8,128)(2,1)S(1)} %collective-permute-done.16) | copy-start | bytes 3538948
  125.9 1.4 copy-start.11
  127.3 13.7 %collective-permute-start.19 = (bf16[12,96,128]{2,1,0:T(8,128)(2,1)S(1)}, bf16[12,96,128]{2,1,0:T(8,128)(2,1)S(1)}, u32[]{:S(2)}, u32[]{:S(2)}) collective-permute-start(bf16[12,96,128]{2,1,0:T(8,128)(2,1)S(1)} %get-tuple-element.20), channel_id=1, source_target_pairs={{0,128},{8,40},{16,144},{24,56},{32,160},{40,8},{48,176},{56,24},{... | collective-permute-start | bytes 884744 | tf_op jit(solution)/shard_map/ppermute | solution.py:225
  128.6 12.5 %collective-permute-start.21 = (bf16[12,96,128]{2,1,0:T(8,128)(2,1)S(1)}, bf16[12,96,128]{2,1,0:T(8,128)(2,1)S(1)}, u32[]{:S(2)}, u32[]{:S(2)}) collective-permute-start(bf16[12,96,128]{2,1,0:T(8,128)(2,1)S(1)} %get-tuple-element.21), channel_id=1, source_target_pairs={{0,192},{8,56},{16,208},{24,8},{32,224},{40,24},{48,240},{56,40},{... | collective-permute-start | bytes 884744 | tf_op jit(solution)/shard_map/ppermute | solution.py:225
  129.4 11.6 %collective-permute-start.20 = (bf16[12,96,128]{2,1,0:T(8,128)(2,1)S(1)}, bf16[12,96,128]{2,1,0:T(8,128)(2,1)S(1)}, u32[]{:S(2)}, u32[]{:S(2)}) collective-permute-start(bf16[12,96,128]{2,1,0:T(8,128)(2,1)S(1)} %get-tuple-element.22), channel_id=1, source_target_pairs={{0,64},{8,24},{16,80},{24,40},{32,96},{40,56},{48,112},{56,8},{64,... | collective-permute-start | bytes 884744 | tf_op jit(solution)/shard_map/ppermute | solution.py:225
  133.6 15.5 %all-to-all-start.1 = ((bf16[8,2,32,384]{3,2,1,0:T(8,128)(2,1)}), bf16[8,2,32,384]{3,2,1,0:T(8,128)(2,1)S(1)}, u32[]{:S(2)}, u32[]{:S(2)}) async-start(bf16[8,2,32,384]{3,2,1,0:T(8,128)(2,1)} %bitcast.44), calls=%async_computation.2 | async-start | bytes 786432 | tf_op jit(solution)/shard_map/all_to_all | solution.py:335
  142.6 6.5 %copy-start.5 = (bf16[1,2,128,3,384]{4,2,3,1,0:T(8,128)(2,1)S(1)}, bf16[1,2,128,3,384]{4,2,3,1,0:T(8,128)(2,1)}, u32[]{:S(2)}) copy-start(bf16[1,2,128,3,384]{4,2,3,1,0:T(8,128)(2,1)} %param.6) | copy-start | bytes 1769476
  142.6 6.5 %copy-start.6 = (bf16[1,2,128,384]{3,2,1,0:T(8,128)(2,1)S(1)}, bf16[1,2,128,384]{3,2,1,0:T(8,128)(2,1)}, u32[]{:S(2)}) copy-start(bf16[1,2,128,384]{3,2,1,0:T(8,128)(2,1)} %param.9) | copy-start | bytes 589828
  142.6 6.5 %copy-start.8 = (s32[1,8]{1,0:T(1,128)S(1)}, s32[1,8]{1,0:T(1,128)}, u32[]{:S(2)}) copy-start(s32[1,8]{1,0:T(1,128)} %patch_ref.3) | copy-start | bytes 100
  (5 other events, 4.7 us)
Sparse Core Ops, SparseCore 0:
  11.2 65.1 all-gather.1
  91.5 42.0 reduce-scatter.1

commit v5 on v4

--- a/solution.py
+++ b/solution.py
@@ -25,12 +25,15 @@
     return expo / jnp.sum(expo, axis=-1, keepdims=True)
 
 
-def attention_grads(query, keys, values, probs, cotangent):
-    d_values = dot(probs.astype(BF), cotangent, TN).astype(BF)
-    d_probs = dot(cotangent, values, NT).astype(BF).astype(F32)
-    inner = jnp.sum(probs * d_probs, axis=-1, keepdims=True)
-    d_scores = (probs * (d_probs - inner) * SCALE).astype(BF)
-    return dot(d_scores, keys).astype(BF), dot(d_scores, query, TN).astype(BF), d_values
+def attention_grads(queries, keys, values, probs, cotangents):
+    each = range(len(probs))
+    d_values = [dot(probs[i].astype(BF), cotangents[i], TN).astype(BF) for i in each]
+    d_probs = [dot(cotangents[i], values[i], NT).astype(BF).astype(F32) for i in each]
+    inner = [jnp.sum(probs[i] * d_probs[i], axis=-1, keepdims=True) for i in each]
+    d_scores = [(probs[i] * (d_probs[i] - inner[i]) * SCALE).astype(BF) for i in each]
+    d_queries = [dot(d_scores[i], keys[i]).astype(BF) for i in each]
+    d_keys = [dot(d_scores[i], queries[i], TN).astype(BF) for i in each]
+    return list(zip(d_queries, d_keys, d_values))
 
 
 def live_rows(row_ref, patch_ref, frame):
@@ -69,22 +72,24 @@
         for f in range(frames):
             part = sums_ref[s, :, f * block : (f + 1) * block, :]
             whole_ref[:, f, s * block : (s + 1) * block, :] = part
+    live, d_mixed = [], []
     for f in range(frames):
         count = live_rows(row_ref, patch_ref, place * frames + f)
         keys_live = lax.broadcasted_iota(jnp.int32, (patches, patches), 1) < count
-        rows_live = lax.broadcasted_iota(jnp.int32, (patches, 1), 0) < count
+        live.append((keys_live, lax.broadcasted_iota(jnp.int32, (patches, 1), 0) < count))
         d_spatial = cot_ref[f].astype(F32) + whole_ref[1, f].astype(F32)
-        d_mixed = jnp.where(rows_live, d_spatial, 0.0).astype(BF)
-        for h in range(width // HD):
-            cols = slice(h * HD, (h + 1) * HD)
-            query, keys, values = (qkv_ref[f, i, :, cols] for i in range(3))
-            probs = softmax(query, keys, keys_live)
-            mixed = dot(probs.astype(BF), values).astype(BF).astype(F32)
-            total = mixed + whole_ref[0, f, :, cols].astype(F32)
-            out_ref[f, :, cols] = jnp.where(rows_live, total, 0.0).astype(BF)
-            grads = attention_grads(query, keys, values, probs, d_mixed[:, cols])
-            for i in range(3):
-                grad_ref[f, i, :, cols] = grads[i]
+        d_mixed.append(jnp.where(live[f][1], d_spatial, 0.0).astype(BF))
+    each = [(f, slice(h * HD, (h + 1) * HD)) for f in range(frames) for h in range(width // HD)]
+    queries, keys, values = ([qkv_ref[f, i, :, cols] for f, cols in each] for i in range(3))
+    cotangents = [d_mixed[f][:, cols] for f, cols in each]
+    probs = [softmax(queries[i], keys[i], live[f][0]) for i, (f, _) in enumerate(each)]
+    grads = attention_grads(queries, keys, values, probs, cotangents)
+    for i, (f, cols) in enumerate(each):
+        mixed = dot(probs[i].astype(BF), values[i]).astype(BF).astype(F32)
+        total = mixed + whole_ref[0, f, :, cols].astype(F32)
+        out_ref[f, :, cols] = jnp.where(live[f][1], total, 0.0).astype(BF)
+        for k in range(3):
+            grad_ref[f, k, :, cols] = grads[i][k]
 
 
 def own_chip():
@@ -121,7 +126,18 @@
             other_ref[a, to] = flip_ref[pl.ds(pl.multiple_of((2 * i + 1 - core) * rows, 16), rows), :]
 
 
-def temporal_kernel(heads, row_key_ref, col_key_ref, feat_hbm, gated_hbm, _, w_hbm, *refs):
+def row_keys(clip_ref, rows, axis):
+    frames = clip_ref.shape[1]
+    block = rows // frames
+    index = lax.broadcasted_iota(jnp.int32, (rows, 1) if axis == 0 else (1, rows), axis)
+    keys = index
+    for f in range(frames):
+        inside = (index >= f * block) & (index < (f + 1) * block)
+        keys = jnp.where(inside, index + (clip_ref[0, f] - f) * block, keys)
+    return keys
+
+
+def temporal_kernel(heads, clip_ref, feat_hbm, gated_hbm, w_hbm, *refs):
     sums_hbm, both_ref, feat_ref, gated_ref, w_ref, sums_ref, in_sem, w_sem, out_sem = refs
     width = heads * HD
     slots = 4 * heads
@@ -135,7 +151,7 @@
     feat_load.start()
     for copy in loads[:6]:
         copy.start()
-    mask = row_key_ref[...] == col_key_ref[...]
+    mask = row_keys(clip_ref, owners * rows, 0) == row_keys(clip_ref, owners * rows, 1)
     feat_load.wait()
     query, keys, values = [], [], []
     for h in range(heads):
@@ -155,11 +171,11 @@
     for copy in loads[9:]:
         copy.wait()
     cotangent = dot(gated_ref[...], w_ref[:, 3 * width :]).astype(BF)
+    cotangents = [cotangent[:, h * HD : (h + 1) * HD] for h in each]
+    grads = attention_grads(query, keys, values, probs, cotangents)
     for h in each:
-        cols = slice(h * HD, (h + 1) * HD)
-        grads = attention_grads(query[h], keys[h], values[h], probs[h], cotangent[:, cols])
         for i in range(3):
-            both_ref[:, (3 * h + i) * HD : (3 * h + i + 1) * HD] = grads[i]
+            both_ref[:, (3 * h + i) * HD : (3 * h + i + 1) * HD] = grads[h][i]
         both_ref[:, 3 * width + h * HD : 3 * width + (h + 1) * HD] = mixed[h]
     stores = []
     pair = 4
@@ -258,9 +274,6 @@
     )
     w_all = lax.all_gather(w_own, ("clip", "frame"), axis=1, tiled=True)
 
-    clips = frame_clip[0][:, None] * block
-    keys = (clips + jnp.arange(block, dtype=jnp.int32)[None, :]).reshape(rows_t)
-
     qkv = spatial_qkv[0].transpose(0, 2, 1, 3)
     cot = out_grad[0]
     smem = pl.BlockSpec(memory_space=pltpu.SMEM)
@@ -294,6 +307,7 @@
         compiler_params=pltpu.CompilerParams(vmem_limit_bytes=58 * 2**20),
     )(*blocks)
     pair_flip = pair_swap(other_flip)
+    feats, pair_flip = lax.optimization_barrier([feats, pair_flip])
 
     wide_scratch = pltpu.VMEM((rows_t, model), BF)
     sums_shape = (width_ranks, ranks, 2, frames * block, width)
@@ -303,7 +317,7 @@
             jax.ShapeDtypeStruct(sums_shape, BF),
             jax.ShapeDtypeStruct((rows_t, 4 * width), BF),
         ],
-        in_specs=[vmem] * 2 + [hbm] * 4,
+        in_specs=[smem] + [hbm] * 3,
         out_specs=[hbm, vmem],
         scratch_shapes=[
             wide_scratch,
@@ -315,7 +329,7 @@
             pltpu.SemaphoreType.DMA((width_ranks,)),
         ],
         compiler_params=pltpu.CompilerParams(vmem_limit_bytes=56 * 2**20),
-    )(keys[:, None], keys[None, :], feats, gated, pair_flip, w_all)
+    )(frame_clip, feats, gated, w_all)
 
     own_sums = lax.psum_scatter(sums, "tensor", scatter_dimension=0, tiled=True)[0]
     pair_both = pair_swap(both)

time: 159 us -> 158 us (level)
  local copies, waits for them, and re-layouts: 7.25 us -> 4.94 us
    ppermute x2, waiting for transfers between devices: 4.61 us -> 6.22 us  [pair_swap(): return lax.ppermute(value, 'frame', [(i, i ^ 1) for i in range(8)])]
    unnamed x56 -> x52, local copies, waits for them, and re-layouts: 4.35 us -> 3.44 us
  transfers between devices with their start and end apart: 25 -> 25, of which waited for: 15 -> 14; matrix products, arithmetic and copies ran while one was open for 3% -> 2% of each run, Pallas kernels for 8% -> 8%
where the time goes in v5:
time: 158 us
  waiting for transfers between devices  47 us (30%)
  starting transfers between devices  43.9 us (28%)
  Pallas kernels  29.1 us (18%)
  blocking collectives  14.7 us (9%)
  between operations  14.4 us (9%)
  local copies, waits for them, and re-layouts  4.94 us (3%)
  other arithmetic  3.66 us (2%)
    ppermute x14, starting transfers between devices, shift(): lax.ppermute(value, axis, [(i, (i + step) % size) for i in range(size)])  21.8 us
    ppermute x6, waiting for transfers between devices, spread(): return lax.ppermute(value, ('clip', 'frame'), pairs)  21.2 us
    all_to_all x1, blocking collectives, body(): lax.all_to_all(sent, 'frame', split_axis=0, concat_axis=0, tiled=True)  14.7 us
    pallas_call x1, Pallas kernels, body(): pl.pallas_call(lambda *refs: temporal_kernel(heads, *refs), out_shape=[ja...  13.5 us
    ppermute x14, waiting for transfers between devices, shift(): lax.ppermute(value, axis, [(i, (i + step) % size) for i in range(size)])  10.9 us
    ppermute x6, starting transfers between devices, spread(): return lax.ppermute(value, ('clip', 'frame'), pairs)  9.52 us
    all_to_all x1, starting transfers between devices, body(): lax.all_to_all(own_sums, 'frame', split_axis=0, concat_axis=0, tiled=True)  7.39 us
    ppermute x2, waiting for transfers between devices, pair_swap(): return lax.ppermute(value, 'frame', [(i, i ^ 1) for i in range(8)])  6.22 us
  transfers between devices with their start and end apart: 25, of which 14 were waited for; matrix products, arithmetic and copies ran while one was open for 2% of the time, Pallas kernels for 8%

profile of v5, /device:TPU:1, one launch (start us, length us, event | category | flops | bytes accessed | tf_op | source)
XLA Modules:
  0.0 157.6 jit_solution(10374710118570018092)
XLA Ops:
  7.2 1.7 %pad_maximum_fusion = bf16[12,96,128]{2,1,0:T(8,128)(2,1)} fusion(bf16[3,96,128]{2,1,0:T(8,128)(2,1)} %bitcast.44, bf16[9,96,128]{2,1,0:T(8,128)(2,1)} %bitcast.43), kind=kLoop, calls=%fused_computation.11 | loop fusion | flops 147456 | bytes 589824 | tf_op jit(solution)/shard_map/concatenate | solution.py:271
  9.0 3.9 %shard_map.93 = bf16[8,2,2,16,384]{4,3,2,1,0:T(8,128)(2,1)} custom-call(s32[1,16]{1,0:T(1,128)} %row_ref.3, s32[1,8]{1,0:T(1,128)} %patch_ref.3, bf16[2,3,128,384]{3,2,1,0:T(8,128)(2,1)} %bitcast.31, bf16[2,128,384]{2,1,0:T(8,128)(2,1)} %bitcast.33), custom_call_target="tpu_custom_call" | custom-call | tf_op jit(solution)/shard_map/pallas_call | solution.py:282
  12.9 14.7 %all_to_all.10 = bf16[8,2,2,16,384]{4,3,2,1,0:T(8,128)(2,1)S(1)} all-to-all(bf16[8,2,2,16,384]{4,3,2,1,0:T(8,128)(2,1)} %shard_map.93), channel_id=1, replica_groups=mesh['clip'=4,'frame'=8,'tensor'=8] {'frame'}, dimensions={0} | all-to-all | bytes 786432 | tf_op jit(solution)/shard_map/all_to_all | solution.py:290
  27.7 0.9 collective-permute-start.3
  28.6 4.0 %collective-permute-start.7 = (bf16[256,384]{1,0:T(8,128)(2,1)S(1)}, bf16[256,384]{1,0:T(8,128)(2,1)S(1)}, u32[]{:S(2)}, u32[]{:S(2)}) collective-permute-start(bf16[256,384]{1,0:T(8,128)(2,1)S(1)} %bitcast.35), channel_id=1, source_target_pairs={{0,7},{1,0},{2,1},{3,2},{4,3},{5,4},{6,5},{7,6},{8,15},{9,8},{10,9... | collective-permute-start | bytes 589832 | tf_op jit(solution)/shard_map/ppermute | solution.py:223
  32.6 1.4 collective-permute-start
  34.1 2.9 %collective-permute-done.3.refs_7_ = bf16[256,384]{1,0:T(8,128)(2,1)S(1)} collective-permute-done((bf16[256,384]{1,0:T(8,128)(2,1)S(1)}, bf16[256,384]{1,0:T(8,128)(2,1)S(1)}, u32[]{:S(2)}, u32[]{:S(2)}) %collective-permute-start.3) | collective-permute-done | bytes 196640 | tf_op jit(solution)/shard_map/ppermute | solution.py:223
  37.0 2.7 %collective-permute-start.8 = (bf16[256,384]{1,0:T(8,128)(2,1)S(1)}, bf16[256,384]{1,0:T(8,128)(2,1)S(1)}, u32[]{:S(2)}, u32[]{:S(2)}) collective-permute-start(bf16[256,384]{1,0:T(8,128)(2,1)S(1)} %collective-permute-done.7.refs_9_), channel_id=1, source_target_pairs={{0,7},{1,0},{2,1},{3,2},{4,3},{5,4},{6,5},{7,6},{8,15},{9,8},{10,9... | collective-permute-start | bytes 589832 | tf_op jit(solution)/shard_map/ppermute | solution.py:223
  39.6 0.6 collective-permute-done.refs_1_
  40.2 3.5 %collective-permute-start.1 = (bf16[256,384]{1,0:T(8,128)(2,1)S(1)}, bf16[256,384]{1,0:T(8,128)(2,1)S(1)}, u32[]{:S(2)}, u32[]{:S(2)}) collective-permute-start(bf16[256,384]{1,0:T(8,128)(2,1)S(1)} %collective-permute-done.refs_1_), channel_id=1, source_target_pairs={{0,7},{1,0},{2,1},{3,2},{4,3},{5,4},{6,5},{7,6},{8,15},{9,8},{10,9... | collective-permute-start | bytes 589832 | tf_op jit(solution)/shard_map/ppermute | solution.py:223
  43.7 1.3 collective-permute-done.4.refs_6_
  45.0 2.7 %collective-permute-start.9 = (bf16[256,384]{1,0:T(8,128)(2,1)S(1)}, bf16[256,384]{1,0:T(8,128)(2,1)S(1)}, u32[]{:S(2)}, u32[]{:S(2)}) collective-permute-start(bf16[256,384]{1,0:T(8,128)(2,1)S(1)} %collective-permute-done.8.refs_10_), channel_id=1, source_target_pairs={{0,7},{1,0},{2,1},{3,2},{4,3},{5,4},{6,5},{7,6},{8,15},{9,8},{10,9... | collective-permute-start | bytes 589832 | tf_op jit(solution)/shard_map/ppermute | solution.py:223
  47.9 3.5 %collective-permute-start.2 = (bf16[256,384]{1,0:T(8,128)(2,1)S(1)}, bf16[256,384]{1,0:T(8,128)(2,1)S(1)}, u32[]{:S(2)}, u32[]{:S(2)}) collective-permute-start(bf16[256,384]{1,0:T(8,128)(2,1)S(1)} %collective-permute-done.1.refs_2_), channel_id=1, source_target_pairs={{0,7},{1,0},{2,1},{3,2},{4,3},{5,4},{6,5},{7,6},{8,15},{9,8},{10,9... | collective-permute-start | bytes 589832 | tf_op jit(solution)/shard_map/ppermute | solution.py:223
  51.4 0.8 collective-permute-done.5.refs_5_
  52.2 3.0 %collective-permute-start.10 = (bf16[256,384]{1,0:T(8,128)(2,1)S(1)}, bf16[256,384]{1,0:T(8,128)(2,1)S(1)}, u32[]{:S(2)}, u32[]{:S(2)}) collective-permute-start(bf16[256,384]{1,0:T(8,128)(2,1)S(1)} %collective-permute-done.9.refs_11_), channel_id=1, source_target_pairs={{0,7},{1,0},{2,1},{3,2},{4,3},{5,4},{6,5},{7,6},{8,15},{9,8},{10,9... | collective-permute-start | bytes 589832 | tf_op jit(solution)/shard_map/ppermute | solution.py:223
  55.2 1.0 collective-permute-done.2.refs_3_
  56.2 2.1 %collective-permute-done.13.refs_13_ = bf16[256,384]{1,0:T(8,128)(2,1)S(1)} collective-permute-done((bf16[256,384]{1,0:T(8,128)(2,1)S(1)}, bf16[256,384]{1,0:T(8,128)(2,1)S(1)}, u32[]{:S(2)}, u32[]{:S(2)}) %collective-permute-start.13) | collective-permute-done | bytes 196640 | tf_op jit(solution)/shard_map/ppermute | solution.py:223
  58.3 2.1 %collective-permute-done.6.refs_4_ = bf16[256,384]{1,0:T(8,128)(2,1)S(1)} collective-permute-done((bf16[256,384]{1,0:T(8,128)(2,1)S(1)}, bf16[256,384]{1,0:T(8,128)(2,1)S(1)}, u32[]{:S(2)}, u32[]{:S(2)}) %collective-permute-start.6) | collective-permute-done | bytes 196640 | tf_op jit(solution)/shard_map/ppermute | solution.py:223
  60.5 0.6 copy-done.24
  61.1 0.7 copy-done.25
  61.8 5.7 %shard_map.94 = (bf16[256,3072]{1,0:T(8,128)(2,1)}, bf16[256,3072]{1,0:T(8,128)(2,1)}, bf16[2,1536,256]{2,1,0:T(8,128)(2,1)}, bf16[2,1536,256]{2,1,0:T(8,128)(2,1)}) custom-call(bf16[256,384]{1,0:T(8,128)(2,1)} %bitcast.40, bf16[256,384]{1,0:T(8,128)(2,1)} %copy-done.14, bf16[256,384]{1,0:T(8,128)(2,1)} %copy-done.18, bf16[256,384]{1,0:T(8,128)(2,1)} %copy-done.22, ...), custom_call_target="tpu_custom_call" | custom-call | tf_op jit(solution)/shard_map/pallas_call | solution.py:298
  67.5 4.7 %collective-permute-start.14 = (bf16[2,1536,256]{2,1,0:T(8,128)(2,1)}, bf16[2,1536,256]{2,1,0:T(8,128)(2,1)S(1)}, u32[]{:S(2)}, u32[]{:S(2)}) collective-permute-start(bf16[2,1536,256]{2,1,0:T(8,128)(2,1)} %get-tuple-element.15), channel_id=1, source_target_pairs={{0,8},{8,0},{16,24},{24,16},{32,40},{40,32},{48,56},{56,48},{1,9},... | collective-permute-start | bytes 4718600 | tf_op jit(solution)/shard_map/ppermute | solution.py:227
  72.1 4.1 %collective-permute-done.14.refs_1_ = bf16[2,1536,256]{2,1,0:T(8,128)(2,1)S(1)} collective-permute-done((bf16[2,1536,256]{2,1,0:T(8,128)(2,1)}, bf16[2,1536,256]{2,1,0:T(8,128)(2,1)S(1)}, u32[]{:S(2)}, u32[]{:S(2)}) %collective-permute-start.14) | collective-permute-done | bytes 1572896 | tf_op jit(solution)/shard_map/ppermute | solution.py:227
  76.2 13.5 %shard_map.95 = (bf16[8,8,2,32,384]{4,3,2,1,0:T(8,128)(2,1)}, bf16[256,1536]{1,0:T(8,128)(2,1)}) custom-call(s32[1,16]{1,0:T(1,128)} %row_ref.3, bf16[256,3072]{1,0:T(8,128)(2,1)} %get-tuple-element.16.refs_1_, bf16[256,3072]{1,0:T(8,128)(2,1)} %get-tuple-element.17.refs_2_, bf16[12,3072,128]{2,1,0:T(8,128)(2,1)} %all-gather.2.cloned.1.call-done.refs_3_), custom_call_target="tpu_custom_call" | custom-call | tf_op jit(solution)/shard_map/pallas_call | solution.py:314
  89.8 0.5 collective-permute-start.15
  90.2 2.1 %collective-permute-done.15.refs_3_ = bf16[256,1536]{1,0:T(8,128)(2,1)S(1)} collective-permute-done((bf16[256,1536]{1,0:T(8,128)(2,1)}, bf16[256,1536]{1,0:T(8,128)(2,1)S(1)}, u32[]{:S(2)}, u32[]{:S(2)}) %collective-permute-start.15) | collective-permute-done | bytes 786464 | tf_op jit(solution)/shard_map/ppermute | solution.py:227
  92.4 1.1 copy-done.1
  93.5 0.9 shard_map.98
  94.4 2.8 %collective-permute-start.16 = (bf16[4,12,96,128]{3,2,1,0:T(8,128)(2,1)S(1)}, bf16[4,12,96,128]{3,2,1,0:T(8,128)(2,1)S(1)}, u32[]{:S(2)}, u32[]{:S(2)}) collective-permute-start(bf16[4,12,96,128]{3,2,1,0:T(8,128)(2,1)S(1)} %shard_map.98), channel_id=1, source_target_pairs={{0,32},{8,136},{16,48},{24,152},{32,0},{40,168},{48,16},{56,184},{... | collective-permute-start | bytes 3538952 | tf_op jit(solution)/shard_map/ppermute | solution.py:241
  97.2 0.9 shard_map.99
  98.0 0.6 collective-permute-start.17
  98.7 0.9 shard_map.100
  99.5 2.4 %collective-permute-start.18 = (bf16[4,12,96,128]{3,2,1,0:T(8,128)(2,1)S(1)}, bf16[4,12,96,128]{3,2,1,0:T(8,128)(2,1)S(1)}, u32[]{:S(2)}, u32[]{:S(2)}) collective-permute-start(bf16[4,12,96,128]{3,2,1,0:T(8,128)(2,1)S(1)} %shard_map.100), channel_id=1, source_target_pairs={{0,48},{8,200},{16,0},{24,216},{32,16},{40,232},{48,32},{56,248},{... | collective-permute-start | bytes 3538952 | tf_op jit(solution)/shard_map/ppermute | solution.py:241
  102.0 0.9 shard_map.97
  102.9 8.5 %collective-permute-done.16 = bf16[4,12,96,128]{3,2,1,0:T(8,128)(2,1)S(1)} collective-permute-done((bf16[4,12,96,128]{3,2,1,0:T(8,128)(2,1)S(1)}, bf16[4,12,96,128]{3,2,1,0:T(8,128)(2,1)S(1)}, u32[]{:S(2)}, u32[]{:S(2)}) %collective-permute-start.16) | collective-permute-done | bytes 1179680 | tf_op jit(solution)/shard_map/ppermute | solution.py:241
  111.4 12.7 %collective-permute-done.17 = bf16[4,12,96,128]{3,2,1,0:T(8,128)(2,1)S(1)} collective-permute-done((bf16[4,12,96,128]{3,2,1,0:T(8,128)(2,1)S(1)}, bf16[4,12,96,128]{3,2,1,0:T(8,128)(2,1)S(1)}, u32[]{:S(2)}, u32[]{:S(2)}) %collective-permute-start.17) | collective-permute-done | bytes 1179680 | tf_op jit(solution)/shard_map/ppermute | solution.py:241
  124.1 0.5 fusion.3
  124.6 0.5 copy-done.8
  125.5 2.2 %collective-permute-start.19 = (bf16[12,96,128]{2,1,0:T(8,128)(2,1)S(1)}, bf16[12,96,128]{2,1,0:T(8,128)(2,1)S(1)}, u32[]{:S(2)}, u32[]{:S(2)}) collective-permute-start(bf16[12,96,128]{2,1,0:T(8,128)(2,1)S(1)} %get-tuple-element.24), channel_id=1, source_target_pairs={{0,128},{8,40},{16,144},{24,56},{32,160},{40,8},{48,176},{56,24},{... | collective-permute-start | bytes 884744 | tf_op jit(solution)/shard_map/ppermute | solution.py:241
  127.8 0.9 collective-permute-start.21
  128.6 0.6 collective-permute-start.20
  129.2 3.6 %reduce-scatter.2.cloned.1.call-done = bf16[1,8,2,32,384]{4,3,2,1,0:T(8,128)(2,1)} async-done(((bf16[8,8,2,32,384]{4,3,2,1,0:T(8,128)(2,1)}), bf16[1,8,2,32,384]{4,3,2,1,0:T(8,128)(2,1)}) %reduce-scatter.2.cloned.1.call-update) | async-done | bytes 393232 | tf_op jit(solution)/shard_map/reduce_scatter | solution.py:334
  132.8 7.4 %all-to-all-start.1 = ((bf16[8,2,32,384]{3,2,1,0:T(8,128)(2,1)}), bf16[8,2,32,384]{3,2,1,0:T(8,128)(2,1)S(1)}, u32[]{:S(2)}, u32[]{:S(2)}) async-start(bf16[8,2,32,384]{3,2,1,0:T(8,128)(2,1)} %bitcast.42), calls=%async_computation.2 | async-start | bytes 786432 | tf_op jit(solution)/shard_map/all_to_all | solution.py:349
  140.2 1.5 fusion.1
  141.7 0.8 slice.98
  142.5 0.7 slice_bitcast_fusion
  143.2 5.1 %all-to-all-done.1.refs_0_ = bf16[8,2,32,384]{3,2,1,0:T(8,128)(2,1)S(1)} async-done(((bf16[8,2,32,384]{3,2,1,0:T(8,128)(2,1)}), bf16[8,2,32,384]{3,2,1,0:T(8,128)(2,1)S(1)}, u32[]{:S(2)}, u32[]{:S(2)}) %all-to-all-start.1) | async-done | bytes 393248 | tf_op jit(solution)/shard_map/all_to_all | solution.py:349
  148.3 2.5 %shard_map.96 = (bf16[2,128,384]{2,1,0:T(8,128)(2,1)}, bf16[2,3,128,384]{3,2,1,0:T(8,128)(2,1)}) custom-call(s32[1,16]{1,0:T(1,128)S(1)} %copy-done.5, s32[1,8]{1,0:T(1,128)S(1)} %copy-done.6, bf16[2,3,128,384]{3,2,1,0:T(8,128)(2,1)S(1)} %bitcast.32, bf16[2,128,384]{2,1,0:T(8,128)(2,1)S(1)} %bitcast.34, bf16[8,2,32,384]{3,2,1,0:T(8,128)(2,1)S(1)} %all-to-all-done.1.refs_0_), custom_call_target="tpu_custom_call" | custom-call | tf_op jit(solution)/shard_map/pallas_call | solution.py:350
  (71 shorter events, 1.0 us)
Async XLA Ops:
  7.2 69.1 %all-gather.2.cloned.1.call-start = ((), (), s32[]{:S(2)}) async-start(), calls=%async_computation.3 | async-start | bytes 9732096 | tf_op jit(solution)/shard_map/all_gather | solution.py:275
  8.9 123.9 %reduce-scatter.2.cloned.1.call-start = ((), (), s32[]{:S(2)}) async-start(), calls=%async_computation.4 | async-start | bytes 3538944 | tf_op jit(solution)/shard_map/reduce_scatter | solution.py:334
  27.6 32.7 %copy-start.10 = (bf16[8,1,2,16,384]{4,3,2,1,0:T(8,128)(2,1)}, bf16[8,1,2,16,384]{4,3,2,1,0:T(8,128)(2,1)S(1)}, u32[]{:S(2)}) copy-start(bf16[8,1,2,16,384]{4,3,2,1,0:T(8,128)(2,1)S(1)} %get-tuple-element.27) | copy-start | bytes 589828
  27.6 32.7 %copy-start.11 = (bf16[8,1,2,16,384]{4,3,2,1,0:T(8,128)(2,1)}, bf16[8,1,2,16,384]{4,3,2,1,0:T(8,128)(2,1)S(1)}, u32[]{:S(2)}) copy-start(bf16[8,1,2,16,384]{4,3,2,1,0:T(8,128)(2,1)S(1)} %get-tuple-element.28) | copy-start | bytes 589828
  27.7 9.3 %collective-permute-start.3 = (bf16[256,384]{1,0:T(8,128)(2,1)S(1)}, bf16[256,384]{1,0:T(8,128)(2,1)S(1)}, u32[]{:S(2)}, u32[]{:S(2)}) collective-permute-start(bf16[256,384]{1,0:T(8,128)(2,1)S(1)} %bitcast.38), channel_id=1, source_target_pairs={{0,1},{1,2},{2,3},{3,4},{4,5},{5,6},{6,7},{7,0},{8,9},{9,10},{10,1... | collective-permute-start | bytes 589832 | tf_op jit(solution)/shard_map/ppermute | solution.py:223
  28.6 8.4 %collective-permute-start.7 = (bf16[256,384]{1,0:T(8,128)(2,1)S(1)}, bf16[256,384]{1,0:T(8,128)(2,1)S(1)}, u32[]{:S(2)}, u32[]{:S(2)}) collective-permute-start(bf16[256,384]{1,0:T(8,128)(2,1)S(1)} %bitcast.35), channel_id=1, source_target_pairs={{0,7},{1,0},{2,1},{3,2},{4,3},{5,4},{6,5},{7,6},{8,15},{9,8},{10,9... | collective-permute-start | bytes 589832 | tf_op jit(solution)/shard_map/ppermute | solution.py:223
  32.6 7.6 %collective-permute-start = (bf16[256,384]{1,0:T(8,128)(2,1)S(1)}, bf16[256,384]{1,0:T(8,128)(2,1)S(1)}, u32[]{:S(2)}, u32[]{:S(2)}) collective-permute-start(bf16[256,384]{1,0:T(8,128)(2,1)S(1)} %bitcast.39), channel_id=1, source_target_pairs={{0,7},{1,0},{2,1},{3,2},{4,3},{5,4},{6,5},{7,6},{8,15},{9,8},{10,9... | collective-permute-start | bytes 589832 | tf_op jit(solution)/shard_map/ppermute | solution.py:223
  34.0 9.7 %collective-permute-start.11 = (bf16[256,384]{1,0:T(8,128)(2,1)S(1)}, bf16[256,384]{1,0:T(8,128)(2,1)S(1)}, u32[]{:S(2)}, u32[]{:S(2)}) collective-permute-start(bf16[256,384]{1,0:T(8,128)(2,1)S(1)} %bitcast.36), channel_id=1, source_target_pairs={{0,1},{1,2},{2,3},{3,4},{4,5},{5,6},{6,7},{7,0},{8,9},{9,10},{10,1... | collective-permute-start | bytes 589832 | tf_op jit(solution)/shard_map/ppermute | solution.py:223
  36.9 23.5 %copy-start.12 = (bf16[256,384]{1,0:T(8,128)(2,1)}, bf16[256,384]{1,0:T(8,128)(2,1)S(1)}, u32[]{:S(2)}) copy-start(bf16[256,384]{1,0:T(8,128)(2,1)S(1)} %collective-permute-done.3.refs_7_) | copy-start | bytes 589828
  36.9 8.1 %collective-permute-start.4 = (bf16[256,384]{1,0:T(8,128)(2,1)S(1)}, bf16[256,384]{1,0:T(8,128)(2,1)S(1)}, u32[]{:S(2)}, u32[]{:S(2)}) collective-permute-start(bf16[256,384]{1,0:T(8,128)(2,1)S(1)} %collective-permute-done.3.refs_7_), channel_id=1, source_target_pairs={{0,1},{1,2},{2,3},{3,4},{4,5},{5,6},{6,7},{7,0},{8,9},{9,10},{10,1... | collective-permute-start | bytes 589832 | tf_op jit(solution)/shard_map/ppermute | solution.py:223
  36.9 23.5 %copy-start.13 = (bf16[256,384]{1,0:T(8,128)(2,1)}, bf16[256,384]{1,0:T(8,128)(2,1)S(1)}, u32[]{:S(2)}) copy-start(bf16[256,384]{1,0:T(8,128)(2,1)S(1)} %collective-permute-done.7.refs_9_) | copy-start | bytes 589828
  37.0 8.1 %collective-permute-start.8 = (bf16[256,384]{1,0:T(8,128)(2,1)S(1)}, bf16[256,384]{1,0:T(8,128)(2,1)S(1)}, u32[]{:S(2)}, u32[]{:S(2)}) collective-permute-start(bf16[256,384]{1,0:T(8,128)(2,1)S(1)} %collective-permute-done.7.refs_9_), channel_id=1, source_target_pairs={{0,7},{1,0},{2,1},{3,2},{4,3},{5,4},{6,5},{7,6},{8,15},{9,8},{10,9... | collective-permute-start | bytes 589832 | tf_op jit(solution)/shard_map/ppermute | solution.py:223
  40.2 20.2 %copy-start.14 = (bf16[256,384]{1,0:T(8,128)(2,1)}, bf16[256,384]{1,0:T(8,128)(2,1)S(1)}, u32[]{:S(2)}) copy-start(bf16[256,384]{1,0:T(8,128)(2,1)S(1)} %collective-permute-done.refs_1_) | copy-start | bytes 589828
  40.2 7.7 %collective-permute-start.1 = (bf16[256,384]{1,0:T(8,128)(2,1)S(1)}, bf16[256,384]{1,0:T(8,128)(2,1)S(1)}, u32[]{:S(2)}, u32[]{:S(2)}) collective-permute-start(bf16[256,384]{1,0:T(8,128)(2,1)S(1)} %collective-permute-done.refs_1_), channel_id=1, source_target_pairs={{0,7},{1,0},{2,1},{3,2},{4,3},{5,4},{6,5},{7,6},{8,15},{9,8},{10,9... | collective-permute-start | bytes 589832 | tf_op jit(solution)/shard_map/ppermute | solution.py:223
  43.7 16.7 %copy-start.15 = (bf16[256,384]{1,0:T(8,128)(2,1)}, bf16[256,384]{1,0:T(8,128)(2,1)S(1)}, u32[]{:S(2)}) copy-start(bf16[256,384]{1,0:T(8,128)(2,1)S(1)} %collective-permute-done.11.refs_15_) | copy-start | bytes 589828
  43.7 7.7 %collective-permute-start.12 = (bf16[256,384]{1,0:T(8,128)(2,1)S(1)}, bf16[256,384]{1,0:T(8,128)(2,1)S(1)}, u32[]{:S(2)}, u32[]{:S(2)}) collective-permute-start(bf16[256,384]{1,0:T(8,128)(2,1)S(1)} %collective-permute-done.11.refs_15_), channel_id=1, source_target_pairs={{0,1},{1,2},{2,3},{3,4},{4,5},{5,6},{6,7},{7,0},{8,9},{9,10},{10,1... | collective-permute-start | bytes 589832 | tf_op jit(solution)/shard_map/ppermute | solution.py:223
  45.0 15.4 %copy-start.16 = (bf16[256,384]{1,0:T(8,128)(2,1)}, bf16[256,384]{1,0:T(8,128)(2,1)S(1)}, u32[]{:S(2)}) copy-start(bf16[256,384]{1,0:T(8,128)(2,1)S(1)} %collective-permute-done.4.refs_6_) | copy-start | bytes 589828
  45.0 7.2 %collective-permute-start.5 = (bf16[256,384]{1,0:T(8,128)(2,1)S(1)}, bf16[256,384]{1,0:T(8,128)(2,1)S(1)}, u32[]{:S(2)}, u32[]{:S(2)}) collective-permute-start(bf16[256,384]{1,0:T(8,128)(2,1)S(1)} %collective-permute-done.4.refs_6_), channel_id=1, source_target_pairs={{0,1},{1,2},{2,3},{3,4},{4,5},{5,6},{6,7},{7,0},{8,9},{9,10},{10,1... | collective-permute-start | bytes 589832 | tf_op jit(solution)/shard_map/ppermute | solution.py:223
  45.0 15.4 %copy-start.17 = (bf16[256,384]{1,0:T(8,128)(2,1)}, bf16[256,384]{1,0:T(8,128)(2,1)S(1)}, u32[]{:S(2)}) copy-start(bf16[256,384]{1,0:T(8,128)(2,1)S(1)} %collective-permute-done.8.refs_10_) | copy-start | bytes 589828
  45.0 7.2 %collective-permute-start.9 = (bf16[256,384]{1,0:T(8,128)(2,1)S(1)}, bf16[256,384]{1,0:T(8,128)(2,1)S(1)}, u32[]{:S(2)}, u32[]{:S(2)}) collective-permute-start(bf16[256,384]{1,0:T(8,128)(2,1)S(1)} %collective-permute-done.8.refs_10_), channel_id=1, source_target_pairs={{0,7},{1,0},{2,1},{3,2},{4,3},{5,4},{6,5},{7,6},{8,15},{9,8},{10,9... | collective-permute-start | bytes 589832 | tf_op jit(solution)/shard_map/ppermute | solution.py:223
  47.9 12.6 %copy-start.18 = (bf16[256,384]{1,0:T(8,128)(2,1)}, bf16[256,384]{1,0:T(8,128)(2,1)S(1)}, u32[]{:S(2)}) copy-start(bf16[256,384]{1,0:T(8,128)(2,1)S(1)} %collective-permute-done.1.refs_2_) | copy-start | bytes 589828
  47.9 8.3 %collective-permute-start.2 = (bf16[256,384]{1,0:T(8,128)(2,1)S(1)}, bf16[256,384]{1,0:T(8,128)(2,1)S(1)}, u32[]{:S(2)}, u32[]{:S(2)}) collective-permute-start(bf16[256,384]{1,0:T(8,128)(2,1)S(1)} %collective-permute-done.1.refs_2_), channel_id=1, source_target_pairs={{0,7},{1,0},{2,1},{3,2},{4,3},{5,4},{6,5},{7,6},{8,15},{9,8},{10,9... | collective-permute-start | bytes 589832 | tf_op jit(solution)/shard_map/ppermute | solution.py:223
  51.4 9.1 %copy-start.19 = (bf16[256,384]{1,0:T(8,128)(2,1)}, bf16[256,384]{1,0:T(8,128)(2,1)S(1)}, u32[]{:S(2)}) copy-start(bf16[256,384]{1,0:T(8,128)(2,1)S(1)} %collective-permute-done.12.refs_14_) | copy-start | bytes 589828
  51.4 6.9 %collective-permute-start.13 = (bf16[256,384]{1,0:T(8,128)(2,1)S(1)}, bf16[256,384]{1,0:T(8,128)(2,1)S(1)}, u32[]{:S(2)}, u32[]{:S(2)}) collective-permute-start(bf16[256,384]{1,0:T(8,128)(2,1)S(1)} %collective-permute-done.12.refs_14_), channel_id=1, source_target_pairs={{0,1},{1,2},{2,3},{3,4},{4,5},{5,6},{6,7},{7,0},{8,9},{9,10},{10,1... | collective-permute-start | bytes 589832 | tf_op jit(solution)/shard_map/ppermute | solution.py:223
  52.2 8.3 %copy-start.20 = (bf16[256,384]{1,0:T(8,128)(2,1)}, bf16[256,384]{1,0:T(8,128)(2,1)S(1)}, u32[]{:S(2)}) copy-start(bf16[256,384]{1,0:T(8,128)(2,1)S(1)} %collective-permute-done.5.refs_5_) | copy-start | bytes 589828
  52.2 8.2 %collective-permute-start.6 = (bf16[256,384]{1,0:T(8,128)(2,1)S(1)}, bf16[256,384]{1,0:T(8,128)(2,1)S(1)}, u32[]{:S(2)}, u32[]{:S(2)}) collective-permute-start(bf16[256,384]{1,0:T(8,128)(2,1)S(1)} %collective-permute-done.5.refs_5_), channel_id=1, source_target_pairs={{0,1},{1,2},{2,3},{3,4},{4,5},{5,6},{6,7},{7,0},{8,9},{9,10},{10,1... | collective-permute-start | bytes 589832 | tf_op jit(solution)/shard_map/ppermute | solution.py:223
  52.2 8.3 %copy-start.21 = (bf16[256,384]{1,0:T(8,128)(2,1)}, bf16[256,384]{1,0:T(8,128)(2,1)S(1)}, u32[]{:S(2)}) copy-start(bf16[256,384]{1,0:T(8,128)(2,1)S(1)} %collective-permute-done.9.refs_11_) | copy-start | bytes 589828
  52.2 8.1 %collective-permute-start.10 = (bf16[256,384]{1,0:T(8,128)(2,1)S(1)}, bf16[256,384]{1,0:T(8,128)(2,1)S(1)}, u32[]{:S(2)}, u32[]{:S(2)}) collective-permute-start(bf16[256,384]{1,0:T(8,128)(2,1)S(1)} %collective-permute-done.9.refs_11_), channel_id=1, source_target_pairs={{0,7},{1,0},{2,1},{3,2},{4,3},{5,4},{6,5},{7,6},{8,15},{9,8},{10,9... | collective-permute-start | bytes 589832 | tf_op jit(solution)/shard_map/ppermute | solution.py:223
  56.2 4.3 %copy-start.22 = (bf16[256,384]{1,0:T(8,128)(2,1)}, bf16[256,384]{1,0:T(8,128)(2,1)S(1)}, u32[]{:S(2)}) copy-start(bf16[256,384]{1,0:T(8,128)(2,1)S(1)} %collective-permute-done.2.refs_3_) | copy-start | bytes 589828
  58.3 2.2 %copy-start.23 = (bf16[256,384]{1,0:T(8,128)(2,1)}, bf16[256,384]{1,0:T(8,128)(2,1)S(1)}, u32[]{:S(2)}) copy-start(bf16[256,384]{1,0:T(8,128)(2,1)S(1)} %collective-permute-done.13.refs_13_) | copy-start | bytes 589828
  67.5 8.7 %collective-permute-start.14 = (bf16[2,1536,256]{2,1,0:T(8,128)(2,1)}, bf16[2,1536,256]{2,1,0:T(8,128)(2,1)S(1)}, u32[]{:S(2)}, u32[]{:S(2)}) collective-permute-start(bf16[2,1536,256]{2,1,0:T(8,128)(2,1)} %get-tuple-element.15), channel_id=1, source_target_pairs={{0,8},{8,0},{16,24},{24,16},{32,40},{40,32},{48,56},{56,48},{1,9},... | collective-permute-start | bytes 4718600 | tf_op jit(solution)/shard_map/ppermute | solution.py:227
  89.8 2.6 %copy-start = (bf16[2,1536,256]{2,1,0:T(8,128)(2,1)S(1)}, bf16[2,1536,256]{2,1,0:T(8,128)(2,1)}, u32[]{:S(2)}) copy-start(bf16[2,1536,256]{2,1,0:T(8,128)(2,1)} %get-tuple-element.21.refs_0_) | copy-start | bytes 4718596
  89.8 2.6 %collective-permute-start.15 = (bf16[256,1536]{1,0:T(8,128)(2,1)}, bf16[256,1536]{1,0:T(8,128)(2,1)S(1)}, u32[]{:S(2)}, u32[]{:S(2)}) collective-permute-start(bf16[256,1536]{1,0:T(8,128)(2,1)} %get-tuple-element.23.refs_2_), channel_id=1, source_target_pairs={{0,8},{8,0},{16,24},{24,16},{32,40},{40,32},{48,56},{56,48},{1,9},... | collective-permute-start | bytes 2359304 | tf_op jit(solution)/shard_map/ppermute | solution.py:227
  92.4 1.1 copy-start.1
  94.4 17.0 %collective-permute-start.16 = (bf16[4,12,96,128]{3,2,1,0:T(8,128)(2,1)S(1)}, bf16[4,12,96,128]{3,2,1,0:T(8,128)(2,1)S(1)}, u32[]{:S(2)}, u32[]{:S(2)}) collective-permute-start(bf16[4,12,96,128]{3,2,1,0:T(8,128)(2,1)S(1)} %shard_map.98), channel_id=1, source_target_pairs={{0,32},{8,136},{16,48},{24,152},{32,0},{40,168},{48,16},{56,184},{... | collective-permute-start | bytes 3538952 | tf_op jit(solution)/shard_map/ppermute | solution.py:241
  98.0 26.0 %collective-permute-start.17 = (bf16[4,12,96,128]{3,2,1,0:T(8,128)(2,1)S(1)}, bf16[4,12,96,128]{3,2,1,0:T(8,128)(2,1)S(1)}, u32[]{:S(2)}, u32[]{:S(2)}) collective-permute-start(bf16[4,12,96,128]{3,2,1,0:T(8,128)(2,1)S(1)} %shard_map.99), channel_id=1, source_target_pairs={{0,16},{8,72},{16,32},{24,88},{32,48},{40,104},{48,0},{56,120},{64... | collective-permute-start | bytes 3538952 | tf_op jit(solution)/shard_map/ppermute | solution.py:241
  99.5 24.5 %collective-permute-start.18 = (bf16[4,12,96,128]{3,2,1,0:T(8,128)(2,1)S(1)}, bf16[4,12,96,128]{3,2,1,0:T(8,128)(2,1)S(1)}, u32[]{:S(2)}, u32[]{:S(2)}) collective-permute-start(bf16[4,12,96,128]{3,2,1,0:T(8,128)(2,1)S(1)} %shard_map.100), channel_id=1, source_target_pairs={{0,48},{8,200},{16,0},{24,216},{32,16},{40,232},{48,32},{56,248},{... | collective-permute-start | bytes 3538952 | tf_op jit(solution)/shard_map/ppermute | solution.py:241
  102.9 21.7 %copy-start.2 = (bf16[4,12,96,128]{3,2,1,0:T(8,128)(2,1)}, bf16[4,12,96,128]{3,2,1,0:T(8,128)(2,1)S(1)}, u32[]{:S(2)}) copy-start(bf16[4,12,96,128]{3,2,1,0:T(8,128)(2,1)S(1)} %shard_map.97) | copy-start | bytes 3538948
  111.4 13.2 %copy-start.7 = (bf16[4,12,96,128]{3,2,1,0:T(8,128)(2,1)}, bf16[4,12,96,128]{3,2,1,0:T(8,128)(2,1)S(1)}, u32[]{:S(2)}) copy-start(bf16[4,12,96,128]{3,2,1,0:T(8,128)(2,1)S(1)} %collective-permute-done.16) | copy-start | bytes 3538948
  124.1 1.4 copy-start.9
  125.5 14.7 %collective-permute-start.19 = (bf16[12,96,128]{2,1,0:T(8,128)(2,1)S(1)}, bf16[12,96,128]{2,1,0:T(8,128)(2,1)S(1)}, u32[]{:S(2)}, u32[]{:S(2)}) collective-permute-start(bf16[12,96,128]{2,1,0:T(8,128)(2,1)S(1)} %get-tuple-element.24), channel_id=1, source_target_pairs={{0,128},{8,40},{16,144},{24,56},{32,160},{40,8},{48,176},{56,24},{... | collective-permute-start | bytes 884744 | tf_op jit(solution)/shard_map/ppermute | solution.py:241
  127.8 12.4 %collective-permute-start.21 = (bf16[12,96,128]{2,1,0:T(8,128)(2,1)S(1)}, bf16[12,96,128]{2,1,0:T(8,128)(2,1)S(1)}, u32[]{:S(2)}, u32[]{:S(2)}) collective-permute-start(bf16[12,96,128]{2,1,0:T(8,128)(2,1)S(1)} %get-tuple-element.25), channel_id=1, source_target_pairs={{0,192},{8,56},{16,208},{24,8},{32,224},{40,24},{48,240},{56,40},{... | collective-permute-start | bytes 884744 | tf_op jit(solution)/shard_map/ppermute | solution.py:241
  128.6 11.6 %collective-permute-start.20 = (bf16[12,96,128]{2,1,0:T(8,128)(2,1)S(1)}, bf16[12,96,128]{2,1,0:T(8,128)(2,1)S(1)}, u32[]{:S(2)}, u32[]{:S(2)}) collective-permute-start(bf16[12,96,128]{2,1,0:T(8,128)(2,1)S(1)} %get-tuple-element.26), channel_id=1, source_target_pairs={{0,64},{8,24},{16,80},{24,40},{32,96},{40,56},{48,112},{56,8},{64,... | collective-permute-start | bytes 884744 | tf_op jit(solution)/shard_map/ppermute | solution.py:241
  132.8 15.5 %all-to-all-start.1 = ((bf16[8,2,32,384]{3,2,1,0:T(8,128)(2,1)}), bf16[8,2,32,384]{3,2,1,0:T(8,128)(2,1)S(1)}, u32[]{:S(2)}, u32[]{:S(2)}) async-start(bf16[8,2,32,384]{3,2,1,0:T(8,128)(2,1)} %bitcast.42), calls=%async_computation.2 | async-start | bytes 786432 | tf_op jit(solution)/shard_map/all_to_all | solution.py:349
  141.7 6.6 %copy-start.3 = (bf16[1,2,128,3,384]{4,2,3,1,0:T(8,128)(2,1)S(1)}, bf16[1,2,128,3,384]{4,2,3,1,0:T(8,128)(2,1)}, u32[]{:S(2)}) copy-start(bf16[1,2,128,3,384]{4,2,3,1,0:T(8,128)(2,1)} %param.6) | copy-start | bytes 1769476
  141.7 6.6 %copy-start.4 = (bf16[1,2,128,384]{3,2,1,0:T(8,128)(2,1)S(1)}, bf16[1,2,128,384]{3,2,1,0:T(8,128)(2,1)}, u32[]{:S(2)}) copy-start(bf16[1,2,128,384]{3,2,1,0:T(8,128)(2,1)} %param.9) | copy-start | bytes 589828
  141.7 6.6 %copy-start.5 = (s32[1,16]{1,0:T(1,128)S(1)}, s32[1,16]{1,0:T(1,128)}, u32[]{:S(2)}) copy-start(s32[1,16]{1,0:T(1,128)} %row_ref.3) | copy-start | bytes 196
  141.7 6.5 %copy-start.6 = (s32[1,8]{1,0:T(1,128)S(1)}, s32[1,8]{1,0:T(1,128)}, u32[]{:S(2)}) copy-start(s32[1,8]{1,0:T(1,128)} %patch_ref.3) | copy-start | bytes 100
  (3 other events, 2.4 us)
Sparse Core Ops, SparseCore 0:
  11.2 64.8 all-gather.1
  89.9 42.8 reduce-scatter.1

commit v6 on v5

--- a/solution.py
+++ b/solution.py
@@ -63,15 +63,16 @@
 
 
 def spatial_backward(row_ref, patch_ref, qkv_ref, cot_ref, *refs):
-    sums_ref, out_ref, grad_ref, whole_ref = refs
+    blocks, (out_ref, grad_ref, whole_ref) = refs[:-3], refs[-3:]
     frames, _, patches, width = qkv_ref.shape
     place = lax.axis_index("frame")
-    owners = sums_ref.shape[0]
-    block = patches // owners
-    for s in range(owners):
-        for f in range(frames):
-            part = sums_ref[s, :, f * block : (f + 1) * block, :]
-            whole_ref[:, f, s * block : (s + 1) * block, :] = part
+    block = blocks[0].shape[2] // frames
+    for m, ref in enumerate(blocks):
+        for i in range(2):
+            start = pl.multiple_of((place ^ (2 * m + i)) * block, 16)
+            for f in range(frames):
+                part = ref[i, :, f * block : (f + 1) * block, :]
+                whole_ref[:, f, pl.ds(start, block), :] = part
     live, d_mixed = [], []
     for f in range(frames):
         count = live_rows(row_ref, patch_ref, place * frames + f)
@@ -186,8 +187,10 @@
         for i in range(pair):
             z, cols = first + i, slice(i * width, (i + 1) * width)
             for s in range(owners):
-                sums_ref[z, s, 0] = projected[s * rows : (s + 1) * rows, cols]
-                sums_ref[z, s, 1] = back[s * rows : (s + 1) * rows, cols]
+                apart = lax.axis_index("frame") ^ s
+                slot = lax.rem(apart, 2) * 4 + apart // 2
+                sums_ref[z, slot, 0] = projected[s * rows : (s + 1) * rows, cols]
+                sums_ref[z, slot, 1] = back[s * rows : (s + 1) * rows, cols]
             stores.append(pltpu.make_async_copy(sums_ref.at[z], sums_hbm.at[z], out_sem.at[z]))
             stores[-1].start()
     for copy in stores:
@@ -346,18 +349,23 @@
     partial = [add(*(part[i] for part in arrived)).astype(BF) for i in range(4)]
     grads = add(partial[0], *(spread(partial[step], step, True) for step in (2, 1, 3)))
 
-    row_sums = lax.all_to_all(own_sums, "frame", split_axis=0, concat_axis=0, tiled=True)
+    own_part, got = own_sums[:4], pair_swap(own_sums[4:])
+    joined = [jnp.concatenate([own_part[m : m + 1], got[m : m + 1]], axis=0) for m in range(4)]
+    row_sums = joined[:1]
+    for m in range(1, 4):
+        pairs = [(i, i ^ (2 * m)) for i in range(8)]
+        row_sums.append(lax.ppermute(joined[m], "frame", pairs))
     block_out, qkv_grad = pl.pallas_call(
         spatial_backward,
         out_shape=[
             jax.ShapeDtypeStruct((frames, patches, width), BF),
             jax.ShapeDtypeStruct((frames, 3, patches, width), BF),
         ],
-        in_specs=[smem, smem] + [vmem] * 3,
+        in_specs=[smem, smem] + [vmem] * 6,
         out_specs=[vmem, vmem],
         scratch_shapes=[pltpu.VMEM((2, frames, patches, width), BF)],
         compiler_params=pltpu.CompilerParams(vmem_limit_bytes=24 * 2**20),
-    )(frame_clip, clip_patches, qkv, cot, row_sums)
+    )(frame_clip, clip_patches, qkv, cot, *row_sums)
 
     w_qkv_grad = grads[: 3 * heads].reshape(heads, 3, w_rows, HD).transpose(2, 0, 1, 3)
     w_out_grad = grads[3 * heads :].transpose(0, 2, 1)

time: 158 us -> 161 us (1.019)
  waiting for transfers between devices: 47 us -> 51.3 us
    all_to_all x1 -> x0, starting transfers between devices: 7.39 us -> none  [body(): lax.all_to_all(own_sums, 'frame', split_axis=0, concat_axis=0, tiled=True)]
    ppermute x6, waiting for transfers between devices: 21.2 us -> 28.2 us  [spread(): return lax.ppermute(value, ('clip', 'frame'), pairs)]
    ppermute x0 -> x3, waiting for transfers between devices: none -> 5.8 us  [body(): row_sums.append(lax.ppermute(joined[m], 'frame', pairs))]
    all_to_all x1 -> x0, waiting for transfers between devices: 5.06 us -> none  [body(): lax.all_to_all(own_sums, 'frame', split_axis=0, concat_axis=0, tiled=True)]
    ppermute x0 -> x3, starting transfers between devices: none -> 4.12 us  [body(): row_sums.append(lax.ppermute(joined[m], 'frame', pairs))]
    reduce_scatter x1, waiting for transfers between devices: 3.58 us -> 0.01 us  [body(): lax.psum_scatter(sums, 'tensor', scatter_dimension=0, tiled=True)[0]]
    ppermute x2 -> x3, starting transfers between devices: 5.1 us -> 7.65 us  [pair_swap(): return lax.ppermute(value, 'frame', [(i, i ^ 1) for i in range(8)])]
    slice x0 -> x3, local copies, waits for them, and re-layouts: none -> 1.86 us  [the longest x1 0.95 us: body(): own_part, got = (own_sums[:4], pair_swap(own_sums[4:]))]
  transfers between devices with their start and end apart: 25 -> 28, of which waited for: 14 -> 19; matrix products, arithmetic and copies ran while one was open for 2% -> 2% of each run, Pallas kernels for 8% -> 8%
where the time goes in v6:
time: 161 us
  waiting for transfers between devices  51.3 us (32%)
  starting transfers between devices  43.1 us (27%)
  Pallas kernels  29 us (18%)
  blocking collectives  14.7 us (9%)
  between operations  14.4 us (9%)
  local copies, waits for them, and re-layouts  5.82 us (4%)
  other arithmetic  2.48 us (2%)
    ppermute x6, waiting for transfers between devices, spread(): return lax.ppermute(value, ('clip', 'frame'), pairs)  28.2 us
    ppermute x14, starting transfers between devices, shift(): lax.ppermute(value, axis, [(i, (i + step) % size) for i in range(size)])  21.8 us
    all_to_all x1, blocking collectives, body(): lax.all_to_all(sent, 'frame', split_axis=0, concat_axis=0, tiled=True)  14.7 us
    pallas_call x1, Pallas kernels, body(): pl.pallas_call(lambda *refs: temporal_kernel(heads, *refs), out_shape=[ja...  13.4 us
    ppermute x14, waiting for transfers between devices, shift(): lax.ppermute(value, axis, [(i, (i + step) % size) for i in range(size)])  10.9 us
    ppermute x6, starting transfers between devices, spread(): return lax.ppermute(value, ('clip', 'frame'), pairs)  9.53 us
    ppermute x3, starting transfers between devices, pair_swap(): return lax.ppermute(value, 'frame', [(i, i ^ 1) for i in range(8)])  7.65 us
    ppermute x3, waiting for transfers between devices, pair_swap(): return lax.ppermute(value, 'frame', [(i, i ^ 1) for i in range(8)])  6.39 us
  transfers between devices with their start and end apart: 28, of which 19 were waited for; matrix products, arithmetic and copies ran while one was open for 2% of the time, Pallas kernels for 8%

profile of v6, /device:TPU:1, one launch (start us, length us, event | category | flops | bytes accessed | tf_op | source)
XLA Modules:
  0.0 160.8 jit_solution(9482266428731840850)
XLA Ops:
  7.2 1.7 %pad_maximum_fusion = bf16[12,96,128]{2,1,0:T(8,128)(2,1)} fusion(bf16[3,96,128]{2,1,0:T(8,128)(2,1)} %bitcast.52, bf16[9,96,128]{2,1,0:T(8,128)(2,1)} %bitcast.51), kind=kLoop, calls=%fused_computation.11 | loop fusion | flops 147456 | bytes 589824 | tf_op jit(solution)/shard_map/concatenate | solution.py:274
  9.0 3.9 %shard_map.93 = bf16[8,2,2,16,384]{4,3,2,1,0:T(8,128)(2,1)} custom-call(s32[1,16]{1,0:T(1,128)} %row_ref.3, s32[1,8]{1,0:T(1,128)} %patch_ref.3, bf16[2,3,128,384]{3,2,1,0:T(8,128)(2,1)} %bitcast.40, bf16[2,128,384]{2,1,0:T(8,128)(2,1)} %bitcast.42), custom_call_target="tpu_custom_call" | custom-call | tf_op jit(solution)/shard_map/pallas_call | solution.py:285
  12.9 14.7 %all_to_all.5 = bf16[8,2,2,16,384]{4,3,2,1,0:T(8,128)(2,1)S(1)} all-to-all(bf16[8,2,2,16,384]{4,3,2,1,0:T(8,128)(2,1)} %shard_map.93), channel_id=1, replica_groups=mesh['clip'=4,'frame'=8,'tensor'=8] {'frame'}, dimensions={0} | all-to-all | bytes 786432 | tf_op jit(solution)/shard_map/all_to_all | solution.py:293
  27.7 0.9 collective-permute-start.3
  28.6 4.0 %collective-permute-start.7 = (bf16[256,384]{1,0:T(8,128)(2,1)S(1)}, bf16[256,384]{1,0:T(8,128)(2,1)S(1)}, u32[]{:S(2)}, u32[]{:S(2)}) collective-permute-start(bf16[256,384]{1,0:T(8,128)(2,1)S(1)} %bitcast.44), channel_id=1, source_target_pairs={{0,7},{1,0},{2,1},{3,2},{4,3},{5,4},{6,5},{7,6},{8,15},{9,8},{10,9... | collective-permute-start | bytes 589832 | tf_op jit(solution)/shard_map/ppermute | solution.py:226
  32.6 1.4 collective-permute-start
  34.1 2.9 %collective-permute-done.3.refs_7_ = bf16[256,384]{1,0:T(8,128)(2,1)S(1)} collective-permute-done((bf16[256,384]{1,0:T(8,128)(2,1)S(1)}, bf16[256,384]{1,0:T(8,128)(2,1)S(1)}, u32[]{:S(2)}, u32[]{:S(2)}) %collective-permute-start.3) | collective-permute-done | bytes 196640 | tf_op jit(solution)/shard_map/ppermute | solution.py:226
  37.0 2.7 %collective-permute-start.8 = (bf16[256,384]{1,0:T(8,128)(2,1)S(1)}, bf16[256,384]{1,0:T(8,128)(2,1)S(1)}, u32[]{:S(2)}, u32[]{:S(2)}) collective-permute-start(bf16[256,384]{1,0:T(8,128)(2,1)S(1)} %collective-permute-done.7.refs_9_), channel_id=1, source_target_pairs={{0,7},{1,0},{2,1},{3,2},{4,3},{5,4},{6,5},{7,6},{8,15},{9,8},{10,9... | collective-permute-start | bytes 589832 | tf_op jit(solution)/shard_map/ppermute | solution.py:226
  40.2 3.5 %collective-permute-start.1 = (bf16[256,384]{1,0:T(8,128)(2,1)S(1)}, bf16[256,384]{1,0:T(8,128)(2,1)S(1)}, u32[]{:S(2)}, u32[]{:S(2)}) collective-permute-start(bf16[256,384]{1,0:T(8,128)(2,1)S(1)} %collective-permute-done.refs_1_), channel_id=1, source_target_pairs={{0,7},{1,0},{2,1},{3,2},{4,3},{5,4},{6,5},{7,6},{8,15},{9,8},{10,9... | collective-permute-start | bytes 589832 | tf_op jit(solution)/shard_map/ppermute | solution.py:226
  43.7 1.3 collective-permute-done.4.refs_6_
  45.0 2.7 %collective-permute-start.9 = (bf16[256,384]{1,0:T(8,128)(2,1)S(1)}, bf16[256,384]{1,0:T(8,128)(2,1)S(1)}, u32[]{:S(2)}, u32[]{:S(2)}) collective-permute-start(bf16[256,384]{1,0:T(8,128)(2,1)S(1)} %collective-permute-done.8.refs_10_), channel_id=1, source_target_pairs={{0,7},{1,0},{2,1},{3,2},{4,3},{5,4},{6,5},{7,6},{8,15},{9,8},{10,9... | collective-permute-start | bytes 589832 | tf_op jit(solution)/shard_map/ppermute | solution.py:226
  47.9 3.5 %collective-permute-start.2 = (bf16[256,384]{1,0:T(8,128)(2,1)S(1)}, bf16[256,384]{1,0:T(8,128)(2,1)S(1)}, u32[]{:S(2)}, u32[]{:S(2)}) collective-permute-start(bf16[256,384]{1,0:T(8,128)(2,1)S(1)} %collective-permute-done.1.refs_2_), channel_id=1, source_target_pairs={{0,7},{1,0},{2,1},{3,2},{4,3},{5,4},{6,5},{7,6},{8,15},{9,8},{10,9... | collective-permute-start | bytes 589832 | tf_op jit(solution)/shard_map/ppermute | solution.py:226
  51.4 0.8 collective-permute-done.5.refs_5_
  52.2 3.0 %collective-permute-start.10 = (bf16[256,384]{1,0:T(8,128)(2,1)S(1)}, bf16[256,384]{1,0:T(8,128)(2,1)S(1)}, u32[]{:S(2)}, u32[]{:S(2)}) collective-permute-start(bf16[256,384]{1,0:T(8,128)(2,1)S(1)} %collective-permute-done.9.refs_11_), channel_id=1, source_target_pairs={{0,7},{1,0},{2,1},{3,2},{4,3},{5,4},{6,5},{7,6},{8,15},{9,8},{10,9... | collective-permute-start | bytes 589832 | tf_op jit(solution)/shard_map/ppermute | solution.py:226
  55.2 1.0 collective-permute-done.2.refs_3_
  56.2 2.1 %collective-permute-done.13.refs_13_ = bf16[256,384]{1,0:T(8,128)(2,1)S(1)} collective-permute-done((bf16[256,384]{1,0:T(8,128)(2,1)S(1)}, bf16[256,384]{1,0:T(8,128)(2,1)S(1)}, u32[]{:S(2)}, u32[]{:S(2)}) %collective-permute-start.13) | collective-permute-done | bytes 196640 | tf_op jit(solution)/shard_map/ppermute | solution.py:226
  58.3 2.1 %collective-permute-done.6.refs_4_ = bf16[256,384]{1,0:T(8,128)(2,1)S(1)} collective-permute-done((bf16[256,384]{1,0:T(8,128)(2,1)S(1)}, bf16[256,384]{1,0:T(8,128)(2,1)S(1)}, u32[]{:S(2)}, u32[]{:S(2)}) %collective-permute-start.6) | collective-permute-done | bytes 196640 | tf_op jit(solution)/shard_map/ppermute | solution.py:226
  61.1 0.7 copy-done.21
  61.8 5.7 %shard_map.94 = (bf16[256,3072]{1,0:T(8,128)(2,1)}, bf16[256,3072]{1,0:T(8,128)(2,1)}, bf16[2,1536,256]{2,1,0:T(8,128)(2,1)}, bf16[2,1536,256]{2,1,0:T(8,128)(2,1)}) custom-call(bf16[256,384]{1,0:T(8,128)(2,1)} %bitcast.49, bf16[256,384]{1,0:T(8,128)(2,1)} %copy-done.10, bf16[256,384]{1,0:T(8,128)(2,1)} %copy-done.14, bf16[256,384]{1,0:T(8,128)(2,1)} %copy-done.18, ...), custom_call_target="tpu_custom_call" | custom-call | tf_op jit(solution)/shard_map/pallas_call | solution.py:301
  67.5 4.7 %collective-permute-start.14 = (bf16[2,1536,256]{2,1,0:T(8,128)(2,1)}, bf16[2,1536,256]{2,1,0:T(8,128)(2,1)S(1)}, u32[]{:S(2)}, u32[]{:S(2)}) collective-permute-start(bf16[2,1536,256]{2,1,0:T(8,128)(2,1)} %get-tuple-element.15), channel_id=1, source_target_pairs={{0,8},{8,0},{16,24},{24,16},{32,40},{40,32},{48,56},{56,48},{1,9},... | collective-permute-start | bytes 4718600 | tf_op jit(solution)/shard_map/ppermute | solution.py:230
  72.1 4.1 %collective-permute-done.14.refs_1_ = bf16[2,1536,256]{2,1,0:T(8,128)(2,1)S(1)} collective-permute-done((bf16[2,1536,256]{2,1,0:T(8,128)(2,1)}, bf16[2,1536,256]{2,1,0:T(8,128)(2,1)S(1)}, u32[]{:S(2)}, u32[]{:S(2)}) %collective-permute-start.14) | collective-permute-done | bytes 1572896 | tf_op jit(solution)/shard_map/ppermute | solution.py:230
  76.2 13.4 %shard_map.95 = (bf16[8,8,2,32,384]{4,3,2,1,0:T(8,128)(2,1)}, bf16[256,1536]{1,0:T(8,128)(2,1)}) custom-call(s32[1,16]{1,0:T(1,128)} %row_ref.3, bf16[256,3072]{1,0:T(8,128)(2,1)} %get-tuple-element.16.refs_1_, bf16[256,3072]{1,0:T(8,128)(2,1)} %get-tuple-element.17.refs_2_, bf16[12,3072,128]{2,1,0:T(8,128)(2,1)} %all-gather.2.cloned.1.call-done.refs_3_), custom_call_target="tpu_custom_call" | custom-call | tf_op jit(solution)/shard_map/pallas_call | solution.py:317
  90.1 2.1 %collective-permute-done.19.refs_3_ = bf16[256,1536]{1,0:T(8,128)(2,1)S(1)} collective-permute-done((bf16[256,1536]{1,0:T(8,128)(2,1)}, bf16[256,1536]{1,0:T(8,128)(2,1)S(1)}, u32[]{:S(2)}, u32[]{:S(2)}) %collective-permute-start.19) | collective-permute-done | bytes 786464 | tf_op jit(solution)/shard_map/ppermute | solution.py:230
  92.2 1.1 copy-done.1
  93.4 0.9 shard_map.98
  94.3 2.8 %collective-permute-start.20 = (bf16[4,12,96,128]{3,2,1,0:T(8,128)(2,1)S(1)}, bf16[4,12,96,128]{3,2,1,0:T(8,128)(2,1)S(1)}, u32[]{:S(2)}, u32[]{:S(2)}) collective-permute-start(bf16[4,12,96,128]{3,2,1,0:T(8,128)(2,1)S(1)} %shard_map.98), channel_id=1, source_target_pairs={{0,32},{8,136},{16,48},{24,152},{32,0},{40,168},{48,16},{56,184},{... | collective-permute-start | bytes 3538952 | tf_op jit(solution)/shard_map/ppermute | solution.py:244
  97.0 0.9 shard_map.99
  97.9 0.6 collective-permute-start.21
  98.5 0.9 shard_map.100
  99.4 2.4 %collective-permute-start.22 = (bf16[4,12,96,128]{3,2,1,0:T(8,128)(2,1)S(1)}, bf16[4,12,96,128]{3,2,1,0:T(8,128)(2,1)S(1)}, u32[]{:S(2)}, u32[]{:S(2)}) collective-permute-start(bf16[4,12,96,128]{3,2,1,0:T(8,128)(2,1)S(1)} %shard_map.100), channel_id=1, source_target_pairs={{0,48},{8,200},{16,0},{24,216},{32,16},{40,232},{48,32},{56,248},{... | collective-permute-start | bytes 3538952 | tf_op jit(solution)/shard_map/ppermute | solution.py:244
  101.8 0.9 shard_map.97
  102.7 8.5 %collective-permute-done.20 = bf16[4,12,96,128]{3,2,1,0:T(8,128)(2,1)S(1)} collective-permute-done((bf16[4,12,96,128]{3,2,1,0:T(8,128)(2,1)S(1)}, bf16[4,12,96,128]{3,2,1,0:T(8,128)(2,1)S(1)}, u32[]{:S(2)}, u32[]{:S(2)}) %collective-permute-start.20) | collective-permute-done | bytes 1179680 | tf_op jit(solution)/shard_map/ppermute | solution.py:244
  111.2 12.7 %collective-permute-done.21 = bf16[4,12,96,128]{3,2,1,0:T(8,128)(2,1)S(1)} collective-permute-done((bf16[4,12,96,128]{3,2,1,0:T(8,128)(2,1)S(1)}, bf16[4,12,96,128]{3,2,1,0:T(8,128)(2,1)S(1)}, u32[]{:S(2)}, u32[]{:S(2)}) %collective-permute-start.21) | collective-permute-done | bytes 1179680 | tf_op jit(solution)/shard_map/ppermute | solution.py:244
  124.5 2.2 %collective-permute-start.23 = (bf16[12,96,128]{2,1,0:T(8,128)(2,1)S(1)}, bf16[12,96,128]{2,1,0:T(8,128)(2,1)S(1)}, u32[]{:S(2)}, u32[]{:S(2)}) collective-permute-start(bf16[12,96,128]{2,1,0:T(8,128)(2,1)S(1)} %get-tuple-element.24), channel_id=1, source_target_pairs={{0,128},{8,40},{16,144},{24,56},{32,160},{40,8},{48,176},{56,24},{... | collective-permute-start | bytes 884744 | tf_op jit(solution)/shard_map/ppermute | solution.py:244
  126.7 0.9 collective-permute-start.25
  127.6 0.6 collective-permute-start.24
  128.2 3.7 %collective-permute-done.23 = bf16[12,96,128]{2,1,0:T(8,128)(2,1)S(1)} collective-permute-done((bf16[12,96,128]{2,1,0:T(8,128)(2,1)S(1)}, bf16[12,96,128]{2,1,0:T(8,128)(2,1)S(1)}, u32[]{:S(2)}, u32[]{:S(2)}) %collective-permute-start.23) | collective-permute-done | bytes 294944 | tf_op jit(solution)/shard_map/ppermute | solution.py:244
  131.9 2.8 %collective-permute-done.25 = bf16[12,96,128]{2,1,0:T(8,128)(2,1)S(1)} collective-permute-done((bf16[12,96,128]{2,1,0:T(8,128)(2,1)S(1)}, bf16[12,96,128]{2,1,0:T(8,128)(2,1)S(1)}, u32[]{:S(2)}, u32[]{:S(2)}) %collective-permute-start.25) | collective-permute-done | bytes 294944 | tf_op jit(solution)/shard_map/ppermute | solution.py:244
  135.4 0.8 slice.169
  136.2 0.7 slice_bitcast_fusion.1
  136.8 0.9 slice_bitcast_fusion
  137.8 2.5 %collective-permute-start.15 = (bf16[4,2,32,384]{3,2,1,0:T(8,128)(2,1)S(1)}, bf16[4,2,32,384]{3,2,1,0:T(8,128)(2,1)S(1)}, u32[]{:S(2)}, u32[]{:S(2)}) collective-permute-start(bf16[4,2,32,384]{3,2,1,0:T(8,128)(2,1)S(1)} %slice_bitcast_fusion), channel_id=1, source_target_pairs={{0,8},{8,0},{16,24},{24,16},{32,40},{40,32},{48,56},{56,48},{1,9},... | collective-permute-start | bytes 589832 | tf_op jit(solution)/shard_map/ppermute | solution.py:230
  140.3 0.9 slice_bitcast_fusion.2
  141.7 2.4 %collective-permute-start.17 = (bf16[2,2,32,384]{3,2,1,0:T(8,128)(2,1)S(1)}, bf16[2,2,32,384]{3,2,1,0:T(8,128)(2,1)S(1)}, u32[]{:S(2)}, u32[]{:S(2)}) collective-permute-start(bf16[2,2,32,384]{3,2,1,0:T(8,128)(2,1)S(1)} %pad_maximum_fusion.3), channel_id=1, source_target_pairs={{0,32},{8,40},{16,48},{24,56},{32,0},{40,8},{48,16},{56,24},{1,33}... | collective-permute-start | bytes 294920 | tf_op jit(solution)/shard_map/ppermute | solution.py:357
  144.1 1.5 collective-permute-start.18
  145.6 3.0 %collective-permute-done.17.refs_2_ = bf16[2,2,32,384]{3,2,1,0:T(8,128)(2,1)S(1)} collective-permute-done((bf16[2,2,32,384]{3,2,1,0:T(8,128)(2,1)S(1)}, bf16[2,2,32,384]{3,2,1,0:T(8,128)(2,1)S(1)}, u32[]{:S(2)}, u32[]{:S(2)}) %collective-permute-start.17) | collective-permute-done | bytes 98336 | tf_op jit(solution)/shard_map/ppermute | solution.py:357
  148.6 2.8 %collective-permute-done.18.refs_3_ = bf16[2,2,32,384]{3,2,1,0:T(8,128)(2,1)S(1)} collective-permute-done((bf16[2,2,32,384]{3,2,1,0:T(8,128)(2,1)S(1)}, bf16[2,2,32,384]{3,2,1,0:T(8,128)(2,1)S(1)}, u32[]{:S(2)}, u32[]{:S(2)}) %collective-permute-start.18) | collective-permute-done | bytes 98336 | tf_op jit(solution)/shard_map/ppermute | solution.py:357
  151.4 2.5 %shard_map.96 = (bf16[2,128,384]{2,1,0:T(8,128)(2,1)}, bf16[2,3,128,384]{3,2,1,0:T(8,128)(2,1)}) custom-call(s32[1,16]{1,0:T(1,128)S(1)} %copy-done.4, s32[1,8]{1,0:T(1,128)S(1)} %copy-done.5, bf16[2,3,128,384]{3,2,1,0:T(8,128)(2,1)S(1)} %bitcast.41, bf16[2,128,384]{2,1,0:T(8,128)(2,1)S(1)} %bitcast.43, ...), custom_call_target="tpu_custom_call" | custom-call | tf_op jit(solution)/shard_map/pallas_call | solution.py:358
  (76 shorter events, 3.8 us)
Async XLA Ops:
  7.2 69.1 %all-gather.2.cloned.1.call-start = ((), (), s32[]{:S(2)}) async-start(), calls=%async_computation.2 | async-start | bytes 9732096 | tf_op jit(solution)/shard_map/all_gather | solution.py:278
  8.9 127.9 %reduce-scatter.2.cloned.1.call-start = ((), (), s32[]{:S(2)}) async-start(), calls=%async_computation.3 | async-start | bytes 3538944 | tf_op jit(solution)/shard_map/reduce_scatter | solution.py:337
  27.6 32.7 %copy-start.6 = (bf16[8,1,2,16,384]{4,3,2,1,0:T(8,128)(2,1)}, bf16[8,1,2,16,384]{4,3,2,1,0:T(8,128)(2,1)S(1)}, u32[]{:S(2)}) copy-start(bf16[8,1,2,16,384]{4,3,2,1,0:T(8,128)(2,1)S(1)} %get-tuple-element.31) | copy-start | bytes 589828
  27.6 32.7 %copy-start.7 = (bf16[8,1,2,16,384]{4,3,2,1,0:T(8,128)(2,1)}, bf16[8,1,2,16,384]{4,3,2,1,0:T(8,128)(2,1)S(1)}, u32[]{:S(2)}) copy-start(bf16[8,1,2,16,384]{4,3,2,1,0:T(8,128)(2,1)S(1)} %get-tuple-element.32) | copy-start | bytes 589828
  27.7 9.3 %collective-permute-start.3 = (bf16[256,384]{1,0:T(8,128)(2,1)S(1)}, bf16[256,384]{1,0:T(8,128)(2,1)S(1)}, u32[]{:S(2)}, u32[]{:S(2)}) collective-permute-start(bf16[256,384]{1,0:T(8,128)(2,1)S(1)} %bitcast.47), channel_id=1, source_target_pairs={{0,1},{1,2},{2,3},{3,4},{4,5},{5,6},{6,7},{7,0},{8,9},{9,10},{10,1... | collective-permute-start | bytes 589832 | tf_op jit(solution)/shard_map/ppermute | solution.py:226
  28.6 8.4 %collective-permute-start.7 = (bf16[256,384]{1,0:T(8,128)(2,1)S(1)}, bf16[256,384]{1,0:T(8,128)(2,1)S(1)}, u32[]{:S(2)}, u32[]{:S(2)}) collective-permute-start(bf16[256,384]{1,0:T(8,128)(2,1)S(1)} %bitcast.44), channel_id=1, source_target_pairs={{0,7},{1,0},{2,1},{3,2},{4,3},{5,4},{6,5},{7,6},{8,15},{9,8},{10,9... | collective-permute-start | bytes 589832 | tf_op jit(solution)/shard_map/ppermute | solution.py:226
  32.6 7.6 %collective-permute-start = (bf16[256,384]{1,0:T(8,128)(2,1)S(1)}, bf16[256,384]{1,0:T(8,128)(2,1)S(1)}, u32[]{:S(2)}, u32[]{:S(2)}) collective-permute-start(bf16[256,384]{1,0:T(8,128)(2,1)S(1)} %bitcast.48), channel_id=1, source_target_pairs={{0,7},{1,0},{2,1},{3,2},{4,3},{5,4},{6,5},{7,6},{8,15},{9,8},{10,9... | collective-permute-start | bytes 589832 | tf_op jit(solution)/shard_map/ppermute | solution.py:226
  34.0 9.7 %collective-permute-start.11 = (bf16[256,384]{1,0:T(8,128)(2,1)S(1)}, bf16[256,384]{1,0:T(8,128)(2,1)S(1)}, u32[]{:S(2)}, u32[]{:S(2)}) collective-permute-start(bf16[256,384]{1,0:T(8,128)(2,1)S(1)} %bitcast.45), channel_id=1, source_target_pairs={{0,1},{1,2},{2,3},{3,4},{4,5},{5,6},{6,7},{7,0},{8,9},{9,10},{10,1... | collective-permute-start | bytes 589832 | tf_op jit(solution)/shard_map/ppermute | solution.py:226
  36.9 23.5 %copy-start.8 = (bf16[256,384]{1,0:T(8,128)(2,1)}, bf16[256,384]{1,0:T(8,128)(2,1)S(1)}, u32[]{:S(2)}) copy-start(bf16[256,384]{1,0:T(8,128)(2,1)S(1)} %collective-permute-done.3.refs_7_) | copy-start | bytes 589828
  36.9 8.1 %collective-permute-start.4 = (bf16[256,384]{1,0:T(8,128)(2,1)S(1)}, bf16[256,384]{1,0:T(8,128)(2,1)S(1)}, u32[]{:S(2)}, u32[]{:S(2)}) collective-permute-start(bf16[256,384]{1,0:T(8,128)(2,1)S(1)} %collective-permute-done.3.refs_7_), channel_id=1, source_target_pairs={{0,1},{1,2},{2,3},{3,4},{4,5},{5,6},{6,7},{7,0},{8,9},{9,10},{10,1... | collective-permute-start | bytes 589832 | tf_op jit(solution)/shard_map/ppermute | solution.py:226
  36.9 23.5 %copy-start.9 = (bf16[256,384]{1,0:T(8,128)(2,1)}, bf16[256,384]{1,0:T(8,128)(2,1)S(1)}, u32[]{:S(2)}) copy-start(bf16[256,384]{1,0:T(8,128)(2,1)S(1)} %collective-permute-done.7.refs_9_) | copy-start | bytes 589828
  37.0 8.1 %collective-permute-start.8 = (bf16[256,384]{1,0:T(8,128)(2,1)S(1)}, bf16[256,384]{1,0:T(8,128)(2,1)S(1)}, u32[]{:S(2)}, u32[]{:S(2)}) collective-permute-start(bf16[256,384]{1,0:T(8,128)(2,1)S(1)} %collective-permute-done.7.refs_9_), channel_id=1, source_target_pairs={{0,7},{1,0},{2,1},{3,2},{4,3},{5,4},{6,5},{7,6},{8,15},{9,8},{10,9... | collective-permute-start | bytes 589832 | tf_op jit(solution)/shard_map/ppermute | solution.py:226
  40.2 20.2 %copy-start.10 = (bf16[256,384]{1,0:T(8,128)(2,1)}, bf16[256,384]{1,0:T(8,128)(2,1)S(1)}, u32[]{:S(2)}) copy-start(bf16[256,384]{1,0:T(8,128)(2,1)S(1)} %collective-permute-done.refs_1_) | copy-start | bytes 589828
  40.2 7.7 %collective-permute-start.1 = (bf16[256,384]{1,0:T(8,128)(2,1)S(1)}, bf16[256,384]{1,0:T(8,128)(2,1)S(1)}, u32[]{:S(2)}, u32[]{:S(2)}) collective-permute-start(bf16[256,384]{1,0:T(8,128)(2,1)S(1)} %collective-permute-done.refs_1_), channel_id=1, source_target_pairs={{0,7},{1,0},{2,1},{3,2},{4,3},{5,4},{6,5},{7,6},{8,15},{9,8},{10,9... | collective-permute-start | bytes 589832 | tf_op jit(solution)/shard_map/ppermute | solution.py:226
  43.7 16.7 %copy-start.11 = (bf16[256,384]{1,0:T(8,128)(2,1)}, bf16[256,384]{1,0:T(8,128)(2,1)S(1)}, u32[]{:S(2)}) copy-start(bf16[256,384]{1,0:T(8,128)(2,1)S(1)} %collective-permute-done.11.refs_15_) | copy-start | bytes 589828
  43.7 7.7 %collective-permute-start.12 = (bf16[256,384]{1,0:T(8,128)(2,1)S(1)}, bf16[256,384]{1,0:T(8,128)(2,1)S(1)}, u32[]{:S(2)}, u32[]{:S(2)}) collective-permute-start(bf16[256,384]{1,0:T(8,128)(2,1)S(1)} %collective-permute-done.11.refs_15_), channel_id=1, source_target_pairs={{0,1},{1,2},{2,3},{3,4},{4,5},{5,6},{6,7},{7,0},{8,9},{9,10},{10,1... | collective-permute-start | bytes 589832 | tf_op jit(solution)/shard_map/ppermute | solution.py:226
  45.0 15.4 %copy-start.12 = (bf16[256,384]{1,0:T(8,128)(2,1)}, bf16[256,384]{1,0:T(8,128)(2,1)S(1)}, u32[]{:S(2)}) copy-start(bf16[256,384]{1,0:T(8,128)(2,1)S(1)} %collective-permute-done.4.refs_6_) | copy-start | bytes 589828
  45.0 7.2 %collective-permute-start.5 = (bf16[256,384]{1,0:T(8,128)(2,1)S(1)}, bf16[256,384]{1,0:T(8,128)(2,1)S(1)}, u32[]{:S(2)}, u32[]{:S(2)}) collective-permute-start(bf16[256,384]{1,0:T(8,128)(2,1)S(1)} %collective-permute-done.4.refs_6_), channel_id=1, source_target_pairs={{0,1},{1,2},{2,3},{3,4},{4,5},{5,6},{6,7},{7,0},{8,9},{9,10},{10,1... | collective-permute-start | bytes 589832 | tf_op jit(solution)/shard_map/ppermute | solution.py:226
  45.0 15.4 %copy-start.13 = (bf16[256,384]{1,0:T(8,128)(2,1)}, bf16[256,384]{1,0:T(8,128)(2,1)S(1)}, u32[]{:S(2)}) copy-start(bf16[256,384]{1,0:T(8,128)(2,1)S(1)} %collective-permute-done.8.refs_10_) | copy-start | bytes 589828
  45.0 7.2 %collective-permute-start.9 = (bf16[256,384]{1,0:T(8,128)(2,1)S(1)}, bf16[256,384]{1,0:T(8,128)(2,1)S(1)}, u32[]{:S(2)}, u32[]{:S(2)}) collective-permute-start(bf16[256,384]{1,0:T(8,128)(2,1)S(1)} %collective-permute-done.8.refs_10_), channel_id=1, source_target_pairs={{0,7},{1,0},{2,1},{3,2},{4,3},{5,4},{6,5},{7,6},{8,15},{9,8},{10,9... | collective-permute-start | bytes 589832 | tf_op jit(solution)/shard_map/ppermute | solution.py:226
  47.9 12.6 %copy-start.14 = (bf16[256,384]{1,0:T(8,128)(2,1)}, bf16[256,384]{1,0:T(8,128)(2,1)S(1)}, u32[]{:S(2)}) copy-start(bf16[256,384]{1,0:T(8,128)(2,1)S(1)} %collective-permute-done.1.refs_2_) | copy-start | bytes 589828
  47.9 8.3 %collective-permute-start.2 = (bf16[256,384]{1,0:T(8,128)(2,1)S(1)}, bf16[256,384]{1,0:T(8,128)(2,1)S(1)}, u32[]{:S(2)}, u32[]{:S(2)}) collective-permute-start(bf16[256,384]{1,0:T(8,128)(2,1)S(1)} %collective-permute-done.1.refs_2_), channel_id=1, source_target_pairs={{0,7},{1,0},{2,1},{3,2},{4,3},{5,4},{6,5},{7,6},{8,15},{9,8},{10,9... | collective-permute-start | bytes 589832 | tf_op jit(solution)/shard_map/ppermute | solution.py:226
  51.4 9.1 %copy-start.15 = (bf16[256,384]{1,0:T(8,128)(2,1)}, bf16[256,384]{1,0:T(8,128)(2,1)S(1)}, u32[]{:S(2)}) copy-start(bf16[256,384]{1,0:T(8,128)(2,1)S(1)} %collective-permute-done.12.refs_14_) | copy-start | bytes 589828
  51.4 6.9 %collective-permute-start.13 = (bf16[256,384]{1,0:T(8,128)(2,1)S(1)}, bf16[256,384]{1,0:T(8,128)(2,1)S(1)}, u32[]{:S(2)}, u32[]{:S(2)}) collective-permute-start(bf16[256,384]{1,0:T(8,128)(2,1)S(1)} %collective-permute-done.12.refs_14_), channel_id=1, source_target_pairs={{0,1},{1,2},{2,3},{3,4},{4,5},{5,6},{6,7},{7,0},{8,9},{9,10},{10,1... | collective-permute-start | bytes 589832 | tf_op jit(solution)/shard_map/ppermute | solution.py:226
  52.2 8.3 %copy-start.16 = (bf16[256,384]{1,0:T(8,128)(2,1)}, bf16[256,384]{1,0:T(8,128)(2,1)S(1)}, u32[]{:S(2)}) copy-start(bf16[256,384]{1,0:T(8,128)(2,1)S(1)} %collective-permute-done.5.refs_5_) | copy-start | bytes 589828
  52.2 8.2 %collective-permute-start.6 = (bf16[256,384]{1,0:T(8,128)(2,1)S(1)}, bf16[256,384]{1,0:T(8,128)(2,1)S(1)}, u32[]{:S(2)}, u32[]{:S(2)}) collective-permute-start(bf16[256,384]{1,0:T(8,128)(2,1)S(1)} %collective-permute-done.5.refs_5_), channel_id=1, source_target_pairs={{0,1},{1,2},{2,3},{3,4},{4,5},{5,6},{6,7},{7,0},{8,9},{9,10},{10,1... | collective-permute-start | bytes 589832 | tf_op jit(solution)/shard_map/ppermute | solution.py:226
  52.2 8.3 %copy-start.17 = (bf16[256,384]{1,0:T(8,128)(2,1)}, bf16[256,384]{1,0:T(8,128)(2,1)S(1)}, u32[]{:S(2)}) copy-start(bf16[256,384]{1,0:T(8,128)(2,1)S(1)} %collective-permute-done.9.refs_11_) | copy-start | bytes 589828
  52.2 8.1 %collective-permute-start.10 = (bf16[256,384]{1,0:T(8,128)(2,1)S(1)}, bf16[256,384]{1,0:T(8,128)(2,1)S(1)}, u32[]{:S(2)}, u32[]{:S(2)}) collective-permute-start(bf16[256,384]{1,0:T(8,128)(2,1)S(1)} %collective-permute-done.9.refs_11_), channel_id=1, source_target_pairs={{0,7},{1,0},{2,1},{3,2},{4,3},{5,4},{6,5},{7,6},{8,15},{9,8},{10,9... | collective-permute-start | bytes 589832 | tf_op jit(solution)/shard_map/ppermute | solution.py:226
  56.2 4.3 %copy-start.18 = (bf16[256,384]{1,0:T(8,128)(2,1)}, bf16[256,384]{1,0:T(8,128)(2,1)S(1)}, u32[]{:S(2)}) copy-start(bf16[256,384]{1,0:T(8,128)(2,1)S(1)} %collective-permute-done.2.refs_3_) | copy-start | bytes 589828
  58.3 2.2 %copy-start.19 = (bf16[256,384]{1,0:T(8,128)(2,1)}, bf16[256,384]{1,0:T(8,128)(2,1)S(1)}, u32[]{:S(2)}) copy-start(bf16[256,384]{1,0:T(8,128)(2,1)S(1)} %collective-permute-done.13.refs_13_) | copy-start | bytes 589828
  67.5 8.7 %collective-permute-start.14 = (bf16[2,1536,256]{2,1,0:T(8,128)(2,1)}, bf16[2,1536,256]{2,1,0:T(8,128)(2,1)S(1)}, u32[]{:S(2)}, u32[]{:S(2)}) collective-permute-start(bf16[2,1536,256]{2,1,0:T(8,128)(2,1)} %get-tuple-element.15), channel_id=1, source_target_pairs={{0,8},{8,0},{16,24},{24,16},{32,40},{40,32},{48,56},{56,48},{1,9},... | collective-permute-start | bytes 4718600 | tf_op jit(solution)/shard_map/ppermute | solution.py:230
  89.6 2.6 %copy-start = (bf16[2,1536,256]{2,1,0:T(8,128)(2,1)S(1)}, bf16[2,1536,256]{2,1,0:T(8,128)(2,1)}, u32[]{:S(2)}) copy-start(bf16[2,1536,256]{2,1,0:T(8,128)(2,1)} %get-tuple-element.21.refs_0_) | copy-start | bytes 4718596
  89.7 2.6 %collective-permute-start.19 = (bf16[256,1536]{1,0:T(8,128)(2,1)}, bf16[256,1536]{1,0:T(8,128)(2,1)S(1)}, u32[]{:S(2)}, u32[]{:S(2)}) collective-permute-start(bf16[256,1536]{1,0:T(8,128)(2,1)} %get-tuple-element.23.refs_2_), channel_id=1, source_target_pairs={{0,8},{8,0},{16,24},{24,16},{32,40},{40,32},{48,56},{56,48},{1,9},... | collective-permute-start | bytes 2359304 | tf_op jit(solution)/shard_map/ppermute | solution.py:230
  92.2 1.1 copy-start.1
  94.3 17.0 %collective-permute-start.20 = (bf16[4,12,96,128]{3,2,1,0:T(8,128)(2,1)S(1)}, bf16[4,12,96,128]{3,2,1,0:T(8,128)(2,1)S(1)}, u32[]{:S(2)}, u32[]{:S(2)}) collective-permute-start(bf16[4,12,96,128]{3,2,1,0:T(8,128)(2,1)S(1)} %shard_map.98), channel_id=1, source_target_pairs={{0,32},{8,136},{16,48},{24,152},{32,0},{40,168},{48,16},{56,184},{... | collective-permute-start | bytes 3538952 | tf_op jit(solution)/shard_map/ppermute | solution.py:244
  97.9 26.0 %collective-permute-start.21 = (bf16[4,12,96,128]{3,2,1,0:T(8,128)(2,1)S(1)}, bf16[4,12,96,128]{3,2,1,0:T(8,128)(2,1)S(1)}, u32[]{:S(2)}, u32[]{:S(2)}) collective-permute-start(bf16[4,12,96,128]{3,2,1,0:T(8,128)(2,1)S(1)} %shard_map.99), channel_id=1, source_target_pairs={{0,16},{8,72},{16,32},{24,88},{32,48},{40,104},{48,0},{56,120},{64... | collective-permute-start | bytes 3538952 | tf_op jit(solution)/shard_map/ppermute | solution.py:244
  99.4 24.6 %collective-permute-start.22 = (bf16[4,12,96,128]{3,2,1,0:T(8,128)(2,1)S(1)}, bf16[4,12,96,128]{3,2,1,0:T(8,128)(2,1)S(1)}, u32[]{:S(2)}, u32[]{:S(2)}) collective-permute-start(bf16[4,12,96,128]{3,2,1,0:T(8,128)(2,1)S(1)} %shard_map.100), channel_id=1, source_target_pairs={{0,48},{8,200},{16,0},{24,216},{32,16},{40,232},{48,32},{56,248},{... | collective-permute-start | bytes 3538952 | tf_op jit(solution)/shard_map/ppermute | solution.py:244
  124.5 7.5 %collective-permute-start.23 = (bf16[12,96,128]{2,1,0:T(8,128)(2,1)S(1)}, bf16[12,96,128]{2,1,0:T(8,128)(2,1)S(1)}, u32[]{:S(2)}, u32[]{:S(2)}) collective-permute-start(bf16[12,96,128]{2,1,0:T(8,128)(2,1)S(1)} %get-tuple-element.24), channel_id=1, source_target_pairs={{0,128},{8,40},{16,144},{24,56},{32,160},{40,8},{48,176},{56,24},{... | collective-permute-start | bytes 884744 | tf_op jit(solution)/shard_map/ppermute | solution.py:244
  126.7 8.0 %collective-permute-start.25 = (bf16[12,96,128]{2,1,0:T(8,128)(2,1)S(1)}, bf16[12,96,128]{2,1,0:T(8,128)(2,1)S(1)}, u32[]{:S(2)}, u32[]{:S(2)}) collective-permute-start(bf16[12,96,128]{2,1,0:T(8,128)(2,1)S(1)} %get-tuple-element.25), channel_id=1, source_target_pairs={{0,192},{8,56},{16,208},{24,8},{32,224},{40,24},{48,240},{56,40},{... | collective-permute-start | bytes 884744 | tf_op jit(solution)/shard_map/ppermute | solution.py:244
  127.6 7.5 %collective-permute-start.24 = (bf16[12,96,128]{2,1,0:T(8,128)(2,1)S(1)}, bf16[12,96,128]{2,1,0:T(8,128)(2,1)S(1)}, u32[]{:S(2)}, u32[]{:S(2)}) collective-permute-start(bf16[12,96,128]{2,1,0:T(8,128)(2,1)S(1)} %get-tuple-element.26), channel_id=1, source_target_pairs={{0,64},{8,24},{16,80},{24,40},{32,96},{40,56},{48,112},{56,8},{64,... | collective-permute-start | bytes 884744 | tf_op jit(solution)/shard_map/ppermute | solution.py:244
  136.1 15.3 %copy-start.2 = (bf16[1,2,128,3,384]{4,2,3,1,0:T(8,128)(2,1)S(1)}, bf16[1,2,128,3,384]{4,2,3,1,0:T(8,128)(2,1)}, u32[]{:S(2)}) copy-start(bf16[1,2,128,3,384]{4,2,3,1,0:T(8,128)(2,1)} %param.6) | copy-start | bytes 1769476
  136.2 15.3 %copy-start.3 = (bf16[1,2,128,384]{3,2,1,0:T(8,128)(2,1)S(1)}, bf16[1,2,128,384]{3,2,1,0:T(8,128)(2,1)}, u32[]{:S(2)}) copy-start(bf16[1,2,128,384]{3,2,1,0:T(8,128)(2,1)} %param.9) | copy-start | bytes 589828
  136.2 15.3 %copy-start.4 = (s32[1,16]{1,0:T(1,128)S(1)}, s32[1,16]{1,0:T(1,128)}, u32[]{:S(2)}) copy-start(s32[1,16]{1,0:T(1,128)} %row_ref.3) | copy-start | bytes 196
  136.2 15.3 %copy-start.5 = (s32[1,8]{1,0:T(1,128)S(1)}, s32[1,8]{1,0:T(1,128)}, u32[]{:S(2)}) copy-start(s32[1,8]{1,0:T(1,128)} %patch_ref.3) | copy-start | bytes 100
  137.8 3.6 %collective-permute-start.15 = (bf16[4,2,32,384]{3,2,1,0:T(8,128)(2,1)S(1)}, bf16[4,2,32,384]{3,2,1,0:T(8,128)(2,1)S(1)}, u32[]{:S(2)}, u32[]{:S(2)}) collective-permute-start(bf16[4,2,32,384]{3,2,1,0:T(8,128)(2,1)S(1)} %slice_bitcast_fusion), channel_id=1, source_target_pairs={{0,8},{8,0},{16,24},{24,16},{32,40},{40,32},{48,56},{56,48},{1,9},... | collective-permute-start | bytes 589832 | tf_op jit(solution)/shard_map/ppermute | solution.py:230
  141.4 4.2 %collective-permute-start.16 = (bf16[2,2,32,384]{3,2,1,0:T(8,128)(2,1)S(1)}, bf16[2,2,32,384]{3,2,1,0:T(8,128)(2,1)S(1)}, u32[]{:S(2)}, u32[]{:S(2)}) collective-permute-start(bf16[2,2,32,384]{3,2,1,0:T(8,128)(2,1)S(1)} %pad_maximum_fusion.2), channel_id=1, source_target_pairs={{0,16},{8,24},{16,0},{24,8},{32,48},{40,56},{48,32},{56,40},{1,17}... | collective-permute-start | bytes 294920 | tf_op jit(solution)/shard_map/ppermute | solution.py:357
  141.7 6.9 %collective-permute-start.17 = (bf16[2,2,32,384]{3,2,1,0:T(8,128)(2,1)S(1)}, bf16[2,2,32,384]{3,2,1,0:T(8,128)(2,1)S(1)}, u32[]{:S(2)}, u32[]{:S(2)}) collective-permute-start(bf16[2,2,32,384]{3,2,1,0:T(8,128)(2,1)S(1)} %pad_maximum_fusion.3), channel_id=1, source_target_pairs={{0,32},{8,40},{16,48},{24,56},{32,0},{40,8},{48,16},{56,24},{1,33}... | collective-permute-start | bytes 294920 | tf_op jit(solution)/shard_map/ppermute | solution.py:357
  144.1 7.3 %collective-permute-start.18 = (bf16[2,2,32,384]{3,2,1,0:T(8,128)(2,1)S(1)}, bf16[2,2,32,384]{3,2,1,0:T(8,128)(2,1)S(1)}, u32[]{:S(2)}, u32[]{:S(2)}) collective-permute-start(bf16[2,2,32,384]{3,2,1,0:T(8,128)(2,1)S(1)} %pad_maximum_fusion.4), channel_id=1, source_target_pairs={{0,48},{8,56},{16,32},{24,40},{32,16},{40,24},{48,0},{56,8},{1,49}... | collective-permute-start | bytes 294920 | tf_op jit(solution)/shard_map/ppermute | solution.py:357
  (2 other events, 1.4 us)
Sparse Core Ops, SparseCore 0:
  11.2 64.8 all-gather.1
  89.8 42.9 reduce-scatter.1

commit v7 on v5

--- a/solution.py
+++ b/solution.py
@@ -178,7 +178,7 @@
             both_ref[:, (3 * h + i) * HD : (3 * h + i + 1) * HD] = grads[h][i]
         both_ref[:, 3 * width + h * HD : 3 * width + (h + 1) * HD] = mixed[h]
     stores = []
-    pair = 4
+    pair = 8
     for first in range(0, ranks, pair):
         w_part = w_ref.at[first * width : (first + pair) * width]
         projected = dot(both_ref[:, 3 * width :], w_part[:, 3 * width :], NT).astype(BF)

time: 158 us -> 158 us (level)
  transfers between devices with their start and end apart: 25 -> 25, of which waited for: 14 -> 15; matrix products, arithmetic and copies ran while one was open for 2% -> 2% of each run, Pallas kernels for 8% -> 8%
where the time goes in v7:
time: 158 us
  waiting for transfers between devices  47.1 us (30%)
  starting transfers between devices  44.1 us (28%)
  Pallas kernels  29.1 us (18%)
  blocking collectives  14.7 us (9%)
  between operations  14.4 us (9%)
  local copies, waits for them, and re-layouts  4.88 us (3%)
  other arithmetic  3.66 us (2%)
    ppermute x14, starting transfers between devices, shift(): lax.ppermute(value, axis, [(i, (i + step) % size) for i in range(size)])  21.8 us
    ppermute x6, waiting for transfers between devices, spread(): return lax.ppermute(value, ('clip', 'frame'), pairs)  21.3 us
    all_to_all x1, blocking collectives, body(): lax.all_to_all(sent, 'frame', split_axis=0, concat_axis=0, tiled=True)  14.7 us
    pallas_call x1, Pallas kernels, body(): pl.pallas_call(lambda *refs: temporal_kernel(heads, *refs), out_shape=[ja...  13.5 us
    ppermute x14, waiting for transfers between devices, shift(): lax.ppermute(value, axis, [(i, (i + step) % size) for i in range(size)])  10.9 us
    ppermute x6, starting transfers between devices, spread(): return lax.ppermute(value, ('clip', 'frame'), pairs)  9.51 us
    all_to_all x1, starting transfers between devices, body(): lax.all_to_all(own_sums, 'frame', split_axis=0, concat_axis=0, tiled=True)  7.67 us
    ppermute x2, waiting for transfers between devices, pair_swap(): return lax.ppermute(value, 'frame', [(i, i ^ 1) for i in range(8)])  6.22 us
  transfers between devices with their start and end apart: 25, of which 15 were waited for; matrix products, arithmetic and copies ran while one was open for 2% of the time, Pallas kernels for 8%

profile of v7, /device:TPU:1, one launch (start us, length us, event | category | flops | bytes accessed | tf_op | source)
XLA Modules:
  0.0 158.0 jit_solution(1739633544993303009)
XLA Ops:
  7.2 1.7 %pad_maximum_fusion = bf16[12,96,128]{2,1,0:T(8,128)(2,1)} fusion(bf16[3,96,128]{2,1,0:T(8,128)(2,1)} %bitcast.44, bf16[9,96,128]{2,1,0:T(8,128)(2,1)} %bitcast.43), kind=kLoop, calls=%fused_computation.11 | loop fusion | flops 147456 | bytes 589824 | tf_op jit(solution)/shard_map/concatenate | solution.py:271
  9.0 3.9 %shard_map.93 = bf16[8,2,2,16,384]{4,3,2,1,0:T(8,128)(2,1)} custom-call(s32[1,16]{1,0:T(1,128)} %row_ref.3, s32[1,8]{1,0:T(1,128)} %patch_ref.3, bf16[2,3,128,384]{3,2,1,0:T(8,128)(2,1)} %bitcast.31, bf16[2,128,384]{2,1,0:T(8,128)(2,1)} %bitcast.33), custom_call_target="tpu_custom_call" | custom-call | tf_op jit(solution)/shard_map/pallas_call | solution.py:282
  12.9 14.7 %all_to_all.10 = bf16[8,2,2,16,384]{4,3,2,1,0:T(8,128)(2,1)S(1)} all-to-all(bf16[8,2,2,16,384]{4,3,2,1,0:T(8,128)(2,1)} %shard_map.93), channel_id=1, replica_groups=mesh['clip'=4,'frame'=8,'tensor'=8] {'frame'}, dimensions={0} | all-to-all | bytes 786432 | tf_op jit(solution)/shard_map/all_to_all | solution.py:290
  27.7 0.9 collective-permute-start.3
  28.6 4.0 %collective-permute-start.7 = (bf16[256,384]{1,0:T(8,128)(2,1)S(1)}, bf16[256,384]{1,0:T(8,128)(2,1)S(1)}, u32[]{:S(2)}, u32[]{:S(2)}) collective-permute-start(bf16[256,384]{1,0:T(8,128)(2,1)S(1)} %bitcast.35), channel_id=1, source_target_pairs={{0,7},{1,0},{2,1},{3,2},{4,3},{5,4},{6,5},{7,6},{8,15},{9,8},{10,9... | collective-permute-start | bytes 589832 | tf_op jit(solution)/shard_map/ppermute | solution.py:223
  32.6 1.4 collective-permute-start
  34.1 2.9 %collective-permute-done.3.refs_7_ = bf16[256,384]{1,0:T(8,128)(2,1)S(1)} collective-permute-done((bf16[256,384]{1,0:T(8,128)(2,1)S(1)}, bf16[256,384]{1,0:T(8,128)(2,1)S(1)}, u32[]{:S(2)}, u32[]{:S(2)}) %collective-permute-start.3) | collective-permute-done | bytes 196640 | tf_op jit(solution)/shard_map/ppermute | solution.py:223
  37.0 2.7 %collective-permute-start.8 = (bf16[256,384]{1,0:T(8,128)(2,1)S(1)}, bf16[256,384]{1,0:T(8,128)(2,1)S(1)}, u32[]{:S(2)}, u32[]{:S(2)}) collective-permute-start(bf16[256,384]{1,0:T(8,128)(2,1)S(1)} %collective-permute-done.7.refs_9_), channel_id=1, source_target_pairs={{0,7},{1,0},{2,1},{3,2},{4,3},{5,4},{6,5},{7,6},{8,15},{9,8},{10,9... | collective-permute-start | bytes 589832 | tf_op jit(solution)/shard_map/ppermute | solution.py:223
  39.6 0.6 collective-permute-done.refs_1_
  40.2 3.5 %collective-permute-start.1 = (bf16[256,384]{1,0:T(8,128)(2,1)S(1)}, bf16[256,384]{1,0:T(8,128)(2,1)S(1)}, u32[]{:S(2)}, u32[]{:S(2)}) collective-permute-start(bf16[256,384]{1,0:T(8,128)(2,1)S(1)} %collective-permute-done.refs_1_), channel_id=1, source_target_pairs={{0,7},{1,0},{2,1},{3,2},{4,3},{5,4},{6,5},{7,6},{8,15},{9,8},{10,9... | collective-permute-start | bytes 589832 | tf_op jit(solution)/shard_map/ppermute | solution.py:223
  43.7 1.3 collective-permute-done.4.refs_6_
  45.0 2.7 %collective-permute-start.9 = (bf16[256,384]{1,0:T(8,128)(2,1)S(1)}, bf16[256,384]{1,0:T(8,128)(2,1)S(1)}, u32[]{:S(2)}, u32[]{:S(2)}) collective-permute-start(bf16[256,384]{1,0:T(8,128)(2,1)S(1)} %collective-permute-done.8.refs_10_), channel_id=1, source_target_pairs={{0,7},{1,0},{2,1},{3,2},{4,3},{5,4},{6,5},{7,6},{8,15},{9,8},{10,9... | collective-permute-start | bytes 589832 | tf_op jit(solution)/shard_map/ppermute | solution.py:223
  47.9 3.5 %collective-permute-start.2 = (bf16[256,384]{1,0:T(8,128)(2,1)S(1)}, bf16[256,384]{1,0:T(8,128)(2,1)S(1)}, u32[]{:S(2)}, u32[]{:S(2)}) collective-permute-start(bf16[256,384]{1,0:T(8,128)(2,1)S(1)} %collective-permute-done.1.refs_2_), channel_id=1, source_target_pairs={{0,7},{1,0},{2,1},{3,2},{4,3},{5,4},{6,5},{7,6},{8,15},{9,8},{10,9... | collective-permute-start | bytes 589832 | tf_op jit(solution)/shard_map/ppermute | solution.py:223
  51.4 0.8 collective-permute-done.5.refs_5_
  52.2 3.0 %collective-permute-start.10 = (bf16[256,384]{1,0:T(8,128)(2,1)S(1)}, bf16[256,384]{1,0:T(8,128)(2,1)S(1)}, u32[]{:S(2)}, u32[]{:S(2)}) collective-permute-start(bf16[256,384]{1,0:T(8,128)(2,1)S(1)} %collective-permute-done.9.refs_11_), channel_id=1, source_target_pairs={{0,7},{1,0},{2,1},{3,2},{4,3},{5,4},{6,5},{7,6},{8,15},{9,8},{10,9... | collective-permute-start | bytes 589832 | tf_op jit(solution)/shard_map/ppermute | solution.py:223
  55.2 1.0 collective-permute-done.2.refs_3_
  56.2 2.1 %collective-permute-done.13.refs_13_ = bf16[256,384]{1,0:T(8,128)(2,1)S(1)} collective-permute-done((bf16[256,384]{1,0:T(8,128)(2,1)S(1)}, bf16[256,384]{1,0:T(8,128)(2,1)S(1)}, u32[]{:S(2)}, u32[]{:S(2)}) %collective-permute-start.13) | collective-permute-done | bytes 196640 | tf_op jit(solution)/shard_map/ppermute | solution.py:223
  58.3 2.1 %collective-permute-done.6.refs_4_ = bf16[256,384]{1,0:T(8,128)(2,1)S(1)} collective-permute-done((bf16[256,384]{1,0:T(8,128)(2,1)S(1)}, bf16[256,384]{1,0:T(8,128)(2,1)S(1)}, u32[]{:S(2)}, u32[]{:S(2)}) %collective-permute-start.6) | collective-permute-done | bytes 196640 | tf_op jit(solution)/shard_map/ppermute | solution.py:223
  60.5 0.6 copy-done.24
  61.1 0.7 copy-done.25
  61.8 5.7 %shard_map.94 = (bf16[256,3072]{1,0:T(8,128)(2,1)}, bf16[256,3072]{1,0:T(8,128)(2,1)}, bf16[2,1536,256]{2,1,0:T(8,128)(2,1)}, bf16[2,1536,256]{2,1,0:T(8,128)(2,1)}) custom-call(bf16[256,384]{1,0:T(8,128)(2,1)} %bitcast.40, bf16[256,384]{1,0:T(8,128)(2,1)} %copy-done.14, bf16[256,384]{1,0:T(8,128)(2,1)} %copy-done.18, bf16[256,384]{1,0:T(8,128)(2,1)} %copy-done.22, ...), custom_call_target="tpu_custom_call" | custom-call | tf_op jit(solution)/shard_map/pallas_call | solution.py:298
  67.5 4.7 %collective-permute-start.14 = (bf16[2,1536,256]{2,1,0:T(8,128)(2,1)}, bf16[2,1536,256]{2,1,0:T(8,128)(2,1)S(1)}, u32[]{:S(2)}, u32[]{:S(2)}) collective-permute-start(bf16[2,1536,256]{2,1,0:T(8,128)(2,1)} %get-tuple-element.15), channel_id=1, source_target_pairs={{0,8},{8,0},{16,24},{24,16},{32,40},{40,32},{48,56},{56,48},{1,9},... | collective-permute-start | bytes 4718600 | tf_op jit(solution)/shard_map/ppermute | solution.py:227
  72.1 4.1 %collective-permute-done.14.refs_1_ = bf16[2,1536,256]{2,1,0:T(8,128)(2,1)S(1)} collective-permute-done((bf16[2,1536,256]{2,1,0:T(8,128)(2,1)}, bf16[2,1536,256]{2,1,0:T(8,128)(2,1)S(1)}, u32[]{:S(2)}, u32[]{:S(2)}) %collective-permute-start.14) | collective-permute-done | bytes 1572896 | tf_op jit(solution)/shard_map/ppermute | solution.py:227
  76.2 13.5 %shard_map.95 = (bf16[8,8,2,32,384]{4,3,2,1,0:T(8,128)(2,1)}, bf16[256,1536]{1,0:T(8,128)(2,1)}) custom-call(s32[1,16]{1,0:T(1,128)} %row_ref.3, bf16[256,3072]{1,0:T(8,128)(2,1)} %get-tuple-element.16.refs_1_, bf16[256,3072]{1,0:T(8,128)(2,1)} %get-tuple-element.17.refs_2_, bf16[12,3072,128]{2,1,0:T(8,128)(2,1)} %all-gather.2.cloned.1.call-done.refs_3_), custom_call_target="tpu_custom_call" | custom-call | tf_op jit(solution)/shard_map/pallas_call | solution.py:314
  89.8 0.5 collective-permute-start.15
  90.2 2.1 %collective-permute-done.15.refs_3_ = bf16[256,1536]{1,0:T(8,128)(2,1)S(1)} collective-permute-done((bf16[256,1536]{1,0:T(8,128)(2,1)}, bf16[256,1536]{1,0:T(8,128)(2,1)S(1)}, u32[]{:S(2)}, u32[]{:S(2)}) %collective-permute-start.15) | collective-permute-done | bytes 786464 | tf_op jit(solution)/shard_map/ppermute | solution.py:227
  92.4 1.1 copy-done.1
  93.5 0.9 shard_map.98
  94.4 2.8 %collective-permute-start.16 = (bf16[4,12,96,128]{3,2,1,0:T(8,128)(2,1)S(1)}, bf16[4,12,96,128]{3,2,1,0:T(8,128)(2,1)S(1)}, u32[]{:S(2)}, u32[]{:S(2)}) collective-permute-start(bf16[4,12,96,128]{3,2,1,0:T(8,128)(2,1)S(1)} %shard_map.98), channel_id=1, source_target_pairs={{0,32},{8,136},{16,48},{24,152},{32,0},{40,168},{48,16},{56,184},{... | collective-permute-start | bytes 3538952 | tf_op jit(solution)/shard_map/ppermute | solution.py:241
  97.2 0.9 shard_map.99
  98.0 0.6 collective-permute-start.17
  98.7 0.9 shard_map.100
  99.5 2.4 %collective-permute-start.18 = (bf16[4,12,96,128]{3,2,1,0:T(8,128)(2,1)S(1)}, bf16[4,12,96,128]{3,2,1,0:T(8,128)(2,1)S(1)}, u32[]{:S(2)}, u32[]{:S(2)}) collective-permute-start(bf16[4,12,96,128]{3,2,1,0:T(8,128)(2,1)S(1)} %shard_map.100), channel_id=1, source_target_pairs={{0,48},{8,200},{16,0},{24,216},{32,16},{40,232},{48,32},{56,248},{... | collective-permute-start | bytes 3538952 | tf_op jit(solution)/shard_map/ppermute | solution.py:241
  102.0 0.9 shard_map.97
  102.9 8.5 %collective-permute-done.16 = bf16[4,12,96,128]{3,2,1,0:T(8,128)(2,1)S(1)} collective-permute-done((bf16[4,12,96,128]{3,2,1,0:T(8,128)(2,1)S(1)}, bf16[4,12,96,128]{3,2,1,0:T(8,128)(2,1)S(1)}, u32[]{:S(2)}, u32[]{:S(2)}) %collective-permute-start.16) | collective-permute-done | bytes 1179680 | tf_op jit(solution)/shard_map/ppermute | solution.py:241
  111.4 12.7 %collective-permute-done.17 = bf16[4,12,96,128]{3,2,1,0:T(8,128)(2,1)S(1)} collective-permute-done((bf16[4,12,96,128]{3,2,1,0:T(8,128)(2,1)S(1)}, bf16[4,12,96,128]{3,2,1,0:T(8,128)(2,1)S(1)}, u32[]{:S(2)}, u32[]{:S(2)}) %collective-permute-start.17) | collective-permute-done | bytes 1179680 | tf_op jit(solution)/shard_map/ppermute | solution.py:241
  124.1 0.5 fusion.3
  124.6 0.5 copy-done.8
  125.5 2.2 %collective-permute-start.19 = (bf16[12,96,128]{2,1,0:T(8,128)(2,1)S(1)}, bf16[12,96,128]{2,1,0:T(8,128)(2,1)S(1)}, u32[]{:S(2)}, u32[]{:S(2)}) collective-permute-start(bf16[12,96,128]{2,1,0:T(8,128)(2,1)S(1)} %get-tuple-element.24), channel_id=1, source_target_pairs={{0,128},{8,40},{16,144},{24,56},{32,160},{40,8},{48,176},{56,24},{... | collective-permute-start | bytes 884744 | tf_op jit(solution)/shard_map/ppermute | solution.py:241
  127.8 0.9 collective-permute-start.21
  128.6 0.6 collective-permute-start.20
  129.2 3.7 %reduce-scatter.2.cloned.1.call-done = bf16[1,8,2,32,384]{4,3,2,1,0:T(8,128)(2,1)} async-done(((bf16[8,8,2,32,384]{4,3,2,1,0:T(8,128)(2,1)}), bf16[1,8,2,32,384]{4,3,2,1,0:T(8,128)(2,1)}) %reduce-scatter.2.cloned.1.call-update) | async-done | bytes 393232 | tf_op jit(solution)/shard_map/reduce_scatter | solution.py:334
  132.9 7.7 %all-to-all-start.1 = ((bf16[8,2,32,384]{3,2,1,0:T(8,128)(2,1)}), bf16[8,2,32,384]{3,2,1,0:T(8,128)(2,1)S(1)}, u32[]{:S(2)}, u32[]{:S(2)}) async-start(bf16[8,2,32,384]{3,2,1,0:T(8,128)(2,1)} %bitcast.42), calls=%async_computation.2 | async-start | bytes 786432 | tf_op jit(solution)/shard_map/all_to_all | solution.py:349
  140.6 1.5 fusion.1
  142.1 0.8 slice.98
  142.9 0.7 slice_bitcast_fusion
  143.6 5.1 %all-to-all-done.1.refs_0_ = bf16[8,2,32,384]{3,2,1,0:T(8,128)(2,1)S(1)} async-done(((bf16[8,2,32,384]{3,2,1,0:T(8,128)(2,1)}), bf16[8,2,32,384]{3,2,1,0:T(8,128)(2,1)S(1)}, u32[]{:S(2)}, u32[]{:S(2)}) %all-to-all-start.1) | async-done | bytes 393248 | tf_op jit(solution)/shard_map/all_to_all | solution.py:349
  148.7 2.5 %shard_map.96 = (bf16[2,128,384]{2,1,0:T(8,128)(2,1)}, bf16[2,3,128,384]{3,2,1,0:T(8,128)(2,1)}) custom-call(s32[1,16]{1,0:T(1,128)S(1)} %copy-done.5, s32[1,8]{1,0:T(1,128)S(1)} %copy-done.6, bf16[2,3,128,384]{3,2,1,0:T(8,128)(2,1)S(1)} %bitcast.32, bf16[2,128,384]{2,1,0:T(8,128)(2,1)S(1)} %bitcast.34, bf16[8,2,32,384]{3,2,1,0:T(8,128)(2,1)S(1)} %all-to-all-done.1.refs_0_), custom_call_target="tpu_custom_call" | custom-call | tf_op jit(solution)/shard_map/pallas_call | solution.py:350
  (71 shorter events, 1.0 us)
Async XLA Ops:
  7.2 69.1 %all-gather.2.cloned.1.call-start = ((), (), s32[]{:S(2)}) async-start(), calls=%async_computation.3 | async-start | bytes 9732096 | tf_op jit(solution)/shard_map/all_gather | solution.py:275
  8.9 123.9 %reduce-scatter.2.cloned.1.call-start = ((), (), s32[]{:S(2)}) async-start(), calls=%async_computation.4 | async-start | bytes 3538944 | tf_op jit(solution)/shard_map/reduce_scatter | solution.py:334
  27.6 32.7 %copy-start.10 = (bf16[8,1,2,16,384]{4,3,2,1,0:T(8,128)(2,1)}, bf16[8,1,2,16,384]{4,3,2,1,0:T(8,128)(2,1)S(1)}, u32[]{:S(2)}) copy-start(bf16[8,1,2,16,384]{4,3,2,1,0:T(8,128)(2,1)S(1)} %get-tuple-element.27) | copy-start | bytes 589828
  27.6 32.7 %copy-start.11 = (bf16[8,1,2,16,384]{4,3,2,1,0:T(8,128)(2,1)}, bf16[8,1,2,16,384]{4,3,2,1,0:T(8,128)(2,1)S(1)}, u32[]{:S(2)}) copy-start(bf16[8,1,2,16,384]{4,3,2,1,0:T(8,128)(2,1)S(1)} %get-tuple-element.28) | copy-start | bytes 589828
  27.7 9.3 %collective-permute-start.3 = (bf16[256,384]{1,0:T(8,128)(2,1)S(1)}, bf16[256,384]{1,0:T(8,128)(2,1)S(1)}, u32[]{:S(2)}, u32[]{:S(2)}) collective-permute-start(bf16[256,384]{1,0:T(8,128)(2,1)S(1)} %bitcast.38), channel_id=1, source_target_pairs={{0,1},{1,2},{2,3},{3,4},{4,5},{5,6},{6,7},{7,0},{8,9},{9,10},{10,1... | collective-permute-start | bytes 589832 | tf_op jit(solution)/shard_map/ppermute | solution.py:223
  28.6 8.4 %collective-permute-start.7 = (bf16[256,384]{1,0:T(8,128)(2,1)S(1)}, bf16[256,384]{1,0:T(8,128)(2,1)S(1)}, u32[]{:S(2)}, u32[]{:S(2)}) collective-permute-start(bf16[256,384]{1,0:T(8,128)(2,1)S(1)} %bitcast.35), channel_id=1, source_target_pairs={{0,7},{1,0},{2,1},{3,2},{4,3},{5,4},{6,5},{7,6},{8,15},{9,8},{10,9... | collective-permute-start | bytes 589832 | tf_op jit(solution)/shard_map/ppermute | solution.py:223
  32.6 7.6 %collective-permute-start = (bf16[256,384]{1,0:T(8,128)(2,1)S(1)}, bf16[256,384]{1,0:T(8,128)(2,1)S(1)}, u32[]{:S(2)}, u32[]{:S(2)}) collective-permute-start(bf16[256,384]{1,0:T(8,128)(2,1)S(1)} %bitcast.39), channel_id=1, source_target_pairs={{0,7},{1,0},{2,1},{3,2},{4,3},{5,4},{6,5},{7,6},{8,15},{9,8},{10,9... | collective-permute-start | bytes 589832 | tf_op jit(solution)/shard_map/ppermute | solution.py:223
  34.0 9.7 %collective-permute-start.11 = (bf16[256,384]{1,0:T(8,128)(2,1)S(1)}, bf16[256,384]{1,0:T(8,128)(2,1)S(1)}, u32[]{:S(2)}, u32[]{:S(2)}) collective-permute-start(bf16[256,384]{1,0:T(8,128)(2,1)S(1)} %bitcast.36), channel_id=1, source_target_pairs={{0,1},{1,2},{2,3},{3,4},{4,5},{5,6},{6,7},{7,0},{8,9},{9,10},{10,1... | collective-permute-start | bytes 589832 | tf_op jit(solution)/shard_map/ppermute | solution.py:223
  36.9 23.5 %copy-start.12 = (bf16[256,384]{1,0:T(8,128)(2,1)}, bf16[256,384]{1,0:T(8,128)(2,1)S(1)}, u32[]{:S(2)}) copy-start(bf16[256,384]{1,0:T(8,128)(2,1)S(1)} %collective-permute-done.3.refs_7_) | copy-start | bytes 589828
  36.9 8.1 %collective-permute-start.4 = (bf16[256,384]{1,0:T(8,128)(2,1)S(1)}, bf16[256,384]{1,0:T(8,128)(2,1)S(1)}, u32[]{:S(2)}, u32[]{:S(2)}) collective-permute-start(bf16[256,384]{1,0:T(8,128)(2,1)S(1)} %collective-permute-done.3.refs_7_), channel_id=1, source_target_pairs={{0,1},{1,2},{2,3},{3,4},{4,5},{5,6},{6,7},{7,0},{8,9},{9,10},{10,1... | collective-permute-start | bytes 589832 | tf_op jit(solution)/shard_map/ppermute | solution.py:223
  36.9 23.5 %copy-start.13 = (bf16[256,384]{1,0:T(8,128)(2,1)}, bf16[256,384]{1,0:T(8,128)(2,1)S(1)}, u32[]{:S(2)}) copy-start(bf16[256,384]{1,0:T(8,128)(2,1)S(1)} %collective-permute-done.7.refs_9_) | copy-start | bytes 589828
  37.0 8.1 %collective-permute-start.8 = (bf16[256,384]{1,0:T(8,128)(2,1)S(1)}, bf16[256,384]{1,0:T(8,128)(2,1)S(1)}, u32[]{:S(2)}, u32[]{:S(2)}) collective-permute-start(bf16[256,384]{1,0:T(8,128)(2,1)S(1)} %collective-permute-done.7.refs_9_), channel_id=1, source_target_pairs={{0,7},{1,0},{2,1},{3,2},{4,3},{5,4},{6,5},{7,6},{8,15},{9,8},{10,9... | collective-permute-start | bytes 589832 | tf_op jit(solution)/shard_map/ppermute | solution.py:223
  40.2 20.2 %copy-start.14 = (bf16[256,384]{1,0:T(8,128)(2,1)}, bf16[256,384]{1,0:T(8,128)(2,1)S(1)}, u32[]{:S(2)}) copy-start(bf16[256,384]{1,0:T(8,128)(2,1)S(1)} %collective-permute-done.refs_1_) | copy-start | bytes 589828
  40.2 7.7 %collective-permute-start.1 = (bf16[256,384]{1,0:T(8,128)(2,1)S(1)}, bf16[256,384]{1,0:T(8,128)(2,1)S(1)}, u32[]{:S(2)}, u32[]{:S(2)}) collective-permute-start(bf16[256,384]{1,0:T(8,128)(2,1)S(1)} %collective-permute-done.refs_1_), channel_id=1, source_target_pairs={{0,7},{1,0},{2,1},{3,2},{4,3},{5,4},{6,5},{7,6},{8,15},{9,8},{10,9... | collective-permute-start | bytes 589832 | tf_op jit(solution)/shard_map/ppermute | solution.py:223
  43.7 16.7 %copy-start.15 = (bf16[256,384]{1,0:T(8,128)(2,1)}, bf16[256,384]{1,0:T(8,128)(2,1)S(1)}, u32[]{:S(2)}) copy-start(bf16[256,384]{1,0:T(8,128)(2,1)S(1)} %collective-permute-done.11.refs_15_) | copy-start | bytes 589828
  43.7 7.7 %collective-permute-start.12 = (bf16[256,384]{1,0:T(8,128)(2,1)S(1)}, bf16[256,384]{1,0:T(8,128)(2,1)S(1)}, u32[]{:S(2)}, u32[]{:S(2)}) collective-permute-start(bf16[256,384]{1,0:T(8,128)(2,1)S(1)} %collective-permute-done.11.refs_15_), channel_id=1, source_target_pairs={{0,1},{1,2},{2,3},{3,4},{4,5},{5,6},{6,7},{7,0},{8,9},{9,10},{10,1... | collective-permute-start | bytes 589832 | tf_op jit(solution)/shard_map/ppermute | solution.py:223
  45.0 15.4 %copy-start.16 = (bf16[256,384]{1,0:T(8,128)(2,1)}, bf16[256,384]{1,0:T(8,128)(2,1)S(1)}, u32[]{:S(2)}) copy-start(bf16[256,384]{1,0:T(8,128)(2,1)S(1)} %collective-permute-done.4.refs_6_) | copy-start | bytes 589828
  45.0 7.2 %collective-permute-start.5 = (bf16[256,384]{1,0:T(8,128)(2,1)S(1)}, bf16[256,384]{1,0:T(8,128)(2,1)S(1)}, u32[]{:S(2)}, u32[]{:S(2)}) collective-permute-start(bf16[256,384]{1,0:T(8,128)(2,1)S(1)} %collective-permute-done.4.refs_6_), channel_id=1, source_target_pairs={{0,1},{1,2},{2,3},{3,4},{4,5},{5,6},{6,7},{7,0},{8,9},{9,10},{10,1... | collective-permute-start | bytes 589832 | tf_op jit(solution)/shard_map/ppermute | solution.py:223
  45.0 15.4 %copy-start.17 = (bf16[256,384]{1,0:T(8,128)(2,1)}, bf16[256,384]{1,0:T(8,128)(2,1)S(1)}, u32[]{:S(2)}) copy-start(bf16[256,384]{1,0:T(8,128)(2,1)S(1)} %collective-permute-done.8.refs_10_) | copy-start | bytes 589828
  45.0 7.2 %collective-permute-start.9 = (bf16[256,384]{1,0:T(8,128)(2,1)S(1)}, bf16[256,384]{1,0:T(8,128)(2,1)S(1)}, u32[]{:S(2)}, u32[]{:S(2)}) collective-permute-start(bf16[256,384]{1,0:T(8,128)(2,1)S(1)} %collective-permute-done.8.refs_10_), channel_id=1, source_target_pairs={{0,7},{1,0},{2,1},{3,2},{4,3},{5,4},{6,5},{7,6},{8,15},{9,8},{10,9... | collective-permute-start | bytes 589832 | tf_op jit(solution)/shard_map/ppermute | solution.py:223
  47.9 12.6 %copy-start.18 = (bf16[256,384]{1,0:T(8,128)(2,1)}, bf16[256,384]{1,0:T(8,128)(2,1)S(1)}, u32[]{:S(2)}) copy-start(bf16[256,384]{1,0:T(8,128)(2,1)S(1)} %collective-permute-done.1.refs_2_) | copy-start | bytes 589828
  47.9 8.3 %collective-permute-start.2 = (bf16[256,384]{1,0:T(8,128)(2,1)S(1)}, bf16[256,384]{1,0:T(8,128)(2,1)S(1)}, u32[]{:S(2)}, u32[]{:S(2)}) collective-permute-start(bf16[256,384]{1,0:T(8,128)(2,1)S(1)} %collective-permute-done.1.refs_2_), channel_id=1, source_target_pairs={{0,7},{1,0},{2,1},{3,2},{4,3},{5,4},{6,5},{7,6},{8,15},{9,8},{10,9... | collective-permute-start | bytes 589832 | tf_op jit(solution)/shard_map/ppermute | solution.py:223
  51.4 9.1 %copy-start.19 = (bf16[256,384]{1,0:T(8,128)(2,1)}, bf16[256,384]{1,0:T(8,128)(2,1)S(1)}, u32[]{:S(2)}) copy-start(bf16[256,384]{1,0:T(8,128)(2,1)S(1)} %collective-permute-done.12.refs_14_) | copy-start | bytes 589828
  51.4 6.9 %collective-permute-start.13 = (bf16[256,384]{1,0:T(8,128)(2,1)S(1)}, bf16[256,384]{1,0:T(8,128)(2,1)S(1)}, u32[]{:S(2)}, u32[]{:S(2)}) collective-permute-start(bf16[256,384]{1,0:T(8,128)(2,1)S(1)} %collective-permute-done.12.refs_14_), channel_id=1, source_target_pairs={{0,1},{1,2},{2,3},{3,4},{4,5},{5,6},{6,7},{7,0},{8,9},{9,10},{10,1... | collective-permute-start | bytes 589832 | tf_op jit(solution)/shard_map/ppermute | solution.py:223
  52.2 8.3 %copy-start.20 = (bf16[256,384]{1,0:T(8,128)(2,1)}, bf16[256,384]{1,0:T(8,128)(2,1)S(1)}, u32[]{:S(2)}) copy-start(bf16[256,384]{1,0:T(8,128)(2,1)S(1)} %collective-permute-done.5.refs_5_) | copy-start | bytes 589828
  52.2 8.2 %collective-permute-start.6 = (bf16[256,384]{1,0:T(8,128)(2,1)S(1)}, bf16[256,384]{1,0:T(8,128)(2,1)S(1)}, u32[]{:S(2)}, u32[]{:S(2)}) collective-permute-start(bf16[256,384]{1,0:T(8,128)(2,1)S(1)} %collective-permute-done.5.refs_5_), channel_id=1, source_target_pairs={{0,1},{1,2},{2,3},{3,4},{4,5},{5,6},{6,7},{7,0},{8,9},{9,10},{10,1... | collective-permute-start | bytes 589832 | tf_op jit(solution)/shard_map/ppermute | solution.py:223
  52.2 8.3 %copy-start.21 = (bf16[256,384]{1,0:T(8,128)(2,1)}, bf16[256,384]{1,0:T(8,128)(2,1)S(1)}, u32[]{:S(2)}) copy-start(bf16[256,384]{1,0:T(8,128)(2,1)S(1)} %collective-permute-done.9.refs_11_) | copy-start | bytes 589828
  52.2 8.1 %collective-permute-start.10 = (bf16[256,384]{1,0:T(8,128)(2,1)S(1)}, bf16[256,384]{1,0:T(8,128)(2,1)S(1)}, u32[]{:S(2)}, u32[]{:S(2)}) collective-permute-start(bf16[256,384]{1,0:T(8,128)(2,1)S(1)} %collective-permute-done.9.refs_11_), channel_id=1, source_target_pairs={{0,7},{1,0},{2,1},{3,2},{4,3},{5,4},{6,5},{7,6},{8,15},{9,8},{10,9... | collective-permute-start | bytes 589832 | tf_op jit(solution)/shard_map/ppermute | solution.py:223
  56.2 4.3 %copy-start.22 = (bf16[256,384]{1,0:T(8,128)(2,1)}, bf16[256,384]{1,0:T(8,128)(2,1)S(1)}, u32[]{:S(2)}) copy-start(bf16[256,384]{1,0:T(8,128)(2,1)S(1)} %collective-permute-done.2.refs_3_) | copy-start | bytes 589828
  58.3 2.2 %copy-start.23 = (bf16[256,384]{1,0:T(8,128)(2,1)}, bf16[256,384]{1,0:T(8,128)(2,1)S(1)}, u32[]{:S(2)}) copy-start(bf16[256,384]{1,0:T(8,128)(2,1)S(1)} %collective-permute-done.13.refs_13_) | copy-start | bytes 589828
  67.5 8.7 %collective-permute-start.14 = (bf16[2,1536,256]{2,1,0:T(8,128)(2,1)}, bf16[2,1536,256]{2,1,0:T(8,128)(2,1)S(1)}, u32[]{:S(2)}, u32[]{:S(2)}) collective-permute-start(bf16[2,1536,256]{2,1,0:T(8,128)(2,1)} %get-tuple-element.15), channel_id=1, source_target_pairs={{0,8},{8,0},{16,24},{24,16},{32,40},{40,32},{48,56},{56,48},{1,9},... | collective-permute-start | bytes 4718600 | tf_op jit(solution)/shard_map/ppermute | solution.py:227
  89.8 2.6 %copy-start = (bf16[2,1536,256]{2,1,0:T(8,128)(2,1)S(1)}, bf16[2,1536,256]{2,1,0:T(8,128)(2,1)}, u32[]{:S(2)}) copy-start(bf16[2,1536,256]{2,1,0:T(8,128)(2,1)} %get-tuple-element.21.refs_0_) | copy-start | bytes 4718596
  89.8 2.6 %collective-permute-start.15 = (bf16[256,1536]{1,0:T(8,128)(2,1)}, bf16[256,1536]{1,0:T(8,128)(2,1)S(1)}, u32[]{:S(2)}, u32[]{:S(2)}) collective-permute-start(bf16[256,1536]{1,0:T(8,128)(2,1)} %get-tuple-element.23.refs_2_), channel_id=1, source_target_pairs={{0,8},{8,0},{16,24},{24,16},{32,40},{40,32},{48,56},{56,48},{1,9},... | collective-permute-start | bytes 2359304 | tf_op jit(solution)/shard_map/ppermute | solution.py:227
  92.4 1.1 copy-start.1
  94.4 17.0 %collective-permute-start.16 = (bf16[4,12,96,128]{3,2,1,0:T(8,128)(2,1)S(1)}, bf16[4,12,96,128]{3,2,1,0:T(8,128)(2,1)S(1)}, u32[]{:S(2)}, u32[]{:S(2)}) collective-permute-start(bf16[4,12,96,128]{3,2,1,0:T(8,128)(2,1)S(1)} %shard_map.98), channel_id=1, source_target_pairs={{0,32},{8,136},{16,48},{24,152},{32,0},{40,168},{48,16},{56,184},{... | collective-permute-start | bytes 3538952 | tf_op jit(solution)/shard_map/ppermute | solution.py:241
  98.0 26.0 %collective-permute-start.17 = (bf16[4,12,96,128]{3,2,1,0:T(8,128)(2,1)S(1)}, bf16[4,12,96,128]{3,2,1,0:T(8,128)(2,1)S(1)}, u32[]{:S(2)}, u32[]{:S(2)}) collective-permute-start(bf16[4,12,96,128]{3,2,1,0:T(8,128)(2,1)S(1)} %shard_map.99), channel_id=1, source_target_pairs={{0,16},{8,72},{16,32},{24,88},{32,48},{40,104},{48,0},{56,120},{64... | collective-permute-start | bytes 3538952 | tf_op jit(solution)/shard_map/ppermute | solution.py:241
  99.5 24.6 %collective-permute-start.18 = (bf16[4,12,96,128]{3,2,1,0:T(8,128)(2,1)S(1)}, bf16[4,12,96,128]{3,2,1,0:T(8,128)(2,1)S(1)}, u32[]{:S(2)}, u32[]{:S(2)}) collective-permute-start(bf16[4,12,96,128]{3,2,1,0:T(8,128)(2,1)S(1)} %shard_map.100), channel_id=1, source_target_pairs={{0,48},{8,200},{16,0},{24,216},{32,16},{40,232},{48,32},{56,248},{... | collective-permute-start | bytes 3538952 | tf_op jit(solution)/shard_map/ppermute | solution.py:241
  102.9 21.8 %copy-start.2 = (bf16[4,12,96,128]{3,2,1,0:T(8,128)(2,1)}, bf16[4,12,96,128]{3,2,1,0:T(8,128)(2,1)S(1)}, u32[]{:S(2)}) copy-start(bf16[4,12,96,128]{3,2,1,0:T(8,128)(2,1)S(1)} %shard_map.97) | copy-start | bytes 3538948
  111.4 13.2 %copy-start.7 = (bf16[4,12,96,128]{3,2,1,0:T(8,128)(2,1)}, bf16[4,12,96,128]{3,2,1,0:T(8,128)(2,1)S(1)}, u32[]{:S(2)}) copy-start(bf16[4,12,96,128]{3,2,1,0:T(8,128)(2,1)S(1)} %collective-permute-done.16) | copy-start | bytes 3538948
  124.1 1.4 copy-start.9
  125.5 15.0 %collective-permute-start.19 = (bf16[12,96,128]{2,1,0:T(8,128)(2,1)S(1)}, bf16[12,96,128]{2,1,0:T(8,128)(2,1)S(1)}, u32[]{:S(2)}, u32[]{:S(2)}) collective-permute-start(bf16[12,96,128]{2,1,0:T(8,128)(2,1)S(1)} %get-tuple-element.24), channel_id=1, source_target_pairs={{0,128},{8,40},{16,144},{24,56},{32,160},{40,8},{48,176},{56,24},{... | collective-permute-start | bytes 884744 | tf_op jit(solution)/shard_map/ppermute | solution.py:241
  127.8 12.8 %collective-permute-start.21 = (bf16[12,96,128]{2,1,0:T(8,128)(2,1)S(1)}, bf16[12,96,128]{2,1,0:T(8,128)(2,1)S(1)}, u32[]{:S(2)}, u32[]{:S(2)}) collective-permute-start(bf16[12,96,128]{2,1,0:T(8,128)(2,1)S(1)} %get-tuple-element.25), channel_id=1, source_target_pairs={{0,192},{8,56},{16,208},{24,8},{32,224},{40,24},{48,240},{56,40},{... | collective-permute-start | bytes 884744 | tf_op jit(solution)/shard_map/ppermute | solution.py:241
  128.6 11.9 %collective-permute-start.20 = (bf16[12,96,128]{2,1,0:T(8,128)(2,1)S(1)}, bf16[12,96,128]{2,1,0:T(8,128)(2,1)S(1)}, u32[]{:S(2)}, u32[]{:S(2)}) collective-permute-start(bf16[12,96,128]{2,1,0:T(8,128)(2,1)S(1)} %get-tuple-element.26), channel_id=1, source_target_pairs={{0,64},{8,24},{16,80},{24,40},{32,96},{40,56},{48,112},{56,8},{64,... | collective-permute-start | bytes 884744 | tf_op jit(solution)/shard_map/ppermute | solution.py:241
  132.9 15.7 %all-to-all-start.1 = ((bf16[8,2,32,384]{3,2,1,0:T(8,128)(2,1)}), bf16[8,2,32,384]{3,2,1,0:T(8,128)(2,1)S(1)}, u32[]{:S(2)}, u32[]{:S(2)}) async-start(bf16[8,2,32,384]{3,2,1,0:T(8,128)(2,1)} %bitcast.42), calls=%async_computation.2 | async-start | bytes 786432 | tf_op jit(solution)/shard_map/all_to_all | solution.py:349
  142.1 6.6 %copy-start.3 = (bf16[1,2,128,3,384]{4,2,3,1,0:T(8,128)(2,1)S(1)}, bf16[1,2,128,3,384]{4,2,3,1,0:T(8,128)(2,1)}, u32[]{:S(2)}) copy-start(bf16[1,2,128,3,384]{4,2,3,1,0:T(8,128)(2,1)} %param.6) | copy-start | bytes 1769476
  142.1 6.6 %copy-start.4 = (bf16[1,2,128,384]{3,2,1,0:T(8,128)(2,1)S(1)}, bf16[1,2,128,384]{3,2,1,0:T(8,128)(2,1)}, u32[]{:S(2)}) copy-start(bf16[1,2,128,384]{3,2,1,0:T(8,128)(2,1)} %param.9) | copy-start | bytes 589828
  142.1 6.6 %copy-start.5 = (s32[1,16]{1,0:T(1,128)S(1)}, s32[1,16]{1,0:T(1,128)}, u32[]{:S(2)}) copy-start(s32[1,16]{1,0:T(1,128)} %row_ref.3) | copy-start | bytes 196
  142.1 6.5 %copy-start.6 = (s32[1,8]{1,0:T(1,128)S(1)}, s32[1,8]{1,0:T(1,128)}, u32[]{:S(2)}) copy-start(s32[1,8]{1,0:T(1,128)} %patch_ref.3) | copy-start | bytes 100
  (3 other events, 2.4 us)
Sparse Core Ops, SparseCore 0:
  11.2 64.8 all-gather.1
  89.9 42.9 reduce-scatter.1
